TPU v7x, 256 devices: a whole 4x4x8 slice. The times are simulated.
256 devices in a mesh: grp: 8 (over z), head: 32 (over y, x, core).
Axes of the slice: x: 4, y: 4, z: 8, core: 2. Of those that a mesh axis runs over, the one named last changes fastest.
Arguments:
- prefill_rows: bfloat16 [4096, 8192], P(('grp', 'head')), may hold values from -300 to 300
- row_group: int32 [4096], P(('grp', 'head')), may hold values from 0 to 7, as said below
- lengths: int32 [8, 16], replicated, may hold values from 1 to 128, 512 in all within a row
- decode_state: float32 [128, 8192], P('grp'), may hold values from -300 to 300
- norm_gain: float32 [8192], replicated, may hold values from 0.1 to 1.9
- w_query: bfloat16 [8192, 4096], P(None, 'head'), may hold values from -1 to 1
- w_key: bfloat16 [8192, 4096], P(None, 'head'), may hold values from -1 to 1
- w_value: bfloat16 [8192, 4096], P(None, 'head'), may hold values from -0.0625 to 0.0625
- w_out: bfloat16 [4096, 8192], P('head'), may hold values from -0.09375 to 0.09375
Outputs:
- final_state: float32 [128, 8192], P('grp', 'head')
Inputs may be any that keep to these rules, and one draw needn't show every extreme that they name: `row_group`: each device's 16 rows name any one group at most 3 times, and some device names some group exactly 3 times; over all devices every group is named exactly 512 times.
All inputs are finite; a program needn't handle non-finite values.
Results may differ from a plain program's by a relative error of at most 0.006.
Values may be sent and summed in bfloat16 or wider, within the bound.
No kernel may reach another device: no remote copies, remote signals or barrier semaphores. Data moves between devices by JAX's collectives and lax.ppermute only.
A program may use at most 64 MiB of HBM per device.

v0:
```python
import math

import jax
import jax.numpy as jnp
from jax import lax
from jax.sharding import PartitionSpec as P

HD = 128
STEPS = 4


EPSILON = 1e-05
ROPE_BASE = 10000.0
MASKED = -1e30


def normed(values, norm_gain):
    widened = values.astype(jnp.float32)
    factor = lax.rsqrt(jnp.mean(widened * widened, axis=-1, keepdims=True) + EPSILON)
    return (widened * factor * norm_gain).astype(jnp.bfloat16)


def rotary(values, positions):
    head_size = HD
    half_size = head_size // 2
    shaped = values.reshape(values.shape[:-1] + (values.shape[-1] // head_size, head_size))
    frequency = jnp.exp(
        jnp.arange(half_size, dtype=jnp.float32) * (-2.0 * math.log(ROPE_BASE) / head_size)
    )
    angles = positions.astype(jnp.float32)[..., None] * frequency
    cosine = jnp.cos(angles)[..., None, :]
    sine_part = jnp.sin(angles)[..., None, :]
    first_half = shaped[..., :half_size]
    second_half = shaped[..., half_size:]
    turned = jnp.concatenate(
        [
            first_half * cosine - second_half * sine_part,
            second_half * cosine + first_half * sine_part,
        ],
        axis=-1,
    )
    return turned.reshape(values.shape)


def locate(groups, cell_ids, row_starts, row_ends):
    group_count = row_starts.shape[0]
    picked = groups[..., None] == jnp.arange(group_count, dtype=jnp.int32)
    first_cells = jnp.sum(jnp.where(picked[..., None], row_starts, 0), axis=-2)
    last_cells = jnp.sum(jnp.where(picked[..., None], row_ends, 0), axis=-2)
    inside = (cell_ids[..., None] >= first_cells) & (cell_ids[..., None] < last_cells)
    return jnp.sum(jnp.where(inside, cell_ids[..., None] - first_cells, 0), axis=-1)


def per_device(
    prefill_rows, row_group, lengths, decode_state, norm_gain, w_query, w_key, w_value, w_out
):
    group_count = lax.axis_size("grp")
    head_count = lax.axis_size("head")
    rows_local, width = prefill_rows.shape
    capacity = rows_local // group_count + rows_local // group_count // 2
    group_rows = rows_local * head_count
    requests = lengths.shape[1]
    kv_width = w_key.shape[1]
    local_heads = kv_width // HD
    my_group = lax.axis_index("grp")
    my_head = lax.axis_index("head")
    group_ids = jnp.arange(group_count, dtype=jnp.int32)
    slot_ids = jnp.arange(capacity, dtype=jnp.int32)
    row_ends = jnp.cumsum(lengths, axis=1)
    row_starts = row_ends - lengths
    chosen = group_ids == my_group
    counts_here = jnp.sum((row_group[:, None] == group_ids[None, :]).astype(jnp.int32), axis=0)
    counts_all = lax.all_gather(counts_here[None, :], ("grp", "head"), axis=0, tiled=True)
    first_all = jnp.cumsum(counts_all, axis=0) - counts_all
    my_counts = jnp.sum(jnp.where(chosen[None, :], counts_all, 0), axis=1)
    my_first = jnp.sum(jnp.where(chosen[None, :], first_all, 0), axis=1)
    normal_rows = normed(prefill_rows, norm_gain)
    matches = (row_group[..., None] == group_ids).astype(jnp.int32)
    earlier = jnp.cumsum(matches, axis=-2) - matches
    order = jnp.sum(earlier * matches, axis=-1)
    same_group = row_group[..., None, None, :] == group_ids[:, None, None]
    same_slot = order[..., None, None, :] == slot_ids[:, None]
    outgoing = jnp.einsum(
        "gkj,jd->gkd",
        (same_group & same_slot).astype(jnp.bfloat16),
        normal_rows,
        preferred_element_type=jnp.float32,
    ).astype(jnp.bfloat16)
    incoming = lax.all_to_all(outgoing, "grp", split_axis=0, concat_axis=0, tiled=True)
    piece = lax.all_gather(
        incoming.reshape(group_count * capacity, width), "head", axis=0, tiled=True
    )
    key_part = jnp.dot(piece, w_key, preferred_element_type=jnp.float32)
    value_part = jnp.dot(piece, w_value, preferred_element_type=jnp.float32)
    projected = jnp.concatenate([key_part, value_part], axis=1)
    projected = projected.reshape(head_count, group_count, capacity, 2 * kv_width)
    slot_counts = my_counts.reshape(group_count, head_count).T
    slot_first = my_first.reshape(group_count, head_count).T
    cell_ids = slot_first[..., None] + slot_ids
    positions = locate(jnp.zeros_like(cell_ids) + my_group, cell_ids, row_starts, row_ends)
    keys = rotary(projected[..., :kv_width], positions).astype(jnp.bfloat16)
    packed = jnp.concatenate([keys, projected[..., kv_width:].astype(jnp.bfloat16)], axis=-1)
    targets = jnp.where(slot_ids < slot_counts[..., None], cell_ids, group_rows).reshape(-1)
    cache = (
        jnp.zeros((group_rows, 2 * kv_width), jnp.bfloat16)
        .at[targets]
        .set(packed.reshape(-1, 2 * kv_width), mode="drop")
    )
    cache_keys = cache[:, :kv_width].reshape(group_rows, local_heads, HD)
    cache_values = cache[:, kv_width:].reshape(group_rows, local_heads, HD)
    my_lengths = jnp.sum(jnp.where(chosen[:, None], lengths, 0), axis=0)
    my_ends = jnp.sum(jnp.where(chosen[:, None], row_ends, 0), axis=0)
    segment = jnp.sum(
        (my_ends[None, :] <= jnp.arange(group_rows, dtype=jnp.int32)[:, None]).astype(jnp.int32),
        axis=1,
    )
    cache_mask = (segment[None, :] == jnp.arange(requests, dtype=jnp.int32)[:, None])[:, None, :]
    step_ids = jnp.arange(STEPS, dtype=jnp.int32)
    scale = HD ** (-0.5)
    new_keys = jnp.zeros((STEPS, requests, local_heads, HD), jnp.bfloat16)
    new_values = jnp.zeros((STEPS, requests, local_heads, HD), jnp.bfloat16)
    share_width = width // head_count
    current = decode_state
    decode_rows = normed(decode_state, norm_gain)
    for step in range(STEPS):
        positions_now = my_lengths + step
        query = (
            rotary(jnp.dot(decode_rows, w_query, preferred_element_type=jnp.float32), positions_now)
            .astype(jnp.bfloat16)
            .reshape(requests, local_heads, HD)
        )
        new_key = (
            rotary(jnp.dot(decode_rows, w_key, preferred_element_type=jnp.float32), positions_now)
            .astype(jnp.bfloat16)
            .reshape(requests, local_heads, HD)
        )
        new_value = (
            jnp.dot(decode_rows, w_value, preferred_element_type=jnp.float32)
            .astype(jnp.bfloat16)
            .reshape(requests, local_heads, HD)
        )
        new_keys = new_keys.at[step].set(new_key)
        new_values = new_values.at[step].set(new_value)
        cache_scores = (
            jnp.einsum("rhd,chd->rhc", query, cache_keys, preferred_element_type=jnp.float32)
            * scale
        )
        fresh_scores = (
            jnp.einsum("rhd,srhd->rhs", query, new_keys, preferred_element_type=jnp.float32) * scale
        )
        fresh_mask = step_ids <= step
        peak = jnp.maximum(
            jnp.max(jnp.where(cache_mask, cache_scores, MASKED), axis=-1),
            jnp.max(jnp.where(fresh_mask, fresh_scores, MASKED), axis=-1),
        )
        cache_exp = jnp.where(cache_mask, jnp.exp(cache_scores - peak[..., None]), 0.0)
        fresh_exp = jnp.where(fresh_mask, jnp.exp(fresh_scores - peak[..., None]), 0.0)
        total = jnp.sum(cache_exp, axis=-1) + jnp.sum(fresh_exp, axis=-1)
        cache_weights = (cache_exp / total[..., None]).astype(jnp.bfloat16)
        fresh_weights = (fresh_exp / total[..., None]).astype(jnp.bfloat16)
        attended = jnp.einsum(
            "rhc,chd->rhd", cache_weights, cache_values, preferred_element_type=jnp.float32
        )
        attended = attended + jnp.einsum(
            "rhs,srhd->rhd", fresh_weights, new_values, preferred_element_type=jnp.float32
        )
        attended = attended.astype(jnp.bfloat16).reshape(requests, kv_width)
        term = jnp.dot(attended, w_out, preferred_element_type=jnp.float32)
        current = current + lax.psum(term, "head")
        if step + 1 < STEPS:
            decode_rows = normed(current, norm_gain)
    return lax.dynamic_slice_in_dim(current, my_head * share_width, share_width, 1)


def solution(mesh):
    return jax.shard_map(
        per_device,
        mesh=mesh,
        in_specs=(
            P(("grp", "head"), None),
            P(("grp", "head")),
            P(),
            P("grp", None),
            P(),
            P(None, "head"),
            P(None, "head"),
            P(None, "head"),
            P("head", None),
        ),
        out_specs=P("grp", "head"),
        check_vma=False,
    )
```

profile of v0, /device:TPU:1, one launch (start us, length us, event | category | flops | bytes accessed | tf_op | source)
XLA Modules:
  0.0 637.7 jit_solution(1571259033235555692)
XLA Ops:
  6.5 0.8 iota_compare_fusion.4
  7.3 0.7 fusion.176
  8.1 1.1 fusion.31
  9.3 0.9 select_reduce_fusion.8
  10.1 1.3 convolution_convert_fusion
  11.4 0.3 copy.34
  11.8 24.9 %all_to_all.5 = bf16[8,3,8192]{2,1,0:T(4,128)(2,1)S(1)} all-to-all(bf16[8,3,8192]{2,1,0:T(4,128)(2,1)S(1)} %copy.34), channel_id=1, replica_groups=mesh['grp'=8,'head'=32] {'grp'}, dimensions={0} | all-to-all | bytes 786432 | tf_op jit(solution)/shard_map/all_to_all | solution.py:89
  36.7 1.1 reshape.1230
  38.1 0.2 dynamic-update-slice.30
  38.3 76.7 %all-reduce.2 = s32[2048]{0:T(1024)S(1)} all-reduce(s32[2048]{0:T(1024)S(1)} %dynamic-update-slice.30), channel_id=2, replica_groups=mesh['grp'=8,'head'=32] {'grp','head'}, use_global_device_ids=true, to_apply=%add.2 | all-reduce | flops 2048 | bytes 16384
  115.1 0.6 reduce-window.6
  115.7 0.2 slice_reduce_fusion
  117.0 0.2 select_n.114
  117.5 0.6 add_convert_fusion
  118.2 2.0 convolution_bitcast_fusion.10
  120.2 0.4 convolution_bitcast_fusion.11
  121.5 2.0 fusion.16
  123.5 0.6 fusion.195
  124.2 0.7 select_reduce_fusion.14
  124.8 9.6 %fusion.221 = f32[768,128]{0,1:T(8,128)S(1)} fusion(bf16[768,8192]{1,0:T(8,128)(2,1)} %all-gather.3.cloned.1.call-done, bf16[8192,128]{1,0:T(8,128)(2,1)} %param.32), kind=kOutput, calls=%fused_computation.317 | convolution fusion | flops 1610612736 | bytes 15073280 | tf_op jit(solution)/shard_map/dot_general | solution.py:94
  134.5 8.9 %fusion.220 = f32[768,128]{0,1:T(8,128)S(1)} fusion(bf16[768,8192]{1,0:T(8,128)(2,1)} %all-gather.3.cloned.1.call-done, bf16[8192,128]{1,0:T(8,128)(2,1)S(1)} %copy-done.4), kind=kOutput, calls=%fused_computation.316 | convolution fusion | flops 1610612736 | bytes 15073280 | tf_op jit(solution)/shard_map/dot_general | solution.py:93
  143.4 0.9 pad_maximum_fusion
  144.3 1.4 copy.35
  145.7 1.3 reshape.1231
  147.0 1.1 slice.299
  148.2 1.1 slice.296
  149.4 1.8 fusion.35
  151.4 0.2 copy.41
  151.6 1.1 reshape.1260
  152.7 6.0 scatter_custom_fusion
  158.7 0.3 select_reduce_fusion.7
  159.7 1.4 fusion.23
  161.1 108.2 %all-reduce.8.cloned.1.call-done = f32[16,8192]{1,0:T(8,128)} async-done(((f32[16,8192]{1,0:T(8,128)}), f32[16,8192]{1,0:T(8,128)}) %all-reduce.8.cloned.1.call-update) | async-done | bytes 524304 | tf_op jit(solution)/shard_map/psum | solution.py:169
  269.4 1.4 multiply_reduce_fusion.2
  270.9 0.2 copy-done.1
  271.1 0.4 fusion.18
  271.5 0.2 copy-done.5
  271.8 0.4 convolution_bitcast_fusion.8
  272.2 0.7 copy-done.9
  272.9 0.4 convolution_bitcast_fusion.9
  273.5 0.3 select_reduce_fusion.6
  274.8 1.4 fusion.24
  276.3 113.2 %all-reduce.10.cloned.1.call-done = f32[16,8192]{1,0:T(8,128)} async-done(((f32[16,8192]{1,0:T(8,128)}), f32[16,8192]{1,0:T(8,128)}) %all-reduce.10.cloned.1.call-update) | async-done | bytes 524304 | tf_op jit(solution)/shard_map/psum | solution.py:169
  389.5 1.4 multiply_reduce_fusion.1
  391.1 0.2 copy-done.2
  391.3 0.4 fusion.20
  391.7 0.2 copy-done.6
  391.9 0.4 convolution_bitcast_fusion.6
  392.3 0.7 copy-done.10
  393.0 0.4 convolution_bitcast_fusion.7
  393.6 0.3 select_reduce_fusion.5
  395.0 1.4 fusion.25
  396.5 113.2 %all-reduce.12.cloned.1.call-done = f32[16,8192]{1,0:T(8,128)} async-done(((f32[16,8192]{1,0:T(8,128)}), f32[16,8192]{1,0:T(8,128)}) %all-reduce.12.cloned.1.call-update) | async-done | bytes 524304 | tf_op jit(solution)/shard_map/psum | solution.py:169
  509.7 1.4 multiply_reduce_fusion
  511.2 0.2 copy-done.3
  511.5 0.4 fusion.22
  511.9 0.2 copy-done.7
  512.1 0.4 convolution_bitcast_fusion.4
  512.5 0.7 copy-done.11
  513.2 0.4 convolution_bitcast_fusion.5
  513.8 0.3 select_reduce_fusion.4
  515.1 1.4 fusion.26
  516.6 113.3 %all-reduce.14.cloned.1.call-done = f32[16,8192]{1,0:T(8,128)} async-done(((f32[16,8192]{1,0:T(8,128)}), f32[16,8192]{1,0:T(8,128)}) %all-reduce.14.cloned.1.call-update) | async-done | bytes 524304 | tf_op jit(solution)/shard_map/psum | solution.py:169
  629.8 1.3 dynamic-slice_add_fusion
  (147 shorter events, 7.8 us)
Async XLA Ops:
  6.5 153.1 %copy-start = (bf16[128,8192]{1,0:T(8,128)(2,1)S(1)}, bf16[128,8192]{1,0:T(8,128)(2,1)}, u32[]{:S(2)}) copy-start(bf16[128,8192]{1,0:T(8,128)(2,1)} %param.33) | copy-start | bytes 6291460
  6.5 118.3 %all-gather.3.cloned.1.call-start = ((), (), s32[]{:S(2)}) async-start(), calls=%async_computation.1 | async-start | bytes 12976128 | tf_op jit(solution)/shard_map/all_gather | solution.py:90
  8.1 29.8 %copy-start.14 = (s32[8,16]{1,0:T(8,128)S(1)}, s32[8,16]{1,0:T(8,128)}, u32[]{:S(2)}) copy-start(s32[8,16]{1,0:T(8,128)} %param.27) | copy-start | bytes 1540
  11.8 105.4 %copy-start.12 = (f32[16,8192]{1,0:T(8,128)S(1)}, f32[16,8192]{1,0:T(8,128)}, u32[]{:S(2)}) copy-start(f32[16,8192]{1,0:T(8,128)} %param.28) | copy-start | bytes 1572868
  11.8 106.3 %copy-start.13 = (f32[8192]{0:T(1024)S(1)}, f32[8192]{0:T(1024)}, u32[]{:S(2)}) copy-start(f32[8192]{0:T(1024)} %param.29) | copy-start | bytes 98308
  37.8 231.6 %all-reduce.8.cloned.1.call-start = ((), (), s32[]{:S(2)}) async-start(), calls=%async_computation.2 | async-start | bytes 1048576 | tf_op jit(solution)/shard_map/psum | solution.py:169
  117.2 3.0 copy-start.8
  117.2 3.4 copy-start.15
  121.5 13.0 %copy-start.18 = (pred[4]{0:T(512)(128)(4,1)}, pred[4]{0:T(512)(128)(4,1)S(1)}, u32[]{:S(2)}) copy-start(pred[4]{0:T(512)(128)(4,1)S(1)} %iota_compare_fusion.9) | copy-start | bytes 16
  124.8 9.6 %copy-start.4 = (bf16[8192,128]{1,0:T(8,128)(2,1)S(1)}, bf16[8192,128]{1,0:T(8,128)(2,1)}, u32[]{:S(2)}) copy-start(bf16[8192,128]{1,0:T(8,128)(2,1)} %param.31) | copy-start | bytes 6291460
  147.0 2.4 copy-start.16
  151.2 7.8 %copy-start.23 = (f32[16]{0:T(128)S(1)}, f32[16]{0:T(128)}, u32[]{:S(2)}) copy-start(f32[16]{0:T(128)} %select_reduce_fusion.14) | copy-start | bytes 196
  151.2 7.9 %copy-start.19 = (pred[4]{0:T(512)(128)(4,1)S(1)}, pred[4]{0:T(512)(128)(4,1)}, u32[]{:S(2)}) copy-start(pred[4]{0:T(512)(128)(4,1)} %copy-done.18) | copy-start | bytes 16
  161.1 228.4 %all-reduce.10.cloned.1.call-start = ((), (), s32[]{:S(2)}) async-start(), calls=%async_computation.3 | async-start | bytes 1048576 | tf_op jit(solution)/shard_map/psum | solution.py:169
  269.4 1.7 copy-start.1
  269.4 2.4 copy-start.5
  271.1 1.7 copy-start.9
  271.8 1.5 copy-start.17
  271.8 1.5 copy-start.22
  276.3 233.4 %all-reduce.12.cloned.1.call-start = ((), (), s32[]{:S(2)}) async-start(), calls=%async_computation.4 | async-start | bytes 1048576 | tf_op jit(solution)/shard_map/psum | solution.py:169
  389.5 1.7 copy-start.2
  389.5 2.4 copy-start.6
  391.3 1.7 copy-start.10
  391.9 1.5 copy-start.21
  396.4 233.4 %all-reduce.14.cloned.1.call-start = ((), (), s32[]{:S(2)}) async-start(), calls=%async_computation.5 | async-start | bytes 1048576 | tf_op jit(solution)/shard_map/psum | solution.py:169
  509.7 1.7 copy-start.3
  509.7 2.4 copy-start.7
  511.4 1.7 copy-start.11
  512.1 1.5 copy-start.20
Sparse Core Ops, SparseCore 0:
  38.0 66.6 all-gather.2
  161.2 108.1 all-reduce.7
  276.4 113.1 all-reduce.9
  396.5 113.1 all-reduce.11
  516.7 113.1 all-reduce.13
where the time goes:
time: 638 us
  waiting for transfers between devices  448 us (70%)
  blocking collectives  102 us (16%)
  matrix products  35.5 us (6%)
  local copies, waits for them, and re-layouts  19.7 us (3%)
  other arithmetic  18.9 us (3%)
  between operations  13.7 us (2%)
    psum x4, waiting for transfers between devices, per_device(): current = current + lax.psum(term, 'head')  448 us
    unnamed x1, blocking collectives  76.7 us
    all_to_all x1, blocking collectives, per_device(): lax.all_to_all(outgoing, 'grp', split_axis=0, concat_axis=0, tiled=True)  24.9 us
  transfers between devices with their start and end apart: 5, of which 4 were waited for; matrix products, arithmetic and copies ran while one was open for 2% of the time, Pallas kernels for 0%

commit v1 on v0

v1 whole, which is shorter than its diff:
```python
import math

import jax
import jax.numpy as jnp
from jax import lax
from jax.sharding import PartitionSpec as P

HD = 128
STEPS = 4
EPSILON = 1e-05
ROPE_BASE = 10000.0
MASKED = -1e30


def normed(values, norm_gain):
    widened = values.astype(jnp.float32)
    factor = lax.rsqrt(jnp.mean(widened * widened, axis=-1, keepdims=True) + EPSILON)
    return (widened * factor * norm_gain).astype(jnp.bfloat16)


def angles_of(positions):
    half = HD // 2
    frequency = jnp.exp(
        jnp.arange(half, dtype=jnp.float32) * (-2.0 * math.log(ROPE_BASE) / HD)
    )
    angles = positions.astype(jnp.float32)[..., None] * frequency
    cosine = jnp.cos(angles)
    sine = jnp.sin(angles)
    return (
        jnp.concatenate([cosine, cosine], axis=-1),
        jnp.concatenate([-sine, sine], axis=-1),
    )


def turned(values, cosine, sine):
    half = HD // 2
    swapped = jnp.concatenate([values[..., half:], values[..., :half]], axis=-1)
    return values * cosine + swapped * sine


def per_device(
    prefill_rows, row_group, lengths, decode_state, norm_gain, w_query, w_key, w_value, w_out
):
    groups = lax.axis_size("grp")
    heads = lax.axis_size("head")
    rows_local, width = prefill_rows.shape
    plane_rows = rows_local * heads
    cap = (rows_local // groups + rows_local // groups // 2) * heads
    requests = lengths.shape[1]
    my_group = lax.axis_index("grp")
    my_head = lax.axis_index("head")
    share = width // heads
    f32, bf16 = jnp.float32, jnp.bfloat16

    group_ids = jnp.arange(groups, dtype=jnp.int32)
    row_ends = jnp.cumsum(lengths, axis=1)
    row_starts = row_ends - lengths

    with jax.named_scope("rows"):
        normal_rows = normed(prefill_rows, norm_gain)
        plane = lax.all_gather(normal_rows, "head", axis=0, tiled=True)
    weights = jnp.concatenate([w_key, w_value, w_query], axis=1)

    with jax.named_scope("ids"):
        ids = lax.all_to_all(
            jnp.broadcast_to(row_group[None, :], (heads, rows_local)),
            "head", split_axis=0, concat_axis=0, tiled=True,
        ).reshape(plane_rows)
        match = ids[:, None] == group_ids[None, :]
        plane_counts = jnp.sum(match.astype(jnp.int32), axis=0)
        counts = lax.all_to_all(
            jnp.broadcast_to(plane_counts[None, :], (groups, groups)),
            "grp", split_axis=0, concat_axis=0, tiled=True,
        )
        first = jnp.cumsum(counts, axis=0) - counts
        lower = jnp.arange(plane_rows)[:, None] > jnp.arange(plane_rows)[None, :]
        order = jnp.dot(
            lower.astype(bf16), match.astype(bf16), preferred_element_type=f32
        ).astype(jnp.int32)
        order = jnp.sum(jnp.where(match, order, 0), axis=1)
        my_first = jnp.sum(jnp.where(group_ids[:, None] == my_group, first, 0), axis=0)
        cell = order + jnp.sum(jnp.where(match, my_first[None, :], 0), axis=1)
        starts = jnp.sum(jnp.where(match[:, :, None], row_starts[None], 0), axis=1)
        ends = jnp.sum(jnp.where(match[:, :, None], row_ends[None], 0), axis=1)
        inside = (cell[:, None] >= starts) & (cell[:, None] < ends)
        places = jnp.sum(jnp.where(inside, cell[:, None] - starts, 0), axis=1)
        slots = jnp.arange(cap, dtype=jnp.int32)
        pick = (
            (ids[None, None, :] == group_ids[:, None, None])
            & (order[None, None, :] == slots[None, :, None])
        ).astype(bf16)
        cosine, sine = angles_of(places)

    with jax.named_scope("project"):
        both = jnp.dot(plane, weights[:, : 2 * HD], preferred_element_type=f32)
        keys = turned(both[:, :HD], cosine, sine)
        packed = jnp.concatenate([keys, both[:, HD:]], axis=1).astype(bf16)
        outgoing = jnp.dot(
            pick.reshape(groups * cap, plane_rows), packed, preferred_element_type=f32
        ).astype(bf16)
        cache = lax.all_to_all(
            outgoing.reshape(groups, cap, 2 * HD), "grp", split_axis=0, concat_axis=0, tiled=True
        ).reshape(groups * cap, 2 * HD)

    mine = group_ids == my_group
    from_counts = jnp.sum(jnp.where(mine[None, :], counts, 0), axis=1)
    from_first = jnp.sum(jnp.where(mine[None, :], first, 0), axis=1)
    my_lengths = jnp.sum(jnp.where(mine[:, None], lengths, 0), axis=0)
    my_ends = jnp.sum(jnp.where(mine[:, None], row_ends, 0), axis=0)
    my_starts = my_ends - my_lengths
    slot_cell = jnp.where(
        slots[None, :] < from_counts[:, None], from_first[:, None] + slots[None, :], -1
    ).reshape(-1)
    mask = (slot_cell[None, :] >= my_starts[:, None]) & (slot_cell[None, :] < my_ends[:, None])
    cache_keys = cache[:, :HD]
    cache_values = cache[:, HD:]

    scale = HD ** (-0.5)
    new_keys, new_values = [], []
    current = lax.dynamic_slice_in_dim(decode_state, my_head * share, share, 1)
    my_gain = lax.dynamic_slice_in_dim(norm_gain, my_head * share, share, 0)
    inverse = 1.0 / norm_gain
    decode_rows = normed(decode_state, norm_gain)
    factor = None
    for step in range(STEPS):
        with jax.named_scope("decode"):
            projected = jnp.dot(decode_rows, weights, preferred_element_type=f32)
            if factor is not None:
                projected = projected * factor
            cos_now, sin_now = angles_of(my_lengths + step)
            new_key = turned(projected[:, :HD], cos_now, sin_now).astype(bf16)
            new_value = projected[:, HD : 2 * HD].astype(bf16)
            query = turned(projected[:, 2 * HD :], cos_now, sin_now).astype(bf16)
            new_keys.append(new_key)
            new_values.append(new_value)
            scores = jnp.einsum("rd,cd->rc", query, cache_keys, preferred_element_type=f32) * scale
            wide = query.astype(f32)
            fresh = jnp.stack(
                [jnp.sum(wide * k.astype(f32), axis=1) * scale for k in new_keys], axis=1
            )
            peak = jnp.maximum(
                jnp.max(jnp.where(mask, scores, MASKED), axis=1), jnp.max(fresh, axis=1)
            )
            cache_exp = jnp.where(mask, jnp.exp(scores - peak[:, None]), 0.0)
            fresh_exp = jnp.exp(fresh - peak[:, None])
            total = jnp.sum(cache_exp, axis=1) + jnp.sum(fresh_exp, axis=1)
            cache_weights = (cache_exp / total[:, None]).astype(bf16)
            fresh_weights = (fresh_exp / total[:, None]).astype(bf16).astype(f32)
            attended = jnp.dot(cache_weights, cache_values, preferred_element_type=f32)
            for back, value in enumerate(new_values):
                attended = attended + fresh_weights[:, back : back + 1] * value.astype(f32)
            term = jnp.dot(attended.astype(bf16), w_out, preferred_element_type=f32).astype(bf16)
        with jax.named_scope("sum"):
            parts = lax.all_to_all(
                term.reshape(requests, heads, share), "head", split_axis=1, concat_axis=1, tiled=True
            )
            current = current + jnp.sum(parts.astype(f32), axis=1)
        if step + 1 < STEPS:
            with jax.named_scope("spread"):
                piece = (current * my_gain[None, :]).astype(bf16)
                decode_rows = lax.all_to_all(
                    jnp.broadcast_to(piece[:, None, :], (requests, heads, share)),
                    "head", split_axis=1, concat_axis=1, tiled=True,
                ).reshape(requests, width)
                plain = decode_rows.astype(f32) * inverse
                factor = lax.rsqrt(jnp.mean(plain * plain, axis=1, keepdims=True) + EPSILON)
    return current


def solution(mesh):
    return jax.shard_map(
        per_device,
        mesh=mesh,
        in_specs=(
            P(("grp", "head"), None),
            P(("grp", "head")),
            P(),
            P("grp", None),
            P(),
            P(None, "head"),
            P(None, "head"),
            P(None, "head"),
            P("head", None),
        ),
        out_specs=P("grp", "head"),
        check_vma=False,
    )
```

time: 638 us -> 220 us (0.34)
  waiting for transfers between devices: 448 us -> 58.6 us
  blocking collectives: 102 us -> 62.3 us
  starting transfers between devices: 0.17 us -> 33 us
  matrix products: 35.5 us -> 24.1 us
  local copies, waits for them, and re-layouts: 19.7 us -> 12.1 us
    psum x4 -> x0, waiting for transfers between devices: 448 us -> none  [per_device(): current = current + lax.psum(term, 'head')]
    unnamed x1 -> x0, blocking collectives: 76.7 us -> none
    all_to_all x1 -> x5, blocking collectives: 24.9 us -> 62.3 us  [the longest x3 37.4 us: per_device(): lax.all_to_all(term.reshape(requests, heads, share), 'head', split_axis=1...]
    all_to_all x0 -> x5, waiting for transfers between devices: none -> 35.6 us  [the longest x1 12.8 us: per_device(): lax.all_to_all(outgoing.reshape(groups, cap, 2 * HD), 'grp', split_axis=0...]
    all_to_all x0 -> x5, starting transfers between devices: none -> 33 us  [the longest x1 8.59 us: per_device(): lax.all_to_all(jnp.broadcast_to(row_group[None, :], (heads, rows_local)),...]
    all_gather x1, waiting for transfers between devices: 0.01 us -> 23 us  [per_device(): plane = lax.all_gather(normal_rows, 'head', axis=0, tiled=True)]
    dot_general x31 -> x15, matrix products: 35.5 us -> 24.1 us  [the longest x4 12.1 us: per_device(): projected = jnp.dot(decode_rows, weights, preferred_element_type=f32)]
  transfers between devices with their start and end apart: 5 -> 6, of which waited for: 4 -> 5; matrix products, arithmetic and copies ran while one was open for 2% -> 8% of each run, Pallas kernels for 0% -> 0%
where the time goes in v1:
time: 220 us; the launch traced here: 219 us
  blocking collectives  62.3 us (28%)
  waiting for transfers between devices  58.6 us (27%)
  starting transfers between devices  33 us (15%)
  matrix products  24.1 us (11%)
  other arithmetic  15 us (7%)
  between operations  13.8 us (6%)
  local copies, waits for them, and re-layouts  12.1 us (6%)
    all_to_all x3, blocking collectives, per_device(): lax.all_to_all(term.reshape(requests, heads, share), 'head', split_axis=1...  37.4 us
    all_to_all x2, blocking collectives, per_device(): lax.all_to_all(jnp.broadcast_to(piece[:, None, :], (requests, heads, shar...  24.9 us
    all_gather x1, waiting for transfers between devices, per_device(): plane = lax.all_gather(normal_rows, 'head', axis=0, tiled=True)  23 us
    all_to_all x1, waiting for transfers between devices, per_device(): lax.all_to_all(outgoing.reshape(groups, cap, 2 * HD), 'grp', split_axis=0...  12.8 us
    dot_general x4, matrix products, per_device(): projected = jnp.dot(decode_rows, weights, preferred_element_type=f32)  12.1 us
    all_to_all x1, waiting for transfers between devices, per_device(): lax.all_to_all(jnp.broadcast_to(piece[:, None, :], (requests, heads, shar...  8.97 us
    all_to_all x1, waiting for transfers between devices, per_device(): lax.all_to_all(term.reshape(requests, heads, share), 'head', split_axis=1...  8.82 us
    all_to_all x1, starting transfers between devices, per_device(): lax.all_to_all(jnp.broadcast_to(row_group[None, :], (heads, rows_local)),...  8.59 us
  transfers between devices with their start and end apart: 6, of which 5 were waited for; matrix products, arithmetic and copies ran while one was open for 8% of the time, Pallas kernels for 0%

profile of v1, /device:TPU:1, one launch (start us, length us, event | category | flops | bytes accessed | tf_op | source)
XLA Modules:
  0.0 218.8 jit_solution(8598874027234571525)
XLA Ops:
  6.5 1.3 fusion.16
  7.8 1.8 fusion.18
  9.6 1.3 broadcast_in_dim.117
  10.9 8.6 %all-to-all-start = ((s32[32,1,16]{2,1,0:T(1,128)}), s32[32,1,16]{2,1,0:T(1,128)S(1)}, u32[]{:S(2)}, u32[]{:S(2)}) async-start(s32[32,1,16]{2,1,0:T(1,128)} %broadcast_in_dim.117), calls=%async_computation | async-start | bytes 32768 | tf_op jit(solution)/shard_map/ids/all_to_all | solution.py:65
  19.5 0.9 reduce_window_sum.23
  20.4 1.4 multiply_reduce_fusion.3
  21.7 0.8 select_reduce_fusion.10
  22.5 2.0 constant_dynamic-update-slice_fusion.2
  24.5 2.1 constant_dynamic-update-slice_fusion.1
  26.7 0.5 constant_dynamic-update-slice_fusion
  27.2 2.7 %copy-done.1 = bf16[8192,384]{1,0:T(8,128)(2,1)} copy-done((bf16[8192,384]{1,0:T(8,128)(2,1)}, bf16[8192,384]{1,0:T(8,128)(2,1)S(1)}, u32[]{:S(2)}) %copy-start.1) | copy-done | bytes 6291480
  29.9 1.0 fusion.19
  31.0 0.5 broadcast.353
  31.5 0.7 reduce.15
  32.3 0.1 convert_reduce_fusion.4
  32.4 0.6 broadcast_in_dim.118
  33.0 8.2 %all-to-all-start.1 = ((s32[8,1,8]{2,1,0:T(1,128)}), s32[8,1,8]{2,1,0:T(1,128)S(1)}, u32[]{:S(2)}, u32[]{:S(2)}) async-start(s32[8,1,8]{2,1,0:T(1,128)} %broadcast_in_dim.118), calls=%async_computation.1 | async-start | bytes 8192 | tf_op jit(solution)/shard_map/ids/all_to_all | solution.py:71
  41.2 0.3 fusion.5
  41.6 1.0 broadcast_and_fusion
  42.5 0.1 select_reduce_fusion
  42.6 5.1 %all-to-all-done.1 = s32[8,1,8]{2,1,0:T(1,128)S(1)} async-done(((s32[8,1,8]{2,1,0:T(1,128)}), s32[8,1,8]{2,1,0:T(1,128)S(1)}, u32[]{:S(2)}, u32[]{:S(2)}) %all-to-all-start.1) | async-done | bytes 288 | tf_op jit(solution)/shard_map/ids/all_to_all | solution.py:71
  47.7 0.7 select_reduce_fusion.11
  48.5 0.5 fusion.39
  49.1 23.0 %all-gather.2.cloned.1.call-done = bf16[512,8192]{1,0:T(8,128)(2,1)} async-done(((bf16[16,8192]{1,0:T(8,128)(2,1)}), bf16[512,8192]{1,0:T(8,128)(2,1)}) %all-gather.2.cloned.1.call-update) | async-done | bytes 8388624 | tf_op jit(solution)/shard_map/rows/all_gather | solution.py:61
  72.1 7.0 %fusion = f32[512,256]{0,1:T(8,128)S(1)} fusion(bf16[512,8192]{1,0:T(8,128)(2,1)} %all-gather.2.cloned.1.call-done, bf16[8192,128]{1,0:T(8,128)(2,1)} %param.16, bf16[8192,128]{1,0:T(8,128)(2,1)} %param.15), kind=kOutput, calls=%fused_computation.4 | convolution fusion | flops 2155872256 | bytes 13107200 | tf_op jit(solution)/shard_map/project/dot_general | solution.py:95
  79.3 1.2 convolution_convert_fusion.4
  80.5 6.7 %all-to-all-start.2 = ((bf16[8,96,256]{2,1,0:T(8,128)(2,1)}), bf16[8,96,256]{2,1,0:T(8,128)(2,1)S(1)}, u32[]{:S(2)}, u32[]{:S(2)}) async-start(bf16[8,96,256]{2,1,0:T(8,128)(2,1)} %bitcast.2), calls=%async_computation.2 | async-start | bytes 786432 | tf_op jit(solution)/shard_map/project/all_to_all | solution.py:101
  87.2 1.4 multiply_cosine_fusion.1
  88.5 0.2 fusion.71
  88.7 0.7 add_select_fusion
  89.5 12.8 %all-to-all-done.2 = bf16[8,96,256]{2,1,0:T(8,128)(2,1)S(1)} async-done(((bf16[8,96,256]{2,1,0:T(8,128)(2,1)}), bf16[8,96,256]{2,1,0:T(8,128)(2,1)S(1)}, u32[]{:S(2)}, u32[]{:S(2)}) %all-to-all-start.2) | async-done | bytes 393248 | tf_op jit(solution)/shard_map/project/all_to_all | solution.py:101
  102.3 0.3 select_reduce_fusion.5
  102.6 0.2 fusion.40
  102.9 0.6 convolution_convert_fusion.3
  103.4 0.7 copy.46
  104.2 5.7 %all-to-all-start.3 = ((bf16[16,32,256]{2,0,1:T(8,128)(2,1)}), bf16[16,32,256]{2,0,1:T(8,128)(2,1)S(1)}, u32[]{:S(2)}, u32[]{:S(2)}) async-start(bf16[16,32,256]{2,0,1:T(8,128)(2,1)} %bitcast.78), calls=%async_computation.3 | async-start | bytes 524288 | tf_op jit(solution)/shard_map/sum/all_to_all | solution.py:154
  110.0 8.8 %all-to-all-done.3 = bf16[16,32,256]{2,0,1:T(8,128)(2,1)S(1)} async-done(((bf16[16,32,256]{2,0,1:T(8,128)(2,1)}), bf16[16,32,256]{2,0,1:T(8,128)(2,1)S(1)}, u32[]{:S(2)}, u32[]{:S(2)}) %all-to-all-start.3) | async-done | bytes 262176 | tf_op jit(solution)/shard_map/sum/all_to_all | solution.py:154
  118.9 0.7 broadcast_in_dim.133
  119.6 3.8 %all-to-all-start.4 = ((bf16[16,32,256]{2,0,1:T(8,128)(2,1)}), bf16[16,32,256]{2,0,1:T(8,128)(2,1)S(1)}, u32[]{:S(2)}, u32[]{:S(2)}) async-start(bf16[16,32,256]{2,0,1:T(8,128)(2,1)} %broadcast_in_dim.133), calls=%async_computation.4 | async-start | bytes 524288 | tf_op jit(solution)/shard_map/spread/all_to_all | solution.py:161
  123.4 9.0 %all-to-all-done.4 = bf16[16,32,256]{2,0,1:T(8,128)(2,1)S(1)} async-done(((bf16[16,32,256]{2,0,1:T(8,128)(2,1)}), bf16[16,32,256]{2,0,1:T(8,128)(2,1)S(1)}, u32[]{:S(2)}, u32[]{:S(2)}) %all-to-all-start.4) | async-done | bytes 262176 | tf_op jit(solution)/shard_map/spread/all_to_all | solution.py:161
  132.4 0.2 multiply_reduce_fusion.2
  132.6 3.7 %convolution_multiply_fusion.6 = f32[16,384]{1,0:T(8,128)S(1)} fusion(bf16[16,8192]{1,0:T(8,128)(2,1)S(1)} %bitcast.98, bf16[8192,384]{1,0:T(8,128)(2,1)} %copy-done.1, f32[16]{0:T(128)S(1)} %add_rsqrt_fusion.2), kind=kOutput, calls=%fused_computation.15 | convolution fusion | flops 100669440 | bytes 6578240 | tf_op jit(solution)/shard_map/decode/dot_general | solution.py:127
  136.4 0.2 fusion.72
  136.6 0.3 select_reduce_fusion.4
  136.9 0.2 fusion.41
  137.2 0.6 convolution_convert_fusion.2
  137.8 12.5 %all_to_all.55 = bf16[16,32,256]{2,0,1:T(8,128)(2,1)S(1)} all-to-all(bf16[16,32,256]{2,0,1:T(8,128)(2,1)S(1)} %bitcast.93), channel_id=1, replica_groups=mesh['grp'=8,'head'=32] {'head'}, dimensions={1} | all-to-all | bytes 524288 | tf_op jit(solution)/shard_map/sum/all_to_all | solution.py:154
  150.4 12.5 %all_to_all.56 = bf16[16,32,256]{2,0,1:T(8,128)(2,1)S(1)} all-to-all(bf16[16,32,256]{2,0,1:T(8,128)(2,1)S(1)} %broadcast_in_dim.134), channel_id=1, replica_groups=mesh['grp'=8,'head'=32] {'head'}, dimensions={1} | all-to-all | bytes 524288 | tf_op jit(solution)/shard_map/spread/all_to_all | solution.py:161
  162.9 0.2 multiply_reduce_fusion.1
  163.1 3.7 %convolution_multiply_fusion.5 = f32[16,384]{1,0:T(8,128)S(1)} fusion(bf16[16,8192]{1,0:T(8,128)(2,1)S(1)} %bitcast.99, bf16[8192,384]{1,0:T(8,128)(2,1)} %copy-done.1, f32[16]{0:T(128)S(1)} %add_rsqrt_fusion.1), kind=kOutput, calls=%fused_computation.14 | convolution fusion | flops 100669440 | bytes 6578240 | tf_op jit(solution)/shard_map/decode/dot_general | solution.py:127
  166.9 0.2 fusion.73
  167.1 0.3 select_reduce_fusion.3
  167.4 0.2 fusion.42
  167.7 0.6 convolution_convert_fusion.1
  168.3 12.5 %all_to_all.57 = bf16[16,32,256]{2,0,1:T(8,128)(2,1)S(1)} all-to-all(bf16[16,32,256]{2,0,1:T(8,128)(2,1)S(1)} %bitcast.94), channel_id=1, replica_groups=mesh['grp'=8,'head'=32] {'head'}, dimensions={1} | all-to-all | bytes 524288 | tf_op jit(solution)/shard_map/sum/all_to_all | solution.py:154
  180.9 12.5 %all_to_all.58 = bf16[16,32,256]{2,0,1:T(8,128)(2,1)S(1)} all-to-all(bf16[16,32,256]{2,0,1:T(8,128)(2,1)S(1)} %broadcast_in_dim.135), channel_id=1, replica_groups=mesh['grp'=8,'head'=32] {'head'}, dimensions={1} | all-to-all | bytes 524288 | tf_op jit(solution)/shard_map/spread/all_to_all | solution.py:161
  193.4 0.2 multiply_reduce_fusion
  193.6 3.7 %convolution_multiply_fusion.4 = f32[16,384]{1,0:T(8,128)S(1)} fusion(bf16[16,8192]{1,0:T(8,128)(2,1)S(1)} %bitcast.97, bf16[8192,384]{1,0:T(8,128)(2,1)} %copy-done.1, f32[16]{0:T(128)S(1)} %add_rsqrt_fusion), kind=kOutput, calls=%fused_computation.13 | convolution fusion | flops 100669440 | bytes 6578240 | tf_op jit(solution)/shard_map/decode/dot_general | solution.py:127
  197.4 0.2 fusion.74
  197.6 0.3 select_reduce_fusion.2
  197.9 0.2 fusion.43
  198.2 0.6 convolution_convert_fusion
  198.8 12.5 %all_to_all.59 = bf16[16,32,256]{2,0,1:T(8,128)(2,1)S(1)} all-to-all(bf16[16,32,256]{2,0,1:T(8,128)(2,1)S(1)} %bitcast.95), channel_id=1, replica_groups=mesh['grp'=8,'head'=32] {'head'}, dimensions={1} | all-to-all | bytes 524288 | tf_op jit(solution)/shard_map/sum/all_to_all | solution.py:154
  211.3 0.6 add.226
  (78 shorter events, 1.7 us)
Async XLA Ops:
  6.5 96.3 %copy-start = (bf16[128,8192]{1,0:T(8,128)(2,1)S(1)}, bf16[128,8192]{1,0:T(8,128)(2,1)}, u32[]{:S(2)}) copy-start(bf16[128,8192]{1,0:T(8,128)(2,1)} %param.17) | copy-start | bytes 6291460
  6.5 65.6 %all-gather.2.cloned.1.call-start = ((), (), s32[]{:S(2)}) async-start(), calls=%async_computation.10 | async-start | bytes 8650752 | tf_op jit(solution)/shard_map/rows/all_gather | solution.py:61
  10.9 20.1 %all-to-all-start = ((s32[32,1,16]{2,1,0:T(1,128)}), s32[32,1,16]{2,1,0:T(1,128)S(1)}, u32[]{:S(2)}, u32[]{:S(2)}) async-start(s32[32,1,16]{2,1,0:T(1,128)} %broadcast_in_dim.117), calls=%async_computation | async-start | bytes 32768 | tf_op jit(solution)/shard_map/ids/all_to_all | solution.py:65
  20.4 6.3 %copy-start.3 = (bf16[8192,128]{1,0:T(8,128)(2,1)S(1)}, bf16[8192,128]{1,0:T(8,128)(2,1)}, u32[]{:S(2)}) copy-start(bf16[8192,128]{1,0:T(8,128)(2,1)} %param.14) | copy-start | bytes 6291460
  22.5 7.4 %copy-start.2 = (f32[16,8192]{1,0:T(8,128)S(1)}, f32[16,8192]{1,0:T(8,128)}, u32[]{:S(2)}) copy-start(f32[16,8192]{1,0:T(8,128)} %param.12) | copy-start | bytes 1572868
  22.5 7.4 %copy-start.5 = (f32[8192]{0:T(1024)S(1)}, f32[8192]{0:T(1024)}, u32[]{:S(2)}) copy-start(f32[8192]{0:T(1024)} %param.13) | copy-start | bytes 98308
  27.2 2.7 %copy-start.1 = (bf16[8192,384]{1,0:T(8,128)(2,1)}, bf16[8192,384]{1,0:T(8,128)(2,1)S(1)}, u32[]{:S(2)}) copy-start(bf16[8192,384]{1,0:T(8,128)(2,1)S(1)} %constant_dynamic-update-slice_fusion) | copy-start | bytes 18874372
  31.0 48.2 %copy-start.7 = (f32[64]{0:T(128)}, f32[64]{0:T(128)S(1)}, u32[]{:S(2)}) copy-start(f32[64]{0:T(128)S(1)} %multiply_exponential_fusion) | copy-start | bytes 772
  33.0 14.7 %all-to-all-start.1 = ((s32[8,1,8]{2,1,0:T(1,128)}), s32[8,1,8]{2,1,0:T(1,128)S(1)}, u32[]{:S(2)}, u32[]{:S(2)}) async-start(s32[8,1,8]{2,1,0:T(1,128)} %broadcast_in_dim.118), calls=%async_computation.1 | async-start | bytes 8192 | tf_op jit(solution)/shard_map/ids/all_to_all | solution.py:71
  72.1 7.2 %copy-start.4 = (pred[8,96,512]{2,1,0:T(32,128)(4,1)S(1)}, pred[8,96,512]{2,1,0:T(32,128)(4,1)}, u32[]{:S(2)}) copy-start(pred[8,96,512]{2,1,0:T(32,128)(4,1)} %broadcast_and_fusion) | copy-start | bytes 1179652
  80.5 21.9 %all-to-all-start.2 = ((bf16[8,96,256]{2,1,0:T(8,128)(2,1)}), bf16[8,96,256]{2,1,0:T(8,128)(2,1)S(1)}, u32[]{:S(2)}, u32[]{:S(2)}) async-start(bf16[8,96,256]{2,1,0:T(8,128)(2,1)} %bitcast.2), calls=%async_computation.2 | async-start | bytes 786432 | tf_op jit(solution)/shard_map/project/all_to_all | solution.py:101
  102.6 33.8 %copy-start.6 = (f32[16,64]{1,0:T(8,128)S(1)}, f32[16,64]{1,0:T(8,128)}, u32[]{:S(2)}) copy-start(f32[16,64]{1,0:T(8,128)} %get-tuple-element.85) | copy-start | bytes 12292
  104.2 14.6 %all-to-all-start.3 = ((bf16[16,32,256]{2,0,1:T(8,128)(2,1)}), bf16[16,32,256]{2,0,1:T(8,128)(2,1)S(1)}, u32[]{:S(2)}, u32[]{:S(2)}) async-start(bf16[16,32,256]{2,0,1:T(8,128)(2,1)} %bitcast.78), calls=%async_computation.3 | async-start | bytes 524288 | tf_op jit(solution)/shard_map/sum/all_to_all | solution.py:154
  119.6 12.8 %all-to-all-start.4 = ((bf16[16,32,256]{2,0,1:T(8,128)(2,1)}), bf16[16,32,256]{2,0,1:T(8,128)(2,1)S(1)}, u32[]{:S(2)}, u32[]{:S(2)}) async-start(bf16[16,32,256]{2,0,1:T(8,128)(2,1)} %broadcast_in_dim.133), calls=%async_computation.4 | async-start | bytes 524288 | tf_op jit(solution)/shard_map/spread/all_to_all | solution.py:161
Sparse Core Ops, SparseCore 0:
  9.9 62.1 all-gather.1

commit v2 on v1

--- a/solution.py
+++ b/solution.py
@@ -36,6 +36,52 @@
     half = HD // 2
     swapped = jnp.concatenate([values[..., half:], values[..., :half]], axis=-1)
     return values * cosine + swapped * sine
+
+
+NX = 4
+NY = 4
+
+
+def head_pairs(move):
+    pairs = []
+    for y in range(NY):
+        for x in range(NX):
+            for c in range(2):
+                ty, tx, tc = move(y, x, c)
+                pairs.append(((y * NX + x) * 2 + c, (ty * NX + tx) * 2 + tc))
+    return pairs
+
+
+def lane(first, second):
+    return head_pairs(
+        lambda y, x, c: (y ^ second, x ^ first, c) if c == 0 else (y ^ first, x ^ second, c)
+    )
+
+
+CORE = head_pairs(lambda y, x, c: (y, x, c ^ 1))
+
+
+def send(values, pairs):
+    return lax.ppermute(values, "head", pairs)
+
+
+def gather_lane(normal_rows, core):
+    half = normal_rows.shape[1] // 2
+    n = normal_rows.shape[0]
+    low, high = normal_rows[:, :half], normal_rows[:, half:]
+    kept = jnp.where(core == 0, low, high)
+    given = jnp.where(core == 0, high, low)
+    start = jnp.concatenate([kept, send(given, CORE)])
+    f1 = send(start, lane(1, 0))
+    f3 = send(start, lane(3, 0))
+    f2 = jnp.concatenate([send(f3[:n], lane(1, 0)), send(f1[n:], lane(3, 0))])
+    line = jnp.concatenate([start, f1, f2, f3])
+    s1 = send(line, lane(0, 1))
+    s3 = send(line, lane(0, 3))
+    early = s3.reshape(NX, 2, n, half)[:, 0].reshape(NX * n, half)
+    late = s1.reshape(NX, 2, n, half)[:, 1].reshape(NX * n, half)
+    s2 = jnp.concatenate([send(early, lane(0, 1)), send(late, lane(0, 3))])
+    return line, s1, s3, s2
 
 
 def per_device(
@@ -56,10 +102,17 @@
     row_ends = jnp.cumsum(lengths, axis=1)
     row_starts = row_ends - lengths
 
+    core = my_head % 2
+    half = width // 2
     with jax.named_scope("rows"):
         normal_rows = normed(prefill_rows, norm_gain)
-        plane = lax.all_gather(normal_rows, "head", axis=0, tiled=True)
-    weights = jnp.concatenate([w_key, w_value, w_query], axis=1)
+        line, s1, s3, s2 = gather_lane(normal_rows, core)
+    with jax.named_scope("weights"):
+        kv = jnp.concatenate([w_key, w_value], axis=1)
+        kept = jnp.where(core == 0, kv[:half], kv[half:])
+        given = jnp.where(core == 0, kv[half:], kv[:half])
+        half_weights = jnp.concatenate([kept, send(given, CORE)], axis=1)
+        weights = jnp.concatenate([kv, w_query], axis=1)
 
     with jax.named_scope("ids"):
         ids = lax.all_to_all(
@@ -85,6 +138,22 @@
         inside = (cell[:, None] >= starts) & (cell[:, None] < ends)
         places = jnp.sum(jnp.where(inside, cell[:, None] - starts, 0), axis=1)
         slots = jnp.arange(cap, dtype=jnp.int32)
+        block = jnp.arange(heads, dtype=jnp.int32)
+        d_second, d_first, d_core = block // (2 * NX), (block // 2) % NX, block % 2
+        dy = jnp.where(core == 0, d_second, d_first)
+        dx = jnp.where(core == 0, d_first, d_second)
+        source = (
+            ((my_head // (2 * NX)) ^ dy) * 2 * NX
+            + (((my_head // 2) % NX) ^ dx) * 2
+            + (core ^ d_core)
+        )
+        from_block = source[:, None] == block[None, :]
+
+        def here(values):
+            blocks = values.reshape(1, heads, rows_local)
+            return jnp.sum(jnp.where(from_block[:, :, None], blocks, 0), axis=1).reshape(-1)
+
+        ids, order, places = here(ids), here(order), here(places)
         pick = (
             (ids[None, None, :] == group_ids[:, None, None])
             & (order[None, None, :] == slots[None, :, None])
@@ -92,7 +161,12 @@
         cosine, sine = angles_of(places)
 
     with jax.named_scope("project"):
-        both = jnp.dot(plane, weights[:, : 2 * HD], preferred_element_type=f32)
+        parts = [jnp.dot(r, half_weights, preferred_element_type=f32) for r in (line, s1, s2, s3)]
+        parts[2] = parts[2].reshape(2, NX, rows_local, 4 * HD).swapaxes(0, 1).reshape(parts[1].shape)
+        parts = jnp.stack(parts).reshape(NY, NX, 2, rows_local, 4 * HD)
+        theirs = parts[..., 2 * HD :].swapaxes(0, 1)[:, :, ::-1]
+        theirs = send(theirs.reshape(plane_rows, 2 * HD), CORE)
+        both = parts[..., : 2 * HD].reshape(plane_rows, 2 * HD) + theirs
         keys = turned(both[:, :HD], cosine, sine)
         packed = jnp.concatenate([keys, both[:, HD:]], axis=1).astype(bf16)
         outgoing = jnp.dot(

time: 220 us -> 231 us (1.050)
  between operations: 13.8 us -> 0.58 us
  starting transfers between devices: 33 us -> 44.1 us
  local copies, waits for them, and re-layouts: 12.1 us -> 23 us
  waiting for transfers between devices: 58.6 us -> 49.9 us
  matrix products: 24.1 us -> 31.6 us
  other arithmetic: 15 us -> 18.1 us
    all_gather x1 -> x0, waiting for transfers between devices: 23 us -> none  [per_device(): plane = lax.all_gather(normal_rows, 'head', axis=0, tiled=True)]
    ppermute x0 -> x11, starting transfers between devices: none -> 18.3 us  [send(): return lax.ppermute(values, 'head', pairs)]
    ppermute x0 -> x11, waiting for transfers between devices: none -> 13.7 us  [send(): return lax.ppermute(values, 'head', pairs)]
    dot_general x1 -> x4, matrix products: 7.03 us -> 11.1 us  [per_device(): jnp.dot(r, half_weights, preferred_element_type=f32)]
    slice x0 -> x6, local copies, waits for them, and re-layouts: none -> 3.95 us  [the longest x1 1.87 us: gather_lane(): late = s1.reshape(NX, 2, n, half)[:, 1].reshape(NX * n, half)]
    concatenate x1 -> x2, local copies, waits for them, and re-layouts: 0.5 us -> 3.84 us  [the longest x1 3.13 us: per_device(): weights = jnp.concatenate([kv, w_query], axis=1)]
    all_to_all x1, starting transfers between devices: 6.72 us -> 3.45 us  [per_device(): lax.all_to_all(outgoing.reshape(groups, cap, 2 * HD), 'grp', split_axis=0...]
    dot_general x4, matrix products: 12.1 us -> 14.9 us  [per_device(): projected = jnp.dot(decode_rows, weights, preferred_element_type=f32)]
  transfers between devices with their start and end apart: 6 -> 16, of which waited for: 5 -> 10; matrix products, arithmetic and copies ran while one was open for 8% -> 14% of each run, Pallas kernels for 0% -> 0%
where the time goes in v2:
time: 231 us; the launch traced here: 229 us
  blocking collectives  62.3 us (27%)
  waiting for transfers between devices  49.9 us (22%)
  starting transfers between devices  44.1 us (19%)
  matrix products  31.6 us (14%)
  local copies, waits for them, and re-layouts  23 us (10%)
  other arithmetic  18.1 us (8%)
    all_to_all x3, blocking collectives, per_device(): lax.all_to_all(term.reshape(requests, heads, share), 'head', split_axis=1...  37.4 us
    all_to_all x2, blocking collectives, per_device(): lax.all_to_all(jnp.broadcast_to(piece[:, None, :], (requests, heads, shar...  24.9 us
    ppermute x11, starting transfers between devices, send(): return lax.ppermute(values, 'head', pairs)  18.3 us
    dot_general x4, matrix products, per_device(): projected = jnp.dot(decode_rows, weights, preferred_element_type=f32)  14.9 us
    ppermute x11, waiting for transfers between devices, send(): return lax.ppermute(values, 'head', pairs)  13.7 us
    all_to_all x1, waiting for transfers between devices, per_device(): lax.all_to_all(outgoing.reshape(groups, cap, 2 * HD), 'grp', split_axis=0...  12.5 us
    dot_general x4, matrix products, per_device(): jnp.dot(r, half_weights, preferred_element_type=f32)  11.1 us
    all_to_all x1, waiting for transfers between devices, per_device(): lax.all_to_all(jnp.broadcast_to(piece[:, None, :], (requests, heads, shar...  8.97 us
  transfers between devices with their start and end apart: 16, of which 10 were waited for; matrix products, arithmetic and copies ran while one was open for 14% of the time, Pallas kernels for 0%

profile of v2, /device:TPU:1, one launch (start us, length us, event | category | flops | bytes accessed | tf_op | source)
XLA Modules:
  0.0 229.5 jit_solution(1145690443438445203)
XLA Ops:
  0.0 1.3 fusion.16
  1.3 1.1 fusion.18
  2.4 0.7 constant_dynamic-update-slice_fusion.8
  3.1 3.2 %collective-permute-start = (bf16[16,4096]{1,0:T(8,128)(2,1)S(1)}, bf16[16,4096]{1,0:T(8,128)(2,1)S(1)}, u32[]{:S(2)}, u32[]{:S(2)}) collective-permute-start(bf16[16,4096]{1,0:T(8,128)(2,1)S(1)} %get-tuple-element.48), channel_id=1, source_target_pairs={{0,1},{1,0},{2,3},{3,2},{4,5},{5,4},{6,7},{7,6},{8,9},{9,8},{10,11... | collective-permute-start | bytes 393224 | tf_op jit(solution)/shard_map/rows/ppermute | solution.py:65
  6.4 3.5 %constant_dynamic-update-slice_fusion.2 = (bf16[8192,384]{1,0:T(8,128)(2,1)}, bf16[8192,256]{1,0:T(8,128)(2,1)S(1)}) fusion(bf16[8192,128]{1,0:T(8,128)(2,1)} %param.15), kind=kLoop, calls=%fused_computation.123 | loop fusion | bytes 6291456
  9.9 1.7 constant_dynamic-update-slice_fusion.1
  11.6 2.2 broadcast_select_fusion.1
  14.4 5.9 %all-to-all-start = ((s32[32,1,16]{2,1,0:T(1,128)}), s32[32,1,16]{2,1,0:T(1,128)S(1)}, u32[]{:S(2)}, u32[]{:S(2)}) async-start(s32[32,1,16]{2,1,0:T(1,128)} %broadcast_in_dim.249), calls=%async_computation | async-start | bytes 32768 | tf_op jit(solution)/shard_map/ids/all_to_all | solution.py:118
  20.7 3.1 %constant_dynamic-update-slice_fusion = bf16[8192,384]{1,0:T(8,128)(2,1)} fusion(bf16[8192,384]{1,0:T(8,128)(2,1)} %get-tuple-element.40, bf16[8192,128]{1,0:T(8,128)(2,1)} %param.14), kind=kLoop, calls=%fused_computation.121 | loop fusion | bytes 4194304 | tf_op jit(solution)/shard_map/weights/concatenate | solution.py:115
  23.8 3.7 %fusion.19 = f32[16,384]{1,0:T(8,128)S(1)} fusion(bf16[8192,384]{1,0:T(8,128)(2,1)} %constant_dynamic-update-slice_fusion, f32[16,8192]{1,0:T(8,128)S(1)} %copy-done.1, f32[8192]{0:T(1024)S(1)} %copy-done.6, f32[16]{0:T(128)S(1)} %add_rsqrt_fusion.4), kind=kOutput, calls=%fused_computation.57 | convolution fusion | flops 101056512 | bytes 6873152 | tf_op jit(solution)/shard_map/decode/dot_general | solution.py:201
  27.7 1.5 collective-permute-start.1
  29.2 1.8 collective-permute-start.2
  31.0 0.7 constant_dynamic-update-slice_fusion.7
  31.6 4.3 %collective-permute-done.2 = bf16[32,4096]{1,0:T(8,128)(2,1)S(1)} collective-permute-done((bf16[32,4096]{1,0:T(8,128)(2,1)S(1)}, bf16[32,4096]{1,0:T(8,128)(2,1)S(1)}, u32[]{:S(2)}, u32[]{:S(2)}) %collective-permute-start.2) | collective-permute-done | bytes 262176 | tf_op jit(solution)/shard_map/rows/ppermute | solution.py:65
  36.0 1.9 collective-permute-start.4
  37.9 0.7 constant_dynamic-update-slice_fusion.6
  38.7 1.2 collective-permute-done.3
  39.8 0.7 constant_dynamic-update-slice_fusion.5
  40.5 0.7 collective-permute-done.4
  41.2 0.7 constant_dynamic-update-slice_fusion.4
  41.8 0.7 constant_dynamic-update-slice_fusion.3
  42.5 0.9 collective-permute-start.6
  43.4 1.8 collective-permute-start.7
  45.3 0.7 fusion.156
  47.0 0.7 reduce.15
  48.5 8.2 %all-to-all-start.1 = ((s32[8,1,8]{2,1,0:T(1,128)}), s32[8,1,8]{2,1,0:T(1,128)S(1)}, u32[]{:S(2)}, u32[]{:S(2)}) async-start(s32[8,1,8]{2,1,0:T(1,128)} %broadcast_in_dim.250), calls=%async_computation.1 | async-start | bytes 8192 | tf_op jit(solution)/shard_map/ids/all_to_all | solution.py:124
  57.3 5.9 %all-to-all-done.1 = s32[8,1,8]{2,1,0:T(1,128)S(1)} async-done(((s32[8,1,8]{2,1,0:T(1,128)}), s32[8,1,8]{2,1,0:T(1,128)S(1)}, u32[]{:S(2)}, u32[]{:S(2)}) %all-to-all-start.1) | async-done | bytes 288 | tf_op jit(solution)/shard_map/ids/all_to_all | solution.py:124
  63.2 0.6 select_reduce_fusion.14
  63.8 1.1 slice.246
  64.9 0.9 collective-permute-start.8
  65.9 1.9 slice.247
  68.6 1.7 select_reduce_fusion
  70.5 2.9 %collective-permute-done.8 = bf16[64,4096]{1,0:T(8,128)(2,1)} collective-permute-done((bf16[64,4096]{1,0:T(8,128)(2,1)S(1)}, bf16[64,4096]{1,0:T(8,128)(2,1)}, u32[]{:S(2)}, u32[]{:S(2)}) %collective-permute-start.8) | collective-permute-done | bytes 524320 | tf_op jit(solution)/shard_map/rows/ppermute | solution.py:65
  73.4 4.2 %collective-permute-done.9 = bf16[64,4096]{1,0:T(8,128)(2,1)} collective-permute-done((bf16[64,4096]{1,0:T(8,128)(2,1)}, bf16[64,4096]{1,0:T(8,128)(2,1)}, u32[]{:S(2)}, u32[]{:S(2)}) %collective-permute-start.9) | collective-permute-done | bytes 524320 | tf_op jit(solution)/shard_map/rows/ppermute | solution.py:65
  77.6 3.4 %fusion.12 = f32[128,512]{1,0:T(8,128)S(1)} fusion(bf16[64,4096]{1,0:T(8,128)(2,1)} %collective-permute-done.9, bf16[64,4096]{1,0:T(8,128)(2,1)} %collective-permute-done.8, bf16[4096,256]{1,0:T(8,128)(2,1)} %collective-permute-done.5, bf16[4096,256]{1,0:T(8,128)(2,1)} %get-tuple-element.38), kind=kOutput, calls=%fused_computation.32 | convolution fusion | flops 547356672 | bytes 5505024 | tf_op jit(solution)/shard_map/project/dot_general | solution.py:164
  81.0 2.4 %fusion.142 = f32[128,512]{1,0:T(8,128)S(1)} fusion(bf16[128,4096]{1,0:T(8,128)(2,1)S(1)} %copy-done.9, bf16[4096,256]{1,0:T(8,128)(2,1)} %collective-permute-done.5, bf16[4096,256]{1,0:T(8,128)(2,1)S(1)} %copy-done.3), kind=kOutput, calls=%fused_computation.327 | convolution fusion | flops 545259520 | bytes 5505024 | tf_op jit(solution)/shard_map/project/dot_general | solution.py:164
  83.4 2.6 %fusion.141 = f32[128,512]{1,0:T(8,128)S(1)} fusion(bf16[128,4096]{1,0:T(8,128)(2,1)} %collective-permute-done.6, bf16[4096,256]{1,0:T(8,128)(2,1)} %collective-permute-done.5, bf16[4096,256]{1,0:T(8,128)(2,1)S(1)} %copy-done.3), kind=kOutput, calls=%fused_computation.326 | convolution fusion | flops 545259520 | bytes 5505024 | tf_op jit(solution)/shard_map/project/dot_general | solution.py:164
  86.1 2.6 %fusion.140 = f32[128,512]{1,0:T(8,128)S(1)} fusion(bf16[128,4096]{1,0:T(8,128)(2,1)} %collective-permute-done.7, bf16[4096,256]{1,0:T(8,128)(2,1)} %collective-permute-done.5, bf16[4096,256]{1,0:T(8,128)(2,1)S(1)} %copy-done.3), kind=kOutput, calls=%fused_computation.325 | convolution fusion | flops 545259520 | bytes 5505024 | tf_op jit(solution)/shard_map/project/dot_general | solution.py:164
  88.8 1.0 fusion.151
  89.8 1.9 rev.3
  91.7 5.5 %collective-permute-start.10 = (f32[512,256]{1,0:T(8,128)}, f32[512,256]{1,0:T(8,128)}, u32[]{:S(2)}, u32[]{:S(2)}) collective-permute-start(f32[512,256]{1,0:T(8,128)} %bitcast.129), channel_id=1, source_target_pairs={{0,1},{1,0},{2,3},{3,2},{4,5},{5,4},{6,7},{7,6},{8,9},{9,8},{10,11... | collective-permute-start | bytes 1572872 | tf_op jit(solution)/shard_map/project/ppermute | solution.py:65
  97.5 1.0 fusion.39
  99.1 1.1 bitcast_add_fusion
  100.6 1.1 convolution_convert_fusion.4
  101.8 3.5 %all-to-all-start.2 = ((bf16[8,96,256]{2,1,0:T(8,128)(2,1)}), bf16[8,96,256]{2,1,0:T(8,128)(2,1)S(1)}, u32[]{:S(2)}, u32[]{:S(2)}) async-start(bf16[8,96,256]{2,1,0:T(8,128)(2,1)} %bitcast.19), calls=%async_computation.2 | async-start | bytes 786432 | tf_op jit(solution)/shard_map/project/all_to_all | solution.py:175
  105.2 0.8 multiply_cosine_fusion.1
  106.0 1.0 fusion.71
  107.0 0.7 add_select_fusion
  107.8 12.5 %all-to-all-done.2 = bf16[8,96,256]{2,1,0:T(8,128)(2,1)S(1)} async-done(((bf16[8,96,256]{2,1,0:T(8,128)(2,1)}), bf16[8,96,256]{2,1,0:T(8,128)(2,1)S(1)}, u32[]{:S(2)}, u32[]{:S(2)}) %all-to-all-start.2) | async-done | bytes 393248 | tf_op jit(solution)/shard_map/project/all_to_all | solution.py:175
  120.8 1.3 convolution_convert_fusion.3
  122.1 0.7 copy.71
  122.9 4.4 %all-to-all-start.3 = ((bf16[16,32,256]{2,0,1:T(8,128)(2,1)}), bf16[16,32,256]{2,0,1:T(8,128)(2,1)S(1)}, u32[]{:S(2)}, u32[]{:S(2)}) async-start(bf16[16,32,256]{2,0,1:T(8,128)(2,1)} %bitcast.104), calls=%async_computation.3 | async-start | bytes 524288 | tf_op jit(solution)/shard_map/sum/all_to_all | solution.py:228
  127.4 8.8 %all-to-all-done.3 = bf16[16,32,256]{2,0,1:T(8,128)(2,1)S(1)} async-done(((bf16[16,32,256]{2,0,1:T(8,128)(2,1)}), bf16[16,32,256]{2,0,1:T(8,128)(2,1)S(1)}, u32[]{:S(2)}, u32[]{:S(2)}) %all-to-all-start.3) | async-done | bytes 262176 | tf_op jit(solution)/shard_map/sum/all_to_all | solution.py:228
  136.3 0.7 broadcast_in_dim.273
  137.0 3.9 %all-to-all-start.4 = ((bf16[16,32,256]{2,0,1:T(8,128)(2,1)}), bf16[16,32,256]{2,0,1:T(8,128)(2,1)S(1)}, u32[]{:S(2)}, u32[]{:S(2)}) async-start(bf16[16,32,256]{2,0,1:T(8,128)(2,1)} %broadcast_in_dim.273), calls=%async_computation.4 | async-start | bytes 524288 | tf_op jit(solution)/shard_map/spread/all_to_all | solution.py:235
  140.9 9.0 %all-to-all-done.4 = bf16[16,32,256]{2,0,1:T(8,128)(2,1)S(1)} async-done(((bf16[16,32,256]{2,0,1:T(8,128)(2,1)}), bf16[16,32,256]{2,0,1:T(8,128)(2,1)S(1)}, u32[]{:S(2)}, u32[]{:S(2)}) %all-to-all-start.4) | async-done | bytes 262176 | tf_op jit(solution)/shard_map/spread/all_to_all | solution.py:235
  150.2 3.7 %convolution_multiply_fusion.6 = f32[16,384]{1,0:T(8,128)S(1)} fusion(bf16[16,8192]{1,0:T(8,128)(2,1)S(1)} %bitcast.126, bf16[8192,384]{1,0:T(8,128)(2,1)} %constant_dynamic-update-slice_fusion, f32[16]{0:T(128)S(1)} %add_rsqrt_fusion.2), kind=kOutput, calls=%fused_computation.14 | convolution fusion | flops 100669440 | bytes 6578240 | tf_op jit(solution)/shard_map/decode/dot_general | solution.py:201
  155.4 12.5 %all_to_all.55 = bf16[16,32,256]{2,0,1:T(8,128)(2,1)S(1)} all-to-all(bf16[16,32,256]{2,0,1:T(8,128)(2,1)S(1)} %bitcast.120), channel_id=1, replica_groups=mesh['grp'=8,'head'=32] {'head'}, dimensions={1} | all-to-all | bytes 524288 | tf_op jit(solution)/shard_map/sum/all_to_all | solution.py:228
  167.9 12.5 %all_to_all.56 = bf16[16,32,256]{2,0,1:T(8,128)(2,1)S(1)} all-to-all(bf16[16,32,256]{2,0,1:T(8,128)(2,1)S(1)} %broadcast_in_dim.274), channel_id=1, replica_groups=mesh['grp'=8,'head'=32] {'head'}, dimensions={1} | all-to-all | bytes 524288 | tf_op jit(solution)/shard_map/spread/all_to_all | solution.py:235
  180.6 3.7 %convolution_multiply_fusion.5 = f32[16,384]{1,0:T(8,128)S(1)} fusion(bf16[16,8192]{1,0:T(8,128)(2,1)S(1)} %bitcast.127, bf16[8192,384]{1,0:T(8,128)(2,1)} %constant_dynamic-update-slice_fusion, f32[16]{0:T(128)S(1)} %add_rsqrt_fusion.1), kind=kOutput, calls=%fused_computation.13 | convolution fusion | flops 100669440 | bytes 6578240 | tf_op jit(solution)/shard_map/decode/dot_general | solution.py:201
  185.9 12.5 %all_to_all.57 = bf16[16,32,256]{2,0,1:T(8,128)(2,1)S(1)} all-to-all(bf16[16,32,256]{2,0,1:T(8,128)(2,1)S(1)} %bitcast.121), channel_id=1, replica_groups=mesh['grp'=8,'head'=32] {'head'}, dimensions={1} | all-to-all | bytes 524288 | tf_op jit(solution)/shard_map/sum/all_to_all | solution.py:228
  198.4 12.5 %all_to_all.58 = bf16[16,32,256]{2,0,1:T(8,128)(2,1)S(1)} all-to-all(bf16[16,32,256]{2,0,1:T(8,128)(2,1)S(1)} %broadcast_in_dim.275), channel_id=1, replica_groups=mesh['grp'=8,'head'=32] {'head'}, dimensions={1} | all-to-all | bytes 524288 | tf_op jit(solution)/shard_map/spread/all_to_all | solution.py:235
  211.1 3.7 %convolution_multiply_fusion.4 = f32[16,384]{1,0:T(8,128)S(1)} fusion(bf16[16,8192]{1,0:T(8,128)(2,1)S(1)} %bitcast.125, bf16[8192,384]{1,0:T(8,128)(2,1)} %constant_dynamic-update-slice_fusion, f32[16]{0:T(128)S(1)} %add_rsqrt_fusion), kind=kOutput, calls=%fused_computation.12 | convolution fusion | flops 100669440 | bytes 6578240 | tf_op jit(solution)/shard_map/decode/dot_general | solution.py:201
  216.4 12.5 %all_to_all.59 = bf16[16,32,256]{2,0,1:T(8,128)(2,1)S(1)} all-to-all(bf16[16,32,256]{2,0,1:T(8,128)(2,1)S(1)} %bitcast.122), channel_id=1, replica_groups=mesh['grp'=8,'head'=32] {'head'}, dimensions={1} | all-to-all | bytes 524288 | tf_op jit(solution)/shard_map/sum/all_to_all | solution.py:228
  (137 shorter events, 12.9 us)
Async XLA Ops:
  0.0 120.8 %copy-start = (bf16[128,8192]{1,0:T(8,128)(2,1)S(1)}, bf16[128,8192]{1,0:T(8,128)(2,1)}, u32[]{:S(2)}) copy-start(bf16[128,8192]{1,0:T(8,128)(2,1)} %param.17) | copy-start | bytes 6291460
  0.0 9.9 %copy-start.2 = (bf16[8192,128]{1,0:T(8,128)(2,1)S(1)}, bf16[8192,128]{1,0:T(8,128)(2,1)}, u32[]{:S(2)}) copy-start(bf16[8192,128]{1,0:T(8,128)(2,1)} %param.16) | copy-start | bytes 6291460
  3.1 24.6 %collective-permute-start = (bf16[16,4096]{1,0:T(8,128)(2,1)S(1)}, bf16[16,4096]{1,0:T(8,128)(2,1)S(1)}, u32[]{:S(2)}, u32[]{:S(2)}) collective-permute-start(bf16[16,4096]{1,0:T(8,128)(2,1)S(1)} %get-tuple-element.48), channel_id=1, source_target_pairs={{0,1},{1,0},{2,3},{3,2},{4,5},{5,4},{6,7},{7,6},{8,9},{9,8},{10,11... | collective-permute-start | bytes 393224 | tf_op jit(solution)/shard_map/rows/ppermute | solution.py:65
  11.6 2.3 copy-start.11
  11.6 8.8 %copy-start.8 = (s32[8,16]{1,0:T(8,128)S(1)}, s32[8,16]{1,0:T(8,128)}, u32[]{:S(2)}) copy-start(s32[8,16]{1,0:T(8,128)} %param.11) | copy-start | bytes 1540
  11.6 8.9 %copy-start.1 = (f32[16,8192]{1,0:T(8,128)S(1)}, f32[16,8192]{1,0:T(8,128)}, u32[]{:S(2)}) copy-start(f32[16,8192]{1,0:T(8,128)} %param.12) | copy-start | bytes 1572868
  13.8 10.0 %copy-start.6 = (f32[8192]{0:T(1024)S(1)}, f32[8192]{0:T(1024)}, u32[]{:S(2)}) copy-start(f32[8192]{0:T(1024)} %param.13) | copy-start | bytes 98308
  13.8 56.7 %collective-permute-start.5 = (bf16[4096,256]{1,0:T(8,128)(2,1)}, bf16[4096,256]{1,0:T(8,128)(2,1)}, u32[]{:S(2)}, u32[]{:S(2)}) collective-permute-start(bf16[4096,256]{1,0:T(8,128)(2,1)} %get-tuple-element.39), channel_id=1, source_target_pairs={{0,1},{1,0},{2,3},{3,2},{4,5},{5,4},{6,7},{7,6},{8,9},{9,8},{10,11... | collective-permute-start | bytes 6291464 | tf_op jit(solution)/shard_map/weights/ppermute | solution.py:65
  14.4 32.1 %all-to-all-start = ((s32[32,1,16]{2,1,0:T(1,128)}), s32[32,1,16]{2,1,0:T(1,128)S(1)}, u32[]{:S(2)}, u32[]{:S(2)}) async-start(s32[32,1,16]{2,1,0:T(1,128)} %broadcast_in_dim.249), calls=%async_computation | async-start | bytes 32768 | tf_op jit(solution)/shard_map/ids/all_to_all | solution.py:118
  27.6 36.3 %copy-start.4 = (f32[16,384]{1,0:T(8,128)}, f32[16,384]{1,0:T(8,128)S(1)}, u32[]{:S(2)}) copy-start(f32[16,384]{1,0:T(8,128)S(1)} %fusion.19) | copy-start | bytes 73732
  27.7 8.3 %collective-permute-start.1 = (bf16[32,4096]{1,0:T(8,128)(2,1)S(1)}, bf16[32,4096]{1,0:T(8,128)(2,1)S(1)}, u32[]{:S(2)}, u32[]{:S(2)}) collective-permute-start(bf16[32,4096]{1,0:T(8,128)(2,1)S(1)} %pad_maximum_fusion.2), channel_id=1, source_target_pairs={{0,2},{1,9},{2,0},{3,11},{4,6},{5,13},{6,4},{7,15},{8,10},{9,1},{1... | collective-permute-start | bytes 786440 | tf_op jit(solution)/shard_map/rows/ppermute | solution.py:65
  29.2 6.7 %collective-permute-start.2 = (bf16[32,4096]{1,0:T(8,128)(2,1)S(1)}, bf16[32,4096]{1,0:T(8,128)(2,1)S(1)}, u32[]{:S(2)}, u32[]{:S(2)}) collective-permute-start(bf16[32,4096]{1,0:T(8,128)(2,1)S(1)} %pad_maximum_fusion.2), channel_id=1, source_target_pairs={{0,6},{1,25},{2,4},{3,27},{4,2},{5,29},{6,0},{7,31},{8,14},{9,17},... | collective-permute-start | bytes 786440 | tf_op jit(solution)/shard_map/rows/ppermute | solution.py:65
  35.9 3.9 %collective-permute-start.3 = (bf16[16,4096]{1,0:T(8,128)(2,1)S(1)}, bf16[16,4096]{1,0:T(8,128)(2,1)S(1)}, u32[]{:S(2)}, u32[]{:S(2)}) collective-permute-start(bf16[16,4096]{1,0:T(8,128)(2,1)S(1)} %slice.242), channel_id=1, source_target_pairs={{0,2},{1,9},{2,0},{3,11},{4,6},{5,13},{6,4},{7,15},{8,10},{9,1},{1... | collective-permute-start | bytes 393224 | tf_op jit(solution)/shard_map/rows/ppermute | solution.py:65
  36.0 5.1 %collective-permute-start.4 = (bf16[16,4096]{1,0:T(8,128)(2,1)S(1)}, bf16[16,4096]{1,0:T(8,128)(2,1)S(1)}, u32[]{:S(2)}, u32[]{:S(2)}) collective-permute-start(bf16[16,4096]{1,0:T(8,128)(2,1)S(1)} %slice.243), channel_id=1, source_target_pairs={{0,6},{1,25},{2,4},{3,27},{4,2},{5,29},{6,0},{7,31},{8,14},{9,17},... | collective-permute-start | bytes 393224 | tf_op jit(solution)/shard_map/rows/ppermute | solution.py:65
  42.5 23.3 %collective-permute-start.6 = (bf16[128,4096]{1,0:T(8,128)(2,1)}, bf16[128,4096]{1,0:T(8,128)(2,1)}, u32[]{:S(2)}, u32[]{:S(2)}) collective-permute-start(bf16[128,4096]{1,0:T(8,128)(2,1)} %constant_dynamic-update-slice_fusion.3), channel_id=1, source_target_pairs={{0,8},{1,3},{2,10},{3,1},{4,12},{5,7},{6,14},{7,5},{8,0},{9,11},{1... | collective-permute-start | bytes 3145736 | tf_op jit(solution)/shard_map/rows/ppermute | solution.py:65
  43.4 20.4 %collective-permute-start.7 = (bf16[128,4096]{1,0:T(8,128)(2,1)}, bf16[128,4096]{1,0:T(8,128)(2,1)}, u32[]{:S(2)}, u32[]{:S(2)}) collective-permute-start(bf16[128,4096]{1,0:T(8,128)(2,1)} %constant_dynamic-update-slice_fusion.3), channel_id=1, source_target_pairs={{0,24},{1,7},{2,26},{3,5},{4,28},{5,3},{6,30},{7,1},{8,16},{9,15},... | collective-permute-start | bytes 3145736 | tf_op jit(solution)/shard_map/rows/ppermute | solution.py:65
  48.5 14.6 %all-to-all-start.1 = ((s32[8,1,8]{2,1,0:T(1,128)}), s32[8,1,8]{2,1,0:T(1,128)S(1)}, u32[]{:S(2)}, u32[]{:S(2)}) async-start(s32[8,1,8]{2,1,0:T(1,128)} %broadcast_in_dim.250), calls=%async_computation.1 | async-start | bytes 8192 | tf_op jit(solution)/shard_map/ids/all_to_all | solution.py:124
  64.9 8.5 %collective-permute-start.8 = (bf16[64,4096]{1,0:T(8,128)(2,1)S(1)}, bf16[64,4096]{1,0:T(8,128)(2,1)}, u32[]{:S(2)}, u32[]{:S(2)}) collective-permute-start(bf16[64,4096]{1,0:T(8,128)(2,1)S(1)} %bitcast.128), channel_id=1, source_target_pairs={{0,8},{1,3},{2,10},{3,1},{4,12},{5,7},{6,14},{7,5},{8,0},{9,11},{1... | collective-permute-start | bytes 1572872 | tf_op jit(solution)/shard_map/rows/ppermute | solution.py:65
  67.7 9.9 %collective-permute-start.9 = (bf16[64,4096]{1,0:T(8,128)(2,1)}, bf16[64,4096]{1,0:T(8,128)(2,1)}, u32[]{:S(2)}, u32[]{:S(2)}) collective-permute-start(bf16[64,4096]{1,0:T(8,128)(2,1)} %bitcast.10), channel_id=1, source_target_pairs={{0,24},{1,7},{2,26},{3,5},{4,28},{5,3},{6,30},{7,1},{8,16},{9,15},... | collective-permute-start | bytes 1572872 | tf_op jit(solution)/shard_map/rows/ppermute | solution.py:65
  77.6 3.4 %copy-start.3 = (bf16[4096,256]{1,0:T(8,128)(2,1)S(1)}, bf16[4096,256]{1,0:T(8,128)(2,1)}, u32[]{:S(2)}) copy-start(bf16[4096,256]{1,0:T(8,128)(2,1)} %get-tuple-element.38) | copy-start | bytes 6291460
  77.6 3.4 %copy-start.9 = (bf16[128,4096]{1,0:T(8,128)(2,1)S(1)}, bf16[128,4096]{1,0:T(8,128)(2,1)}, u32[]{:S(2)}) copy-start(bf16[128,4096]{1,0:T(8,128)(2,1)} %constant_dynamic-update-slice_fusion.3) | copy-start | bytes 3145732
  88.7 8.8 %copy-start.10 = (f32[64]{0:T(128)S(1)}, f32[64]{0:T(128)}, u32[]{:S(2)}) copy-start(f32[64]{0:T(128)} %multiply_exponential_fusion) | copy-start | bytes 772
  91.7 7.4 %collective-permute-start.10 = (f32[512,256]{1,0:T(8,128)}, f32[512,256]{1,0:T(8,128)}, u32[]{:S(2)}, u32[]{:S(2)}) collective-permute-start(f32[512,256]{1,0:T(8,128)} %bitcast.129), channel_id=1, source_target_pairs={{0,1},{1,0},{2,3},{3,2},{4,5},{5,4},{6,7},{7,6},{8,9},{9,8},{10,11... | collective-permute-start | bytes 1572872 | tf_op jit(solution)/shard_map/project/ppermute | solution.py:65
  100.3 27.0 %copy-start.7 = (f32[8192]{0:T(1024)S(1)}, f32[8192]{0:T(1024)}, u32[]{:S(2)}) copy-start(f32[8192]{0:T(1024)} %param.13) | copy-start | bytes 98308
  101.8 18.5 %all-to-all-start.2 = ((bf16[8,96,256]{2,1,0:T(8,128)(2,1)}), bf16[8,96,256]{2,1,0:T(8,128)(2,1)S(1)}, u32[]{:S(2)}, u32[]{:S(2)}) async-start(bf16[8,96,256]{2,1,0:T(8,128)(2,1)} %bitcast.19), calls=%async_computation.2 | async-start | bytes 786432 | tf_op jit(solution)/shard_map/project/all_to_all | solution.py:175
  122.9 13.4 %all-to-all-start.3 = ((bf16[16,32,256]{2,0,1:T(8,128)(2,1)}), bf16[16,32,256]{2,0,1:T(8,128)(2,1)S(1)}, u32[]{:S(2)}, u32[]{:S(2)}) async-start(bf16[16,32,256]{2,0,1:T(8,128)(2,1)} %bitcast.104), calls=%async_computation.3 | async-start | bytes 524288 | tf_op jit(solution)/shard_map/sum/all_to_all | solution.py:228
  137.0 17.7 %copy-start.5 = (f32[16,384]{1,0:T(8,128)S(1)}, f32[16,384]{1,0:T(8,128)}, u32[]{:S(2)}) copy-start(f32[16,384]{1,0:T(8,128)} %copy-done.4) | copy-start | bytes 73732
  137.0 12.9 %all-to-all-start.4 = ((bf16[16,32,256]{2,0,1:T(8,128)(2,1)}), bf16[16,32,256]{2,0,1:T(8,128)(2,1)S(1)}, u32[]{:S(2)}, u32[]{:S(2)}) async-start(bf16[16,32,256]{2,0,1:T(8,128)(2,1)} %broadcast_in_dim.273), calls=%async_computation.4 | async-start | bytes 524288 | tf_op jit(solution)/shard_map/spread/all_to_all | solution.py:235

commit v3 on v1

v3 whole, which is shorter than its diff:
```python
import math

import jax
import jax.numpy as jnp
from jax import lax
from jax.experimental import pallas as pl
from jax.experimental.pallas import tpu as pltpu
from jax.sharding import PartitionSpec as P

HD = 128
STEPS = 4
EPSILON = 1e-05
ROPE_BASE = 10000.0
MASKED = -1e30


def normed(values, norm_gain):
    widened = values.astype(jnp.float32)
    factor = lax.rsqrt(jnp.mean(widened * widened, axis=-1, keepdims=True) + EPSILON)
    return (widened * factor * norm_gain).astype(jnp.bfloat16)


def angles_of(positions):
    half = HD // 2
    frequency = jnp.exp(
        jnp.arange(half, dtype=jnp.float32) * (-2.0 * math.log(ROPE_BASE) / HD)
    )
    angles = positions.astype(jnp.float32)[..., None] * frequency
    cosine = jnp.cos(angles)
    sine = jnp.sin(angles)
    return (
        jnp.concatenate([cosine, cosine], axis=-1),
        jnp.concatenate([-sine, sine], axis=-1),
    )


def turned(values, cosine, sine):
    half = HD // 2
    swapped = jnp.concatenate([values[..., half:], values[..., :half]], axis=-1)
    return values * cosine + swapped * sine


NX = 4
NY = 4
HELD = ((0, 0), (0, 1), (1, 0), (1, 1), (3, 0), (3, 1), (2, 0), (2, 1))
EARLY = 6
EMPTY = 1e30


def head_pairs(move):
    pairs = []
    for y in range(NY):
        for x in range(NX):
            for c in range(2):
                ty, tx, tc = move(y, x, c)
                pairs.append(((y * NX + x) * 2 + c, (ty * NX + tx) * 2 + tc))
    return pairs


def lane(first, second):
    return head_pairs(
        lambda y, x, c: (y ^ second, x ^ first, c) if c == 0 else (y ^ first, x ^ second, c)
    )


CORE = head_pairs(lambda y, x, c: (y, x, c ^ 1))


def send(values, pairs):
    return lax.ppermute(values, "head", pairs)


def after(values, piece):
    return values + (piece[0, 0].astype(jnp.float32) * 0.0).astype(values.dtype)


def params(mib):
    return pltpu.CompilerParams(vmem_limit_bytes=mib * 1024 * 1024)


def norm_split_kernel(group_ref, rows_ref, gain_ref, kept_ref, given_ref):
    n, half = rows_ref.shape[0], rows_ref.shape[1] // 2
    core = lax.rem(lax.axis_index("head"), 2)
    rows = rows_ref[...].astype(jnp.float32)
    factor = lax.rsqrt(jnp.mean(rows * rows, axis=1, keepdims=True) + EPSILON)
    result = (rows * factor * gain_ref[...]).astype(jnp.bfloat16)
    row = lax.broadcasted_iota(jnp.int32, (n, HD), 0)
    ids = jnp.zeros((n, HD), jnp.int32)
    for j in range(n):
        ids = jnp.where(row == j, group_ref[j], ids)
    ids = ids.astype(jnp.float32).astype(jnp.bfloat16)
    kept_ref[:, half:] = ids
    given_ref[:, half:] = ids

    @pl.when(core == 0)
    def _():
        kept_ref[:, :half] = result[:, :half]
        given_ref[:, :half] = result[:, half:]

    @pl.when(core == 1)
    def _():
        kept_ref[:, :half] = result[:, half:]
        given_ref[:, :half] = result[:, :half]


def norm_split(groups, rows, gain):
    shape = jax.ShapeDtypeStruct((rows.shape[0], rows.shape[1] // 2 + HD), jnp.bfloat16)
    whole = pl.BlockSpec(memory_space=pltpu.VMEM)
    return pl.pallas_call(
        norm_split_kernel,
        out_shape=(shape, shape),
        in_specs=[pl.BlockSpec(memory_space=pltpu.SMEM), whole, whole],
        compiler_params=params(8),
        name="norm_split",
    )(groups, rows, gain.reshape(1, -1))


def other_half_kernel(key_ref, value_ref, dep_ref, out_ref, sems):
    half = out_ref.shape[0]
    core = lax.rem(lax.axis_index("head"), 2)
    rows = pl.ds(pl.multiple_of((1 - core) * half, half), half)
    one = pltpu.make_async_copy(key_ref.at[rows], out_ref.at[:, :HD], sems.at[0])
    two = pltpu.make_async_copy(value_ref.at[rows], out_ref.at[:, HD:], sems.at[1])
    one.start()
    two.start()
    one.wait()
    two.wait()


def other_half(w_key, w_value, dep):
    anywhere = pl.BlockSpec(memory_space=pl.ANY)
    return pl.pallas_call(
        other_half_kernel,
        out_shape=jax.ShapeDtypeStruct((w_key.shape[0] // 2, 2 * HD), jnp.bfloat16),
        in_specs=[anywhere] * 3,
        out_specs=anywhere,
        scratch_shapes=[pltpu.SemaphoreType.DMA((2,))],
        compiler_params=params(4),
        name="other_half",
    )(w_key, w_value, dep)


CHUNKS = 4


def project_kernel(count, *refs):
    pieces = refs[:count]
    key_ref, value_ref, their_ref, own_ref, other_ref, ids_ref, x, w, piece_sems, weight_sems = refs[count:]
    size = pieces[0].shape[0]
    half = w.shape[0]
    depth = half // CHUNKS
    core = lax.rem(lax.axis_index("head"), 2)
    loads = []
    for k in range(CHUNKS):
        mine = pl.ds(pl.multiple_of(core * half + k * depth, depth), depth)
        here = slice(k * depth, (k + 1) * depth)
        loads.append(
            [
                pltpu.make_async_copy(key_ref.at[mine], w.at[here, :HD], weight_sems.at[k, 0]),
                pltpu.make_async_copy(
                    value_ref.at[mine], w.at[here, HD : 2 * HD], weight_sems.at[k, 1]
                ),
                pltpu.make_async_copy(
                    their_ref.at[here], w.at[here, 2 * HD :], weight_sems.at[k, 2]
                ),
            ]
        )
    rows = [
        pltpu.make_async_copy(p, x.at[i * size : (i + 1) * size], piece_sems.at[i])
        for i, p in enumerate(pieces)
    ]
    for load in loads[0]:
        load.start()
    for row in rows:
        row.start()
    for k in range(1, CHUNKS):
        for load in loads[k]:
            load.start()
    for row in rows:
        row.wait()
    ids_ref[...] = x[:, half:]
    for k in range(CHUNKS):
        for load in loads[k]:
            load.wait()
        here = slice(k * depth, (k + 1) * depth)
        term = jnp.dot(x[:, here], w[here, :], preferred_element_type=jnp.float32)
        if k == 0:
            own_ref[...] = term[:, : 2 * HD]
            other_ref[...] = term[:, 2 * HD :]
        else:
            own_ref[...] += term[:, : 2 * HD]
            other_ref[...] += term[:, 2 * HD :]


def project(pieces, w_key, w_value, their_half):
    count = len(pieces)
    size, wide = pieces[0].shape
    half = wide - HD
    rows = count * size
    anywhere = pl.BlockSpec(memory_space=pl.ANY)
    shape = jax.ShapeDtypeStruct((rows, 2 * HD), jnp.float32)
    return pl.pallas_call(
        lambda *refs: project_kernel(count, *refs),
        out_shape=(shape, shape, jax.ShapeDtypeStruct((rows, HD), jnp.bfloat16)),
        in_specs=[anywhere] * (count + 3),
        scratch_shapes=[
            pltpu.VMEM((rows, wide), jnp.bfloat16),
            pltpu.VMEM((half, 4 * HD), jnp.bfloat16),
            pltpu.SemaphoreType.DMA((count,)),
            pltpu.SemaphoreType.DMA((CHUNKS, 3)),
        ],
        compiler_params=params(16),
        name="project",
    )(*pieces, w_key, w_value, their_half)


def origin(shape, dim, head):
    at = lax.broadcasted_iota(jnp.int32, shape, dim)
    block, row = at >> 4, at & 15
    turn = block >> 3
    d_second, d_first, d_core = turn ^ (turn >> 1), block & 3, (block >> 2) & 1
    core = head & 1
    dy = jnp.where(core == 0, d_second, d_first)
    dx = jnp.where(core == 0, d_first, d_second)
    y, x, c = (head >> 3) ^ dy, ((head >> 1) & 3) ^ dx, core ^ d_core
    return (((y * NX + x) * 2 + c) << 4) + row


def finish_kernel(groups, own_a, own_b, their_a, their_b, ids_a, ids_b, out_ref, packed):
    total = packed.shape[0]
    n = total // (len(HELD) * NX)
    early = EARLY * NX
    head = lax.axis_index("head")
    cap = out_ref.shape[0] // groups

    def block(first, second, i):
        return first[i * n : (i + 1) * n] if i < early else second[(i - early) * n : (i - early + 1) * n]

    for at, (d_second, d_core) in enumerate(HELD):
        for d_first in range(NX):
            i = at * NX + d_first
            j = HELD.index((d_first, 1 - d_core)) * NX + d_second
            both = block(own_a, own_b, i) + block(their_a, their_b, j)
            packed[i * n : (i + 1) * n, :] = both.astype(jnp.bfloat16)
    ids = jnp.concatenate([ids_a[...], ids_b[...]], axis=0).astype(jnp.float32)
    lanes = lax.broadcasted_iota(jnp.int32, (total, HD), 1).astype(jnp.float32)
    match = jnp.where(ids == lanes, 1.0, 0.0)
    earlier = origin((total, total), 1, head) < origin((total, total), 0, head)
    ranks = jnp.dot(
        jnp.where(earlier, 1.0, 0.0).astype(jnp.bfloat16),
        match.astype(jnp.bfloat16),
        preferred_element_type=jnp.float32,
    )
    order = jnp.sum(ranks * match, axis=1, keepdims=True)
    slot = ids[:, :1] * cap + order
    slots = lax.broadcasted_iota(jnp.int32, (total, groups * cap), 1).astype(jnp.float32)
    pick = jnp.where(slots == slot, 1.0, 0.0).astype(jnp.bfloat16)
    routed = lax.dot_general(
        pick, packed[...], (((0,), (0,)), ((), ())), preferred_element_type=jnp.float32
    )
    counts = jnp.sum(match, axis=0, keepdims=True)
    step = lax.broadcasted_iota(jnp.int32, (cap, HD), 0).astype(jnp.float32)
    for g in range(groups):
        rows = slice(g * cap, (g + 1) * cap)
        filled = step < counts[:, g : g + 1]
        out_ref[rows, :HD] = jnp.where(filled, routed[rows, :HD], EMPTY).astype(jnp.bfloat16)
        out_ref[rows, HD:] = routed[rows, HD:].astype(jnp.bfloat16)


def finish(groups, slots, own_a, own_b, their_a, their_b, ids_a, ids_b):
    return pl.pallas_call(
        lambda *refs: finish_kernel(groups, *refs),
        out_shape=jax.ShapeDtypeStruct((slots, 2 * HD), jnp.bfloat16),
        scratch_shapes=[pltpu.VMEM((own_a.shape[0] + own_b.shape[0], 2 * HD), jnp.bfloat16)],
        compiler_params=params(24),
        name="finish",
    )(own_a, own_b, their_a, their_b, ids_a, ids_b)


def settle_kernel(groups, cache_ref, edge_row, edge_col, high_ref, low_ref, key_ref, bias_ref, hot):
    slots = cache_ref.shape[0]
    cap = slots // groups
    starts, ends = edge_row[0:1, :], edge_row[1:2, :]
    lanes = lax.broadcasted_iota(jnp.int32, (cap, HD), 1).astype(jnp.float32)
    step = lax.broadcasted_iota(jnp.int32, (cap, 1), 0).astype(jnp.float32)
    across = lax.broadcasted_iota(jnp.int32, (1, slots), 1).astype(jnp.float32)
    cells = across
    open_slots = across < 0.0
    base = jnp.zeros((1, 1), jnp.float32)
    for g in range(groups):
        rows = slice(g * cap, (g + 1) * cap)
        full = cache_ref[rows, :HD].astype(jnp.float32) < EMPTY / 2
        count = jnp.sum(jnp.where(full, 1.0, 0.0), axis=0, keepdims=True)[:, :1]
        cell = base + step
        inside = (cell >= starts) & (cell < ends)
        place = cell - jnp.sum(jnp.where(inside, starts, 0.0), axis=1, keepdims=True)
        hot[rows, :] = jnp.where(lanes == place, 1.0, 0.0).astype(jnp.bfloat16)
        here = (across >= g * cap) & (across < (g + 1) * cap)
        cells = jnp.where(here, across - g * cap + base, cells)
        open_slots = open_slots | (here & (across - g * cap < count))
        base = base + count
    low_edge, high_edge = edge_col[:, 0:1], edge_col[:, HD : HD + 1]
    mine = (cells >= low_edge) & (cells < high_edge) & open_slots
    bias_ref[...] = jnp.where(mine, 0.0, MASKED)
    trig = jnp.dot(hot[...], high_ref[...], preferred_element_type=jnp.float32)
    trig = trig + jnp.dot(hot[...], low_ref[...], preferred_element_type=jnp.float32)
    keys = cache_ref[:, :HD].astype(jnp.float32)
    keys = jnp.where(keys < EMPTY / 2, keys, 0.0)
    key_ref[...] = (keys * trig[:, :HD] + pltpu.roll(keys, HD // 2, 1) * trig[:, HD:]).astype(
        jnp.bfloat16
    )


def settle(groups, cache, edge_row, edge_col, high, low):
    slots = cache.shape[0]
    return pl.pallas_call(
        lambda *refs: settle_kernel(groups, *refs),
        out_shape=(
            jax.ShapeDtypeStruct((slots, HD), jnp.bfloat16),
            jax.ShapeDtypeStruct((edge_col.shape[0], slots), jnp.float32),
        ),
        scratch_shapes=[pltpu.VMEM((slots, HD), jnp.bfloat16)],
        compiler_params=params(16),
        name="settle",
    )(cache, edge_row, edge_col, high, low)


def per_device(
    prefill_rows, row_group, lengths, decode_state, norm_gain, w_query, w_key, w_value, w_out
):
    groups = lax.axis_size("grp")
    heads = lax.axis_size("head")
    rows_local, width = prefill_rows.shape
    plane_rows = rows_local * heads
    cap = (rows_local // groups + rows_local // groups // 2) * heads
    requests = lengths.shape[1]
    my_group = lax.axis_index("grp")
    my_head = lax.axis_index("head")
    share = width // heads
    f32, bf16 = jnp.float32, jnp.bfloat16

    core = my_head % 2
    with jax.named_scope("rows"):
        n = rows_local
        kept, given = norm_split(row_group, prefill_rows, norm_gain)
        got = send(given, CORE)
        start = jnp.concatenate([kept, got])
        f2 = send(start, lane(2, 0))
        f1 = send(start, lane(1, 0))
        f3 = send(start, lane(3, 0))
        l0 = jnp.concatenate([kept, f1[:n], f2[:n], f3[:n]])
        l1 = jnp.concatenate([got, f1[n:], f2[n:], f3[n:]])
        s11 = send(l1, lane(0, 1))
        s30 = send(l0, lane(0, 3))
        s10 = send(l0, lane(0, 1))
        s31 = send(l1, lane(0, 3))
        s20 = send(s30, lane(0, 1))
        s21 = send(s11, lane(0, 3))
    with jax.named_scope("weights"):
        their_half = send(other_half(w_key, w_value, f1), CORE)

    with jax.named_scope("places"):
        group_ids = jnp.arange(groups, dtype=jnp.int32)
        late_lengths = after(lengths, f1)
        my_lengths = jnp.sum(
            jnp.where((group_ids == my_group)[:, None], late_lengths, 0), axis=0
        )
        request = jnp.arange(requests, dtype=jnp.int32)
        my_ends = jnp.sum(jnp.where(request[None, :] <= request[:, None], my_lengths[None, :], 0), axis=1)
        my_starts = my_ends - my_lengths
        edges = jnp.stack([my_starts, my_ends]).astype(f32)
        edge_row = jnp.pad(edges, ((0, 0), (0, HD - requests)), constant_values=1e9)
        edge_col = jnp.repeat(edges, HD, axis=0).T.reshape(requests, 2 * HD)
        spots = jnp.arange(HD, dtype=jnp.int32) + 0 * my_lengths[0]
        table = jnp.concatenate(angles_of(spots), axis=1)
        table_high = table.astype(bf16)
        table_low = (table - table_high.astype(f32)).astype(bf16)

    with jax.named_scope("project"):
        own_a, other_a, ids_a = project([l0, l1, s10, s11, s30, s31], w_key, w_value, their_half)
        own_b, other_b, ids_b = project([s20, s21], w_key, w_value, their_half)
        outgoing = finish(
            groups, groups * cap, own_a, own_b, send(other_a, CORE), send(other_b, CORE), ids_a, ids_b
        )
        cache = lax.all_to_all(
            outgoing.reshape(groups, cap, 2 * HD), "grp", split_axis=0, concat_axis=0, tiled=True
        ).reshape(groups * cap, 2 * HD)
        cache_keys, bias = settle(groups, cache, edge_row, edge_col, table_high, table_low)
        cache_values = cache[:, HD:]

    scale = HD ** (-0.5)
    new_keys, new_values = [], []
    current = lax.dynamic_slice_in_dim(decode_state, my_head * share, share, 1)
    my_gain = lax.dynamic_slice_in_dim(norm_gain, my_head * share, share, 0)
    inverse = 1.0 / norm_gain
    decode_rows = normed(after(decode_state, f1), norm_gain)
    factor = None
    for step in range(STEPS):
        with jax.named_scope("decode"):
            scaled = 1.0 if factor is None else factor
            key_now = jnp.dot(decode_rows, w_key, preferred_element_type=f32) * scaled
            value_now = jnp.dot(decode_rows, w_value, preferred_element_type=f32) * scaled
            query_now = jnp.dot(decode_rows, w_query, preferred_element_type=f32) * scaled
            cos_now, sin_now = angles_of(my_lengths + step)
            new_key = turned(key_now, cos_now, sin_now).astype(bf16)
            new_value = value_now.astype(bf16)
            query = turned(query_now, cos_now, sin_now).astype(bf16)
            new_keys.append(new_key)
            new_values.append(new_value)
            scores = jnp.einsum("rd,cd->rc", query, cache_keys, preferred_element_type=f32) * scale
            wide = query.astype(f32)
            fresh = jnp.stack(
                [jnp.sum(wide * k.astype(f32), axis=1) * scale for k in new_keys], axis=1
            )
            scores = scores + bias
            peak = jnp.maximum(jnp.max(scores, axis=1), jnp.max(fresh, axis=1))
            cache_exp = jnp.exp(scores - peak[:, None])
            fresh_exp = jnp.exp(fresh - peak[:, None])
            total = jnp.sum(cache_exp, axis=1) + jnp.sum(fresh_exp, axis=1)
            cache_weights = (cache_exp / total[:, None]).astype(bf16)
            fresh_weights = (fresh_exp / total[:, None]).astype(bf16).astype(f32)
            attended = jnp.dot(cache_weights, cache_values, preferred_element_type=f32)
            for back, value in enumerate(new_values):
                attended = attended + fresh_weights[:, back : back + 1] * value.astype(f32)
            term = jnp.dot(attended.astype(bf16), w_out, preferred_element_type=f32).astype(bf16)
        with jax.named_scope("sum"):
            parts = lax.all_to_all(
                term.reshape(requests, heads, share), "head", split_axis=1, concat_axis=1, tiled=True
            )
            current = current + jnp.sum(parts.astype(f32), axis=1)
        if step + 1 < STEPS:
            with jax.named_scope("spread"):
                piece = (current * my_gain[None, :]).astype(bf16)
                decode_rows = lax.all_to_all(
                    jnp.broadcast_to(piece[:, None, :], (requests, heads, share)),
                    "head", split_axis=1, concat_axis=1, tiled=True,
                ).reshape(requests, width)
                plain = decode_rows.astype(f32) * inverse
                factor = lax.rsqrt(jnp.mean(plain * plain, axis=1, keepdims=True) + EPSILON)
    return current


def solution(mesh):
    return jax.shard_map(
        per_device,
        mesh=mesh,
        in_specs=(
            P(("grp", "head"), None),
            P(("grp", "head")),
            P(),
            P("grp", None),
            P(),
            P(None, "head"),
            P(None, "head"),
            P(None, "head"),
            P("head", None),
        ),
        out_specs=P("grp", "head"),
        check_vma=False,
    )
```

time: 220 us -> 186 us (0.85)
  waiting for transfers between devices: 58.6 us -> 39.5 us
  between operations: 13.8 us -> 1.28 us
  Pallas kernels: 0 us -> 12.3 us
  matrix products: 24.1 us -> 14.8 us
  other arithmetic: 15 us -> 8.35 us
  starting transfers between devices: 33 us -> 36.2 us
  local copies, waits for them, and re-layouts: 12.1 us -> 9.39 us
    all_gather x1 -> x0, waiting for transfers between devices: 23 us -> none  [per_device(): plane = lax.all_gather(normal_rows, 'head', axis=0, tiled=True)]
    ppermute x0 -> x13, starting transfers between devices: none -> 18.6 us  [send(): return lax.ppermute(values, 'head', pairs)]
    all_to_all x2 -> x0, starting transfers between devices: 16.8 us -> none  [the longest x1 8.59 us: per_device(): lax.all_to_all(jnp.broadcast_to(row_group[None, :], (heads, rows_local)),...]
    pallas_call x0 -> x6, Pallas kernels: none -> 12.3 us  [the longest x2 6.45 us: project(): pl.pallas_call(lambda *refs: project_kernel(count, *refs), out_shape=(sha...]
    dot_general x7 -> x12, matrix products: 20.6 us -> 11.3 us  [the longest x4 4.89 us: per_device(): key_now = jnp.dot(decode_rows, w_key, preferred_element_type=f32) * scaled]
    ppermute x0 -> x13, waiting for transfers between devices: none -> 8.85 us  [send(): return lax.ppermute(values, 'head', pairs)]
    all_to_all x2 -> x0, waiting for transfers between devices: 5.05 us -> none  [the longest x1 5.05 us: per_device(): lax.all_to_all(jnp.broadcast_to(plane_counts[None, :], (groups, groups)),...]
    unnamed x18 -> x42, local copies, waits for them, and re-layouts: 6.9 us -> 5.74 us
  transfers between devices with their start and end apart: 6 -> 16, of which waited for: 5 -> 7; matrix products, arithmetic and copies ran while one was open for 8% -> 6% of each run, Pallas kernels for 0% -> 4%
where the time goes in v3:
time: 186 us; the launch traced here: 185 us
  blocking collectives  62.7 us (34%)
  waiting for transfers between devices  39.5 us (21%)
  starting transfers between devices  36.2 us (19%)
  matrix products  14.8 us (8%)
  Pallas kernels  12.3 us (7%)
  local copies, waits for them, and re-layouts  9.39 us (5%)
  other arithmetic  8.35 us (4%)
    all_to_all x3, blocking collectives, per_device(): lax.all_to_all(term.reshape(requests, heads, share), 'head', split_axis=1...  37.6 us
    all_to_all x2, blocking collectives, per_device(): lax.all_to_all(jnp.broadcast_to(piece[:, None, :], (requests, heads, shar...  25 us
    ppermute x13, starting transfers between devices, send(): return lax.ppermute(values, 'head', pairs)  18.6 us
    all_to_all x1, waiting for transfers between devices, per_device(): lax.all_to_all(outgoing.reshape(groups, cap, 2 * HD), 'grp', split_axis=0...  12.9 us
    all_to_all x1, waiting for transfers between devices, per_device(): lax.all_to_all(jnp.broadcast_to(piece[:, None, :], (requests, heads, shar...  8.97 us
    ppermute x13, waiting for transfers between devices, send(): return lax.ppermute(values, 'head', pairs)  8.85 us
    all_to_all x1, waiting for transfers between devices, per_device(): lax.all_to_all(term.reshape(requests, heads, share), 'head', split_axis=1...  8.82 us
    all_to_all x1, starting transfers between devices, per_device(): lax.all_to_all(outgoing.reshape(groups, cap, 2 * HD), 'grp', split_axis=0...  7.07 us
  transfers between devices with their start and end apart: 16, of which 7 were waited for; matrix products, arithmetic and copies ran while one was open for 6% of the time, Pallas kernels for 4%

profile of v3, /device:TPU:1, one launch (start us, length us, event | category | flops | bytes accessed | tf_op | source)
XLA Modules:
  0.0 184.6 jit_solution(16337327983658000236)
XLA Ops:
  0.0 0.9 copy-done.10
  0.9 0.9 copy-done.12
  1.9 0.7 copy-done.13
  2.5 0.8 norm_split.1
  3.3 3.3 %collective-permute-start = (bf16[16,4224]{1,0:T(8,128)(2,1)S(1)}, bf16[16,4224]{1,0:T(8,128)(2,1)S(1)}, u32[]{:S(2)}, u32[]{:S(2)}) collective-permute-start(bf16[16,4224]{1,0:T(8,128)(2,1)S(1)} %get-tuple-element.16), channel_id=1, source_target_pairs={{0,1},{1,0},{2,3},{3,2},{4,5},{5,4},{6,7},{7,6},{8,9},{9,8},{10,11... | collective-permute-start | bytes 405512 | tf_op jit(solution)/shard_map/rows/ppermute | solution.py:70
  6.7 0.7 constant_dynamic-update-slice_fusion.1
  7.3 0.3 multiply_cosine_fusion
  7.6 0.7 constant_dynamic-update-slice_fusion
  8.3 1.0 collective-permute-start.3
  9.5 0.4 collective-permute-start.2
  10.0 1.9 %collective-permute-start.1 = (bf16[32,4224]{1,0:T(8,128)(2,1)}, bf16[32,4224]{1,0:T(8,128)(2,1)S(1)}, u32[]{:S(2)}, u32[]{:S(2)}) collective-permute-start(bf16[32,4224]{1,0:T(8,128)(2,1)} %constant_dynamic-update-slice_fusion), channel_id=1, source_target_pairs={{0,2},{1,9},{2,0},{3,11},{4,6},{5,13},{6,4},{7,15},{8,10},{9,1},{1... | collective-permute-start | bytes 811016 | tf_op jit(solution)/shard_map/rows/ppermute | solution.py:70
  11.9 6.3 %collective-permute-done.3 = bf16[32,4224]{1,0:T(8,128)(2,1)S(1)} collective-permute-done((bf16[32,4224]{1,0:T(8,128)(2,1)}, bf16[32,4224]{1,0:T(8,128)(2,1)S(1)}, u32[]{:S(2)}, u32[]{:S(2)}) %collective-permute-start.3) | collective-permute-done | bytes 270368 | tf_op jit(solution)/shard_map/rows/ppermute | solution.py:70
  18.3 0.9 collective-permute-done.1.dep_ref
  19.3 1.4 collective-permute-start.6
  20.8 0.4 collective-permute-start.5
  21.2 1.9 %collective-permute-start.7 = (bf16[64,4224]{1,0:T(8,128)(2,1)S(1)}, bf16[64,4224]{1,0:T(8,128)(2,1)}, u32[]{:S(2)}, u32[]{:S(2)}) collective-permute-start(bf16[64,4224]{1,0:T(8,128)(2,1)S(1)} %pad_maximum_fusion.1.refs_1_), channel_id=1, source_target_pairs={{0,24},{1,7},{2,26},{3,5},{4,28},{5,3},{6,30},{7,1},{8,16},{9,15},... | collective-permute-start | bytes 1622024 | tf_op jit(solution)/shard_map/rows/ppermute | solution.py:70
  23.0 1.3 other_half.1
  24.4 2.7 %collective-permute-start.8 = (bf16[4096,256]{1,0:T(8,128)(2,1)}, bf16[4096,256]{1,0:T(8,128)(2,1)}, u32[]{:S(2)}, u32[]{:S(2)}) collective-permute-start(bf16[4096,256]{1,0:T(8,128)(2,1)} %other_half.1), channel_id=1, source_target_pairs={{0,1},{1,0},{2,3},{3,2},{4,5},{5,4},{6,7},{7,6},{8,9},{9,8},{10,11... | collective-permute-start | bytes 6291464 | tf_op jit(solution)/shard_map/weights/ppermute | solution.py:70
  27.0 0.5 slice.133
  28.2 1.2 multiply_reduce_fusion.3
  29.5 1.2 multiply_convert_fusion
  30.8 2.0 %fusion.135 = f32[16,128]{1,0:T(8,128)S(1)} fusion(bf16[16,8192]{1,0:T(8,128)(2,1)S(1)} %multiply_convert_fusion, bf16[8192,128]{1,0:T(8,128)(2,1)} %refs_2_.1), kind=kOutput, calls=%fused_computation.251 | convolution fusion | flops 33554432 | bytes 2367488 | tf_op jit(solution)/shard_map/decode/dot_general | solution.py:401
  32.9 0.8 collective-permute-done.5.refs_3_
  33.7 0.9 collective-permute-start.10
  34.8 2.2 %fusion.134 = f32[16,128]{1,0:T(8,128)S(1)} fusion(bf16[16,8192]{1,0:T(8,128)(2,1)} %copy-done.17, bf16[8192,128]{1,0:T(8,128)(2,1)} %param.14), kind=kOutput, calls=%fused_computation.250 | convolution fusion | flops 33554432 | bytes 2367488 | tf_op jit(solution)/shard_map/decode/dot_general | solution.py:403
  37.0 1.6 copy-done.6
  38.6 3.9 %project.2 = (f32[384,256]{1,0:T(8,128)S(1)}, f32[384,256]{1,0:T(8,128)S(1)}, bf16[384,128]{1,0:T(8,128)(2,1)S(1)}) custom-call(bf16[64,4224]{1,0:T(8,128)(2,1)S(1)} %pad_maximum_fusion.refs_0_, bf16[64,4224]{1,0:T(8,128)(2,1)S(1)} %pad_maximum_fusion.1.refs_1_, bf16[64,4224]{1,0:T(8,128)(2,1)} %collective-permute-done.4.refs_2_, ...), custom_call_target="tpu_custom_call" | custom-call | tf_op jit(solution)/shard_map/project/project/pallas_call | solution.py:202
  42.6 2.9 %collective-permute-start.11 = (f32[384,256]{1,0:T(8,128)S(1)}, f32[384,256]{1,0:T(8,128)S(1)}, u32[]{:S(2)}, u32[]{:S(2)}) collective-permute-start(f32[384,256]{1,0:T(8,128)S(1)} %get-tuple-element.19), channel_id=1, source_target_pairs={{0,1},{1,0},{2,3},{3,2},{4,5},{5,4},{6,7},{7,6},{8,9},{9,8},{10,11... | collective-permute-start | bytes 1179656 | tf_op jit(solution)/shard_map/project/ppermute | solution.py:70
  45.4 2.5 %project.3 = (f32[128,256]{1,0:T(8,128)S(1)}, f32[128,256]{1,0:T(8,128)S(1)}, bf16[128,128]{1,0:T(8,128)(2,1)S(1)}) custom-call(bf16[64,4224]{1,0:T(8,128)(2,1)} %collective-permute-done.9.refs_0_, bf16[64,4224]{1,0:T(8,128)(2,1)} %collective-permute-done.10.refs_1_, bf16[8192,128]{1,0:T(8,128)(2,1)S(1)} %copy-done.2, bf16[8192,128]{1,0:T(8,128)(2,1)S(1)} %copy-done.6, ...), custom_call_target="tpu_custom_call" | custom-call | tf_op jit(solution)/shard_map/project/project/pallas_call | solution.py:202
  48.0 1.8 collective-permute-start.12
  49.9 0.8 collective-permute-done.12.refs_3_
  50.7 2.2 %finish.1 = bf16[768,256]{1,0:T(8,128)(2,1)} custom-call(f32[384,256]{1,0:T(8,128)S(1)} %get-tuple-element.17.refs_0_, f32[128,256]{1,0:T(8,128)S(1)} %get-tuple-element.18.refs_1_, f32[384,256]{1,0:T(8,128)S(1)} %collective-permute-done.11.refs_2_, f32[128,256]{1,0:T(8,128)S(1)} %collective-permute-done.12.refs_3_, ...), custom_call_target="tpu_custom_call" | custom-call | tf_op jit(solution)/shard_map/project/finish/pallas_call | solution.py:271
  52.9 7.1 %all-to-all-start = ((bf16[8,96,256]{2,1,0:T(8,128)(2,1)}), bf16[8,96,256]{2,1,0:T(8,128)(2,1)S(1)}, u32[]{:S(2)}, u32[]{:S(2)}) async-start(bf16[8,96,256]{2,1,0:T(8,128)(2,1)} %bitcast.2), calls=%async_computation | async-start | bytes 786432 | tf_op jit(solution)/shard_map/project/all_to_all | solution.py:385
  60.2 2.0 %fusion.21 = f32[16,128]{1,0:T(8,128)S(1)} fusion(bf16[16,8192]{1,0:T(8,128)(2,1)S(1)} %copy-done.18, bf16[8192,128]{1,0:T(8,128)(2,1)} %refs_3_.1), kind=kOutput, calls=%fused_computation.43 | convolution fusion | flops 33558528 | bytes 2367488 | tf_op jit(solution)/shard_map/decode/dot_general | solution.py:402
  62.2 12.9 %all-to-all-done = bf16[8,96,256]{2,1,0:T(8,128)(2,1)S(1)} async-done(((bf16[8,96,256]{2,1,0:T(8,128)(2,1)}), bf16[8,96,256]{2,1,0:T(8,128)(2,1)S(1)}, u32[]{:S(2)}, u32[]{:S(2)}) %all-to-all-start) | async-done | bytes 393248 | tf_op jit(solution)/shard_map/project/all_to_all | solution.py:385
  75.1 1.6 settle.1
  77.2 0.6 convolution_convert_fusion.3
  77.8 0.7 copy.57
  78.5 6.8 %all-to-all-start.1 = ((bf16[16,32,256]{2,0,1:T(8,128)(2,1)}), bf16[16,32,256]{2,0,1:T(8,128)(2,1)S(1)}, u32[]{:S(2)}, u32[]{:S(2)}) async-start(bf16[16,32,256]{2,0,1:T(8,128)(2,1)} %bitcast.108), calls=%async_computation.1 | async-start | bytes 524288 | tf_op jit(solution)/shard_map/sum/all_to_all | solution.py:427
  85.4 8.8 %all-to-all-done.1 = bf16[16,32,256]{2,0,1:T(8,128)(2,1)S(1)} async-done(((bf16[16,32,256]{2,0,1:T(8,128)(2,1)}), bf16[16,32,256]{2,0,1:T(8,128)(2,1)S(1)}, u32[]{:S(2)}, u32[]{:S(2)}) %all-to-all-start.1) | async-done | bytes 262176 | tf_op jit(solution)/shard_map/sum/all_to_all | solution.py:427
  94.2 0.7 multiply_convert_fusion.3
  95.0 0.7 broadcast_in_dim.37
  95.7 3.8 %all-to-all-start.2 = ((bf16[16,32,256]{2,0,1:T(8,128)(2,1)}), bf16[16,32,256]{2,0,1:T(8,128)(2,1)S(1)}, u32[]{:S(2)}, u32[]{:S(2)}) async-start(bf16[16,32,256]{2,0,1:T(8,128)(2,1)} %broadcast_in_dim.37), calls=%async_computation.2 | async-start | bytes 524288 | tf_op jit(solution)/shard_map/spread/all_to_all | solution.py:434
  99.5 9.0 %all-to-all-done.2 = bf16[16,32,256]{2,0,1:T(8,128)(2,1)S(1)} async-done(((bf16[16,32,256]{2,0,1:T(8,128)(2,1)}), bf16[16,32,256]{2,0,1:T(8,128)(2,1)S(1)}, u32[]{:S(2)}, u32[]{:S(2)}) %all-to-all-start.2) | async-done | bytes 262176 | tf_op jit(solution)/shard_map/spread/all_to_all | solution.py:434
  108.7 2.1 %convolution_multiply_fusion.11 = f32[16,128]{1,0:T(8,128)S(1)} fusion(bf16[16,8192]{1,0:T(8,128)(2,1)S(1)} %bitcast.121, bf16[8192,128]{1,0:T(8,128)(2,1)} %refs_2_.1, f32[16]{0:T(128)S(1)} %add_rsqrt_fusion.2), kind=kOutput, calls=%fused_computation.29 | convolution fusion | flops 33556480 | bytes 2367552 | tf_op jit(solution)/shard_map/decode/dot_general | solution.py:401
  110.9 0.4 convolution_multiply_fusion.12
  111.4 0.4 fusion.15
  112.7 0.6 convolution_convert_fusion.2
  113.3 12.6 %all_to_all.40 = bf16[16,32,256]{2,0,1:T(8,128)(2,1)S(1)} all-to-all(bf16[16,32,256]{2,0,1:T(8,128)(2,1)S(1)} %bitcast.133), channel_id=1, replica_groups=mesh['grp'=8,'head'=32] {'head'}, dimensions={1} | all-to-all | bytes 524288 | tf_op jit(solution)/shard_map/sum/all_to_all | solution.py:427
  126.0 0.9 multiply_convert_fusion.2
  126.9 12.5 %all_to_all.41 = bf16[16,32,256]{2,0,1:T(8,128)(2,1)S(1)} all-to-all(bf16[16,32,256]{2,0,1:T(8,128)(2,1)S(1)} %broadcast_in_dim.38), channel_id=1, replica_groups=mesh['grp'=8,'head'=32] {'head'}, dimensions={1} | all-to-all | bytes 524288 | tf_op jit(solution)/shard_map/spread/all_to_all | solution.py:434
  139.6 0.4 convolution_multiply_fusion.8
  140.0 0.4 convolution_multiply_fusion.9
  140.4 0.8 copy-done.8
  141.2 0.4 fusion.17
  142.5 0.6 convolution_convert_fusion.1
  143.1 12.6 %all_to_all.42 = bf16[16,32,256]{2,0,1:T(8,128)(2,1)S(1)} all-to-all(bf16[16,32,256]{2,0,1:T(8,128)(2,1)S(1)} %bitcast.134), channel_id=1, replica_groups=mesh['grp'=8,'head'=32] {'head'}, dimensions={1} | all-to-all | bytes 524288 | tf_op jit(solution)/shard_map/sum/all_to_all | solution.py:427
  155.8 12.6 %all_to_all.43 = bf16[16,32,256]{2,0,1:T(8,128)(2,1)S(1)} all-to-all(bf16[16,32,256]{2,0,1:T(8,128)(2,1)S(1)} %broadcast_in_dim.39), channel_id=1, replica_groups=mesh['grp'=8,'head'=32] {'head'}, dimensions={1} | all-to-all | bytes 524288 | tf_op jit(solution)/shard_map/spread/all_to_all | solution.py:434
  168.7 0.4 convolution_multiply_fusion.5
  169.1 0.4 convolution_multiply_fusion.6
  170.4 0.4 fusion.20
  170.8 0.6 convolution_convert_fusion
  171.5 12.5 %all_to_all.44 = bf16[16,32,256]{2,0,1:T(8,128)(2,1)S(1)} all-to-all(bf16[16,32,256]{2,0,1:T(8,128)(2,1)S(1)} %bitcast.135), channel_id=1, replica_groups=mesh['grp'=8,'head'=32] {'head'}, dimensions={1} | all-to-all | bytes 524288 | tf_op jit(solution)/shard_map/sum/all_to_all | solution.py:427
  184.0 0.6 add.221
  (125 shorter events, 6.1 us)
Async XLA Ops:
  0.0 77.2 %copy-start = (bf16[128,8192]{1,0:T(8,128)(2,1)S(1)}, bf16[128,8192]{1,0:T(8,128)(2,1)}, u32[]{:S(2)}) copy-start(bf16[128,8192]{1,0:T(8,128)(2,1)} %param.17) | copy-start | bytes 6291460
  0.0 0.9 copy-start.10
  0.9 0.9 copy-start.12
  1.9 0.7 copy-start.13
  3.3 4.3 %collective-permute-start = (bf16[16,4224]{1,0:T(8,128)(2,1)S(1)}, bf16[16,4224]{1,0:T(8,128)(2,1)S(1)}, u32[]{:S(2)}, u32[]{:S(2)}) collective-permute-start(bf16[16,4224]{1,0:T(8,128)(2,1)S(1)} %get-tuple-element.16), channel_id=1, source_target_pairs={{0,1},{1,0},{2,3},{3,2},{4,5},{5,4},{6,7},{7,6},{8,9},{9,8},{10,11... | collective-permute-start | bytes 405512 | tf_op jit(solution)/shard_map/rows/ppermute | solution.py:70
  8.3 9.9 %collective-permute-start.3 = (bf16[32,4224]{1,0:T(8,128)(2,1)}, bf16[32,4224]{1,0:T(8,128)(2,1)S(1)}, u32[]{:S(2)}, u32[]{:S(2)}) collective-permute-start(bf16[32,4224]{1,0:T(8,128)(2,1)} %constant_dynamic-update-slice_fusion), channel_id=1, source_target_pairs={{0,6},{1,25},{2,4},{3,27},{4,2},{5,29},{6,0},{7,31},{8,14},{9,17},... | collective-permute-start | bytes 811016 | tf_op jit(solution)/shard_map/rows/ppermute | solution.py:70
  9.3 13.7 %copy-start.1 = (bf16[8192,128]{1,0:T(8,128)(2,1)S(1)}, bf16[8192,128]{1,0:T(8,128)(2,1)}, u32[]{:S(2)}) copy-start(bf16[8192,128]{1,0:T(8,128)(2,1)} %refs_2_.1) | copy-start | bytes 6291460
  9.3 13.7 %copy-start.5 = (bf16[8192,128]{1,0:T(8,128)(2,1)S(1)}, bf16[8192,128]{1,0:T(8,128)(2,1)}, u32[]{:S(2)}) copy-start(bf16[8192,128]{1,0:T(8,128)(2,1)} %refs_3_.1) | copy-start | bytes 6291460
  9.5 8.7 %collective-permute-start.2 = (bf16[32,4224]{1,0:T(8,128)(2,1)}, bf16[32,4224]{1,0:T(8,128)(2,1)S(1)}, u32[]{:S(2)}, u32[]{:S(2)}) collective-permute-start(bf16[32,4224]{1,0:T(8,128)(2,1)} %constant_dynamic-update-slice_fusion), channel_id=1, source_target_pairs={{0,4},{1,17},{2,6},{3,19},{4,0},{5,21},{6,2},{7,23},{8,12},{9,25},... | collective-permute-start | bytes 811016 | tf_op jit(solution)/shard_map/rows/ppermute | solution.py:70
  10.0 9.2 %collective-permute-start.1 = (bf16[32,4224]{1,0:T(8,128)(2,1)}, bf16[32,4224]{1,0:T(8,128)(2,1)S(1)}, u32[]{:S(2)}, u32[]{:S(2)}) collective-permute-start(bf16[32,4224]{1,0:T(8,128)(2,1)} %constant_dynamic-update-slice_fusion), channel_id=1, source_target_pairs={{0,2},{1,9},{2,0},{3,11},{4,6},{5,13},{6,4},{7,15},{8,10},{9,1},{1... | collective-permute-start | bytes 811016 | tf_op jit(solution)/shard_map/rows/ppermute | solution.py:70
  19.2 17.7 %collective-permute-start.4 = (bf16[64,4224]{1,0:T(8,128)(2,1)S(1)}, bf16[64,4224]{1,0:T(8,128)(2,1)}, u32[]{:S(2)}, u32[]{:S(2)}) collective-permute-start(bf16[64,4224]{1,0:T(8,128)(2,1)S(1)} %pad_maximum_fusion.refs_0_), channel_id=1, source_target_pairs={{0,8},{1,3},{2,10},{3,1},{4,12},{5,7},{6,14},{7,5},{8,0},{9,11},{1... | collective-permute-start | bytes 1622024 | tf_op jit(solution)/shard_map/rows/ppermute | solution.py:70
  19.3 13.5 %collective-permute-start.6 = (bf16[64,4224]{1,0:T(8,128)(2,1)S(1)}, bf16[64,4224]{1,0:T(8,128)(2,1)}, u32[]{:S(2)}, u32[]{:S(2)}) collective-permute-start(bf16[64,4224]{1,0:T(8,128)(2,1)S(1)} %pad_maximum_fusion.refs_0_), channel_id=1, source_target_pairs={{0,24},{1,7},{2,26},{3,5},{4,28},{5,3},{6,30},{7,1},{8,16},{9,15},... | collective-permute-start | bytes 1622024 | tf_op jit(solution)/shard_map/rows/ppermute | solution.py:70
  20.7 8.7 %copy-start.19 = (s32[8,16]{1,0:T(8,128)S(1)}, s32[8,16]{1,0:T(8,128)}, u32[]{:S(2)}) copy-start(s32[8,16]{1,0:T(8,128)} %param.11) | copy-start | bytes 1540
  20.8 8.8 %copy-start.11 = (f32[8192]{0:T(1024)S(1)}, f32[8192]{0:T(1024)}, u32[]{:S(2)}) copy-start(f32[8192]{0:T(1024)} %param.13) | copy-start | bytes 98308
  20.8 13.0 %collective-permute-start.5 = (bf16[64,4224]{1,0:T(8,128)(2,1)S(1)}, bf16[64,4224]{1,0:T(8,128)(2,1)}, u32[]{:S(2)}, u32[]{:S(2)}) collective-permute-start(bf16[64,4224]{1,0:T(8,128)(2,1)S(1)} %pad_maximum_fusion.1.refs_1_), channel_id=1, source_target_pairs={{0,8},{1,3},{2,10},{3,1},{4,12},{5,7},{6,14},{7,5},{8,0},{9,11},{1... | collective-permute-start | bytes 1622024 | tf_op jit(solution)/shard_map/rows/ppermute | solution.py:70
  21.2 15.8 %collective-permute-start.7 = (bf16[64,4224]{1,0:T(8,128)(2,1)S(1)}, bf16[64,4224]{1,0:T(8,128)(2,1)}, u32[]{:S(2)}, u32[]{:S(2)}) collective-permute-start(bf16[64,4224]{1,0:T(8,128)(2,1)S(1)} %pad_maximum_fusion.1.refs_1_), channel_id=1, source_target_pairs={{0,24},{1,7},{2,26},{3,5},{4,28},{5,3},{6,30},{7,1},{8,16},{9,15},... | collective-permute-start | bytes 1622024 | tf_op jit(solution)/shard_map/rows/ppermute | solution.py:70
  24.4 12.6 %collective-permute-start.8 = (bf16[4096,256]{1,0:T(8,128)(2,1)}, bf16[4096,256]{1,0:T(8,128)(2,1)}, u32[]{:S(2)}, u32[]{:S(2)}) collective-permute-start(bf16[4096,256]{1,0:T(8,128)(2,1)} %other_half.1), channel_id=1, source_target_pairs={{0,1},{1,0},{2,3},{3,2},{4,5},{5,4},{6,7},{7,6},{8,9},{9,8},{10,11... | collective-permute-start | bytes 6291464 | tf_op jit(solution)/shard_map/weights/ppermute | solution.py:70
  30.7 3.0 %copy-start.17 = (bf16[16,8192]{1,0:T(8,128)(2,1)}, bf16[16,8192]{1,0:T(8,128)(2,1)S(1)}, u32[]{:S(2)}) copy-start(bf16[16,8192]{1,0:T(8,128)(2,1)S(1)} %multiply_convert_fusion) | copy-start | bytes 786436
  32.8 12.6 %collective-permute-start.9 = (bf16[64,4224]{1,0:T(8,128)(2,1)}, bf16[64,4224]{1,0:T(8,128)(2,1)}, u32[]{:S(2)}, u32[]{:S(2)}) collective-permute-start(bf16[64,4224]{1,0:T(8,128)(2,1)} %collective-permute-done.6.refs_4_), channel_id=1, source_target_pairs={{0,8},{1,3},{2,10},{3,1},{4,12},{5,7},{6,14},{7,5},{8,0},{9,11},{1... | collective-permute-start | bytes 1622024 | tf_op jit(solution)/shard_map/rows/ppermute | solution.py:70
  33.7 11.7 %collective-permute-start.10 = (bf16[64,4224]{1,0:T(8,128)(2,1)}, bf16[64,4224]{1,0:T(8,128)(2,1)}, u32[]{:S(2)}, u32[]{:S(2)}) collective-permute-start(bf16[64,4224]{1,0:T(8,128)(2,1)} %collective-permute-done.5.refs_3_), channel_id=1, source_target_pairs={{0,24},{1,7},{2,26},{3,5},{4,28},{5,3},{6,30},{7,1},{8,16},{9,15},... | collective-permute-start | bytes 1622024 | tf_op jit(solution)/shard_map/rows/ppermute | solution.py:70
  34.7 2.3 %copy-start.2 = (bf16[8192,128]{1,0:T(8,128)(2,1)S(1)}, bf16[8192,128]{1,0:T(8,128)(2,1)}, u32[]{:S(2)}) copy-start(bf16[8192,128]{1,0:T(8,128)(2,1)} %refs_2_.1) | copy-start | bytes 6291460
  37.0 1.6 copy-start.6
  42.6 8.1 %collective-permute-start.11 = (f32[384,256]{1,0:T(8,128)S(1)}, f32[384,256]{1,0:T(8,128)S(1)}, u32[]{:S(2)}, u32[]{:S(2)}) collective-permute-start(f32[384,256]{1,0:T(8,128)S(1)} %get-tuple-element.19), channel_id=1, source_target_pairs={{0,1},{1,0},{2,3},{3,2},{4,5},{5,4},{6,7},{7,6},{8,9},{9,8},{10,11... | collective-permute-start | bytes 1179656 | tf_op jit(solution)/shard_map/project/ppermute | solution.py:70
  47.9 12.2 %copy-start.18 = (bf16[16,8192]{1,0:T(8,128)(2,1)S(1)}, bf16[16,8192]{1,0:T(8,128)(2,1)}, u32[]{:S(2)}) copy-start(bf16[16,8192]{1,0:T(8,128)(2,1)} %copy-done.17) | copy-start | bytes 786436
  48.0 2.7 %collective-permute-start.12 = (f32[128,256]{1,0:T(8,128)S(1)}, f32[128,256]{1,0:T(8,128)S(1)}, u32[]{:S(2)}, u32[]{:S(2)}) collective-permute-start(f32[128,256]{1,0:T(8,128)S(1)} %get-tuple-element.20), channel_id=1, source_target_pairs={{0,1},{1,0},{2,3},{3,2},{4,5},{5,4},{6,7},{7,6},{8,9},{9,8},{10,11... | collective-permute-start | bytes 393224 | tf_op jit(solution)/shard_map/project/ppermute | solution.py:70
  52.9 22.2 %all-to-all-start = ((bf16[8,96,256]{2,1,0:T(8,128)(2,1)}), bf16[8,96,256]{2,1,0:T(8,128)(2,1)S(1)}, u32[]{:S(2)}, u32[]{:S(2)}) async-start(bf16[8,96,256]{2,1,0:T(8,128)(2,1)} %bitcast.2), calls=%async_computation | async-start | bytes 786432 | tf_op jit(solution)/shard_map/project/all_to_all | solution.py:385
  78.5 15.7 %all-to-all-start.1 = ((bf16[16,32,256]{2,0,1:T(8,128)(2,1)}), bf16[16,32,256]{2,0,1:T(8,128)(2,1)S(1)}, u32[]{:S(2)}, u32[]{:S(2)}) async-start(bf16[16,32,256]{2,0,1:T(8,128)(2,1)} %bitcast.108), calls=%async_computation.1 | async-start | bytes 524288 | tf_op jit(solution)/shard_map/sum/all_to_all | solution.py:427
  95.7 12.8 %all-to-all-start.2 = ((bf16[16,32,256]{2,0,1:T(8,128)(2,1)}), bf16[16,32,256]{2,0,1:T(8,128)(2,1)S(1)}, u32[]{:S(2)}, u32[]{:S(2)}) async-start(bf16[16,32,256]{2,0,1:T(8,128)(2,1)} %broadcast_in_dim.37), calls=%async_computation.2 | async-start | bytes 524288 | tf_op jit(solution)/shard_map/spread/all_to_all | solution.py:434
  108.5 2.4 %copy-start.14 = (bf16[8192,128]{1,0:T(8,128)(2,1)S(1)}, bf16[8192,128]{1,0:T(8,128)(2,1)}, u32[]{:S(2)}) copy-start(bf16[8192,128]{1,0:T(8,128)(2,1)} %param.14) | copy-start | bytes 6291460
  108.7 2.7 %copy-start.7 = (bf16[8192,128]{1,0:T(8,128)(2,1)S(1)}, bf16[8192,128]{1,0:T(8,128)(2,1)}, u32[]{:S(2)}) copy-start(bf16[8192,128]{1,0:T(8,128)(2,1)} %refs_3_.1) | copy-start | bytes 6291460
  113.3 26.3 %copy-start.3 = (bf16[8192,128]{1,0:T(8,128)(2,1)S(1)}, bf16[8192,128]{1,0:T(8,128)(2,1)}, u32[]{:S(2)}) copy-start(bf16[8192,128]{1,0:T(8,128)(2,1)} %refs_2_.1) | copy-start | bytes 6291460
  125.9 14.0 %copy-start.15 = (bf16[8192,128]{1,0:T(8,128)(2,1)S(1)}, bf16[8192,128]{1,0:T(8,128)(2,1)}, u32[]{:S(2)}) copy-start(bf16[8192,128]{1,0:T(8,128)(2,1)} %param.14) | copy-start | bytes 6291460
  139.6 1.6 copy-start.8
  143.1 25.6 %copy-start.4 = (bf16[8192,128]{1,0:T(8,128)(2,1)S(1)}, bf16[8192,128]{1,0:T(8,128)(2,1)}, u32[]{:S(2)}) copy-start(bf16[8192,128]{1,0:T(8,128)(2,1)} %refs_2_.1) | copy-start | bytes 6291460
  155.7 13.3 %copy-start.16 = (bf16[8192,128]{1,0:T(8,128)(2,1)S(1)}, bf16[8192,128]{1,0:T(8,128)(2,1)}, u32[]{:S(2)}) copy-start(bf16[8192,128]{1,0:T(8,128)(2,1)} %param.14) | copy-start | bytes 6291460
  168.7 1.8 copy-start.9

commit v4 on v3

--- a/solution.py
+++ b/solution.py
@@ -325,6 +325,104 @@
     )(cache, edge_row, edge_col, high, low)
 
 
+def rotated(values, turn):
+    return values * turn[:, :HD] + pltpu.roll(values, HD // 2, 1) * turn[:, HD:]
+
+
+def attend_kernel(step, *refs):
+    f32, bf16 = jnp.float32, jnp.bfloat16
+    turn_ref, key_ref, cache_ref, bias_ref, out_weight, *rest = refs
+    turn = turn_ref[step]
+    olds = [(rest[2 * i], rest[2 * i + 1]) for i in range(step)]
+    rest = rest[2 * step :]
+    if step:
+        row_ref, inverse_ref, wq_ref, wk_ref, wv_ref, term_ref, new_key_ref, new_value_ref = rest
+        blocks, n, share = row_ref.shape
+        squares = jnp.zeros((n, share), f32)
+        for i in range(blocks):
+            plain = row_ref[i].astype(f32) * inverse_ref[:, i * share : (i + 1) * share]
+            squares = squares + plain * plain
+        mean = jnp.sum(squares, axis=1, keepdims=True) * (1.0 / (blocks * share))
+        factor = lax.rsqrt(mean + EPSILON)
+        rows = jnp.concatenate([row_ref[i] for i in range(blocks)], axis=1)
+        query = jnp.dot(rows, wq_ref[...], preferred_element_type=f32) * factor
+        key = jnp.dot(rows, wk_ref[...], preferred_element_type=f32) * factor
+        value = jnp.dot(rows, wv_ref[...], preferred_element_type=f32) * factor
+    else:
+        query_ref, first_key, first_value, _, _, _, term_ref, new_key_ref, new_value_ref = rest
+        query, key, value = query_ref[...], first_key[...], first_value[...]
+    query = rotated(query, turn).astype(bf16)
+    key = rotated(key, turn).astype(bf16)
+    value = value.astype(bf16)
+    new_key_ref[...] = key
+    new_value_ref[...] = value
+    scale = HD ** (-0.5)
+    scores = lax.dot_general(
+        query, key_ref[...], (((1,), (1,)), ((), ())), preferred_element_type=f32
+    )
+    scores = scores * scale + bias_ref[...]
+    wide = query.astype(f32)
+    pairs = [(k[...], v[...]) for k, v in olds] + [(key, value)]
+    fresh = [jnp.sum(wide * k.astype(f32), axis=1, keepdims=True) * scale for k, _ in pairs]
+    peak = jnp.max(scores, axis=1, keepdims=True)
+    for f in fresh:
+        peak = jnp.maximum(peak, f)
+    cache_exp = jnp.exp(scores - peak)
+    fresh_exp = [jnp.exp(f - peak) for f in fresh]
+    total = jnp.sum(cache_exp, axis=1, keepdims=True)
+    for f in fresh_exp:
+        total = total + f
+    weights = (cache_exp / total).astype(bf16)
+    attended = jnp.dot(weights, cache_ref[:, HD:], preferred_element_type=f32)
+    for f, (_, v) in zip(fresh_exp, pairs):
+        attended = attended + (f / total).astype(bf16).astype(f32) * v.astype(f32)
+    attended = attended.astype(bf16)
+    blocks, _, share = term_ref.shape
+    wide_share = 4 * share
+    for j in range(blocks // 4):
+        term = jnp.dot(
+            attended, out_weight[:, j * wide_share : (j + 1) * wide_share], preferred_element_type=f32
+        ).astype(bf16)
+        for i in range(4):
+            term_ref[4 * j + i] = term[:, i * share : (i + 1) * share]
+
+
+def attend(step, blocks, turns, keys, cache, bias, w_out, olds, extra):
+    n = bias.shape[0]
+    share = w_out.shape[1] // blocks
+    flat = [x for pair in olds for x in pair]
+    small = jax.ShapeDtypeStruct((n, HD), jnp.bfloat16)
+    return pl.pallas_call(
+        lambda *refs: attend_kernel(step, *refs),
+        out_shape=(jax.ShapeDtypeStruct((blocks, n, share), jnp.bfloat16), small, small),
+        compiler_params=params(20),
+        name="attend",
+    )(turns, keys, cache, bias, w_out, *flat, *extra)
+
+
+def spread_kernel(last, part_ref, current_ref, gain_ref, next_ref, *out):
+    total = current_ref[...]
+    for i in range(part_ref.shape[0]):
+        total = total + part_ref[i].astype(jnp.float32)
+    next_ref[...] = total
+    if not last:
+        piece = (total * gain_ref[...]).astype(jnp.bfloat16)
+        for i in range(part_ref.shape[0]):
+            out[0][i] = piece
+
+
+def spread(last, parts, current, gain):
+    shapes = [jax.ShapeDtypeStruct(current.shape, jnp.float32)]
+    if not last:
+        shapes.append(jax.ShapeDtypeStruct(parts.shape, jnp.bfloat16))
+    return pl.pallas_call(
+        lambda *refs: spread_kernel(last, *refs),
+        out_shape=tuple(shapes),
+        compiler_params=params(4),
+        name="spread",
+    )(parts, current, gain)
+
+
 def per_device(
     prefill_rows, row_group, lengths, decode_state, norm_gain, w_query, w_key, w_value, w_out
 ):
@@ -386,57 +484,32 @@
             outgoing.reshape(groups, cap, 2 * HD), "grp", split_axis=0, concat_axis=0, tiled=True
         ).reshape(groups * cap, 2 * HD)
         cache_keys, bias = settle(groups, cache, edge_row, edge_col, table_high, table_low)
-        cache_values = cache[:, HD:]
-
-    scale = HD ** (-0.5)
-    new_keys, new_values = [], []
-    current = lax.dynamic_slice_in_dim(decode_state, my_head * share, share, 1)
-    my_gain = lax.dynamic_slice_in_dim(norm_gain, my_head * share, share, 0)
-    inverse = 1.0 / norm_gain
-    decode_rows = normed(after(decode_state, f1), norm_gain)
-    factor = None
+
+    with jax.named_scope("first"):
+        late_state = after(decode_state, f1)
+        current = lax.dynamic_slice_in_dim(late_state, my_head * share, share, 1)
+        late_gain = after(norm_gain, f1)
+        my_gain = lax.dynamic_slice_in_dim(late_gain, my_head * share, share, 0)[None, :]
+        inverse = (1.0 / late_gain)[None, :]
+        decode_rows = normed(late_state, norm_gain)
+        extra = [
+            jnp.dot(decode_rows, w, preferred_element_type=f32) for w in (w_query, w_key, w_value)
+        ]
+        at_step = my_lengths[None, :] + jnp.arange(STEPS, dtype=jnp.int32)[:, None]
+        turns = jnp.concatenate(angles_of(at_step), axis=-1)
+        extra += [current, my_gain, inverse]
+    olds = []
     for step in range(STEPS):
-        with jax.named_scope("decode"):
-            scaled = 1.0 if factor is None else factor
-            key_now = jnp.dot(decode_rows, w_key, preferred_element_type=f32) * scaled
-            value_now = jnp.dot(decode_rows, w_value, preferred_element_type=f32) * scaled
-            query_now = jnp.dot(decode_rows, w_query, preferred_element_type=f32) * scaled
-            cos_now, sin_now = angles_of(my_lengths + step)
-            new_key = turned(key_now, cos_now, sin_now).astype(bf16)
-            new_value = value_now.astype(bf16)
-            query = turned(query_now, cos_now, sin_now).astype(bf16)
-            new_keys.append(new_key)
-            new_values.append(new_value)
-            scores = jnp.einsum("rd,cd->rc", query, cache_keys, preferred_element_type=f32) * scale
-            wide = query.astype(f32)
-            fresh = jnp.stack(
-                [jnp.sum(wide * k.astype(f32), axis=1) * scale for k in new_keys], axis=1
-            )
-            scores = scores + bias
-            peak = jnp.maximum(jnp.max(scores, axis=1), jnp.max(fresh, axis=1))
-            cache_exp = jnp.exp(scores - peak[:, None])
-            fresh_exp = jnp.exp(fresh - peak[:, None])
-            total = jnp.sum(cache_exp, axis=1) + jnp.sum(fresh_exp, axis=1)
-            cache_weights = (cache_exp / total[:, None]).astype(bf16)
-            fresh_weights = (fresh_exp / total[:, None]).astype(bf16).astype(f32)
-            attended = jnp.dot(cache_weights, cache_values, preferred_element_type=f32)
-            for back, value in enumerate(new_values):
-                attended = attended + fresh_weights[:, back : back + 1] * value.astype(f32)
-            term = jnp.dot(attended.astype(bf16), w_out, preferred_element_type=f32).astype(bf16)
-        with jax.named_scope("sum"):
-            parts = lax.all_to_all(
-                term.reshape(requests, heads, share), "head", split_axis=1, concat_axis=1, tiled=True
-            )
-            current = current + jnp.sum(parts.astype(f32), axis=1)
-        if step + 1 < STEPS:
-            with jax.named_scope("spread"):
-                piece = (current * my_gain[None, :]).astype(bf16)
-                decode_rows = lax.all_to_all(
-                    jnp.broadcast_to(piece[:, None, :], (requests, heads, share)),
-                    "head", split_axis=1, concat_axis=1, tiled=True,
-                ).reshape(requests, width)
-                plain = decode_rows.astype(f32) * inverse
-                factor = lax.rsqrt(jnp.mean(plain * plain, axis=1, keepdims=True) + EPSILON)
+        term, new_key, new_value = attend(
+            step, heads, turns, cache_keys, cache, bias, w_out, olds, extra
+        )
+        olds.append((new_key, new_value))
+        parts = lax.all_to_all(term, "head", split_axis=0, concat_axis=0, tiled=True)
+        last = step + 1 == STEPS
+        current, *spreading = spread(last, parts, current, my_gain)
+        if not last:
+            rows = lax.all_to_all(spreading[0], "head", split_axis=0, concat_axis=0, tiled=True)
+            extra = [rows, inverse, w_query, w_key, w_value]
     return current
 
 

time: 186 us -> 175 us (0.941)
  blocking collectives: 62.7 us -> 90.7 us
  waiting for transfers between devices: 39.5 us -> 24.8 us
  matrix products: 14.8 us -> 2.78 us
  starting transfers between devices: 36.2 us -> 27.4 us
  other arithmetic: 8.35 us -> 3.29 us
  Pallas kernels: 12.3 us -> 17.3 us
  local copies, waits for them, and re-layouts: 9.39 us -> 7.26 us
    all_to_all x5 -> x7, blocking collectives: 62.7 us -> 90.7 us  [the longest x4 53.3 us: per_device(): lax.all_to_all(term, 'head', split_axis=0, concat_axis=0, tiled=True)]
    all_to_all x2 -> x0, waiting for transfers between devices: 17.8 us -> none  [the longest x1 8.97 us: per_device(): lax.all_to_all(jnp.broadcast_to(piece[:, None, :], (requests, heads, shar...]
    dot_general x20 -> x3, matrix products: 14.8 us -> 2.78 us  [per_device(): jnp.dot(decode_rows, w, preferred_element_type=f32)]
    all_to_all x2 -> x0, starting transfers between devices: 10.5 us -> none  [the longest x1 6.77 us: per_device(): lax.all_to_all(term.reshape(requests, heads, share), 'head', split_axis=1...]
    pallas_call x0 -> x8, Pallas kernels: none -> 6.82 us  [the longest x4 5.99 us: attend(): pl.pallas_call(lambda *refs: attend_kernel(step, *refs), out_shape=(jax.S...]
    ppermute x13, waiting for transfers between devices: 8.85 us -> 13.3 us  [send(): return lax.ppermute(values, 'head', pairs)]
    reduce_sum x18 -> x0, other arithmetic: 2.55 us -> none  [the longest x7 0.87 us: per_device(): total = jnp.sum(cache_exp, axis=1) + jnp.sum(fresh_exp, axis=1)]
    ppermute x13, starting transfers between devices: 18.6 us -> 20.9 us  [send(): return lax.ppermute(values, 'head', pairs)]
  transfers between devices with their start and end apart: 16 -> 14, of which waited for: 7 -> 7; matrix products, arithmetic and copies ran while one was open for 6% -> 4% of each run, Pallas kernels for 4% -> 3%
where the time goes in v4:
time: 175 us
  blocking collectives  90.7 us (52%)
  starting transfers between devices  27.4 us (16%)
  waiting for transfers between devices  24.8 us (14%)
  Pallas kernels  17.3 us (10%)
  local copies, waits for them, and re-layouts  7.26 us (4%)
  other arithmetic  3.29 us (2%)
  matrix products  2.78 us (2%)
    all_to_all x4, blocking collectives, per_device(): lax.all_to_all(term, 'head', split_axis=0, concat_axis=0, tiled=True)  53.3 us
    all_to_all x3, blocking collectives, per_device(): lax.all_to_all(spreading[0], 'head', split_axis=0, concat_axis=0, tiled=T...  37.4 us
    ppermute x13, starting transfers between devices, send(): return lax.ppermute(values, 'head', pairs)  20.9 us
    ppermute x13, waiting for transfers between devices, send(): return lax.ppermute(values, 'head', pairs)  13.3 us
    all_to_all x1, waiting for transfers between devices, per_device(): lax.all_to_all(outgoing.reshape(groups, cap, 2 * HD), 'grp', split_axis=0...  11.5 us
    all_to_all x1, starting transfers between devices, per_device(): lax.all_to_all(outgoing.reshape(groups, cap, 2 * HD), 'grp', split_axis=0...  6.5 us
    pallas_call x4, Pallas kernels, attend(): pl.pallas_call(lambda *refs: attend_kernel(step, *refs), out_shape=(jax.S...  5.99 us
    unnamed x40, local copies, waits for them, and re-layouts  5.62 us
  transfers between devices with their start and end apart: 14, of which 7 were waited for; matrix products, arithmetic and copies ran while one was open for 4% of the time, Pallas kernels for 3%

profile of v4, /device:TPU:1, one launch (start us, length us, event | category | flops | bytes accessed | tf_op | source)
XLA Modules:
  0.0 174.6 jit_solution(9110164084329446254)
XLA Ops:
  0.0 0.8 copy-done.7
  0.8 0.9 copy-done.9
  1.7 0.7 copy-done.11
  2.4 0.8 norm_split.1
  3.2 3.3 %collective-permute-start = (bf16[16,4224]{1,0:T(8,128)(2,1)S(1)}, bf16[16,4224]{1,0:T(8,128)(2,1)S(1)}, u32[]{:S(2)}, u32[]{:S(2)}) collective-permute-start(bf16[16,4224]{1,0:T(8,128)(2,1)S(1)} %get-tuple-element.32), channel_id=1, source_target_pairs={{0,1},{1,0},{2,3},{3,2},{4,5},{5,4},{6,7},{7,6},{8,9},{9,8},{10,11... | collective-permute-start | bytes 405512 | tf_op jit(solution)/shard_map/rows/ppermute | solution.py:70
  6.5 0.3 multiply_cosine_fusion
  6.8 0.6 collective-permute-done
  7.5 1.1 collective-permute-start.3
  8.6 0.1 fusion.refs_3_
  8.7 0.0 copy-start
  8.7 0.7 subtract_convert_fusion.refs_4_
  9.5 2.9 %collective-permute-start.2 = (bf16[32,4224]{1,0:T(8,128)(2,1)S(1)}, bf16[32,4224]{1,0:T(8,128)(2,1)S(1)}, u32[]{:S(2)}, u32[]{:S(2)}) collective-permute-start(bf16[32,4224]{1,0:T(8,128)(2,1)S(1)} %constant_dynamic-update-slice_fusion), channel_id=1, source_target_pairs={{0,4},{1,17},{2,6},{3,19},{4,0},{5,21},{6,2},{7,23},{8,12},{9,25},... | collective-permute-start | bytes 811016 | tf_op jit(solution)/shard_map/rows/ppermute | solution.py:70
  12.3 2.1 %collective-permute-done.3 = bf16[32,4224]{1,0:T(8,128)(2,1)S(1)} collective-permute-done((bf16[32,4224]{1,0:T(8,128)(2,1)S(1)}, bf16[32,4224]{1,0:T(8,128)(2,1)S(1)}, u32[]{:S(2)}, u32[]{:S(2)}) %collective-permute-start.3) | collective-permute-done | bytes 270368 | tf_op jit(solution)/shard_map/rows/ppermute | solution.py:70
  14.4 4.9 %collective-permute-done.2 = bf16[32,4224]{1,0:T(8,128)(2,1)S(1)} collective-permute-done((bf16[32,4224]{1,0:T(8,128)(2,1)S(1)}, bf16[32,4224]{1,0:T(8,128)(2,1)S(1)}, u32[]{:S(2)}, u32[]{:S(2)}) %collective-permute-start.2) | collective-permute-done | bytes 270368 | tf_op jit(solution)/shard_map/rows/ppermute | solution.py:70
  19.5 0.1 collective-permute-start.4
  19.6 1.6 collective-permute-start.6
  21.2 0.7 collective-permute-start.5
  21.9 1.3 collective-permute-start.7
  23.2 0.5 slice.30
  24.4 1.6 copy-done.1
  26.0 0.4 other_half.1
  26.4 0.0 copy-start.2
  26.4 2.7 %collective-permute-start.8 = (bf16[4096,256]{1,0:T(8,128)(2,1)S(1)}, bf16[4096,256]{1,0:T(8,128)(2,1)S(1)}, u32[]{:S(2)}, u32[]{:S(2)}) collective-permute-start(bf16[4096,256]{1,0:T(8,128)(2,1)S(1)} %other_half.1), channel_id=1, source_target_pairs={{0,1},{1,0},{2,3},{3,2},{4,5},{5,4},{6,7},{7,6},{8,9},{9,8},{10,11... | collective-permute-start | bytes 6291464 | tf_op jit(solution)/shard_map/weights/ppermute | solution.py:70
  29.1 0.2 multiply_reduce_fusion
  29.3 0.1 multiply_convert_fusion
  29.5 0.1 select_reduce_fusion.1
  29.6 0.8 multiply_cosine_fusion.1
  30.4 3.6 %collective-permute-done.5.refs_3_ = bf16[64,4224]{1,0:T(8,128)(2,1)} collective-permute-done((bf16[64,4224]{1,0:T(8,128)(2,1)S(1)}, bf16[64,4224]{1,0:T(8,128)(2,1)}, u32[]{:S(2)}, u32[]{:S(2)}) %collective-permute-start.5) | collective-permute-done | bytes 540704 | tf_op jit(solution)/shard_map/rows/ppermute | solution.py:70
  34.0 1.3 collective-permute-start.10
  35.3 0.6 broadcast_divide_fusion
  35.9 0.4 fusion.7.refs_6_
  36.3 3.9 %project.2 = (f32[384,256]{1,0:T(8,128)S(1)}, f32[384,256]{1,0:T(8,128)S(1)}, bf16[384,128]{1,0:T(8,128)(2,1)S(1)}) custom-call(bf16[64,4224]{1,0:T(8,128)(2,1)S(1)} %pad_maximum_fusion.refs_0_, bf16[64,4224]{1,0:T(8,128)(2,1)S(1)} %pad_maximum_fusion.1.refs_1_, bf16[64,4224]{1,0:T(8,128)(2,1)} %collective-permute-done.4.refs_2_, ...), custom_call_target="tpu_custom_call" | custom-call | tf_op jit(solution)/shard_map/project/project/pallas_call | solution.py:202
  40.3 2.4 %collective-permute-start.11 = (f32[384,256]{1,0:T(8,128)S(1)}, f32[384,256]{1,0:T(8,128)S(1)}, u32[]{:S(2)}, u32[]{:S(2)}) collective-permute-start(f32[384,256]{1,0:T(8,128)S(1)} %get-tuple-element.35), channel_id=1, source_target_pairs={{0,1},{1,0},{2,3},{3,2},{4,5},{5,4},{6,7},{7,6},{8,9},{9,8},{10,11... | collective-permute-start | bytes 1179656 | tf_op jit(solution)/shard_map/project/ppermute | solution.py:70
  42.7 0.1 select_reduce_fusion
  42.8 1.1 collective-permute-done.10.refs_1_
  43.9 1.7 project.3
  45.6 3.5 %collective-permute-start.12 = (f32[128,256]{1,0:T(8,128)S(1)}, f32[128,256]{1,0:T(8,128)S(1)}, u32[]{:S(2)}, u32[]{:S(2)}) collective-permute-start(f32[128,256]{1,0:T(8,128)S(1)} %get-tuple-element.36), channel_id=1, source_target_pairs={{0,1},{1,0},{2,3},{3,2},{4,5},{5,4},{6,7},{7,6},{8,9},{9,8},{10,11... | collective-permute-start | bytes 393224 | tf_op jit(solution)/shard_map/project/ppermute | solution.py:70
  49.1 1.0 collective-permute-done.12.refs_3_
  50.1 2.2 %finish.1 = bf16[768,256]{1,0:T(8,128)(2,1)} custom-call(f32[384,256]{1,0:T(8,128)S(1)} %get-tuple-element.33.refs_0_, f32[128,256]{1,0:T(8,128)S(1)} %get-tuple-element.34.refs_1_, f32[384,256]{1,0:T(8,128)S(1)} %collective-permute-done.11.refs_2_, f32[128,256]{1,0:T(8,128)S(1)} %collective-permute-done.12.refs_3_, ...), custom_call_target="tpu_custom_call" | custom-call | tf_op jit(solution)/shard_map/project/finish/pallas_call | solution.py:271
  52.2 6.5 %all-to-all-start = ((bf16[8,96,256]{2,1,0:T(8,128)(2,1)}), bf16[8,96,256]{2,1,0:T(8,128)(2,1)S(1)}, u32[]{:S(2)}, u32[]{:S(2)}) async-start(bf16[8,96,256]{2,1,0:T(8,128)(2,1)} %bitcast.2), calls=%async_computation | async-start | bytes 786432 | tf_op jit(solution)/shard_map/project/all_to_all | solution.py:483
  58.7 0.1 copy.12
  58.8 0.1 broadcast_in_dim.49
  58.9 0.9 dynamic_slice.7
  59.8 0.1 pad_maximum_fusion.3.refs_0_
  59.9 2.0 %fusion.8.refs_7_ = f32[16,128]{1,0:T(8,128)S(1)} fusion(bf16[16,8192]{1,0:T(8,128)(2,1)S(1)} %copy-done.13, bf16[8192,128]{1,0:T(8,128)(2,1)} %refs_15_.1), kind=kOutput, calls=%fused_computation.36 | convolution fusion | flops 33554432 | bytes 2367488 | tf_op jit(solution)/shard_map/first/dot_general | solution.py:496
  61.9 0.4 fusion.6.refs_5_
  62.3 11.5 %all-to-all-done = bf16[8,96,256]{2,1,0:T(8,128)(2,1)S(1)} async-done(((bf16[8,96,256]{2,1,0:T(8,128)(2,1)}), bf16[8,96,256]{2,1,0:T(8,128)(2,1)S(1)}, u32[]{:S(2)}, u32[]{:S(2)}) %all-to-all-start) | async-done | bytes 393248 | tf_op jit(solution)/shard_map/project/all_to_all | solution.py:483
  73.9 1.6 settle.1
  75.4 1.6 copy-done.4
  77.0 0.9 attend.4
  77.9 15.9 %all_to_all.40.refs_0_ = bf16[32,16,256]{2,1,0:T(8,128)(2,1)S(1)} all-to-all(bf16[32,16,256]{2,1,0:T(8,128)(2,1)S(1)} %get-tuple-element.43), channel_id=1, replica_groups=mesh['grp'=8,'head'=32] {'head'}, dimensions={0} | all-to-all | bytes 524288 | tf_op jit(solution)/shard_map/all_to_all | solution.py:507
  93.9 0.1 spread.4
  93.9 12.5 %all_to_all.41.refs_7_ = bf16[32,16,256]{2,1,0:T(8,128)(2,1)S(1)} all-to-all(bf16[32,16,256]{2,1,0:T(8,128)(2,1)S(1)} %get-tuple-element.44), channel_id=1, replica_groups=mesh['grp'=8,'head'=32] {'head'}, dimensions={0} | all-to-all | bytes 524288 | tf_op jit(solution)/shard_map/all_to_all | solution.py:511
  106.4 1.7 attend.5
  108.1 12.5 %all_to_all.42.refs_0_ = bf16[32,16,256]{2,1,0:T(8,128)(2,1)S(1)} all-to-all(bf16[32,16,256]{2,1,0:T(8,128)(2,1)S(1)} %get-tuple-element.47), channel_id=1, replica_groups=mesh['grp'=8,'head'=32] {'head'}, dimensions={0} | all-to-all | bytes 524288 | tf_op jit(solution)/shard_map/all_to_all | solution.py:507
  120.6 0.1 spread.5
  120.6 12.5 %all_to_all.43.refs_9_ = bf16[32,16,256]{2,1,0:T(8,128)(2,1)S(1)} all-to-all(bf16[32,16,256]{2,1,0:T(8,128)(2,1)S(1)} %get-tuple-element.49), channel_id=1, replica_groups=mesh['grp'=8,'head'=32] {'head'}, dimensions={0} | all-to-all | bytes 524288 | tf_op jit(solution)/shard_map/all_to_all | solution.py:511
  133.1 1.7 attend.6
  134.8 12.5 %all_to_all.44.refs_0_ = bf16[32,16,256]{2,1,0:T(8,128)(2,1)S(1)} all-to-all(bf16[32,16,256]{2,1,0:T(8,128)(2,1)S(1)} %get-tuple-element.52), channel_id=1, replica_groups=mesh['grp'=8,'head'=32] {'head'}, dimensions={0} | all-to-all | bytes 524288 | tf_op jit(solution)/shard_map/all_to_all | solution.py:507
  147.2 0.1 spread.6
  147.3 12.5 %all_to_all.45.refs_11_ = bf16[32,16,256]{2,1,0:T(8,128)(2,1)S(1)} all-to-all(bf16[32,16,256]{2,1,0:T(8,128)(2,1)S(1)} %get-tuple-element.54), channel_id=1, replica_groups=mesh['grp'=8,'head'=32] {'head'}, dimensions={0} | all-to-all | bytes 524288 | tf_op jit(solution)/shard_map/all_to_all | solution.py:511
  159.8 1.7 attend.7
  161.5 12.5 %all_to_all.46.refs_0_ = bf16[32,16,256]{2,1,0:T(8,128)(2,1)S(1)} all-to-all(bf16[32,16,256]{2,1,0:T(8,128)(2,1)S(1)} %get-tuple-element.55), channel_id=1, replica_groups=mesh['grp'=8,'head'=32] {'head'}, dimensions={0} | all-to-all | bytes 524288 | tf_op jit(solution)/shard_map/all_to_all | solution.py:507
  173.9 0.7 spread.7
  (57 shorter events, 0.3 us)
Async XLA Ops:
  0.0 0.8 copy-start.7
  0.8 0.9 copy-start.9
  1.7 0.7 copy-start.11
  3.2 4.3 %collective-permute-start = (bf16[16,4224]{1,0:T(8,128)(2,1)S(1)}, bf16[16,4224]{1,0:T(8,128)(2,1)S(1)}, u32[]{:S(2)}, u32[]{:S(2)}) collective-permute-start(bf16[16,4224]{1,0:T(8,128)(2,1)S(1)} %get-tuple-element.32), channel_id=1, source_target_pairs={{0,1},{1,0},{2,3},{3,2},{4,5},{5,4},{6,7},{7,6},{8,9},{9,8},{10,11... | collective-permute-start | bytes 405512 | tf_op jit(solution)/shard_map/rows/ppermute | solution.py:70
  7.5 1.1 copy-start.14
  7.5 6.9 %collective-permute-start.3 = (bf16[32,4224]{1,0:T(8,128)(2,1)S(1)}, bf16[32,4224]{1,0:T(8,128)(2,1)S(1)}, u32[]{:S(2)}, u32[]{:S(2)}) collective-permute-start(bf16[32,4224]{1,0:T(8,128)(2,1)S(1)} %constant_dynamic-update-slice_fusion), channel_id=1, source_target_pairs={{0,6},{1,25},{2,4},{3,27},{4,2},{5,29},{6,0},{7,31},{8,14},{9,17},... | collective-permute-start | bytes 811016 | tf_op jit(solution)/shard_map/rows/ppermute | solution.py:70
  8.7 12.4 %copy-start.15 = (bf16[16,4224]{1,0:T(8,128)(2,1)S(1)}, bf16[16,4224]{1,0:T(8,128)(2,1)}, u32[]{:S(2)}) copy-start(bf16[16,4224]{1,0:T(8,128)(2,1)} %copy-done.14) | copy-start | bytes 405508
  8.7 15.7 %copy-start = (bf16[8192,128]{1,0:T(8,128)(2,1)S(1)}, bf16[8192,128]{1,0:T(8,128)(2,1)}, u32[]{:S(2)}) copy-start(bf16[8192,128]{1,0:T(8,128)(2,1)} %refs_14_.1) | copy-start | bytes 6291460
  9.5 9.9 %collective-permute-start.1 = (bf16[32,4224]{1,0:T(8,128)(2,1)S(1)}, bf16[32,4224]{1,0:T(8,128)(2,1)S(1)}, u32[]{:S(2)}, u32[]{:S(2)}) collective-permute-start(bf16[32,4224]{1,0:T(8,128)(2,1)S(1)} %constant_dynamic-update-slice_fusion), channel_id=1, source_target_pairs={{0,2},{1,9},{2,0},{3,11},{4,6},{5,13},{6,4},{7,15},{8,10},{9,1},{1... | collective-permute-start | bytes 811016 | tf_op jit(solution)/shard_map/rows/ppermute | solution.py:70
  9.5 9.9 %collective-permute-start.2 = (bf16[32,4224]{1,0:T(8,128)(2,1)S(1)}, bf16[32,4224]{1,0:T(8,128)(2,1)S(1)}, u32[]{:S(2)}, u32[]{:S(2)}) collective-permute-start(bf16[32,4224]{1,0:T(8,128)(2,1)S(1)} %constant_dynamic-update-slice_fusion), channel_id=1, source_target_pairs={{0,4},{1,17},{2,6},{3,19},{4,0},{5,21},{6,2},{7,23},{8,12},{9,25},... | collective-permute-start | bytes 811016 | tf_op jit(solution)/shard_map/rows/ppermute | solution.py:70
  19.5 16.8 %collective-permute-start.4 = (bf16[64,4224]{1,0:T(8,128)(2,1)S(1)}, bf16[64,4224]{1,0:T(8,128)(2,1)}, u32[]{:S(2)}, u32[]{:S(2)}) collective-permute-start(bf16[64,4224]{1,0:T(8,128)(2,1)S(1)} %pad_maximum_fusion.refs_0_), channel_id=1, source_target_pairs={{0,8},{1,3},{2,10},{3,1},{4,12},{5,7},{6,14},{7,5},{8,0},{9,11},{1... | collective-permute-start | bytes 1622024 | tf_op jit(solution)/shard_map/rows/ppermute | solution.py:70
  19.6 10.8 %collective-permute-start.6 = (bf16[64,4224]{1,0:T(8,128)(2,1)S(1)}, bf16[64,4224]{1,0:T(8,128)(2,1)}, u32[]{:S(2)}, u32[]{:S(2)}) collective-permute-start(bf16[64,4224]{1,0:T(8,128)(2,1)S(1)} %pad_maximum_fusion.refs_0_), channel_id=1, source_target_pairs={{0,24},{1,7},{2,26},{3,5},{4,28},{5,3},{6,30},{7,1},{8,16},{9,15},... | collective-permute-start | bytes 1622024 | tf_op jit(solution)/shard_map/rows/ppermute | solution.py:70
  21.2 12.8 %collective-permute-start.5 = (bf16[64,4224]{1,0:T(8,128)(2,1)S(1)}, bf16[64,4224]{1,0:T(8,128)(2,1)}, u32[]{:S(2)}, u32[]{:S(2)}) collective-permute-start(bf16[64,4224]{1,0:T(8,128)(2,1)S(1)} %pad_maximum_fusion.1.refs_1_), channel_id=1, source_target_pairs={{0,8},{1,3},{2,10},{3,1},{4,12},{5,7},{6,14},{7,5},{8,0},{9,11},{1... | collective-permute-start | bytes 1622024 | tf_op jit(solution)/shard_map/rows/ppermute | solution.py:70
  21.9 14.4 %collective-permute-start.7 = (bf16[64,4224]{1,0:T(8,128)(2,1)S(1)}, bf16[64,4224]{1,0:T(8,128)(2,1)}, u32[]{:S(2)}, u32[]{:S(2)}) collective-permute-start(bf16[64,4224]{1,0:T(8,128)(2,1)S(1)} %pad_maximum_fusion.1.refs_1_), channel_id=1, source_target_pairs={{0,24},{1,7},{2,26},{3,5},{4,28},{5,3},{6,30},{7,1},{8,16},{9,15},... | collective-permute-start | bytes 1622024 | tf_op jit(solution)/shard_map/rows/ppermute | solution.py:70
  24.4 1.6 copy-start.1
  26.0 3.1 %copy-start.16 = (f32[16,8192]{1,0:T(8,128)S(1)}, f32[16,8192]{1,0:T(8,128)}, u32[]{:S(2)}) copy-start(f32[16,8192]{1,0:T(8,128)} %param.12) | copy-start | bytes 1572868
  26.0 3.3 %copy-start.8 = (f32[8192]{0:T(1024)S(1)}, f32[8192]{0:T(1024)}, u32[]{:S(2)}) copy-start(f32[8192]{0:T(1024)} %param.13) | copy-start | bytes 98308
  26.0 3.4 %copy-start.18 = (s32[8,16]{1,0:T(8,128)S(1)}, s32[8,16]{1,0:T(8,128)}, u32[]{:S(2)}) copy-start(s32[8,16]{1,0:T(8,128)} %param.11) | copy-start | bytes 1540
  26.4 9.9 %copy-start.2 = (bf16[8192,128]{1,0:T(8,128)(2,1)S(1)}, bf16[8192,128]{1,0:T(8,128)(2,1)}, u32[]{:S(2)}) copy-start(bf16[8192,128]{1,0:T(8,128)(2,1)} %refs_15_.1) | copy-start | bytes 6291460
  26.4 9.9 %collective-permute-start.8 = (bf16[4096,256]{1,0:T(8,128)(2,1)S(1)}, bf16[4096,256]{1,0:T(8,128)(2,1)S(1)}, u32[]{:S(2)}, u32[]{:S(2)}) collective-permute-start(bf16[4096,256]{1,0:T(8,128)(2,1)S(1)} %other_half.1), channel_id=1, source_target_pairs={{0,1},{1,0},{2,3},{3,2},{4,5},{5,4},{6,7},{7,6},{8,9},{9,8},{10,11... | collective-permute-start | bytes 6291464 | tf_op jit(solution)/shard_map/weights/ppermute | solution.py:70
  29.5 10.8 %copy-start.12 = (bf16[16,8192]{1,0:T(8,128)(2,1)}, bf16[16,8192]{1,0:T(8,128)(2,1)S(1)}, u32[]{:S(2)}) copy-start(bf16[16,8192]{1,0:T(8,128)(2,1)S(1)} %multiply_convert_fusion) | copy-start | bytes 786436
  30.4 12.4 %collective-permute-start.9 = (bf16[64,4224]{1,0:T(8,128)(2,1)}, bf16[64,4224]{1,0:T(8,128)(2,1)S(1)}, u32[]{:S(2)}, u32[]{:S(2)}) collective-permute-start(bf16[64,4224]{1,0:T(8,128)(2,1)} %collective-permute-done.6.refs_4_), channel_id=1, source_target_pairs={{0,8},{1,3},{2,10},{3,1},{4,12},{5,7},{6,14},{7,5},{8,0},{9,11},{1... | collective-permute-start | bytes 1622024 | tf_op jit(solution)/shard_map/rows/ppermute | solution.py:70
  34.0 9.9 %collective-permute-start.10 = (bf16[64,4224]{1,0:T(8,128)(2,1)}, bf16[64,4224]{1,0:T(8,128)(2,1)S(1)}, u32[]{:S(2)}, u32[]{:S(2)}) collective-permute-start(bf16[64,4224]{1,0:T(8,128)(2,1)} %collective-permute-done.5.refs_3_), channel_id=1, source_target_pairs={{0,24},{1,7},{2,26},{3,5},{4,28},{5,3},{6,30},{7,1},{8,16},{9,15},... | collective-permute-start | bytes 1622024 | tf_op jit(solution)/shard_map/rows/ppermute | solution.py:70
  40.3 9.8 %collective-permute-start.11 = (f32[384,256]{1,0:T(8,128)S(1)}, f32[384,256]{1,0:T(8,128)S(1)}, u32[]{:S(2)}, u32[]{:S(2)}) collective-permute-start(f32[384,256]{1,0:T(8,128)S(1)} %get-tuple-element.35), channel_id=1, source_target_pairs={{0,1},{1,0},{2,3},{3,2},{4,5},{5,4},{6,7},{7,6},{8,9},{9,8},{10,11... | collective-permute-start | bytes 1179656 | tf_op jit(solution)/shard_map/project/ppermute | solution.py:70
  45.6 14.2 %copy-start.17 = (f32[4,16,64]{2,1,0:T(8,128)S(1)}, f32[4,16,64]{2,1,0:T(8,128)}, u32[]{:S(2)}) copy-start(f32[4,16,64]{2,1,0:T(8,128)} %get-tuple-element.69) | copy-start | bytes 49156
  45.6 14.3 %copy-start.13 = (bf16[16,8192]{1,0:T(8,128)(2,1)S(1)}, bf16[16,8192]{1,0:T(8,128)(2,1)}, u32[]{:S(2)}) copy-start(bf16[16,8192]{1,0:T(8,128)(2,1)} %copy-done.12) | copy-start | bytes 786436
  45.6 4.5 %collective-permute-start.12 = (f32[128,256]{1,0:T(8,128)S(1)}, f32[128,256]{1,0:T(8,128)S(1)}, u32[]{:S(2)}, u32[]{:S(2)}) collective-permute-start(f32[128,256]{1,0:T(8,128)S(1)} %get-tuple-element.36), channel_id=1, source_target_pairs={{0,1},{1,0},{2,3},{3,2},{4,5},{5,4},{6,7},{7,6},{8,9},{9,8},{10,11... | collective-permute-start | bytes 393224 | tf_op jit(solution)/shard_map/project/ppermute | solution.py:70
  52.2 21.6 %all-to-all-start = ((bf16[8,96,256]{2,1,0:T(8,128)(2,1)}), bf16[8,96,256]{2,1,0:T(8,128)(2,1)S(1)}, u32[]{:S(2)}, u32[]{:S(2)}) async-start(bf16[8,96,256]{2,1,0:T(8,128)(2,1)} %bitcast.2), calls=%async_computation | async-start | bytes 786432 | tf_op jit(solution)/shard_map/project/all_to_all | solution.py:483
  58.8 3.1 %copy-start.5 = (bf16[8192,128]{1,0:T(8,128)(2,1)S(1)}, bf16[8192,128]{1,0:T(8,128)(2,1)}, u32[]{:S(2)}) copy-start(bf16[8192,128]{1,0:T(8,128)(2,1)} %refs_13_.3) | copy-start | bytes 6291460
  59.9 14.0 %copy-start.10 = (bf16[128,256]{1,0:T(8,128)(2,1)S(1)}, bf16[128,256]{1,0:T(8,128)(2,1)}, u32[]{:S(2)}) copy-start(bf16[128,256]{1,0:T(8,128)(2,1)} %subtract_convert_fusion.refs_4_) | copy-start | bytes 196612
  75.4 1.6 copy-start.4
  77.0 29.3 %copy-start.3 = (bf16[8192,128]{1,0:T(8,128)(2,1)S(1)}, bf16[8192,128]{1,0:T(8,128)(2,1)}, u32[]{:S(2)}) copy-start(bf16[8192,128]{1,0:T(8,128)(2,1)} %refs_15_.1) | copy-start | bytes 6291460
  77.0 29.3 %copy-start.6 = (bf16[8192,128]{1,0:T(8,128)(2,1)S(1)}, bf16[8192,128]{1,0:T(8,128)(2,1)}, u32[]{:S(2)}) copy-start(bf16[8192,128]{1,0:T(8,128)(2,1)} %refs_13_.3) | copy-start | bytes 6291460

commit v5 on v4

--- a/solution.py
+++ b/solution.py
@@ -110,7 +110,7 @@
         norm_split_kernel,
         out_shape=(shape, shape),
         in_specs=[pl.BlockSpec(memory_space=pltpu.SMEM), whole, whole],
-        compiler_params=params(8),
+        compiler_params=params(56),
         name="norm_split",
     )(groups, rows, gain.reshape(1, -1))
 
@@ -145,7 +145,9 @@
 
 def project_kernel(count, *refs):
     pieces = refs[:count]
-    key_ref, value_ref, their_ref, own_ref, other_ref, ids_ref, x, w, piece_sems, weight_sems = refs[count:]
+    key_ref, value_ref, their_ref, own_ref, other_ref, ids_ref, w, x, piece_sems, weight_sems = refs[
+        count:
+    ]
     size = pieces[0].shape[0]
     half = w.shape[0]
     depth = half // CHUNKS
@@ -201,17 +203,41 @@
     shape = jax.ShapeDtypeStruct((rows, 2 * HD), jnp.float32)
     return pl.pallas_call(
         lambda *refs: project_kernel(count, *refs),
-        out_shape=(shape, shape, jax.ShapeDtypeStruct((rows, HD), jnp.bfloat16)),
+        out_shape=(
+            shape,
+            shape,
+            jax.ShapeDtypeStruct((rows, HD), jnp.bfloat16),
+            jax.ShapeDtypeStruct((half, 4 * HD), jnp.bfloat16),
+        ),
         in_specs=[anywhere] * (count + 3),
         scratch_shapes=[
             pltpu.VMEM((rows, wide), jnp.bfloat16),
-            pltpu.VMEM((half, 4 * HD), jnp.bfloat16),
             pltpu.SemaphoreType.DMA((count,)),
             pltpu.SemaphoreType.DMA((CHUNKS, 3)),
         ],
-        compiler_params=params(16),
+        compiler_params=params(14),
         name="project",
     )(*pieces, w_key, w_value, their_half)
+
+
+def project_last_kernel(first, second, w, own_ref, other_ref, ids_ref):
+    n, half = first.shape[0], w.shape[0]
+    x = jnp.concatenate([first[...], second[...]], axis=0)
+    ids_ref[...] = x[:, half:]
+    term = jnp.dot(x[:, :half], w[...], preferred_element_type=jnp.float32)
+    own_ref[...] = term[:, : 2 * HD]
+    other_ref[...] = term[:, 2 * HD :]
+
+
+def project_last(first, second, weights):
+    rows = 2 * first.shape[0]
+    shape = jax.ShapeDtypeStruct((rows, 2 * HD), jnp.float32)
+    return pl.pallas_call(
+        project_last_kernel,
+        out_shape=(shape, shape, jax.ShapeDtypeStruct((rows, HD), jnp.bfloat16)),
+        compiler_params=params(10),
+        name="project_last",
+    )(first, second, weights)
 
 
 def origin(shape, dim, head):
@@ -226,12 +252,13 @@
     return (((y * NX + x) * 2 + c) << 4) + row
 
 
-def finish_kernel(groups, own_a, own_b, their_a, their_b, ids_a, ids_b, out_ref, packed):
+def finish_kernel(groups, cap, own_a, own_b, their_a, their_b, ids_a, ids_b, *refs):
+    outs, packed = refs[:groups], refs[groups]
     total = packed.shape[0]
     n = total // (len(HELD) * NX)
     early = EARLY * NX
     head = lax.axis_index("head")
-    cap = out_ref.shape[0] // groups
+    group = lax.axis_index("grp").astype(jnp.float32)
 
     def block(first, second, i):
         return first[i * n : (i + 1) * n] if i < early else second[(i - early) * n : (i - early + 1) * n]
@@ -242,87 +269,122 @@
             j = HELD.index((d_first, 1 - d_core)) * NX + d_second
             both = block(own_a, own_b, i) + block(their_a, their_b, j)
             packed[i * n : (i + 1) * n, :] = both.astype(jnp.bfloat16)
-    ids = jnp.concatenate([ids_a[...], ids_b[...]], axis=0).astype(jnp.float32)
-    lanes = lax.broadcasted_iota(jnp.int32, (total, HD), 1).astype(jnp.float32)
-    match = jnp.where(ids == lanes, 1.0, 0.0)
-    earlier = origin((total, total), 1, head) < origin((total, total), 0, head)
+    hop = jnp.concatenate([ids_a[...], ids_b[...]], axis=0).astype(jnp.float32) - group
+    hop = jnp.where(hop < 0.0, hop + groups, hop)
+    lanes = lax.broadcasted_iota(jnp.int32, (1, HD), 1).astype(jnp.float32)
+    match = jnp.where(hop == lanes, 1.0, 0.0)
+    earlier = origin((1, total), 1, head) < origin((total, 1), 0, head)
     ranks = jnp.dot(
         jnp.where(earlier, 1.0, 0.0).astype(jnp.bfloat16),
         match.astype(jnp.bfloat16),
         preferred_element_type=jnp.float32,
     )
     order = jnp.sum(ranks * match, axis=1, keepdims=True)
-    slot = ids[:, :1] * cap + order
-    slots = lax.broadcasted_iota(jnp.int32, (total, groups * cap), 1).astype(jnp.float32)
+    slot = hop[:, :1] * cap + order
+    slots = lax.broadcasted_iota(jnp.int32, (1, groups * cap), 1).astype(jnp.float32)
     pick = jnp.where(slots == slot, 1.0, 0.0).astype(jnp.bfloat16)
     routed = lax.dot_general(
         pick, packed[...], (((0,), (0,)), ((), ())), preferred_element_type=jnp.float32
     )
     counts = jnp.sum(match, axis=0, keepdims=True)
-    step = lax.broadcasted_iota(jnp.int32, (cap, HD), 0).astype(jnp.float32)
+    step = lax.broadcasted_iota(jnp.int32, (cap, 1), 0).astype(jnp.float32)
     for g in range(groups):
         rows = slice(g * cap, (g + 1) * cap)
         filled = step < counts[:, g : g + 1]
-        out_ref[rows, :HD] = jnp.where(filled, routed[rows, :HD], EMPTY).astype(jnp.bfloat16)
-        out_ref[rows, HD:] = routed[rows, HD:].astype(jnp.bfloat16)
-
-
-def finish(groups, slots, own_a, own_b, their_a, their_b, ids_a, ids_b):
-    return pl.pallas_call(
-        lambda *refs: finish_kernel(groups, *refs),
-        out_shape=jax.ShapeDtypeStruct((slots, 2 * HD), jnp.bfloat16),
+        outs[g][:, :HD] = jnp.where(filled, routed[rows, :HD], EMPTY).astype(jnp.bfloat16)
+        outs[g][:, HD:] = routed[rows, HD:].astype(jnp.bfloat16)
+
+
+def finish(groups, cap, own_a, own_b, their_a, their_b, ids_a, ids_b):
+    shape = jax.ShapeDtypeStruct((cap, 2 * HD), jnp.bfloat16)
+    return pl.pallas_call(
+        lambda *refs: finish_kernel(groups, cap, *refs),
+        out_shape=(shape,) * groups,
         scratch_shapes=[pltpu.VMEM((own_a.shape[0] + own_b.shape[0], 2 * HD), jnp.bfloat16)],
-        compiler_params=params(24),
+        compiler_params=params(12),
         name="finish",
     )(own_a, own_b, their_a, their_b, ids_a, ids_b)
 
 
-def settle_kernel(groups, cache_ref, edge_row, edge_col, high_ref, low_ref, key_ref, bias_ref, hot):
-    slots = cache_ref.shape[0]
-    cap = slots // groups
+def settle_kernel(groups, edge_row, edge_col, high_ref, low_ref, *refs):
+    parts = refs[:groups]
+    key_ref, value_ref, bias_ref, hot = refs[groups:]
+    cap = parts[0].shape[0]
+    slots = groups * cap
+    me = lax.axis_index("grp")
+    sources = [lax.rem(me + groups - g, groups) for g in range(groups)]
     starts, ends = edge_row[0:1, :], edge_row[1:2, :]
-    lanes = lax.broadcasted_iota(jnp.int32, (cap, HD), 1).astype(jnp.float32)
+    lanes = lax.broadcasted_iota(jnp.int32, (1, HD), 1).astype(jnp.float32)
     step = lax.broadcasted_iota(jnp.int32, (cap, 1), 0).astype(jnp.float32)
     across = lax.broadcasted_iota(jnp.int32, (1, slots), 1).astype(jnp.float32)
+    counts = []
+    for part in parts:
+        full = part[:, :HD].astype(jnp.float32) < EMPTY / 2
+        counts.append(jnp.sum(jnp.where(full, 1.0, 0.0), axis=0, keepdims=True)[:, :1])
     cells = across
     open_slots = across < 0.0
-    base = jnp.zeros((1, 1), jnp.float32)
     for g in range(groups):
+        base = jnp.zeros((1, 1), jnp.float32)
+        for other in range(groups):
+            if other != g:
+                before = jnp.where(sources[other] < sources[g], 1.0, 0.0)
+                base = base + counts[other] * before
         rows = slice(g * cap, (g + 1) * cap)
-        full = cache_ref[rows, :HD].astype(jnp.float32) < EMPTY / 2
-        count = jnp.sum(jnp.where(full, 1.0, 0.0), axis=0, keepdims=True)[:, :1]
         cell = base + step
         inside = (cell >= starts) & (cell < ends)
         place = cell - jnp.sum(jnp.where(inside, starts, 0.0), axis=1, keepdims=True)
         hot[rows, :] = jnp.where(lanes == place, 1.0, 0.0).astype(jnp.bfloat16)
         here = (across >= g * cap) & (across < (g + 1) * cap)
         cells = jnp.where(here, across - g * cap + base, cells)
-        open_slots = open_slots | (here & (across - g * cap < count))
-        base = base + count
+        open_slots = open_slots | (here & (across - g * cap < counts[g]))
+        value_ref[rows, :] = parts[g][:, HD:]
     low_edge, high_edge = edge_col[:, 0:1], edge_col[:, HD : HD + 1]
     mine = (cells >= low_edge) & (cells < high_edge) & open_slots
     bias_ref[...] = jnp.where(mine, 0.0, MASKED)
     trig = jnp.dot(hot[...], high_ref[...], preferred_element_type=jnp.float32)
     trig = trig + jnp.dot(hot[...], low_ref[...], preferred_element_type=jnp.float32)
-    keys = cache_ref[:, :HD].astype(jnp.float32)
-    keys = jnp.where(keys < EMPTY / 2, keys, 0.0)
-    key_ref[...] = (keys * trig[:, :HD] + pltpu.roll(keys, HD // 2, 1) * trig[:, HD:]).astype(
-        jnp.bfloat16
-    )
-
-
-def settle(groups, cache, edge_row, edge_col, high, low):
-    slots = cache.shape[0]
-    return pl.pallas_call(
-        lambda *refs: settle_kernel(groups, *refs),
-        out_shape=(
-            jax.ShapeDtypeStruct((slots, HD), jnp.bfloat16),
-            jax.ShapeDtypeStruct((edge_col.shape[0], slots), jnp.float32),
-        ),
+    for g in range(groups):
+        rows = slice(g * cap, (g + 1) * cap)
+        keys = parts[g][:, :HD].astype(jnp.float32)
+        keys = jnp.where(keys < EMPTY / 2, keys, 0.0)
+        turned_keys = keys * trig[rows, :HD] + pltpu.roll(keys, HD // 2, 1) * trig[rows, HD:]
+        key_ref[rows, :] = turned_keys.astype(jnp.bfloat16)
+
+
+def settle(edge_row, edge_col, high, low, parts):
+    slots = len(parts) * parts[0].shape[0]
+    wide = jax.ShapeDtypeStruct((slots, HD), jnp.bfloat16)
+    return pl.pallas_call(
+        lambda *refs: settle_kernel(len(parts), *refs),
+        out_shape=(wide, wide, jax.ShapeDtypeStruct((edge_col.shape[0], slots), jnp.float32)),
         scratch_shapes=[pltpu.VMEM((slots, HD), jnp.bfloat16)],
-        compiler_params=params(16),
+        compiler_params=params(8),
         name="settle",
-    )(cache, edge_row, edge_col, high, low)
+    )(edge_row, edge_col, high, low, *parts)
+
+
+def hold_kernel(count, *refs):
+    sems = refs[-1]
+    copies = [
+        pltpu.make_async_copy(refs[i], refs[count + 1 + i], sems.at[i]) for i in range(count)
+    ]
+    for copy in copies:
+        copy.start()
+    for copy in copies:
+        copy.wait()
+
+
+def hold(arrays, dep):
+    count = len(arrays)
+    return pl.pallas_call(
+        lambda *refs: hold_kernel(count, *refs),
+        out_shape=tuple(jax.ShapeDtypeStruct(a.shape, a.dtype) for a in arrays),
+        in_specs=[pl.BlockSpec(memory_space=pl.ANY)] * (count + 1),
+        out_specs=(pl.BlockSpec(memory_space=pltpu.VMEM),) * count,
+        scratch_shapes=[pltpu.SemaphoreType.DMA((count,))],
+        compiler_params=params(10),
+        name="hold",
+    )(*arrays, dep)
 
 
 def rotated(values, turn):
@@ -373,7 +435,7 @@
     for f in fresh_exp:
         total = total + f
     weights = (cache_exp / total).astype(bf16)
-    attended = jnp.dot(weights, cache_ref[:, HD:], preferred_element_type=f32)
+    attended = jnp.dot(weights, cache_ref[...], preferred_element_type=f32)
     for f, (_, v) in zip(fresh_exp, pairs):
         attended = attended + (f / total).astype(bf16).astype(f32) * v.astype(f32)
     attended = attended.astype(bf16)
@@ -395,12 +457,13 @@
     return pl.pallas_call(
         lambda *refs: attend_kernel(step, *refs),
         out_shape=(jax.ShapeDtypeStruct((blocks, n, share), jnp.bfloat16), small, small),
-        compiler_params=params(20),
+        compiler_params=params(10),
         name="attend",
     )(turns, keys, cache, bias, w_out, *flat, *extra)
 
 
-def spread_kernel(last, part_ref, current_ref, gain_ref, next_ref, *out):
+def spread_kernel(last, part_ref, current_ref, gain_ref, *refs):
+    next_ref, *out = refs[-1:] if last else refs[-2:]
     total = current_ref[...]
     for i in range(part_ref.shape[0]):
         total = total + part_ref[i].astype(jnp.float32)
@@ -411,7 +474,7 @@
             out[0][i] = piece
 
 
-def spread(last, parts, current, gain):
+def spread(last, parts, current, gain, held):
     shapes = [jax.ShapeDtypeStruct(current.shape, jnp.float32)]
     if not last:
         shapes.append(jax.ShapeDtypeStruct(parts.shape, jnp.bfloat16))
@@ -420,7 +483,7 @@
         out_shape=tuple(shapes),
         compiler_params=params(4),
         name="spread",
-    )(parts, current, gain)
+    )(parts, current, gain, *held)
 
 
 def per_device(
@@ -475,15 +538,19 @@
         table_low = (table - table_high.astype(f32)).astype(bf16)
 
     with jax.named_scope("project"):
-        own_a, other_a, ids_a = project([l0, l1, s10, s11, s30, s31], w_key, w_value, their_half)
-        own_b, other_b, ids_b = project([s20, s21], w_key, w_value, their_half)
-        outgoing = finish(
-            groups, groups * cap, own_a, own_b, send(other_a, CORE), send(other_b, CORE), ids_a, ids_b
+        own_a, other_a, ids_a, half_weights = project(
+            [l0, l1, s10, s11, s30, s31], w_key, w_value, their_half
         )
-        cache = lax.all_to_all(
-            outgoing.reshape(groups, cap, 2 * HD), "grp", split_axis=0, concat_axis=0, tiled=True
-        ).reshape(groups * cap, 2 * HD)
-        cache_keys, bias = settle(groups, cache, edge_row, edge_col, table_high, table_low)
+        own_b, other_b, ids_b = project_last(s20, s21, half_weights)
+        leaving = finish(
+            groups, cap, own_a, own_b, send(other_a, CORE), send(other_b, CORE), ids_a, ids_b
+        )
+        arrived = [leaving[0]]
+        for hop in range(1, groups):
+            pairs = [(g, (g + hop) % groups) for g in range(groups)]
+            arrived.append(lax.ppermute(leaving[hop], "grp", pairs))
+        (w_out,) = hold([w_out], leaving[0])
+        cache_keys, cache_values, bias = settle(edge_row, edge_col, table_high, table_low, arrived)
 
     with jax.named_scope("first"):
         late_state = after(decode_state, f1)
@@ -498,15 +565,16 @@
         at_step = my_lengths[None, :] + jnp.arange(STEPS, dtype=jnp.int32)[:, None]
         turns = jnp.concatenate(angles_of(at_step), axis=-1)
         extra += [current, my_gain, inverse]
+    held = [w_query, w_key, w_value, w_out]
     olds = []
     for step in range(STEPS):
         term, new_key, new_value = attend(
-            step, heads, turns, cache_keys, cache, bias, w_out, olds, extra
+            step, heads, turns, cache_keys, cache_values, bias, w_out, olds, extra
         )
         olds.append((new_key, new_value))
         parts = lax.all_to_all(term, "head", split_axis=0, concat_axis=0, tiled=True)
         last = step + 1 == STEPS
-        current, *spreading = spread(last, parts, current, my_gain)
+        current, *spreading = spread(last, parts, current, my_gain, [] if last else held)
         if not last:
             rows = lax.all_to_all(spreading[0], "head", split_axis=0, concat_axis=0, tiled=True)
             extra = [rows, inverse, w_query, w_key, w_value]

time: 175 us -> 170 us (0.971)
  waiting for transfers between devices: 24.8 us -> 13.1 us
  starting transfers between devices: 27.4 us -> 35.6 us
  local copies, waits for them, and re-layouts: 7.26 us -> 4.98 us
    ppermute x0 -> x7, starting transfers between devices: none -> 14.8 us  [per_device(): arrived.append(lax.ppermute(leaving[hop], 'grp', pairs))]
    all_to_all x1 -> x0, waiting for transfers between devices: 11.5 us -> none  [per_device(): lax.all_to_all(outgoing.reshape(groups, cap, 2 * HD), 'grp', split_axis=0...]
    all_to_all x1 -> x0, starting transfers between devices: 6.5 us -> none  [per_device(): lax.all_to_all(outgoing.reshape(groups, cap, 2 * HD), 'grp', split_axis=0...]
    ppermute x13, waiting for transfers between devices: 13.3 us -> 10 us  [send(): return lax.ppermute(values, 'head', pairs)]
    ppermute x0 -> x7, waiting for transfers between devices: none -> 3.07 us  [per_device(): arrived.append(lax.ppermute(leaving[hop], 'grp', pairs))]
    unnamed x40 -> x30, local copies, waits for them, and re-layouts: 5.62 us -> 3.43 us
    pallas_call x2 -> x1, Pallas kernels: 5.6 us -> 3.96 us  [project(): pl.pallas_call(lambda *refs: project_kernel(count, *refs), out_shape=(sha...]
    pallas_call x2 -> x4, Pallas kernels: 3.74 us -> 3.89 us  [the longest x1 1.63 us: settle(): pl.pallas_call(lambda *refs: settle_kernel(len(parts), *refs), out_shape=...]
  transfers between devices with their start and end apart: 14 -> 20, of which waited for: 7 -> 7; matrix products, arithmetic and copies ran while one was open for 4% -> 5% of each run, Pallas kernels for 3% -> 4%
where the time goes in v5:
time: 170 us; the launch traced here: 169 us
  blocking collectives  91.3 us (54%)
  starting transfers between devices  35.6 us (21%)
  Pallas kernels  18 us (11%)
  waiting for transfers between devices  13.1 us (8%)
  local copies, waits for them, and re-layouts  4.98 us (3%)
  other arithmetic  3.06 us (2%)
  matrix products  2.25 us (1%)
    all_to_all x4, blocking collectives, per_device(): lax.all_to_all(term, 'head', split_axis=0, concat_axis=0, tiled=True)  53.9 us
    all_to_all x3, blocking collectives, per_device(): lax.all_to_all(spreading[0], 'head', split_axis=0, concat_axis=0, tiled=T...  37.4 us
    ppermute x13, starting transfers between devices, send(): return lax.ppermute(values, 'head', pairs)  20.8 us
    ppermute x7, starting transfers between devices, per_device(): arrived.append(lax.ppermute(leaving[hop], 'grp', pairs))  14.8 us
    ppermute x13, waiting for transfers between devices, send(): return lax.ppermute(values, 'head', pairs)  10 us
    pallas_call x4, Pallas kernels, attend(): pl.pallas_call(lambda *refs: attend_kernel(step, *refs), out_shape=(jax.S...  6.01 us
    pallas_call x1, Pallas kernels, project(): pl.pallas_call(lambda *refs: project_kernel(count, *refs), out_shape=(sha...  3.96 us
    unnamed x30, local copies, waits for them, and re-layouts  3.43 us
  transfers between devices with their start and end apart: 20, of which 7 were waited for; matrix products, arithmetic and copies ran while one was open for 5% of the time, Pallas kernels for 4%

profile of v5, /device:TPU:1, one launch (start us, length us, event | category | flops | bytes accessed | tf_op | source)
XLA Modules:
  0.0 169.3 jit_solution(2412408984099884979)
XLA Ops:
  0.0 1.9 %norm_split.1 = (bf16[16,4224]{1,0:T(8,128)(2,1)}, bf16[16,4224]{1,0:T(8,128)(2,1)}) custom-call(s32[16]{0:T(128)} %group_ref.1, bf16[16,8192]{1,0:T(8,128)(2,1)} %rows_ref.1, f32[1,8192]{1,0:T(1,128)} %bitcast.33), custom_call_target="tpu_custom_call" | custom-call | tf_op jit(solution)/shard_map/rows/norm_split/pallas_call | solution.py:109
  1.9 3.2 %collective-permute-start = (bf16[16,4224]{1,0:T(8,128)(2,1)}, bf16[16,4224]{1,0:T(8,128)(2,1)S(1)}, u32[]{:S(2)}, u32[]{:S(2)}) collective-permute-start(bf16[16,4224]{1,0:T(8,128)(2,1)} %get-tuple-element.42), channel_id=1, source_target_pairs={{0,1},{1,0},{2,3},{3,2},{4,5},{5,4},{6,7},{7,6},{8,9},{9,8},{10,11... | collective-permute-start | bytes 405512 | tf_op jit(solution)/shard_map/rows/ppermute | solution.py:70
  5.2 0.9 constant_dynamic-update-slice_fusion.1
  6.1 0.3 multiply_cosine_fusion
  6.5 1.1 collective-permute-start.3
  7.6 0.1 fusion.refs_2_
  7.7 0.1 subtract_convert_fusion.refs_3_
  7.8 0.1 collective-permute-start.1
  7.9 2.8 %collective-permute-start.2 = (bf16[32,4224]{1,0:T(8,128)(2,1)S(1)}, bf16[32,4224]{1,0:T(8,128)(2,1)S(1)}, u32[]{:S(2)}, u32[]{:S(2)}) collective-permute-start(bf16[32,4224]{1,0:T(8,128)(2,1)S(1)} %constant_dynamic-update-slice_fusion), channel_id=1, source_target_pairs={{0,4},{1,17},{2,6},{3,19},{4,0},{5,21},{6,2},{7,23},{8,12},{9,25},... | collective-permute-start | bytes 811016 | tf_op jit(solution)/shard_map/rows/ppermute | solution.py:70
  10.7 2.6 %collective-permute-done.3 = bf16[32,4224]{1,0:T(8,128)(2,1)S(1)} collective-permute-done((bf16[32,4224]{1,0:T(8,128)(2,1)S(1)}, bf16[32,4224]{1,0:T(8,128)(2,1)S(1)}, u32[]{:S(2)}, u32[]{:S(2)}) %collective-permute-start.3) | collective-permute-done | bytes 270368 | tf_op jit(solution)/shard_map/rows/ppermute | solution.py:70
  13.4 4.4 %collective-permute-done.2 = bf16[32,4224]{1,0:T(8,128)(2,1)S(1)} collective-permute-done((bf16[32,4224]{1,0:T(8,128)(2,1)S(1)}, bf16[32,4224]{1,0:T(8,128)(2,1)S(1)}, u32[]{:S(2)}, u32[]{:S(2)}) %collective-permute-start.2) | collective-permute-done | bytes 270368 | tf_op jit(solution)/shard_map/rows/ppermute | solution.py:70
  17.9 0.1 collective-permute-start.4
  18.0 1.6 collective-permute-start.6
  19.6 0.9 pad_maximum_fusion.1.refs_1_
  20.6 0.7 collective-permute-start.5
  21.3 1.3 collective-permute-start.7
  22.6 1.4 other_half.1
  24.0 2.6 %collective-permute-start.8 = (bf16[4096,256]{1,0:T(8,128)(2,1)}, bf16[4096,256]{1,0:T(8,128)(2,1)}, u32[]{:S(2)}, u32[]{:S(2)}) collective-permute-start(bf16[4096,256]{1,0:T(8,128)(2,1)} %other_half.1), channel_id=1, source_target_pairs={{0,1},{1,0},{2,3},{3,2},{4,5},{5,4},{6,7},{7,6},{8,9},{9,8},{10,11... | collective-permute-start | bytes 6291464 | tf_op jit(solution)/shard_map/weights/ppermute | solution.py:70
  26.6 0.5 slice.30
  27.8 0.2 multiply_reduce_fusion
  28.0 0.8 copy-done.8
  28.8 0.8 multiply_convert_fusion
  29.6 0.1 select_reduce_fusion.1
  29.7 1.5 fusion.7.refs_6_
  31.3 0.4 fusion.8.refs_7_
  31.7 0.2 multiply_cosine_fusion.1
  31.9 0.1 collective-permute-start.9
  32.0 0.4 collective-permute-done.5.refs_3_
  32.4 1.3 collective-permute-start.10
  33.7 0.4 fusion.6.refs_5_
  34.2 4.0 %project.1 = (f32[384,256]{1,0:T(8,128)S(1)}, f32[384,256]{1,0:T(8,128)S(1)}, bf16[384,128]{1,0:T(8,128)(2,1)S(1)}, bf16[4096,512]{1,0:T(8,128)(2,1)S(1)}) custom-call(bf16[64,4224]{1,0:T(8,128)(2,1)S(1)} %pad_maximum_fusion.refs_0_, bf16[64,4224]{1,0:T(8,128)(2,1)S(1)} %pad_maximum_fusion.1.refs_1_, bf16[64,4224]{1,0:T(8,128)(2,1)} %collective-permute-done.4.refs_2_, ...), custom_call_target="tpu_custom_call" | custom-call | tf_op jit(solution)/shard_map/project/project/pallas_call | solution.py:204
  38.1 2.4 %collective-permute-start.11 = (f32[384,256]{1,0:T(8,128)S(1)}, f32[384,256]{1,0:T(8,128)S(1)}, u32[]{:S(2)}, u32[]{:S(2)}) collective-permute-start(f32[384,256]{1,0:T(8,128)S(1)} %get-tuple-element.46), channel_id=1, source_target_pairs={{0,1},{1,0},{2,3},{3,2},{4,5},{5,4},{6,7},{7,6},{8,9},{9,8},{10,11... | collective-permute-start | bytes 1179656 | tf_op jit(solution)/shard_map/project/ppermute | solution.py:70
  40.5 0.1 select_reduce_fusion
  40.7 1.6 collective-permute-done.10.second
  42.3 0.7 project_last.1
  43.0 3.4 %collective-permute-start.12 = (f32[128,256]{1,0:T(8,128)S(1)}, f32[128,256]{1,0:T(8,128)S(1)}, u32[]{:S(2)}, u32[]{:S(2)}) collective-permute-start(f32[128,256]{1,0:T(8,128)S(1)} %get-tuple-element.47), channel_id=1, source_target_pairs={{0,1},{1,0},{2,3},{3,2},{4,5},{5,4},{6,7},{7,6},{8,9},{9,8},{10,11... | collective-permute-start | bytes 393224 | tf_op jit(solution)/shard_map/project/ppermute | solution.py:70
  46.4 0.1 pad_maximum_fusion.3.refs_0_
  46.5 0.9 collective-permute-done.12.refs_3_
  47.4 1.4 finish.1
  48.9 2.9 %collective-permute-start.14 = (bf16[96,256]{1,0:T(8,128)(2,1)S(1)}, bf16[96,256]{1,0:T(8,128)(2,1)S(1)}, u32[]{:S(2)}, u32[]{:S(2)}) collective-permute-start(bf16[96,256]{1,0:T(8,128)(2,1)S(1)} %get-tuple-element.52), channel_id=1, source_target_pairs={{0,64},{32,96},{64,128},{96,160},{128,192},{160,224},{192,0},{224,... | collective-permute-start | bytes 147464 | tf_op jit(solution)/shard_map/project/ppermute | solution.py:551
  51.9 0.7 constant_dynamic-slice_fusion.refs_8_.refs_1_
  52.6 3.8 %collective-permute-start.15 = (bf16[96,256]{1,0:T(8,128)(2,1)S(1)}, bf16[96,256]{1,0:T(8,128)(2,1)S(1)}, u32[]{:S(2)}, u32[]{:S(2)}) collective-permute-start(bf16[96,256]{1,0:T(8,128)(2,1)S(1)} %get-tuple-element.53), channel_id=1, source_target_pairs={{0,96},{32,128},{64,160},{96,192},{128,224},{160,0},{192,32},{224,... | collective-permute-start | bytes 147464 | tf_op jit(solution)/shard_map/project/ppermute | solution.py:551
  56.3 0.5 collective-permute-start.16
  56.8 4.5 %collective-permute-start.17 = (bf16[96,256]{1,0:T(8,128)(2,1)S(1)}, bf16[96,256]{1,0:T(8,128)(2,1)S(1)}, u32[]{:S(2)}, u32[]{:S(2)}) collective-permute-start(bf16[96,256]{1,0:T(8,128)(2,1)S(1)} %get-tuple-element.55), channel_id=1, source_target_pairs={{0,160},{32,192},{64,224},{96,0},{128,32},{160,64},{192,96},{224,1... | collective-permute-start | bytes 147464 | tf_op jit(solution)/shard_map/project/ppermute | solution.py:551
  61.3 2.4 %collective-permute-start.18 = (bf16[96,256]{1,0:T(8,128)(2,1)S(1)}, bf16[96,256]{1,0:T(8,128)(2,1)S(1)}, u32[]{:S(2)}, u32[]{:S(2)}) collective-permute-start(bf16[96,256]{1,0:T(8,128)(2,1)S(1)} %get-tuple-element.56), channel_id=1, source_target_pairs={{0,192},{32,224},{64,0},{96,32},{128,64},{160,96},{192,128},{224,1... | collective-permute-start | bytes 147464 | tf_op jit(solution)/shard_map/project/ppermute | solution.py:551
  63.7 0.7 collective-permute-start.19
  64.4 0.1 copy.12
  64.7 1.6 copy-done.6
  66.3 0.1 hold.1.refs_4_.refs_6_
  66.5 2.7 %collective-permute-done.18.refs_10_ = bf16[96,256]{1,0:T(8,128)(2,1)S(1)} collective-permute-done((bf16[96,256]{1,0:T(8,128)(2,1)S(1)}, bf16[96,256]{1,0:T(8,128)(2,1)S(1)}, u32[]{:S(2)}, u32[]{:S(2)}) %collective-permute-start.18) | collective-permute-done | bytes 49184 | tf_op jit(solution)/shard_map/project/ppermute | solution.py:551
  69.1 0.4 collective-permute-done.19.refs_11_
  69.5 1.6 settle.1
  71.1 0.9 attend.4
  72.0 16.5 %all_to_all.35.refs_0_ = bf16[32,16,256]{2,1,0:T(8,128)(2,1)S(1)} all-to-all(bf16[32,16,256]{2,1,0:T(8,128)(2,1)S(1)} %get-tuple-element.63), channel_id=1, replica_groups=mesh['grp'=8,'head'=32] {'head'}, dimensions={0} | all-to-all | bytes 524288 | tf_op jit(solution)/shard_map/all_to_all | solution.py:575
  88.6 12.5 %all_to_all.36.refs_7_ = bf16[32,16,256]{2,1,0:T(8,128)(2,1)S(1)} all-to-all(bf16[32,16,256]{2,1,0:T(8,128)(2,1)S(1)} %get-tuple-element.64), channel_id=1, replica_groups=mesh['grp'=8,'head'=32] {'head'}, dimensions={0} | all-to-all | bytes 524288 | tf_op jit(solution)/shard_map/all_to_all | solution.py:579
  101.1 1.7 %attend.5 = (bf16[32,16,256]{2,1,0:T(8,128)(2,1)S(1)}, bf16[16,128]{1,0:T(8,128)(2,1)S(1)}, bf16[16,128]{1,0:T(8,128)(2,1)S(1)}) custom-call(f32[4,16,256]{2,1,0:T(8,128)S(1)} %pad_maximum_fusion.3.refs_0_, bf16[768,128]{1,0:T(8,128)(2,1)S(1)} %get-tuple-element.58.refs_1_, bf16[768,128]{1,0:T(8,128)(2,1)S(1)} %get-tuple-element.59.refs_2_, ...), custom_call_target="tpu_custom_call" | custom-call | tf_op jit(solution)/shard_map/attend/pallas_call | solution.py:457
  102.8 12.5 %all_to_all.37.refs_0_ = bf16[32,16,256]{2,1,0:T(8,128)(2,1)S(1)} all-to-all(bf16[32,16,256]{2,1,0:T(8,128)(2,1)S(1)} %get-tuple-element.67), channel_id=1, replica_groups=mesh['grp'=8,'head'=32] {'head'}, dimensions={0} | all-to-all | bytes 524288 | tf_op jit(solution)/shard_map/all_to_all | solution.py:575
  115.3 12.5 %all_to_all.38.refs_9_ = bf16[32,16,256]{2,1,0:T(8,128)(2,1)S(1)} all-to-all(bf16[32,16,256]{2,1,0:T(8,128)(2,1)S(1)} %get-tuple-element.69), channel_id=1, replica_groups=mesh['grp'=8,'head'=32] {'head'}, dimensions={0} | all-to-all | bytes 524288 | tf_op jit(solution)/shard_map/all_to_all | solution.py:579
  127.8 1.7 %attend.6 = (bf16[32,16,256]{2,1,0:T(8,128)(2,1)S(1)}, bf16[16,128]{1,0:T(8,128)(2,1)S(1)}, bf16[16,128]{1,0:T(8,128)(2,1)S(1)}) custom-call(f32[4,16,256]{2,1,0:T(8,128)S(1)} %pad_maximum_fusion.3.refs_0_, bf16[768,128]{1,0:T(8,128)(2,1)S(1)} %get-tuple-element.58.refs_1_, bf16[768,128]{1,0:T(8,128)(2,1)S(1)} %get-tuple-element.59.refs_2_, ...), custom_call_target="tpu_custom_call" | custom-call | tf_op jit(solution)/shard_map/attend/pallas_call | solution.py:457
  129.5 12.5 %all_to_all.39.refs_0_ = bf16[32,16,256]{2,1,0:T(8,128)(2,1)S(1)} all-to-all(bf16[32,16,256]{2,1,0:T(8,128)(2,1)S(1)} %get-tuple-element.72), channel_id=1, replica_groups=mesh['grp'=8,'head'=32] {'head'}, dimensions={0} | all-to-all | bytes 524288 | tf_op jit(solution)/shard_map/all_to_all | solution.py:575
  142.0 12.5 %all_to_all.40.refs_11_ = bf16[32,16,256]{2,1,0:T(8,128)(2,1)S(1)} all-to-all(bf16[32,16,256]{2,1,0:T(8,128)(2,1)S(1)} %get-tuple-element.74), channel_id=1, replica_groups=mesh['grp'=8,'head'=32] {'head'}, dimensions={0} | all-to-all | bytes 524288 | tf_op jit(solution)/shard_map/all_to_all | solution.py:579
  154.5 1.7 %attend.7 = (bf16[32,16,256]{2,1,0:T(8,128)(2,1)S(1)}, bf16[16,128]{1,0:T(8,128)(2,1)}, bf16[16,128]{1,0:T(8,128)(2,1)}) custom-call(f32[4,16,256]{2,1,0:T(8,128)S(1)} %pad_maximum_fusion.3.refs_0_, bf16[768,128]{1,0:T(8,128)(2,1)S(1)} %get-tuple-element.58.refs_1_, bf16[768,128]{1,0:T(8,128)(2,1)S(1)} %get-tuple-element.59.refs_2_, ...), custom_call_target="tpu_custom_call" | custom-call | tf_op jit(solution)/shard_map/attend/pallas_call | solution.py:457
  156.2 12.5 %all_to_all.41.refs_0_ = bf16[32,16,256]{2,1,0:T(8,128)(2,1)S(1)} all-to-all(bf16[32,16,256]{2,1,0:T(8,128)(2,1)S(1)} %get-tuple-element.75), channel_id=1, replica_groups=mesh['grp'=8,'head'=32] {'head'}, dimensions={0} | all-to-all | bytes 524288 | tf_op jit(solution)/shard_map/all_to_all | solution.py:575
  168.7 0.7 spread.7
  (60 shorter events, 0.8 us)
Async XLA Ops:
  1.9 15.9 %copy-start.10 = (bf16[16,4224]{1,0:T(8,128)(2,1)S(1)}, bf16[16,4224]{1,0:T(8,128)(2,1)}, u32[]{:S(2)}) copy-start(bf16[16,4224]{1,0:T(8,128)(2,1)} %get-tuple-element.41) | copy-start | bytes 405508
  1.9 4.5 %collective-permute-start = (bf16[16,4224]{1,0:T(8,128)(2,1)}, bf16[16,4224]{1,0:T(8,128)(2,1)S(1)}, u32[]{:S(2)}, u32[]{:S(2)}) collective-permute-start(bf16[16,4224]{1,0:T(8,128)(2,1)} %get-tuple-element.42), channel_id=1, source_target_pairs={{0,1},{1,0},{2,3},{3,2},{4,5},{5,4},{6,7},{7,6},{8,9},{9,8},{10,11... | collective-permute-start | bytes 405512 | tf_op jit(solution)/shard_map/rows/ppermute | solution.py:70
  6.4 1.1 copy-start.9
  6.5 6.9 %collective-permute-start.3 = (bf16[32,4224]{1,0:T(8,128)(2,1)S(1)}, bf16[32,4224]{1,0:T(8,128)(2,1)S(1)}, u32[]{:S(2)}, u32[]{:S(2)}) collective-permute-start(bf16[32,4224]{1,0:T(8,128)(2,1)S(1)} %constant_dynamic-update-slice_fusion), channel_id=1, source_target_pairs={{0,6},{1,25},{2,4},{3,27},{4,2},{5,29},{6,0},{7,31},{8,14},{9,17},... | collective-permute-start | bytes 811016 | tf_op jit(solution)/shard_map/rows/ppermute | solution.py:70
  7.5 15.0 %copy-start = (bf16[8192,128]{1,0:T(8,128)(2,1)S(1)}, bf16[8192,128]{1,0:T(8,128)(2,1)}, u32[]{:S(2)}) copy-start(bf16[8192,128]{1,0:T(8,128)(2,1)} %refs_14_.1) | copy-start | bytes 6291460
  7.6 15.0 %copy-start.1 = (bf16[8192,128]{1,0:T(8,128)(2,1)S(1)}, bf16[8192,128]{1,0:T(8,128)(2,1)}, u32[]{:S(2)}) copy-start(bf16[8192,128]{1,0:T(8,128)(2,1)} %refs_15_.1) | copy-start | bytes 6291460
  7.8 10.0 %collective-permute-start.1 = (bf16[32,4224]{1,0:T(8,128)(2,1)S(1)}, bf16[32,4224]{1,0:T(8,128)(2,1)S(1)}, u32[]{:S(2)}, u32[]{:S(2)}) collective-permute-start(bf16[32,4224]{1,0:T(8,128)(2,1)S(1)} %constant_dynamic-update-slice_fusion), channel_id=1, source_target_pairs={{0,2},{1,9},{2,0},{3,11},{4,6},{5,13},{6,4},{7,15},{8,10},{9,1},{1... | collective-permute-start | bytes 811016 | tf_op jit(solution)/shard_map/rows/ppermute | solution.py:70
  7.9 9.9 %collective-permute-start.2 = (bf16[32,4224]{1,0:T(8,128)(2,1)S(1)}, bf16[32,4224]{1,0:T(8,128)(2,1)S(1)}, u32[]{:S(2)}, u32[]{:S(2)}) collective-permute-start(bf16[32,4224]{1,0:T(8,128)(2,1)S(1)} %constant_dynamic-update-slice_fusion), channel_id=1, source_target_pairs={{0,4},{1,17},{2,6},{3,19},{4,0},{5,21},{6,2},{7,23},{8,12},{9,25},... | collective-permute-start | bytes 811016 | tf_op jit(solution)/shard_map/rows/ppermute | solution.py:70
  17.9 16.2 %collective-permute-start.4 = (bf16[64,4224]{1,0:T(8,128)(2,1)S(1)}, bf16[64,4224]{1,0:T(8,128)(2,1)}, u32[]{:S(2)}, u32[]{:S(2)}) collective-permute-start(bf16[64,4224]{1,0:T(8,128)(2,1)S(1)} %pad_maximum_fusion.refs_0_), channel_id=1, source_target_pairs={{0,8},{1,3},{2,10},{3,1},{4,12},{5,7},{6,14},{7,5},{8,0},{9,11},{1... | collective-permute-start | bytes 1622024 | tf_op jit(solution)/shard_map/rows/ppermute | solution.py:70
  18.0 13.9 %collective-permute-start.6 = (bf16[64,4224]{1,0:T(8,128)(2,1)S(1)}, bf16[64,4224]{1,0:T(8,128)(2,1)}, u32[]{:S(2)}, u32[]{:S(2)}) collective-permute-start(bf16[64,4224]{1,0:T(8,128)(2,1)S(1)} %pad_maximum_fusion.refs_0_), channel_id=1, source_target_pairs={{0,24},{1,7},{2,26},{3,5},{4,28},{5,3},{6,30},{7,1},{8,16},{9,15},... | collective-permute-start | bytes 1622024 | tf_op jit(solution)/shard_map/rows/ppermute | solution.py:70
  20.5 7.3 %copy-start.11 = (f32[16,8192]{1,0:T(8,128)S(1)}, f32[16,8192]{1,0:T(8,128)}, u32[]{:S(2)}) copy-start(f32[16,8192]{1,0:T(8,128)} %param.12) | copy-start | bytes 1572868
  20.5 8.2 %copy-start.12 = (f32[8192]{0:T(1024)S(1)}, f32[8192]{0:T(1024)}, u32[]{:S(2)}) copy-start(f32[8192]{0:T(1024)} %param.13) | copy-start | bytes 98308
  20.5 9.0 %copy-start.13 = (s32[8,16]{1,0:T(8,128)S(1)}, s32[8,16]{1,0:T(8,128)}, u32[]{:S(2)}) copy-start(s32[8,16]{1,0:T(8,128)} %param.11) | copy-start | bytes 1540
  20.6 11.8 %collective-permute-start.5 = (bf16[64,4224]{1,0:T(8,128)(2,1)S(1)}, bf16[64,4224]{1,0:T(8,128)(2,1)}, u32[]{:S(2)}, u32[]{:S(2)}) collective-permute-start(bf16[64,4224]{1,0:T(8,128)(2,1)S(1)} %pad_maximum_fusion.1.refs_1_), channel_id=1, source_target_pairs={{0,8},{1,3},{2,10},{3,1},{4,12},{5,7},{6,14},{7,5},{8,0},{9,11},{1... | collective-permute-start | bytes 1622024 | tf_op jit(solution)/shard_map/rows/ppermute | solution.py:70
  21.3 12.9 %collective-permute-start.7 = (bf16[64,4224]{1,0:T(8,128)(2,1)S(1)}, bf16[64,4224]{1,0:T(8,128)(2,1)}, u32[]{:S(2)}, u32[]{:S(2)}) collective-permute-start(bf16[64,4224]{1,0:T(8,128)(2,1)S(1)} %pad_maximum_fusion.1.refs_1_), channel_id=1, source_target_pairs={{0,24},{1,7},{2,26},{3,5},{4,28},{5,3},{6,30},{7,1},{8,16},{9,15},... | collective-permute-start | bytes 1622024 | tf_op jit(solution)/shard_map/rows/ppermute | solution.py:70
  24.0 10.2 %collective-permute-start.8 = (bf16[4096,256]{1,0:T(8,128)(2,1)}, bf16[4096,256]{1,0:T(8,128)(2,1)}, u32[]{:S(2)}, u32[]{:S(2)}) collective-permute-start(bf16[4096,256]{1,0:T(8,128)(2,1)} %other_half.1), channel_id=1, source_target_pairs={{0,1},{1,0},{2,3},{3,2},{4,5},{5,4},{6,7},{7,6},{8,9},{9,8},{10,11... | collective-permute-start | bytes 6291464 | tf_op jit(solution)/shard_map/weights/ppermute | solution.py:70
  28.0 0.8 copy-start.8
  29.6 1.7 copy-start.2
  29.6 1.7 copy-start.7
  29.7 4.1 %copy-start.4 = (bf16[8192,128]{1,0:T(8,128)(2,1)S(1)}, bf16[8192,128]{1,0:T(8,128)(2,1)}, u32[]{:S(2)}) copy-start(bf16[8192,128]{1,0:T(8,128)(2,1)} %refs_13_.3) | copy-start | bytes 6291460
  31.9 8.8 %collective-permute-start.9 = (bf16[64,4224]{1,0:T(8,128)(2,1)}, bf16[64,4224]{1,0:T(8,128)(2,1)S(1)}, u32[]{:S(2)}, u32[]{:S(2)}) collective-permute-start(bf16[64,4224]{1,0:T(8,128)(2,1)} %collective-permute-done.6.refs_4_), channel_id=1, source_target_pairs={{0,8},{1,3},{2,10},{3,1},{4,12},{5,7},{6,14},{7,5},{8,0},{9,11},{1... | collective-permute-start | bytes 1622024 | tf_op jit(solution)/shard_map/rows/ppermute | solution.py:70
  32.4 9.9 %collective-permute-start.10 = (bf16[64,4224]{1,0:T(8,128)(2,1)}, bf16[64,4224]{1,0:T(8,128)(2,1)S(1)}, u32[]{:S(2)}, u32[]{:S(2)}) collective-permute-start(bf16[64,4224]{1,0:T(8,128)(2,1)} %collective-permute-done.5.refs_3_), channel_id=1, source_target_pairs={{0,24},{1,7},{2,26},{3,5},{4,28},{5,3},{6,30},{7,1},{8,16},{9,15},... | collective-permute-start | bytes 1622024 | tf_op jit(solution)/shard_map/rows/ppermute | solution.py:70
  38.1 9.3 %collective-permute-start.11 = (f32[384,256]{1,0:T(8,128)S(1)}, f32[384,256]{1,0:T(8,128)S(1)}, u32[]{:S(2)}, u32[]{:S(2)}) collective-permute-start(f32[384,256]{1,0:T(8,128)S(1)} %get-tuple-element.46), channel_id=1, source_target_pairs={{0,1},{1,0},{2,3},{3,2},{4,5},{5,4},{6,7},{7,6},{8,9},{9,8},{10,11... | collective-permute-start | bytes 1179656 | tf_op jit(solution)/shard_map/project/ppermute | solution.py:70
  43.0 4.4 %collective-permute-start.12 = (f32[128,256]{1,0:T(8,128)S(1)}, f32[128,256]{1,0:T(8,128)S(1)}, u32[]{:S(2)}, u32[]{:S(2)}) collective-permute-start(f32[128,256]{1,0:T(8,128)S(1)} %get-tuple-element.47), channel_id=1, source_target_pairs={{0,1},{1,0},{2,3},{3,2},{4,5},{5,4},{6,7},{7,6},{8,9},{9,8},{10,11... | collective-permute-start | bytes 393224 | tf_op jit(solution)/shard_map/project/ppermute | solution.py:70
  48.8 12.4 %collective-permute-start.13 = (bf16[96,256]{1,0:T(8,128)(2,1)S(1)}, bf16[96,256]{1,0:T(8,128)(2,1)S(1)}, u32[]{:S(2)}, u32[]{:S(2)}) collective-permute-start(bf16[96,256]{1,0:T(8,128)(2,1)S(1)} %get-tuple-element.51), channel_id=1, source_target_pairs={{0,32},{32,64},{64,96},{96,128},{128,160},{160,192},{192,224},{224... | collective-permute-start | bytes 147464 | tf_op jit(solution)/shard_map/project/ppermute | solution.py:551
  48.9 14.7 %collective-permute-start.14 = (bf16[96,256]{1,0:T(8,128)(2,1)S(1)}, bf16[96,256]{1,0:T(8,128)(2,1)S(1)}, u32[]{:S(2)}, u32[]{:S(2)}) collective-permute-start(bf16[96,256]{1,0:T(8,128)(2,1)S(1)} %get-tuple-element.52), channel_id=1, source_target_pairs={{0,64},{32,96},{64,128},{96,160},{128,192},{160,224},{192,0},{224,... | collective-permute-start | bytes 147464 | tf_op jit(solution)/shard_map/project/ppermute | solution.py:551
  52.6 13.8 %collective-permute-start.15 = (bf16[96,256]{1,0:T(8,128)(2,1)S(1)}, bf16[96,256]{1,0:T(8,128)(2,1)S(1)}, u32[]{:S(2)}, u32[]{:S(2)}) collective-permute-start(bf16[96,256]{1,0:T(8,128)(2,1)S(1)} %get-tuple-element.53), channel_id=1, source_target_pairs={{0,96},{32,128},{64,160},{96,192},{128,224},{160,0},{192,32},{224,... | collective-permute-start | bytes 147464 | tf_op jit(solution)/shard_map/project/ppermute | solution.py:551
  56.3 10.1 %collective-permute-start.16 = (bf16[96,256]{1,0:T(8,128)(2,1)S(1)}, bf16[96,256]{1,0:T(8,128)(2,1)S(1)}, u32[]{:S(2)}, u32[]{:S(2)}) collective-permute-start(bf16[96,256]{1,0:T(8,128)(2,1)S(1)} %get-tuple-element.54), channel_id=1, source_target_pairs={{0,128},{32,160},{64,192},{96,224},{128,0},{160,32},{192,64},{224,... | collective-permute-start | bytes 147464 | tf_op jit(solution)/shard_map/project/ppermute | solution.py:551
  56.8 9.7 %collective-permute-start.17 = (bf16[96,256]{1,0:T(8,128)(2,1)S(1)}, bf16[96,256]{1,0:T(8,128)(2,1)S(1)}, u32[]{:S(2)}, u32[]{:S(2)}) collective-permute-start(bf16[96,256]{1,0:T(8,128)(2,1)S(1)} %get-tuple-element.55), channel_id=1, source_target_pairs={{0,160},{32,192},{64,224},{96,0},{128,32},{160,64},{192,96},{224,1... | collective-permute-start | bytes 147464 | tf_op jit(solution)/shard_map/project/ppermute | solution.py:551
  61.3 7.9 %collective-permute-start.18 = (bf16[96,256]{1,0:T(8,128)(2,1)S(1)}, bf16[96,256]{1,0:T(8,128)(2,1)S(1)}, u32[]{:S(2)}, u32[]{:S(2)}) collective-permute-start(bf16[96,256]{1,0:T(8,128)(2,1)S(1)} %get-tuple-element.56), channel_id=1, source_target_pairs={{0,192},{32,224},{64,0},{96,32},{128,64},{160,96},{192,128},{224,1... | collective-permute-start | bytes 147464 | tf_op jit(solution)/shard_map/project/ppermute | solution.py:551
  63.7 5.9 %collective-permute-start.19 = (bf16[96,256]{1,0:T(8,128)(2,1)S(1)}, bf16[96,256]{1,0:T(8,128)(2,1)S(1)}, u32[]{:S(2)}, u32[]{:S(2)}) collective-permute-start(bf16[96,256]{1,0:T(8,128)(2,1)S(1)} %get-tuple-element.57), channel_id=1, source_target_pairs={{0,224},{32,0},{64,32},{96,64},{128,96},{160,128},{192,160},{224,1... | collective-permute-start | bytes 147464 | tf_op jit(solution)/shard_map/project/ppermute | solution.py:551
  64.7 1.6 copy-start.6
  66.2 22.3 %copy-start.5 = (bf16[8192,128]{1,0:T(8,128)(2,1)S(1)}, bf16[8192,128]{1,0:T(8,128)(2,1)}, u32[]{:S(2)}) copy-start(bf16[8192,128]{1,0:T(8,128)(2,1)} %refs_13_.3) | copy-start | bytes 6291460
  66.4 22.2 %copy-start.3 = (bf16[8192,128]{1,0:T(8,128)(2,1)S(1)}, bf16[8192,128]{1,0:T(8,128)(2,1)}, u32[]{:S(2)}) copy-start(bf16[8192,128]{1,0:T(8,128)(2,1)} %refs_15_.1) | copy-start | bytes 6291460

commit v6 on v5

--- a/solution.py
+++ b/solution.py
@@ -138,6 +138,22 @@
         compiler_params=params(4),
         name="other_half",
     )(w_key, w_value, dep)
+
+
+def lines_kernel(kept, got, f1, f2, f3, l0_ref, l1_ref):
+    n = kept.shape[0]
+    for i, (first, second) in enumerate(
+        [(kept[...], got[...])] + [(f[:n, :], f[n:, :]) for f in (f1, f2, f3)]
+    ):
+        l0_ref[i * n : (i + 1) * n, :] = first
+        l1_ref[i * n : (i + 1) * n, :] = second
+
+
+def lines(kept, got, f1, f2, f3):
+    shape = jax.ShapeDtypeStruct((NX * kept.shape[0], kept.shape[1]), kept.dtype)
+    return pl.pallas_call(
+        lines_kernel, out_shape=(shape, shape), compiler_params=params(6), name="lines"
+    )(kept, got, f1, f2, f3)
 
 
 CHUNKS = 4
@@ -502,15 +518,13 @@
 
     core = my_head % 2
     with jax.named_scope("rows"):
-        n = rows_local
         kept, given = norm_split(row_group, prefill_rows, norm_gain)
         got = send(given, CORE)
         start = jnp.concatenate([kept, got])
         f2 = send(start, lane(2, 0))
         f1 = send(start, lane(1, 0))
         f3 = send(start, lane(3, 0))
-        l0 = jnp.concatenate([kept, f1[:n], f2[:n], f3[:n]])
-        l1 = jnp.concatenate([got, f1[n:], f2[n:], f3[n:]])
+        l0, l1 = lines(kept, got, f1, f2, f3)
         s11 = send(l1, lane(0, 1))
         s30 = send(l0, lane(0, 3))
         s10 = send(l0, lane(0, 1))
@@ -553,9 +567,9 @@
         cache_keys, cache_values, bias = settle(edge_row, edge_col, table_high, table_low, arrived)
 
     with jax.named_scope("first"):
-        late_state = after(decode_state, f1)
+        late_state = after(decode_state, got)
         current = lax.dynamic_slice_in_dim(late_state, my_head * share, share, 1)
-        late_gain = after(norm_gain, f1)
+        late_gain = after(norm_gain, got)
         my_gain = lax.dynamic_slice_in_dim(late_gain, my_head * share, share, 0)[None, :]
         inverse = (1.0 / late_gain)[None, :]
         decode_rows = normed(late_state, norm_gain)

time: 170 us -> 166 us (0.976)
  blocking collectives: 91.3 us -> 88.3 us
    all_to_all x4, blocking collectives: 53.9 us -> 51 us  [per_device(): lax.all_to_all(term, 'head', split_axis=0, concat_axis=0, tiled=True)]
    ppermute x13, starting transfers between devices: 20.8 us -> 19 us  [send(): return lax.ppermute(values, 'head', pairs)]
    ppermute x7, starting transfers between devices: 14.8 us -> 16.6 us  [per_device(): arrived.append(lax.ppermute(leaving[hop], 'grp', pairs))]
    unnamed x30 -> x22, local copies, waits for them, and re-layouts: 3.43 us -> 4.22 us
  transfers between devices with their start and end apart: 20 -> 20, of which waited for: 7 -> 7; matrix products, arithmetic and copies ran while one was open for 5% -> 3% of each run, Pallas kernels for 4% -> 3%
where the time goes in v6:
time: 166 us
  blocking collectives  88.3 us (53%)
  starting transfers between devices  35.6 us (21%)
  Pallas kernels  16.3 us (10%)
  waiting for transfers between devices  14.7 us (9%)
  local copies, waits for them, and re-layouts  5.52 us (3%)
  other arithmetic  2.41 us (1%)
    all_to_all x4, blocking collectives, per_device(): lax.all_to_all(term, 'head', split_axis=0, concat_axis=0, tiled=True)  51 us
    all_to_all x3, blocking collectives, per_device(): lax.all_to_all(spreading[0], 'head', split_axis=0, concat_axis=0, tiled=T...  37.4 us
    ppermute x13, starting transfers between devices, send(): return lax.ppermute(values, 'head', pairs)  19 us
    ppermute x7, starting transfers between devices, per_device(): arrived.append(lax.ppermute(leaving[hop], 'grp', pairs))  16.6 us
    ppermute x13, waiting for transfers between devices, send(): return lax.ppermute(values, 'head', pairs)  11.5 us
    pallas_call x4, Pallas kernels, attend(): pl.pallas_call(lambda *refs: attend_kernel(step, *refs), out_shape=(jax.S...  6 us
    unnamed x22, local copies, waits for them, and re-layouts  4.22 us
  transfers between devices with their start and end apart: 20, of which 7 were waited for; matrix products, arithmetic and copies ran while one was open for 3% of the time, Pallas kernels for 3%

profile of v6, /device:TPU:1, one launch (start us, length us, event | category | flops | bytes accessed | tf_op | source)
XLA Modules:
  0.0 165.6 jit_solution(290667488032295531)
XLA Ops:
  0.0 2.1 %norm_split.1 = (bf16[16,4224]{1,0:T(8,128)(2,1)}, bf16[16,4224]{1,0:T(8,128)(2,1)}) custom-call(s32[16]{0:T(128)} %group_ref.1, bf16[16,8192]{1,0:T(8,128)(2,1)} %rows_ref.1, f32[1,8192]{1,0:T(1,128)} %bitcast.34), custom_call_target="tpu_custom_call" | custom-call | tf_op jit(solution)/shard_map/rows/norm_split/pallas_call | solution.py:109
  2.1 3.2 %collective-permute-start = (bf16[16,4224]{1,0:T(8,128)(2,1)}, bf16[16,4224]{1,0:T(8,128)(2,1)S(1)}, u32[]{:S(2)}, u32[]{:S(2)}) collective-permute-start(bf16[16,4224]{1,0:T(8,128)(2,1)} %get-tuple-element.44), channel_id=1, source_target_pairs={{0,1},{1,0},{2,3},{3,2},{4,5},{5,4},{6,7},{7,6},{8,9},{9,8},{10,11... | collective-permute-start | bytes 405512 | tf_op jit(solution)/shard_map/rows/ppermute | solution.py:70
  5.3 0.9 constant_dynamic-update-slice_fusion.1
  6.2 0.3 multiply_cosine_fusion
  6.6 0.1 fusion.refs_2_
  6.7 0.1 subtract_convert_fusion.refs_3_
  6.8 0.1 collective-permute-start.1
  6.9 2.2 %collective-permute-start.2 = (bf16[32,4224]{1,0:T(8,128)(2,1)S(1)}, bf16[32,4224]{1,0:T(8,128)(2,1)S(1)}, u32[]{:S(2)}, u32[]{:S(2)}) collective-permute-start(bf16[32,4224]{1,0:T(8,128)(2,1)S(1)} %constant_dynamic-update-slice_fusion), channel_id=1, source_target_pairs={{0,4},{1,17},{2,6},{3,19},{4,0},{5,21},{6,2},{7,23},{8,12},{9,25},... | collective-permute-start | bytes 811016 | tf_op jit(solution)/shard_map/rows/ppermute | solution.py:70
  9.1 1.7 %collective-permute-start.3 = (bf16[32,4224]{1,0:T(8,128)(2,1)S(1)}, bf16[32,4224]{1,0:T(8,128)(2,1)S(1)}, u32[]{:S(2)}, u32[]{:S(2)}) collective-permute-start(bf16[32,4224]{1,0:T(8,128)(2,1)S(1)} %constant_dynamic-update-slice_fusion), channel_id=1, source_target_pairs={{0,6},{1,25},{2,4},{3,27},{4,2},{5,29},{6,0},{7,31},{8,14},{9,17},... | collective-permute-start | bytes 811016 | tf_op jit(solution)/shard_map/rows/ppermute | solution.py:70
  10.8 0.5 slice.10
  12.0 1.2 multiply_reduce_fusion
  13.2 1.6 copy-done.1
  14.8 0.4 other_half.1
  15.2 1.0 collective-permute-start.8
  16.2 0.1 multiply_convert_fusion
  16.3 0.4 fusion.4.refs_6_
  16.7 0.1 copy-done.2
  16.8 0.4 fusion.5.refs_7_
  17.2 1.6 collective-permute-done.3.f3
  18.9 1.0 collective-permute-start.5
  19.9 1.8 %collective-permute-start.6 = (bf16[64,4224]{1,0:T(8,128)(2,1)S(1)}, bf16[64,4224]{1,0:T(8,128)(2,1)S(1)}, u32[]{:S(2)}, u32[]{:S(2)}) collective-permute-start(bf16[64,4224]{1,0:T(8,128)(2,1)S(1)} %get-tuple-element.45.refs_0_), channel_id=1, source_target_pairs={{0,24},{1,7},{2,26},{3,5},{4,28},{5,3},{6,30},{7,1},{8,16},{9,15},... | collective-permute-start | bytes 1622024 | tf_op jit(solution)/shard_map/rows/ppermute | solution.py:70
  21.8 0.6 collective-permute-start.4
  22.4 0.6 collective-permute-start.7
  23.0 0.4 fusion.3.refs_5_
  23.4 0.5 slice.9
  24.6 0.1 select_reduce_fusion.1
  24.7 5.0 %collective-permute-done.6.refs_4_ = bf16[64,4224]{1,0:T(8,128)(2,1)S(1)} collective-permute-done((bf16[64,4224]{1,0:T(8,128)(2,1)S(1)}, bf16[64,4224]{1,0:T(8,128)(2,1)S(1)}, u32[]{:S(2)}, u32[]{:S(2)}) %collective-permute-start.6) | collective-permute-done | bytes 540704 | tf_op jit(solution)/shard_map/rows/ppermute | solution.py:70
  29.6 1.8 %collective-permute-start.10 = (bf16[64,4224]{1,0:T(8,128)(2,1)S(1)}, bf16[64,4224]{1,0:T(8,128)(2,1)S(1)}, u32[]{:S(2)}, u32[]{:S(2)}) collective-permute-start(bf16[64,4224]{1,0:T(8,128)(2,1)S(1)} %collective-permute-done.5.refs_3_), channel_id=1, source_target_pairs={{0,24},{1,7},{2,26},{3,5},{4,28},{5,3},{6,30},{7,1},{8,16},{9,15},... | collective-permute-start | bytes 1622024 | tf_op jit(solution)/shard_map/rows/ppermute | solution.py:70
  31.4 1.8 %collective-permute-done.4.refs_2_ = bf16[64,4224]{1,0:T(8,128)(2,1)S(1)} collective-permute-done((bf16[64,4224]{1,0:T(8,128)(2,1)S(1)}, bf16[64,4224]{1,0:T(8,128)(2,1)S(1)}, u32[]{:S(2)}, u32[]{:S(2)}) %collective-permute-start.4) | collective-permute-done | bytes 540704 | tf_op jit(solution)/shard_map/rows/ppermute | solution.py:70
  33.3 2.1 %collective-permute-done.7.refs_5_ = bf16[64,4224]{1,0:T(8,128)(2,1)S(1)} collective-permute-done((bf16[64,4224]{1,0:T(8,128)(2,1)S(1)}, bf16[64,4224]{1,0:T(8,128)(2,1)S(1)}, u32[]{:S(2)}, u32[]{:S(2)}) %collective-permute-start.7) | collective-permute-done | bytes 540704 | tf_op jit(solution)/shard_map/rows/ppermute | solution.py:70
  35.4 3.0 %project.1 = (f32[384,256]{1,0:T(8,128)S(1)}, f32[384,256]{1,0:T(8,128)S(1)}, bf16[384,128]{1,0:T(8,128)(2,1)S(1)}, bf16[4096,512]{1,0:T(8,128)(2,1)S(1)}) custom-call(bf16[64,4224]{1,0:T(8,128)(2,1)S(1)} %get-tuple-element.45.refs_0_, bf16[64,4224]{1,0:T(8,128)(2,1)S(1)} %get-tuple-element.46.refs_1_, bf16[64,4224]{1,0:T(8,128)(2,1)S(1)} %collective-permute-done.4.refs_2_, ...), custom_call_target="tpu_custom_call" | custom-call | tf_op jit(solution)/shard_map/project/project/pallas_call | solution.py:220
  38.4 2.5 %collective-permute-start.11 = (f32[384,256]{1,0:T(8,128)S(1)}, f32[384,256]{1,0:T(8,128)S(1)}, u32[]{:S(2)}, u32[]{:S(2)}) collective-permute-start(f32[384,256]{1,0:T(8,128)S(1)} %get-tuple-element.50), channel_id=1, source_target_pairs={{0,1},{1,0},{2,3},{3,2},{4,5},{5,4},{6,7},{7,6},{8,9},{9,8},{10,11... | collective-permute-start | bytes 1179656 | tf_op jit(solution)/shard_map/project/ppermute | solution.py:70
  40.9 0.2 multiply_cosine_fusion.1
  41.1 0.1 select_reduce_fusion
  41.2 0.7 project_last.1
  41.9 2.6 %collective-permute-start.12 = (f32[128,256]{1,0:T(8,128)S(1)}, f32[128,256]{1,0:T(8,128)S(1)}, u32[]{:S(2)}, u32[]{:S(2)}) collective-permute-start(f32[128,256]{1,0:T(8,128)S(1)} %get-tuple-element.51), channel_id=1, source_target_pairs={{0,1},{1,0},{2,3},{3,2},{4,5},{5,4},{6,7},{7,6},{8,9},{9,8},{10,11... | collective-permute-start | bytes 393224 | tf_op jit(solution)/shard_map/project/ppermute | solution.py:70
  44.6 1.0 collective-permute-done.12.refs_3_
  45.5 1.4 finish.1
  47.0 1.7 %collective-permute-start.13 = (bf16[96,256]{1,0:T(8,128)(2,1)S(1)}, bf16[96,256]{1,0:T(8,128)(2,1)S(1)}, u32[]{:S(2)}, u32[]{:S(2)}) collective-permute-start(bf16[96,256]{1,0:T(8,128)(2,1)S(1)} %get-tuple-element.55), channel_id=1, source_target_pairs={{0,32},{32,64},{64,96},{96,128},{128,160},{160,192},{192,224},{224... | collective-permute-start | bytes 147464 | tf_op jit(solution)/shard_map/project/ppermute | solution.py:565
  48.7 3.0 %collective-permute-start.14 = (bf16[96,256]{1,0:T(8,128)(2,1)S(1)}, bf16[96,256]{1,0:T(8,128)(2,1)S(1)}, u32[]{:S(2)}, u32[]{:S(2)}) collective-permute-start(bf16[96,256]{1,0:T(8,128)(2,1)S(1)} %get-tuple-element.56), channel_id=1, source_target_pairs={{0,64},{32,96},{64,128},{96,160},{128,192},{160,224},{192,0},{224,... | collective-permute-start | bytes 147464 | tf_op jit(solution)/shard_map/project/ppermute | solution.py:565
  51.7 0.1 pad_maximum_fusion.1.refs_0_
  51.8 3.8 %collective-permute-start.15 = (bf16[96,256]{1,0:T(8,128)(2,1)S(1)}, bf16[96,256]{1,0:T(8,128)(2,1)S(1)}, u32[]{:S(2)}, u32[]{:S(2)}) collective-permute-start(bf16[96,256]{1,0:T(8,128)(2,1)S(1)} %get-tuple-element.57), channel_id=1, source_target_pairs={{0,96},{32,128},{64,160},{96,192},{128,224},{160,0},{192,32},{224,... | collective-permute-start | bytes 147464 | tf_op jit(solution)/shard_map/project/ppermute | solution.py:565
  55.6 0.6 collective-permute-start.16
  56.1 4.4 %collective-permute-start.17 = (bf16[96,256]{1,0:T(8,128)(2,1)S(1)}, bf16[96,256]{1,0:T(8,128)(2,1)S(1)}, u32[]{:S(2)}, u32[]{:S(2)}) collective-permute-start(bf16[96,256]{1,0:T(8,128)(2,1)S(1)} %get-tuple-element.59), channel_id=1, source_target_pairs={{0,160},{32,192},{64,224},{96,0},{128,32},{160,64},{192,96},{224,1... | collective-permute-start | bytes 147464 | tf_op jit(solution)/shard_map/project/ppermute | solution.py:565
  60.5 2.4 %collective-permute-start.18 = (bf16[96,256]{1,0:T(8,128)(2,1)S(1)}, bf16[96,256]{1,0:T(8,128)(2,1)S(1)}, u32[]{:S(2)}, u32[]{:S(2)}) collective-permute-start(bf16[96,256]{1,0:T(8,128)(2,1)S(1)} %get-tuple-element.60), channel_id=1, source_target_pairs={{0,192},{32,224},{64,0},{96,32},{128,64},{160,96},{192,128},{224,1... | collective-permute-start | bytes 147464 | tf_op jit(solution)/shard_map/project/ppermute | solution.py:565
  62.9 0.7 collective-permute-start.19
  63.7 0.1 copy.12
  63.8 1.6 copy-done.6
  65.4 0.1 hold.1.refs_4_.refs_6_
  65.6 2.8 %collective-permute-done.18.refs_10_ = bf16[96,256]{1,0:T(8,128)(2,1)S(1)} collective-permute-done((bf16[96,256]{1,0:T(8,128)(2,1)S(1)}, bf16[96,256]{1,0:T(8,128)(2,1)S(1)}, u32[]{:S(2)}, u32[]{:S(2)}) %collective-permute-start.18) | collective-permute-done | bytes 49184 | tf_op jit(solution)/shard_map/project/ppermute | solution.py:565
  68.4 0.4 collective-permute-done.19.refs_11_
  68.8 1.6 settle.1
  70.4 0.9 attend.4
  71.3 13.6 %all_to_all.35.refs_0_ = bf16[32,16,256]{2,1,0:T(8,128)(2,1)S(1)} all-to-all(bf16[32,16,256]{2,1,0:T(8,128)(2,1)S(1)} %get-tuple-element.67), channel_id=1, replica_groups=mesh['grp'=8,'head'=32] {'head'}, dimensions={0} | all-to-all | bytes 524288 | tf_op jit(solution)/shard_map/all_to_all | solution.py:589
  84.9 12.5 %all_to_all.36.refs_7_ = bf16[32,16,256]{2,1,0:T(8,128)(2,1)S(1)} all-to-all(bf16[32,16,256]{2,1,0:T(8,128)(2,1)S(1)} %get-tuple-element.68), channel_id=1, replica_groups=mesh['grp'=8,'head'=32] {'head'}, dimensions={0} | all-to-all | bytes 524288 | tf_op jit(solution)/shard_map/all_to_all | solution.py:593
  97.4 1.7 %attend.5 = (bf16[32,16,256]{2,1,0:T(8,128)(2,1)S(1)}, bf16[16,128]{1,0:T(8,128)(2,1)S(1)}, bf16[16,128]{1,0:T(8,128)(2,1)S(1)}) custom-call(f32[4,16,256]{2,1,0:T(8,128)S(1)} %pad_maximum_fusion.1.refs_0_, bf16[768,128]{1,0:T(8,128)(2,1)S(1)} %get-tuple-element.62.refs_1_, bf16[768,128]{1,0:T(8,128)(2,1)S(1)} %get-tuple-element.63.refs_2_, ...), custom_call_target="tpu_custom_call" | custom-call | tf_op jit(solution)/shard_map/attend/pallas_call | solution.py:473
  99.1 12.5 %all_to_all.37.refs_0_ = bf16[32,16,256]{2,1,0:T(8,128)(2,1)S(1)} all-to-all(bf16[32,16,256]{2,1,0:T(8,128)(2,1)S(1)} %get-tuple-element.71), channel_id=1, replica_groups=mesh['grp'=8,'head'=32] {'head'}, dimensions={0} | all-to-all | bytes 524288 | tf_op jit(solution)/shard_map/all_to_all | solution.py:589
  111.6 12.5 %all_to_all.38.refs_9_ = bf16[32,16,256]{2,1,0:T(8,128)(2,1)S(1)} all-to-all(bf16[32,16,256]{2,1,0:T(8,128)(2,1)S(1)} %get-tuple-element.73), channel_id=1, replica_groups=mesh['grp'=8,'head'=32] {'head'}, dimensions={0} | all-to-all | bytes 524288 | tf_op jit(solution)/shard_map/all_to_all | solution.py:593
  124.1 1.7 %attend.6 = (bf16[32,16,256]{2,1,0:T(8,128)(2,1)S(1)}, bf16[16,128]{1,0:T(8,128)(2,1)S(1)}, bf16[16,128]{1,0:T(8,128)(2,1)S(1)}) custom-call(f32[4,16,256]{2,1,0:T(8,128)S(1)} %pad_maximum_fusion.1.refs_0_, bf16[768,128]{1,0:T(8,128)(2,1)S(1)} %get-tuple-element.62.refs_1_, bf16[768,128]{1,0:T(8,128)(2,1)S(1)} %get-tuple-element.63.refs_2_, ...), custom_call_target="tpu_custom_call" | custom-call | tf_op jit(solution)/shard_map/attend/pallas_call | solution.py:473
  125.8 12.5 %all_to_all.39.refs_0_ = bf16[32,16,256]{2,1,0:T(8,128)(2,1)S(1)} all-to-all(bf16[32,16,256]{2,1,0:T(8,128)(2,1)S(1)} %get-tuple-element.76), channel_id=1, replica_groups=mesh['grp'=8,'head'=32] {'head'}, dimensions={0} | all-to-all | bytes 524288 | tf_op jit(solution)/shard_map/all_to_all | solution.py:589
  138.3 12.5 %all_to_all.40.refs_11_ = bf16[32,16,256]{2,1,0:T(8,128)(2,1)S(1)} all-to-all(bf16[32,16,256]{2,1,0:T(8,128)(2,1)S(1)} %get-tuple-element.78), channel_id=1, replica_groups=mesh['grp'=8,'head'=32] {'head'}, dimensions={0} | all-to-all | bytes 524288 | tf_op jit(solution)/shard_map/all_to_all | solution.py:593
  150.8 1.7 %attend.7 = (bf16[32,16,256]{2,1,0:T(8,128)(2,1)S(1)}, bf16[16,128]{1,0:T(8,128)(2,1)}, bf16[16,128]{1,0:T(8,128)(2,1)}) custom-call(f32[4,16,256]{2,1,0:T(8,128)S(1)} %pad_maximum_fusion.1.refs_0_, bf16[768,128]{1,0:T(8,128)(2,1)S(1)} %get-tuple-element.62.refs_1_, bf16[768,128]{1,0:T(8,128)(2,1)S(1)} %get-tuple-element.63.refs_2_, ...), custom_call_target="tpu_custom_call" | custom-call | tf_op jit(solution)/shard_map/attend/pallas_call | solution.py:473
  152.5 12.5 %all_to_all.41.refs_0_ = bf16[32,16,256]{2,1,0:T(8,128)(2,1)S(1)} all-to-all(bf16[32,16,256]{2,1,0:T(8,128)(2,1)S(1)} %get-tuple-element.79), channel_id=1, replica_groups=mesh['grp'=8,'head'=32] {'head'}, dimensions={0} | all-to-all | bytes 524288 | tf_op jit(solution)/shard_map/all_to_all | solution.py:589
  164.9 0.7 spread.7
  (49 shorter events, 0.6 us)
Async XLA Ops:
  0.0 13.2 %copy-start = (bf16[8192,128]{1,0:T(8,128)(2,1)S(1)}, bf16[8192,128]{1,0:T(8,128)(2,1)}, u32[]{:S(2)}) copy-start(bf16[8192,128]{1,0:T(8,128)(2,1)} %refs_14_.1) | copy-start | bytes 6291460
  2.1 4.7 %collective-permute-start = (bf16[16,4224]{1,0:T(8,128)(2,1)}, bf16[16,4224]{1,0:T(8,128)(2,1)S(1)}, u32[]{:S(2)}, u32[]{:S(2)}) collective-permute-start(bf16[16,4224]{1,0:T(8,128)(2,1)} %get-tuple-element.44), channel_id=1, source_target_pairs={{0,1},{1,0},{2,3},{3,2},{4,5},{5,4},{6,7},{7,6},{8,9},{9,8},{10,11... | collective-permute-start | bytes 405512 | tf_op jit(solution)/shard_map/rows/ppermute | solution.py:70
  6.8 6.3 %collective-permute-start.1 = (bf16[32,4224]{1,0:T(8,128)(2,1)S(1)}, bf16[32,4224]{1,0:T(8,128)(2,1)S(1)}, u32[]{:S(2)}, u32[]{:S(2)}) collective-permute-start(bf16[32,4224]{1,0:T(8,128)(2,1)S(1)} %constant_dynamic-update-slice_fusion), channel_id=1, source_target_pairs={{0,2},{1,9},{2,0},{3,11},{4,6},{5,13},{6,4},{7,15},{8,10},{9,1},{1... | collective-permute-start | bytes 811016 | tf_op jit(solution)/shard_map/rows/ppermute | solution.py:70
  6.9 10.3 %collective-permute-start.2 = (bf16[32,4224]{1,0:T(8,128)(2,1)S(1)}, bf16[32,4224]{1,0:T(8,128)(2,1)S(1)}, u32[]{:S(2)}, u32[]{:S(2)}) collective-permute-start(bf16[32,4224]{1,0:T(8,128)(2,1)S(1)} %constant_dynamic-update-slice_fusion), channel_id=1, source_target_pairs={{0,4},{1,17},{2,6},{3,19},{4,0},{5,21},{6,2},{7,23},{8,12},{9,25},... | collective-permute-start | bytes 811016 | tf_op jit(solution)/shard_map/rows/ppermute | solution.py:70
  9.1 9.7 %collective-permute-start.3 = (bf16[32,4224]{1,0:T(8,128)(2,1)S(1)}, bf16[32,4224]{1,0:T(8,128)(2,1)S(1)}, u32[]{:S(2)}, u32[]{:S(2)}) collective-permute-start(bf16[32,4224]{1,0:T(8,128)(2,1)S(1)} %constant_dynamic-update-slice_fusion), channel_id=1, source_target_pairs={{0,6},{1,25},{2,4},{3,27},{4,2},{5,29},{6,0},{7,31},{8,14},{9,17},... | collective-permute-start | bytes 811016 | tf_op jit(solution)/shard_map/rows/ppermute | solution.py:70
  13.2 1.6 copy-start.1
  14.8 1.4 copy-start.8
  15.2 1.6 copy-start.2
  15.2 20.2 %collective-permute-start.8 = (bf16[4096,256]{1,0:T(8,128)(2,1)S(1)}, bf16[4096,256]{1,0:T(8,128)(2,1)S(1)}, u32[]{:S(2)}, u32[]{:S(2)}) collective-permute-start(bf16[4096,256]{1,0:T(8,128)(2,1)S(1)} %other_half.1), channel_id=1, source_target_pairs={{0,1},{1,0},{2,3},{3,2},{4,5},{5,4},{6,7},{7,6},{8,9},{9,8},{10,11... | collective-permute-start | bytes 6291464 | tf_op jit(solution)/shard_map/weights/ppermute | solution.py:70
  16.3 2.5 %copy-start.7 = (bf16[16,4224]{1,0:T(8,128)(2,1)S(1)}, bf16[16,4224]{1,0:T(8,128)(2,1)}, u32[]{:S(2)}) copy-start(bf16[16,4224]{1,0:T(8,128)(2,1)} %get-tuple-element.43.kept) | copy-start | bytes 405508
  16.8 6.2 %copy-start.4 = (bf16[8192,128]{1,0:T(8,128)(2,1)S(1)}, bf16[8192,128]{1,0:T(8,128)(2,1)}, u32[]{:S(2)}) copy-start(bf16[8192,128]{1,0:T(8,128)(2,1)} %refs_13_.3) | copy-start | bytes 6291460
  17.2 7.4 %copy-start.9 = (s32[8,16]{1,0:T(8,128)S(1)}, s32[8,16]{1,0:T(8,128)}, u32[]{:S(2)}) copy-start(s32[8,16]{1,0:T(8,128)} %param.11) | copy-start | bytes 1540
  18.9 10.7 %collective-permute-start.5 = (bf16[64,4224]{1,0:T(8,128)(2,1)S(1)}, bf16[64,4224]{1,0:T(8,128)(2,1)S(1)}, u32[]{:S(2)}, u32[]{:S(2)}) collective-permute-start(bf16[64,4224]{1,0:T(8,128)(2,1)S(1)} %get-tuple-element.46.refs_1_), channel_id=1, source_target_pairs={{0,8},{1,3},{2,10},{3,1},{4,12},{5,7},{6,14},{7,5},{8,0},{9,11},{1... | collective-permute-start | bytes 1622024 | tf_op jit(solution)/shard_map/rows/ppermute | solution.py:70
  19.9 9.7 %collective-permute-start.6 = (bf16[64,4224]{1,0:T(8,128)(2,1)S(1)}, bf16[64,4224]{1,0:T(8,128)(2,1)S(1)}, u32[]{:S(2)}, u32[]{:S(2)}) collective-permute-start(bf16[64,4224]{1,0:T(8,128)(2,1)S(1)} %get-tuple-element.45.refs_0_), channel_id=1, source_target_pairs={{0,24},{1,7},{2,26},{3,5},{4,28},{5,3},{6,30},{7,1},{8,16},{9,15},... | collective-permute-start | bytes 1622024 | tf_op jit(solution)/shard_map/rows/ppermute | solution.py:70
  21.8 11.5 %collective-permute-start.4 = (bf16[64,4224]{1,0:T(8,128)(2,1)S(1)}, bf16[64,4224]{1,0:T(8,128)(2,1)S(1)}, u32[]{:S(2)}, u32[]{:S(2)}) collective-permute-start(bf16[64,4224]{1,0:T(8,128)(2,1)S(1)} %get-tuple-element.45.refs_0_), channel_id=1, source_target_pairs={{0,8},{1,3},{2,10},{3,1},{4,12},{5,7},{6,14},{7,5},{8,0},{9,11},{1... | collective-permute-start | bytes 1622024 | tf_op jit(solution)/shard_map/rows/ppermute | solution.py:70
  22.4 13.0 %collective-permute-start.7 = (bf16[64,4224]{1,0:T(8,128)(2,1)S(1)}, bf16[64,4224]{1,0:T(8,128)(2,1)S(1)}, u32[]{:S(2)}, u32[]{:S(2)}) collective-permute-start(bf16[64,4224]{1,0:T(8,128)(2,1)S(1)} %get-tuple-element.46.refs_1_), channel_id=1, source_target_pairs={{0,24},{1,7},{2,26},{3,5},{4,28},{5,3},{6,30},{7,1},{8,16},{9,15},... | collective-permute-start | bytes 1622024 | tf_op jit(solution)/shard_map/rows/ppermute | solution.py:70
  29.6 11.6 %collective-permute-start.9 = (bf16[64,4224]{1,0:T(8,128)(2,1)S(1)}, bf16[64,4224]{1,0:T(8,128)(2,1)S(1)}, u32[]{:S(2)}, u32[]{:S(2)}) collective-permute-start(bf16[64,4224]{1,0:T(8,128)(2,1)S(1)} %collective-permute-done.6.refs_4_), channel_id=1, source_target_pairs={{0,8},{1,3},{2,10},{3,1},{4,12},{5,7},{6,14},{7,5},{8,0},{9,11},{1... | collective-permute-start | bytes 1622024 | tf_op jit(solution)/shard_map/rows/ppermute | solution.py:70
  29.6 11.6 %collective-permute-start.10 = (bf16[64,4224]{1,0:T(8,128)(2,1)S(1)}, bf16[64,4224]{1,0:T(8,128)(2,1)S(1)}, u32[]{:S(2)}, u32[]{:S(2)}) collective-permute-start(bf16[64,4224]{1,0:T(8,128)(2,1)S(1)} %collective-permute-done.5.refs_3_), channel_id=1, source_target_pairs={{0,24},{1,7},{2,26},{3,5},{4,28},{5,3},{6,30},{7,1},{8,16},{9,15},... | collective-permute-start | bytes 1622024 | tf_op jit(solution)/shard_map/rows/ppermute | solution.py:70
  38.4 7.1 %collective-permute-start.11 = (f32[384,256]{1,0:T(8,128)S(1)}, f32[384,256]{1,0:T(8,128)S(1)}, u32[]{:S(2)}, u32[]{:S(2)}) collective-permute-start(f32[384,256]{1,0:T(8,128)S(1)} %get-tuple-element.50), channel_id=1, source_target_pairs={{0,1},{1,0},{2,3},{3,2},{4,5},{5,4},{6,7},{7,6},{8,9},{9,8},{10,11... | collective-permute-start | bytes 1179656 | tf_op jit(solution)/shard_map/project/ppermute | solution.py:70
  41.9 3.6 %collective-permute-start.12 = (f32[128,256]{1,0:T(8,128)S(1)}, f32[128,256]{1,0:T(8,128)S(1)}, u32[]{:S(2)}, u32[]{:S(2)}) collective-permute-start(f32[128,256]{1,0:T(8,128)S(1)} %get-tuple-element.51), channel_id=1, source_target_pairs={{0,1},{1,0},{2,3},{3,2},{4,5},{5,4},{6,7},{7,6},{8,9},{9,8},{10,11... | collective-permute-start | bytes 393224 | tf_op jit(solution)/shard_map/project/ppermute | solution.py:70
  47.0 13.6 %collective-permute-start.13 = (bf16[96,256]{1,0:T(8,128)(2,1)S(1)}, bf16[96,256]{1,0:T(8,128)(2,1)S(1)}, u32[]{:S(2)}, u32[]{:S(2)}) collective-permute-start(bf16[96,256]{1,0:T(8,128)(2,1)S(1)} %get-tuple-element.55), channel_id=1, source_target_pairs={{0,32},{32,64},{64,96},{96,128},{128,160},{160,192},{192,224},{224... | collective-permute-start | bytes 147464 | tf_op jit(solution)/shard_map/project/ppermute | solution.py:565
  48.7 14.2 %collective-permute-start.14 = (bf16[96,256]{1,0:T(8,128)(2,1)S(1)}, bf16[96,256]{1,0:T(8,128)(2,1)S(1)}, u32[]{:S(2)}, u32[]{:S(2)}) collective-permute-start(bf16[96,256]{1,0:T(8,128)(2,1)S(1)} %get-tuple-element.56), channel_id=1, source_target_pairs={{0,64},{32,96},{64,128},{96,160},{128,192},{160,224},{192,0},{224,... | collective-permute-start | bytes 147464 | tf_op jit(solution)/shard_map/project/ppermute | solution.py:565
  51.8 13.8 %collective-permute-start.15 = (bf16[96,256]{1,0:T(8,128)(2,1)S(1)}, bf16[96,256]{1,0:T(8,128)(2,1)S(1)}, u32[]{:S(2)}, u32[]{:S(2)}) collective-permute-start(bf16[96,256]{1,0:T(8,128)(2,1)S(1)} %get-tuple-element.57), channel_id=1, source_target_pairs={{0,96},{32,128},{64,160},{96,192},{128,224},{160,0},{192,32},{224,... | collective-permute-start | bytes 147464 | tf_op jit(solution)/shard_map/project/ppermute | solution.py:565
  55.6 10.0 %collective-permute-start.16 = (bf16[96,256]{1,0:T(8,128)(2,1)S(1)}, bf16[96,256]{1,0:T(8,128)(2,1)S(1)}, u32[]{:S(2)}, u32[]{:S(2)}) collective-permute-start(bf16[96,256]{1,0:T(8,128)(2,1)S(1)} %get-tuple-element.58), channel_id=1, source_target_pairs={{0,128},{32,160},{64,192},{96,224},{128,0},{160,32},{192,64},{224,... | collective-permute-start | bytes 147464 | tf_op jit(solution)/shard_map/project/ppermute | solution.py:565
  56.1 9.5 %collective-permute-start.17 = (bf16[96,256]{1,0:T(8,128)(2,1)S(1)}, bf16[96,256]{1,0:T(8,128)(2,1)S(1)}, u32[]{:S(2)}, u32[]{:S(2)}) collective-permute-start(bf16[96,256]{1,0:T(8,128)(2,1)S(1)} %get-tuple-element.59), channel_id=1, source_target_pairs={{0,160},{32,192},{64,224},{96,0},{128,32},{160,64},{192,96},{224,1... | collective-permute-start | bytes 147464 | tf_op jit(solution)/shard_map/project/ppermute | solution.py:565
  60.5 7.9 %collective-permute-start.18 = (bf16[96,256]{1,0:T(8,128)(2,1)S(1)}, bf16[96,256]{1,0:T(8,128)(2,1)S(1)}, u32[]{:S(2)}, u32[]{:S(2)}) collective-permute-start(bf16[96,256]{1,0:T(8,128)(2,1)S(1)} %get-tuple-element.60), channel_id=1, source_target_pairs={{0,192},{32,224},{64,0},{96,32},{128,64},{160,96},{192,128},{224,1... | collective-permute-start | bytes 147464 | tf_op jit(solution)/shard_map/project/ppermute | solution.py:565
  62.9 5.9 %collective-permute-start.19 = (bf16[96,256]{1,0:T(8,128)(2,1)S(1)}, bf16[96,256]{1,0:T(8,128)(2,1)S(1)}, u32[]{:S(2)}, u32[]{:S(2)}) collective-permute-start(bf16[96,256]{1,0:T(8,128)(2,1)S(1)} %get-tuple-element.61), channel_id=1, source_target_pairs={{0,224},{32,0},{64,32},{96,64},{128,96},{160,128},{192,160},{224,1... | collective-permute-start | bytes 147464 | tf_op jit(solution)/shard_map/project/ppermute | solution.py:565
  63.8 1.6 copy-start.6
  65.4 19.4 %copy-start.5 = (bf16[8192,128]{1,0:T(8,128)(2,1)S(1)}, bf16[8192,128]{1,0:T(8,128)(2,1)}, u32[]{:S(2)}) copy-start(bf16[8192,128]{1,0:T(8,128)(2,1)} %refs_13_.3) | copy-start | bytes 6291460
  65.6 19.3 %copy-start.3 = (bf16[8192,128]{1,0:T(8,128)(2,1)S(1)}, bf16[8192,128]{1,0:T(8,128)(2,1)}, u32[]{:S(2)}) copy-start(bf16[8192,128]{1,0:T(8,128)(2,1)} %refs_15_.1) | copy-start | bytes 6291460

commit v7 on v5

--- a/solution.py
+++ b/solution.py
@@ -42,8 +42,6 @@
 
 NX = 4
 NY = 4
-HELD = ((0, 0), (0, 1), (1, 0), (1, 1), (3, 0), (3, 1), (2, 0), (2, 1))
-EARLY = 6
 EMPTY = 1e30
 
 
@@ -78,9 +76,8 @@
     return pltpu.CompilerParams(vmem_limit_bytes=mib * 1024 * 1024)
 
 
-def norm_split_kernel(group_ref, rows_ref, gain_ref, kept_ref, given_ref):
+def norm_kernel(group_ref, rows_ref, gain_ref, out_ref):
     n, half = rows_ref.shape[0], rows_ref.shape[1] // 2
-    core = lax.rem(lax.axis_index("head"), 2)
     rows = rows_ref[...].astype(jnp.float32)
     factor = lax.rsqrt(jnp.mean(rows * rows, axis=1, keepdims=True) + EPSILON)
     result = (rows * factor * gain_ref[...]).astype(jnp.bfloat16)
@@ -89,187 +86,177 @@
     for j in range(n):
         ids = jnp.where(row == j, group_ref[j], ids)
     ids = ids.astype(jnp.float32).astype(jnp.bfloat16)
-    kept_ref[:, half:] = ids
-    given_ref[:, half:] = ids
-
-    @pl.when(core == 0)
-    def _():
-        kept_ref[:, :half] = result[:, :half]
-        given_ref[:, :half] = result[:, half:]
-
-    @pl.when(core == 1)
-    def _():
-        kept_ref[:, :half] = result[:, half:]
-        given_ref[:, :half] = result[:, :half]
-
-
-def norm_split(groups, rows, gain):
-    shape = jax.ShapeDtypeStruct((rows.shape[0], rows.shape[1] // 2 + HD), jnp.bfloat16)
+    for side in range(2):
+        out_ref[side * n : (side + 1) * n, :half] = result[:, side * half : (side + 1) * half]
+        out_ref[side * n : (side + 1) * n, half:] = ids
+
+
+def norm_rows(groups, rows, gain):
+    n, width = rows.shape
     whole = pl.BlockSpec(memory_space=pltpu.VMEM)
     return pl.pallas_call(
-        norm_split_kernel,
-        out_shape=(shape, shape),
+        norm_kernel,
+        out_shape=jax.ShapeDtypeStruct((2 * n, width // 2 + HD), jnp.bfloat16),
         in_specs=[pl.BlockSpec(memory_space=pltpu.SMEM), whole, whole],
         compiler_params=params(56),
-        name="norm_split",
+        name="norm_rows",
     )(groups, rows, gain.reshape(1, -1))
 
 
-def other_half_kernel(key_ref, value_ref, dep_ref, out_ref, sems):
-    half = out_ref.shape[0]
-    core = lax.rem(lax.axis_index("head"), 2)
-    rows = pl.ds(pl.multiple_of((1 - core) * half, half), half)
-    one = pltpu.make_async_copy(key_ref.at[rows], out_ref.at[:, :HD], sems.at[0])
-    two = pltpu.make_async_copy(value_ref.at[rows], out_ref.at[:, HD:], sems.at[1])
-    one.start()
-    two.start()
-    one.wait()
-    two.wait()
-
-
-def other_half(w_key, w_value, dep):
-    anywhere = pl.BlockSpec(memory_space=pl.ANY)
-    return pl.pallas_call(
-        other_half_kernel,
-        out_shape=jax.ShapeDtypeStruct((w_key.shape[0] // 2, 2 * HD), jnp.bfloat16),
-        in_specs=[anywhere] * 3,
-        out_specs=anywhere,
-        scratch_shapes=[pltpu.SemaphoreType.DMA((2,))],
-        compiler_params=params(4),
-        name="other_half",
-    )(w_key, w_value, dep)
-
-
-CHUNKS = 4
+def lines_kernel(start, f1, f2, f3, *refs):
+    l0_ref, l1_ref = refs[-2:]
+    n = start.shape[0] // 2
+    for i, f in enumerate((start, f1, f2, f3)):
+        l0_ref[i * n : (i + 1) * n, :] = f[:n, :]
+        l1_ref[i * n : (i + 1) * n, :] = f[n:, :]
+
+
+def lines(start, f1, f2, f3, *deps):
+    shape = jax.ShapeDtypeStruct((NX * start.shape[0] // 2, start.shape[1]), start.dtype)
+    return pl.pallas_call(
+        lines_kernel, out_shape=(shape, shape), compiler_params=params(6), name="lines"
+    )(start, f1, f2, f3, *deps)
+
+
+CHUNKS = 8
 
 
 def project_kernel(count, *refs):
-    pieces = refs[:count]
-    key_ref, value_ref, their_ref, own_ref, other_ref, ids_ref, w, x, piece_sems, weight_sems = refs[
-        count:
-    ]
+    pieces = refs[: 2 * count]
+    weights = refs[2 * count : 2 * count + 4]
+    own_ref, other_ref, ids_ref, w, x, total, piece_sems, weight_sems = refs[2 * count + 4 :]
     size = pieces[0].shape[0]
-    half = w.shape[0]
-    depth = half // CHUNKS
-    core = lax.rem(lax.axis_index("head"), 2)
+    rows = count * size
+    depth = w.shape[0] // CHUNKS
+    half = w.shape[0] // 2
     loads = []
     for k in range(CHUNKS):
-        mine = pl.ds(pl.multiple_of(core * half + k * depth, depth), depth)
         here = slice(k * depth, (k + 1) * depth)
         loads.append(
             [
-                pltpu.make_async_copy(key_ref.at[mine], w.at[here, :HD], weight_sems.at[k, 0]),
                 pltpu.make_async_copy(
-                    value_ref.at[mine], w.at[here, HD : 2 * HD], weight_sems.at[k, 1]
-                ),
-                pltpu.make_async_copy(
-                    their_ref.at[here], w.at[here, 2 * HD :], weight_sems.at[k, 2]
-                ),
+                    weight.at[here], w.at[here, i * HD : (i + 1) * HD], weight_sems.at[k, i]
+                )
+                for i, weight in enumerate(weights)
             ]
         )
-    rows = [
+    fetches = [
         pltpu.make_async_copy(p, x.at[i * size : (i + 1) * size], piece_sems.at[i])
         for i, p in enumerate(pieces)
     ]
     for load in loads[0]:
         load.start()
-    for row in rows:
-        row.start()
+    for fetch in fetches:
+        fetch.start()
     for k in range(1, CHUNKS):
         for load in loads[k]:
             load.start()
-    for row in rows:
-        row.wait()
-    ids_ref[...] = x[:, half:]
+    for fetch in fetches[:count]:
+        fetch.wait()
     for k in range(CHUNKS):
+        if k == CHUNKS // 2:
+            for fetch in fetches[count:]:
+                fetch.wait()
         for load in loads[k]:
             load.wait()
         here = slice(k * depth, (k + 1) * depth)
-        term = jnp.dot(x[:, here], w[here, :], preferred_element_type=jnp.float32)
+        side = 2 * k // CHUNKS
+        columns = slice(k * depth - side * half, (k + 1) * depth - side * half)
+        term = jnp.dot(
+            x[side * rows : (side + 1) * rows, columns], w[here, :], preferred_element_type=jnp.float32
+        )
         if k == 0:
-            own_ref[...] = term[:, : 2 * HD]
-            other_ref[...] = term[:, 2 * HD :]
+            total[...] = term
         else:
-            own_ref[...] += term[:, : 2 * HD]
-            other_ref[...] += term[:, 2 * HD :]
-
-
-def project(pieces, w_key, w_value, their_half):
-    count = len(pieces)
-    size, wide = pieces[0].shape
-    half = wide - HD
-    rows = count * size
-    anywhere = pl.BlockSpec(memory_space=pl.ANY)
-    shape = jax.ShapeDtypeStruct((rows, 2 * HD), jnp.float32)
+            total[...] += term
+    ids_ref[...] = x[:rows, half:]
+    own_ref[...] = total[:, : 2 * HD].astype(jnp.bfloat16)
+    other_ref[:, : 2 * HD] = total[:, 2 * HD :].astype(jnp.bfloat16)
+    other_ref[:, 2 * HD :] = x[:rows, half:]
+
+
+def projected_shapes(rows):
+    return (
+        jax.ShapeDtypeStruct((rows, 2 * HD), jnp.bfloat16),
+        jax.ShapeDtypeStruct((rows, 3 * HD), jnp.bfloat16),
+        jax.ShapeDtypeStruct((rows, HD), jnp.bfloat16),
+    )
+
+
+def project(lows, highs, weights):
+    count = len(lows)
+    size, wide = lows[0].shape
+    rows, width = count * size, 2 * (wide - HD)
     return pl.pallas_call(
         lambda *refs: project_kernel(count, *refs),
-        out_shape=(
-            shape,
-            shape,
-            jax.ShapeDtypeStruct((rows, HD), jnp.bfloat16),
-            jax.ShapeDtypeStruct((half, 4 * HD), jnp.bfloat16),
-        ),
-        in_specs=[anywhere] * (count + 3),
+        out_shape=projected_shapes(rows)
+        + (jax.ShapeDtypeStruct((width, 4 * HD), jnp.bfloat16),),
+        in_specs=[pl.BlockSpec(memory_space=pl.ANY)] * (2 * count + 4),
         scratch_shapes=[
-            pltpu.VMEM((rows, wide), jnp.bfloat16),
-            pltpu.SemaphoreType.DMA((count,)),
-            pltpu.SemaphoreType.DMA((CHUNKS, 3)),
+            pltpu.VMEM((2 * rows, wide), jnp.bfloat16),
+            pltpu.VMEM((rows, 4 * HD), jnp.float32),
+            pltpu.SemaphoreType.DMA((2 * count,)),
+            pltpu.SemaphoreType.DMA((CHUNKS, 4)),
         ],
-        compiler_params=params(14),
+        compiler_params=params(18),
         name="project",
-    )(*pieces, w_key, w_value, their_half)
-
-
-def project_last_kernel(first, second, w, own_ref, other_ref, ids_ref):
-    n, half = first.shape[0], w.shape[0]
-    x = jnp.concatenate([first[...], second[...]], axis=0)
-    ids_ref[...] = x[:, half:]
-    term = jnp.dot(x[:, :half], w[...], preferred_element_type=jnp.float32)
-    own_ref[...] = term[:, : 2 * HD]
-    other_ref[...] = term[:, 2 * HD :]
-
-
-def project_last(first, second, weights):
-    rows = 2 * first.shape[0]
-    shape = jax.ShapeDtypeStruct((rows, 2 * HD), jnp.float32)
-    return pl.pallas_call(
-        project_last_kernel,
-        out_shape=(shape, shape, jax.ShapeDtypeStruct((rows, HD), jnp.bfloat16)),
+    )(*lows, *highs, *weights)
+
+
+def project_low_kernel(low, w, total_ref):
+    half = w.shape[0] // 2
+    total_ref[...] = jnp.dot(low[:, :half], w[:half, :], preferred_element_type=jnp.float32)
+
+
+def project_high_kernel(high, w, low_ref, own_ref, other_ref, ids_ref):
+    half = w.shape[0] // 2
+    total = low_ref[...]
+    total = total + jnp.dot(high[:, :half], w[half:, :], preferred_element_type=jnp.float32)
+    ids_ref[...] = high[:, half:]
+    own_ref[...] = total[:, : 2 * HD].astype(jnp.bfloat16)
+    other_ref[:, : 2 * HD] = total[:, 2 * HD :].astype(jnp.bfloat16)
+    other_ref[:, 2 * HD :] = high[:, half:]
+
+
+def project_last(low, high, weights):
+    rows = low.shape[0]
+    total = pl.pallas_call(
+        project_low_kernel,
+        out_shape=jax.ShapeDtypeStruct((rows, weights.shape[1]), jnp.float32),
         compiler_params=params(10),
-        name="project_last",
-    )(first, second, weights)
+        name="project_low",
+    )(low, weights)
+    return pl.pallas_call(
+        project_high_kernel,
+        out_shape=projected_shapes(rows),
+        compiler_params=params(10),
+        name="project_high",
+    )(high, weights, total)
 
 
 def origin(shape, dim, head):
     at = lax.broadcasted_iota(jnp.int32, shape, dim)
-    block, row = at >> 4, at & 15
-    turn = block >> 3
-    d_second, d_first, d_core = turn ^ (turn >> 1), block & 3, (block >> 2) & 1
-    core = head & 1
-    dy = jnp.where(core == 0, d_second, d_first)
-    dx = jnp.where(core == 0, d_first, d_second)
-    y, x, c = (head >> 3) ^ dy, ((head >> 1) & 3) ^ dx, core ^ d_core
+    turn, d_first, row = (at >> 6) & 3, (at >> 4) & 3, at & 15
+    d_second = turn ^ (turn >> 1)
+    c = (head & 1) ^ (at >> 8)
+    dy = jnp.where(c == 0, d_second, d_first)
+    dx = jnp.where(c == 0, d_first, d_second)
+    y, x = (head >> 3) ^ dy, ((head >> 1) & 3) ^ dx
     return (((y * NX + x) * 2 + c) << 4) + row
 
 
-def finish_kernel(groups, cap, own_a, own_b, their_a, their_b, ids_a, ids_b, *refs):
+def finish_kernel(groups, cap, own_a, own_b, ids_a, ids_b, their_a, their_b, *refs):
     outs, packed = refs[:groups], refs[groups]
     total = packed.shape[0]
-    n = total // (len(HELD) * NX)
-    early = EARLY * NX
+    early, half = own_a.shape[0], total // 2
     head = lax.axis_index("head")
     group = lax.axis_index("grp").astype(jnp.float32)
-
-    def block(first, second, i):
-        return first[i * n : (i + 1) * n] if i < early else second[(i - early) * n : (i - early + 1) * n]
-
-    for at, (d_second, d_core) in enumerate(HELD):
-        for d_first in range(NX):
-            i = at * NX + d_first
-            j = HELD.index((d_first, 1 - d_core)) * NX + d_second
-            both = block(own_a, own_b, i) + block(their_a, their_b, j)
-            packed[i * n : (i + 1) * n, :] = both.astype(jnp.bfloat16)
-    hop = jnp.concatenate([ids_a[...], ids_b[...]], axis=0).astype(jnp.float32) - group
+    packed[:early, :] = own_a[...]
+    packed[early:half, :] = own_b[...]
+    packed[half : half + early, :] = their_a[:, : 2 * HD]
+    packed[half + early :, :] = their_b[:, : 2 * HD]
+    ids = [ids_a[...], ids_b[...], their_a[:, 2 * HD :], their_b[:, 2 * HD :]]
+    hop = jnp.concatenate(ids, axis=0).astype(jnp.float32) - group
     hop = jnp.where(hop < 0.0, hop + groups, hop)
     lanes = lax.broadcasted_iota(jnp.int32, (1, HD), 1).astype(jnp.float32)
     match = jnp.where(hop == lanes, 1.0, 0.0)
@@ -295,15 +282,16 @@
         outs[g][:, HD:] = routed[rows, HD:].astype(jnp.bfloat16)
 
 
-def finish(groups, cap, own_a, own_b, their_a, their_b, ids_a, ids_b):
+def finish(groups, cap, own_a, own_b, ids_a, ids_b, their_a, their_b):
     shape = jax.ShapeDtypeStruct((cap, 2 * HD), jnp.bfloat16)
+    rows = 2 * (own_a.shape[0] + own_b.shape[0])
     return pl.pallas_call(
         lambda *refs: finish_kernel(groups, cap, *refs),
         out_shape=(shape,) * groups,
-        scratch_shapes=[pltpu.VMEM((own_a.shape[0] + own_b.shape[0], 2 * HD), jnp.bfloat16)],
+        scratch_shapes=[pltpu.VMEM((rows, 2 * HD), jnp.bfloat16)],
         compiler_params=params(12),
         name="finish",
-    )(own_a, own_b, their_a, their_b, ids_a, ids_b)
+    )(own_a, own_b, ids_a, ids_b, their_a, their_b)
 
 
 def settle_kernel(groups, edge_row, edge_col, high_ref, low_ref, *refs):
@@ -391,6 +379,36 @@
     return values * turn[:, :HD] + pltpu.roll(values, HD // 2, 1) * turn[:, HD:]
 
 
+def first_kernel(state_ref, gain_ref, wq_ref, wk_ref, wv_ref, *refs):
+    query_ref, key_ref, value_ref, current_ref, my_gain_ref, inverse_ref = refs[-6:]
+    share = current_ref.shape[1]
+    mine = pl.ds(pl.multiple_of(lax.axis_index("head") * share, share), share)
+    state = state_ref[...]
+    gain = gain_ref[...]
+    factor = lax.rsqrt(jnp.mean(state * state, axis=1, keepdims=True) + EPSILON)
+    rows = (state * factor * gain).astype(jnp.bfloat16)
+    query_ref[...] = jnp.dot(rows, wq_ref[...], preferred_element_type=jnp.float32)
+    key_ref[...] = jnp.dot(rows, wk_ref[...], preferred_element_type=jnp.float32)
+    value_ref[...] = jnp.dot(rows, wv_ref[...], preferred_element_type=jnp.float32)
+    current_ref[...] = state_ref[:, mine]
+    my_gain_ref[...] = gain_ref[:, mine]
+    inverse_ref[...] = 1.0 / gain
+
+
+def first(state, gain, weights, share, *deps):
+    n, width = state.shape
+    small = jax.ShapeDtypeStruct((n, HD), jnp.float32)
+    whole = pl.BlockSpec(memory_space=pltpu.VMEM)
+    return pl.pallas_call(
+        first_kernel,
+        out_shape=(small,) * 3
+        + tuple(jax.ShapeDtypeStruct(d, jnp.float32) for d in ((n, share), (1, share), (1, width))),
+        in_specs=[whole] * 5 + [pl.BlockSpec(memory_space=pl.ANY)] * len(deps),
+        compiler_params=params(54),
+        name="first",
+    )(state, gain.reshape(1, -1), *weights, *deps)
+
+
 def attend_kernel(step, *refs):
     f32, bf16 = jnp.float32, jnp.bfloat16
     turn_ref, key_ref, cache_ref, bias_ref, out_weight, *rest = refs
@@ -492,7 +510,6 @@
     groups = lax.axis_size("grp")
     heads = lax.axis_size("head")
     rows_local, width = prefill_rows.shape
-    plane_rows = rows_local * heads
     cap = (rows_local // groups + rows_local // groups // 2) * heads
     requests = lengths.shape[1]
     my_group = lax.axis_index("grp")
@@ -500,26 +517,19 @@
     share = width // heads
     f32, bf16 = jnp.float32, jnp.bfloat16
 
-    core = my_head % 2
     with jax.named_scope("rows"):
-        n = rows_local
-        kept, given = norm_split(row_group, prefill_rows, norm_gain)
-        got = send(given, CORE)
-        start = jnp.concatenate([kept, got])
+        start = norm_rows(row_group, prefill_rows, norm_gain)
         f2 = send(start, lane(2, 0))
         f1 = send(start, lane(1, 0))
         f3 = send(start, lane(3, 0))
-        l0 = jnp.concatenate([kept, f1[:n], f2[:n], f3[:n]])
-        l1 = jnp.concatenate([got, f1[n:], f2[n:], f3[n:]])
+        both_weights = [w_key, w_value, send(w_key, CORE), send(w_value, CORE)]
+        l0, l1 = lines(start, f1, f2, f3, both_weights[2][:16])
         s11 = send(l1, lane(0, 1))
         s30 = send(l0, lane(0, 3))
         s10 = send(l0, lane(0, 1))
         s31 = send(l1, lane(0, 3))
         s20 = send(s30, lane(0, 1))
         s21 = send(s11, lane(0, 3))
-    with jax.named_scope("weights"):
-        their_half = send(other_half(w_key, w_value, f1), CORE)
-
     with jax.named_scope("places"):
         group_ids = jnp.arange(groups, dtype=jnp.int32)
         late_lengths = after(lengths, f1)
@@ -538,12 +548,10 @@
         table_low = (table - table_high.astype(f32)).astype(bf16)
 
     with jax.named_scope("project"):
-        own_a, other_a, ids_a, half_weights = project(
-            [l0, l1, s10, s11, s30, s31], w_key, w_value, their_half
-        )
-        own_b, other_b, ids_b = project_last(s20, s21, half_weights)
+        own_a, other_a, ids_a, wide_weights = project([l0, s10, s30], [l1, s11, s31], both_weights)
+        own_b, other_b, ids_b = project_last(s20, s21, wide_weights)
         leaving = finish(
-            groups, cap, own_a, own_b, send(other_a, CORE), send(other_b, CORE), ids_a, ids_b
+            groups, cap, own_a, own_b, ids_a, ids_b, send(other_a, CORE), send(other_b, CORE)
         )
         arrived = [leaving[0]]
         for hop in range(1, groups):
@@ -553,18 +561,10 @@
         cache_keys, cache_values, bias = settle(edge_row, edge_col, table_high, table_low, arrived)
 
     with jax.named_scope("first"):
-        late_state = after(decode_state, f1)
-        current = lax.dynamic_slice_in_dim(late_state, my_head * share, share, 1)
-        late_gain = after(norm_gain, f1)
-        my_gain = lax.dynamic_slice_in_dim(late_gain, my_head * share, share, 0)[None, :]
-        inverse = (1.0 / late_gain)[None, :]
-        decode_rows = normed(late_state, norm_gain)
-        extra = [
-            jnp.dot(decode_rows, w, preferred_element_type=f32) for w in (w_query, w_key, w_value)
-        ]
+        extra = first(decode_state, norm_gain, (w_query, w_key, w_value), share)
+        current, my_gain, inverse = extra[3:]
         at_step = my_lengths[None, :] + jnp.arange(STEPS, dtype=jnp.int32)[:, None]
         turns = jnp.concatenate(angles_of(at_step), axis=-1)
-        extra += [current, my_gain, inverse]
     held = [w_query, w_key, w_value, w_out]
     olds = []
     for step in range(STEPS):

time: 170 us -> 166 us (0.976)
  Pallas kernels: 18 us -> 22.4 us
  waiting for transfers between devices: 13.1 us -> 16.8 us
  blocking collectives: 91.3 us -> 87.9 us
  starting transfers between devices: 35.6 us -> 33 us
  matrix products: 2.25 us -> 0 us
  other arithmetic: 3.06 us -> 1.05 us
  local copies, waits for them, and re-layouts: 4.98 us -> 3.08 us
    pallas_call x4 -> x6, Pallas kernels: 7.95 us -> 12.4 us  [the longest x1 4.86 us: first(): pl.pallas_call(first_kernel, out_shape=(small,) * 3 + tuple((jax.ShapeDty...]
    ppermute x13, starting transfers between devices: 20.8 us -> 16.4 us  [send(): return lax.ppermute(values, 'head', pairs)]
    ppermute x13, waiting for transfers between devices: 10 us -> 13.7 us  [send(): return lax.ppermute(values, 'head', pairs)]
    all_to_all x4, blocking collectives: 53.9 us -> 50.5 us  [per_device(): lax.all_to_all(term, 'head', split_axis=0, concat_axis=0, tiled=True)]
    dot_general x3 -> x0, matrix products: 2.25 us -> none  [per_device(): jnp.dot(decode_rows, w, preferred_element_type=f32)]
    unnamed x30 -> x27, local copies, waits for them, and re-layouts: 3.43 us -> 1.65 us
    ppermute x7, starting transfers between devices: 14.8 us -> 16.6 us  [per_device(): arrived.append(lax.ppermute(leaving[hop], 'grp', pairs))]
  transfers between devices with their start and end apart: 20 -> 20, of which waited for: 7 -> 6; matrix products, arithmetic and copies ran while one was open for 5% -> 2% of each run, Pallas kernels for 4% -> 8%
where the time goes in v7:
time: 166 us; the launch traced here: 165 us
  blocking collectives  87.9 us (53%)
  starting transfers between devices  33 us (20%)
  Pallas kernels  22.4 us (13%)
  waiting for transfers between devices  16.8 us (10%)
  local copies, waits for them, and re-layouts  3.08 us (2%)
    all_to_all x4, blocking collectives, per_device(): lax.all_to_all(term, 'head', split_axis=0, concat_axis=0, tiled=True)  50.5 us
    all_to_all x3, blocking collectives, per_device(): lax.all_to_all(spreading[0], 'head', split_axis=0, concat_axis=0, tiled=T...  37.4 us
    ppermute x7, starting transfers between devices, per_device(): arrived.append(lax.ppermute(leaving[hop], 'grp', pairs))  16.6 us
    ppermute x13, starting transfers between devices, send(): return lax.ppermute(values, 'head', pairs)  16.4 us
    ppermute x13, waiting for transfers between devices, send(): return lax.ppermute(values, 'head', pairs)  13.7 us
    pallas_call x4, Pallas kernels, attend(): pl.pallas_call(lambda *refs: attend_kernel(step, *refs), out_shape=(jax.S...  5.99 us
    pallas_call x1, Pallas kernels, first(): pl.pallas_call(first_kernel, out_shape=(small,) * 3 + tuple((jax.ShapeDty...  4.86 us
    pallas_call x1, Pallas kernels, project(): pl.pallas_call(lambda *refs: project_kernel(count, *refs), out_shape=proj...  3.92 us
  transfers between devices with their start and end apart: 20, of which 6 were waited for; matrix products, arithmetic and copies ran while one was open for 2% of the time, Pallas kernels for 8%

profile of v7, /device:TPU:1, one launch (start us, length us, event | category | flops | bytes accessed | tf_op | source)
XLA Modules:
  0.0 165.2 jit_solution(13023041416674791779)
XLA Ops:
  0.0 3.2 %collective-permute-start.3 = (bf16[8192,128]{1,0:T(8,128)(2,1)}, bf16[8192,128]{1,0:T(8,128)(2,1)}, u32[]{:S(2)}, u32[]{:S(2)}) collective-permute-start(bf16[8192,128]{1,0:T(8,128)(2,1)} %refs_14_.1), channel_id=1, source_target_pairs={{0,1},{1,0},{2,3},{3,2},{4,5},{5,4},{6,7},{7,6},{8,9},{9,8},{10,11... | collective-permute-start | bytes 6291464 | tf_op jit(solution)/shard_map/rows/ppermute | solution.py:68
  3.2 1.9 %norm_rows.1.start = bf16[32,4224]{1,0:T(8,128)(2,1)} custom-call(s32[16]{0:T(128)} %group_ref.1, bf16[16,8192]{1,0:T(8,128)(2,1)} %rows_ref.1, f32[1,8192]{1,0:T(1,128)} %bitcast.16), custom_call_target="tpu_custom_call" | custom-call | tf_op jit(solution)/shard_map/rows/norm_rows/pallas_call | solution.py:97
  5.2 2.2 %collective-permute-start.1 = (bf16[32,4224]{1,0:T(8,128)(2,1)}, bf16[32,4224]{1,0:T(8,128)(2,1)S(1)}, u32[]{:S(2)}, u32[]{:S(2)}) collective-permute-start(bf16[32,4224]{1,0:T(8,128)(2,1)} %norm_rows.1.start), channel_id=1, source_target_pairs={{0,4},{1,17},{2,6},{3,19},{4,0},{5,21},{6,2},{7,23},{8,12},{9,25},... | collective-permute-start | bytes 811016 | tf_op jit(solution)/shard_map/rows/ppermute | solution.py:68
  7.3 1.7 %collective-permute-start.2 = (bf16[32,4224]{1,0:T(8,128)(2,1)}, bf16[32,4224]{1,0:T(8,128)(2,1)S(1)}, u32[]{:S(2)}, u32[]{:S(2)}) collective-permute-start(bf16[32,4224]{1,0:T(8,128)(2,1)} %norm_rows.1.start), channel_id=1, source_target_pairs={{0,6},{1,25},{2,4},{3,27},{4,2},{5,29},{6,0},{7,31},{8,14},{9,17},... | collective-permute-start | bytes 811016 | tf_op jit(solution)/shard_map/rows/ppermute | solution.py:68
  9.0 0.0 copy-start.12
  9.0 0.0 copy-start
  9.0 0.0 copy-start.1
  9.1 4.9 %first.1 = (f32[16,128]{1,0:T(8,128)}, f32[16,128]{1,0:T(8,128)}, f32[16,128]{1,0:T(8,128)}, f32[16,256]{1,0:T(8,128)}, f32[1,256]{1,0:T(1,128)}, /*index=5*/f32[1,8192]{1,0:T(1,128)}) custom-call(f32[16,8192]{1,0:T(8,128)} %state_ref.1, f32[1,8192]{1,0:T(1,128)} %bitcast.17, bf16[8192,128]{1,0:T(8,128)(2,1)} %refs_13_.3, bf16[8192,128]{1,0:T(8,128)(2,1)} %refs_14_.1, ...), custom_call_target="tpu_custom_call" | custom-call | tf_op jit(solution)/shard_map/first/first/pallas_call | solution.py:402
  13.9 0.7 slice.9.refs_0_
  14.6 2.6 %collective-permute-done.2.f3 = bf16[32,4224]{1,0:T(8,128)(2,1)S(1)} collective-permute-done((bf16[32,4224]{1,0:T(8,128)(2,1)}, bf16[32,4224]{1,0:T(8,128)(2,1)S(1)}, u32[]{:S(2)}, u32[]{:S(2)}) %collective-permute-start.2) | collective-permute-done | bytes 270368 | tf_op jit(solution)/shard_map/rows/ppermute | solution.py:68
  17.3 0.1 lines.1
  17.3 2.6 %collective-permute-start.5 = (bf16[64,4224]{1,0:T(8,128)(2,1)S(1)}, bf16[64,4224]{1,0:T(8,128)(2,1)S(1)}, u32[]{:S(2)}, u32[]{:S(2)}) collective-permute-start(bf16[64,4224]{1,0:T(8,128)(2,1)S(1)} %get-tuple-element.47.refs_0_), channel_id=1, source_target_pairs={{0,24},{1,7},{2,26},{3,5},{4,28},{5,3},{6,30},{7,1},{8,16},{9,15},... | collective-permute-start | bytes 1622024 | tf_op jit(solution)/shard_map/rows/ppermute | solution.py:68
  19.9 0.3 multiply_cosine_fusion
  20.2 0.1 fusion.refs_2_
  20.3 0.1 subtract_convert_fusion.refs_3_
  20.4 0.6 slice.8
  21.7 0.1 select_reduce_fusion.1
  21.8 1.5 collective-permute-start.4
  23.3 0.2 collective-permute-start.7
  23.5 4.9 %collective-permute-done.6.refs_4_ = bf16[64,4224]{1,0:T(8,128)(2,1)S(1)} collective-permute-done((bf16[64,4224]{1,0:T(8,128)(2,1)S(1)}, bf16[64,4224]{1,0:T(8,128)(2,1)S(1)}, u32[]{:S(2)}, u32[]{:S(2)}) %collective-permute-start.6) | collective-permute-done | bytes 540704 | tf_op jit(solution)/shard_map/rows/ppermute | solution.py:68
  28.4 0.2 collective-permute-start.9
  28.6 0.1 select_reduce_fusion
  28.7 0.2 multiply_cosine_fusion.1
  28.9 5.2 %collective-permute-done.4.refs_1_ = bf16[64,4224]{1,0:T(8,128)(2,1)S(1)} collective-permute-done((bf16[64,4224]{1,0:T(8,128)(2,1)S(1)}, bf16[64,4224]{1,0:T(8,128)(2,1)S(1)}, u32[]{:S(2)}, u32[]{:S(2)}) %collective-permute-start.4) | collective-permute-done | bytes 540704 | tf_op jit(solution)/shard_map/rows/ppermute | solution.py:68
  34.2 3.9 %project.1 = (bf16[192,256]{1,0:T(8,128)(2,1)S(1)}, bf16[192,384]{1,0:T(8,128)(2,1)S(1)}, bf16[192,128]{1,0:T(8,128)(2,1)S(1)}, bf16[8192,512]{1,0:T(8,128)(2,1)S(1)}) custom-call(bf16[64,4224]{1,0:T(8,128)(2,1)S(1)} %get-tuple-element.47.refs_0_, bf16[64,4224]{1,0:T(8,128)(2,1)S(1)} %collective-permute-done.4.refs_1_, ...), custom_call_target="tpu_custom_call" | custom-call | tf_op jit(solution)/shard_map/project/project/pallas_call | solution.py:190
  38.1 2.8 %collective-permute-start.11 = (bf16[192,384]{1,0:T(8,128)(2,1)S(1)}, bf16[192,384]{1,0:T(8,128)(2,1)S(1)}, u32[]{:S(2)}, u32[]{:S(2)}) collective-permute-start(bf16[192,384]{1,0:T(8,128)(2,1)S(1)} %get-tuple-element.54), channel_id=1, source_target_pairs={{0,1},{1,0},{2,3},{3,2},{4,5},{5,4},{6,7},{7,6},{8,9},{9,8},{10,11... | collective-permute-start | bytes 442376 | tf_op jit(solution)/shard_map/project/ppermute | solution.py:68
  40.9 0.8 project_low.1.low_ref
  41.8 0.8 project_high.1
  42.6 2.0 %collective-permute-start.12 = (bf16[64,384]{1,0:T(8,128)(2,1)S(1)}, bf16[64,384]{1,0:T(8,128)(2,1)S(1)}, u32[]{:S(2)}, u32[]{:S(2)}) collective-permute-start(bf16[64,384]{1,0:T(8,128)(2,1)S(1)} %get-tuple-element.55), channel_id=1, source_target_pairs={{0,1},{1,0},{2,3},{3,2},{4,5},{5,4},{6,7},{7,6},{8,9},{9,8},{10,11... | collective-permute-start | bytes 147464 | tf_op jit(solution)/shard_map/project/ppermute | solution.py:68
  44.7 0.9 collective-permute-done.12.refs_5_
  45.5 1.4 finish.1
  47.0 1.7 %collective-permute-start.13 = (bf16[96,256]{1,0:T(8,128)(2,1)S(1)}, bf16[96,256]{1,0:T(8,128)(2,1)S(1)}, u32[]{:S(2)}, u32[]{:S(2)}) collective-permute-start(bf16[96,256]{1,0:T(8,128)(2,1)S(1)} %get-tuple-element.57), channel_id=1, source_target_pairs={{0,32},{32,64},{64,96},{96,128},{128,160},{160,192},{192,224},{224... | collective-permute-start | bytes 147464 | tf_op jit(solution)/shard_map/project/ppermute | solution.py:559
  48.7 3.0 %collective-permute-start.14 = (bf16[96,256]{1,0:T(8,128)(2,1)S(1)}, bf16[96,256]{1,0:T(8,128)(2,1)S(1)}, u32[]{:S(2)}, u32[]{:S(2)}) collective-permute-start(bf16[96,256]{1,0:T(8,128)(2,1)S(1)} %get-tuple-element.58), channel_id=1, source_target_pairs={{0,64},{32,96},{64,128},{96,160},{128,192},{160,224},{192,0},{224,... | collective-permute-start | bytes 147464 | tf_op jit(solution)/shard_map/project/ppermute | solution.py:559
  51.7 0.1 pad_maximum_fusion.1.refs_0_
  51.8 3.8 %collective-permute-start.15 = (bf16[96,256]{1,0:T(8,128)(2,1)S(1)}, bf16[96,256]{1,0:T(8,128)(2,1)S(1)}, u32[]{:S(2)}, u32[]{:S(2)}) collective-permute-start(bf16[96,256]{1,0:T(8,128)(2,1)S(1)} %get-tuple-element.59), channel_id=1, source_target_pairs={{0,96},{32,128},{64,160},{96,192},{128,224},{160,0},{192,32},{224,... | collective-permute-start | bytes 147464 | tf_op jit(solution)/shard_map/project/ppermute | solution.py:559
  55.6 0.6 collective-permute-start.16
  56.1 4.4 %collective-permute-start.17 = (bf16[96,256]{1,0:T(8,128)(2,1)S(1)}, bf16[96,256]{1,0:T(8,128)(2,1)S(1)}, u32[]{:S(2)}, u32[]{:S(2)}) collective-permute-start(bf16[96,256]{1,0:T(8,128)(2,1)S(1)} %get-tuple-element.61), channel_id=1, source_target_pairs={{0,160},{32,192},{64,224},{96,0},{128,32},{160,64},{192,96},{224,1... | collective-permute-start | bytes 147464 | tf_op jit(solution)/shard_map/project/ppermute | solution.py:559
  60.5 2.4 %collective-permute-start.18 = (bf16[96,256]{1,0:T(8,128)(2,1)S(1)}, bf16[96,256]{1,0:T(8,128)(2,1)S(1)}, u32[]{:S(2)}, u32[]{:S(2)}) collective-permute-start(bf16[96,256]{1,0:T(8,128)(2,1)S(1)} %get-tuple-element.62), channel_id=1, source_target_pairs={{0,192},{32,224},{64,0},{96,32},{128,64},{160,96},{192,128},{224,1... | collective-permute-start | bytes 147464 | tf_op jit(solution)/shard_map/project/ppermute | solution.py:559
  62.9 0.7 collective-permute-start.19
  63.7 0.1 copy.12
  63.7 0.1 broadcast_in_dim.41
  63.8 0.0 copy-start.4
  63.8 1.6 copy-done.4
  65.5 0.0 copy-start.3
  65.5 0.2 hold.1.refs_4_.refs_6_
  65.6 0.0 copy-start.2
  65.7 2.7 %collective-permute-done.18.refs_10_ = bf16[96,256]{1,0:T(8,128)(2,1)S(1)} collective-permute-done((bf16[96,256]{1,0:T(8,128)(2,1)S(1)}, bf16[96,256]{1,0:T(8,128)(2,1)S(1)}, u32[]{:S(2)}, u32[]{:S(2)}) %collective-permute-start.18) | collective-permute-done | bytes 49184 | tf_op jit(solution)/shard_map/project/ppermute | solution.py:559
  68.4 0.4 collective-permute-done.19.refs_11_
  68.8 1.6 settle.1
  70.4 0.9 attend.4
  71.3 12.9 %all_to_all.35.refs_0_ = bf16[32,16,256]{2,1,0:T(8,128)(2,1)S(1)} all-to-all(bf16[32,16,256]{2,1,0:T(8,128)(2,1)S(1)} %get-tuple-element.75), channel_id=1, replica_groups=mesh['grp'=8,'head'=32] {'head'}, dimensions={0} | all-to-all | bytes 524288 | tf_op jit(solution)/shard_map/all_to_all | solution.py:575
  84.2 0.1 spread.4
  84.3 12.5 %all_to_all.36.refs_7_ = bf16[32,16,256]{2,1,0:T(8,128)(2,1)S(1)} all-to-all(bf16[32,16,256]{2,1,0:T(8,128)(2,1)S(1)} %get-tuple-element.76), channel_id=1, replica_groups=mesh['grp'=8,'head'=32] {'head'}, dimensions={0} | all-to-all | bytes 524288 | tf_op jit(solution)/shard_map/all_to_all | solution.py:579
  96.8 1.7 %attend.5 = (bf16[32,16,256]{2,1,0:T(8,128)(2,1)S(1)}, bf16[16,128]{1,0:T(8,128)(2,1)S(1)}, bf16[16,128]{1,0:T(8,128)(2,1)S(1)}) custom-call(f32[4,16,256]{2,1,0:T(8,128)S(1)} %pad_maximum_fusion.1.refs_0_, bf16[768,128]{1,0:T(8,128)(2,1)S(1)} %get-tuple-element.64.refs_1_, bf16[768,128]{1,0:T(8,128)(2,1)S(1)} %get-tuple-element.65.refs_2_, ...), custom_call_target="tpu_custom_call" | custom-call | tf_op jit(solution)/shard_map/attend/pallas_call | solution.py:475
  98.5 12.5 %all_to_all.37.refs_0_ = bf16[32,16,256]{2,1,0:T(8,128)(2,1)S(1)} all-to-all(bf16[32,16,256]{2,1,0:T(8,128)(2,1)S(1)} %get-tuple-element.79), channel_id=1, replica_groups=mesh['grp'=8,'head'=32] {'head'}, dimensions={0} | all-to-all | bytes 524288 | tf_op jit(solution)/shard_map/all_to_all | solution.py:575
  110.9 0.1 spread.5
  111.0 12.5 %all_to_all.38.refs_9_ = bf16[32,16,256]{2,1,0:T(8,128)(2,1)S(1)} all-to-all(bf16[32,16,256]{2,1,0:T(8,128)(2,1)S(1)} %get-tuple-element.81), channel_id=1, replica_groups=mesh['grp'=8,'head'=32] {'head'}, dimensions={0} | all-to-all | bytes 524288 | tf_op jit(solution)/shard_map/all_to_all | solution.py:579
  123.4 1.7 %attend.6 = (bf16[32,16,256]{2,1,0:T(8,128)(2,1)S(1)}, bf16[16,128]{1,0:T(8,128)(2,1)S(1)}, bf16[16,128]{1,0:T(8,128)(2,1)S(1)}) custom-call(f32[4,16,256]{2,1,0:T(8,128)S(1)} %pad_maximum_fusion.1.refs_0_, bf16[768,128]{1,0:T(8,128)(2,1)S(1)} %get-tuple-element.64.refs_1_, bf16[768,128]{1,0:T(8,128)(2,1)S(1)} %get-tuple-element.65.refs_2_, ...), custom_call_target="tpu_custom_call" | custom-call | tf_op jit(solution)/shard_map/attend/pallas_call | solution.py:475
  125.1 12.7 %all_to_all.39.refs_0_ = bf16[32,16,256]{2,1,0:T(8,128)(2,1)S(1)} all-to-all(bf16[32,16,256]{2,1,0:T(8,128)(2,1)S(1)} %get-tuple-element.84), channel_id=1, replica_groups=mesh['grp'=8,'head'=32] {'head'}, dimensions={0} | all-to-all | bytes 524288 | tf_op jit(solution)/shard_map/all_to_all | solution.py:575
  137.8 0.1 spread.6
  137.9 12.5 %all_to_all.40.refs_11_ = bf16[32,16,256]{2,1,0:T(8,128)(2,1)S(1)} all-to-all(bf16[32,16,256]{2,1,0:T(8,128)(2,1)S(1)} %get-tuple-element.86), channel_id=1, replica_groups=mesh['grp'=8,'head'=32] {'head'}, dimensions={0} | all-to-all | bytes 524288 | tf_op jit(solution)/shard_map/all_to_all | solution.py:579
  150.4 1.7 %attend.7 = (bf16[32,16,256]{2,1,0:T(8,128)(2,1)S(1)}, bf16[16,128]{1,0:T(8,128)(2,1)}, bf16[16,128]{1,0:T(8,128)(2,1)}) custom-call(f32[4,16,256]{2,1,0:T(8,128)S(1)} %pad_maximum_fusion.1.refs_0_, bf16[768,128]{1,0:T(8,128)(2,1)S(1)} %get-tuple-element.64.refs_1_, bf16[768,128]{1,0:T(8,128)(2,1)S(1)} %get-tuple-element.65.refs_2_, ...), custom_call_target="tpu_custom_call" | custom-call | tf_op jit(solution)/shard_map/attend/pallas_call | solution.py:475
  152.1 12.5 %all_to_all.41.refs_0_ = bf16[32,16,256]{2,1,0:T(8,128)(2,1)S(1)} all-to-all(bf16[32,16,256]{2,1,0:T(8,128)(2,1)S(1)} %get-tuple-element.87), channel_id=1, replica_groups=mesh['grp'=8,'head'=32] {'head'}, dimensions={0} | all-to-all | bytes 524288 | tf_op jit(solution)/shard_map/all_to_all | solution.py:575
  164.5 0.7 spread.7
  (45 shorter events, 0.1 us)
Async XLA Ops:
  0.0 13.9 %collective-permute-start.3 = (bf16[8192,128]{1,0:T(8,128)(2,1)}, bf16[8192,128]{1,0:T(8,128)(2,1)}, u32[]{:S(2)}, u32[]{:S(2)}) collective-permute-start(bf16[8192,128]{1,0:T(8,128)(2,1)} %refs_14_.1), channel_id=1, source_target_pairs={{0,1},{1,0},{2,3},{3,2},{4,5},{5,4},{6,7},{7,6},{8,9},{9,8},{10,11... | collective-permute-start | bytes 6291464 | tf_op jit(solution)/shard_map/rows/ppermute | solution.py:68
  3.2 25.7 %collective-permute-start.8 = (bf16[8192,128]{1,0:T(8,128)(2,1)}, bf16[8192,128]{1,0:T(8,128)(2,1)}, u32[]{:S(2)}, u32[]{:S(2)}) collective-permute-start(bf16[8192,128]{1,0:T(8,128)(2,1)} %refs_15_.1), channel_id=1, source_target_pairs={{0,1},{1,0},{2,3},{3,2},{4,5},{5,4},{6,7},{7,6},{8,9},{9,8},{10,11... | collective-permute-start | bytes 6291464 | tf_op jit(solution)/shard_map/rows/ppermute | solution.py:68
  5.1 9.5 %collective-permute-start = (bf16[32,4224]{1,0:T(8,128)(2,1)}, bf16[32,4224]{1,0:T(8,128)(2,1)S(1)}, u32[]{:S(2)}, u32[]{:S(2)}) collective-permute-start(bf16[32,4224]{1,0:T(8,128)(2,1)} %norm_rows.1.start), channel_id=1, source_target_pairs={{0,2},{1,9},{2,0},{3,11},{4,6},{5,13},{6,4},{7,15},{8,10},{9,1},{1... | collective-permute-start | bytes 811016 | tf_op jit(solution)/shard_map/rows/ppermute | solution.py:68
  5.2 9.5 %collective-permute-start.1 = (bf16[32,4224]{1,0:T(8,128)(2,1)}, bf16[32,4224]{1,0:T(8,128)(2,1)S(1)}, u32[]{:S(2)}, u32[]{:S(2)}) collective-permute-start(bf16[32,4224]{1,0:T(8,128)(2,1)} %norm_rows.1.start), channel_id=1, source_target_pairs={{0,4},{1,17},{2,6},{3,19},{4,0},{5,21},{6,2},{7,23},{8,12},{9,25},... | collective-permute-start | bytes 811016 | tf_op jit(solution)/shard_map/rows/ppermute | solution.py:68
  7.3 9.9 %collective-permute-start.2 = (bf16[32,4224]{1,0:T(8,128)(2,1)}, bf16[32,4224]{1,0:T(8,128)(2,1)S(1)}, u32[]{:S(2)}, u32[]{:S(2)}) collective-permute-start(bf16[32,4224]{1,0:T(8,128)(2,1)} %norm_rows.1.start), channel_id=1, source_target_pairs={{0,6},{1,25},{2,4},{3,27},{4,2},{5,29},{6,0},{7,31},{8,14},{9,17},... | collective-permute-start | bytes 811016 | tf_op jit(solution)/shard_map/rows/ppermute | solution.py:68
  9.0 8.2 %copy-start.5 = (bf16[32,4224]{1,0:T(8,128)(2,1)S(1)}, bf16[32,4224]{1,0:T(8,128)(2,1)}, u32[]{:S(2)}) copy-start(bf16[32,4224]{1,0:T(8,128)(2,1)} %norm_rows.1.start) | copy-start | bytes 811012
  9.0 12.7 %copy-start.12 = (s32[8,16]{1,0:T(8,128)S(1)}, s32[8,16]{1,0:T(8,128)}, u32[]{:S(2)}) copy-start(s32[8,16]{1,0:T(8,128)} %param.11) | copy-start | bytes 1540
  9.0 25.2 %copy-start = (bf16[8192,128]{1,0:T(8,128)(2,1)S(1)}, bf16[8192,128]{1,0:T(8,128)(2,1)}, u32[]{:S(2)}) copy-start(bf16[8192,128]{1,0:T(8,128)(2,1)} %refs_14_.1) | copy-start | bytes 6291460
  9.0 25.2 %copy-start.1 = (bf16[8192,128]{1,0:T(8,128)(2,1)S(1)}, bf16[8192,128]{1,0:T(8,128)(2,1)}, u32[]{:S(2)}) copy-start(bf16[8192,128]{1,0:T(8,128)(2,1)} %refs_15_.1) | copy-start | bytes 6291460
  17.3 11.3 %collective-permute-start.5 = (bf16[64,4224]{1,0:T(8,128)(2,1)S(1)}, bf16[64,4224]{1,0:T(8,128)(2,1)S(1)}, u32[]{:S(2)}, u32[]{:S(2)}) collective-permute-start(bf16[64,4224]{1,0:T(8,128)(2,1)S(1)} %get-tuple-element.47.refs_0_), channel_id=1, source_target_pairs={{0,24},{1,7},{2,26},{3,5},{4,28},{5,3},{6,30},{7,1},{8,16},{9,15},... | collective-permute-start | bytes 1622024 | tf_op jit(solution)/shard_map/rows/ppermute | solution.py:68
  19.9 8.5 %collective-permute-start.6 = (bf16[64,4224]{1,0:T(8,128)(2,1)S(1)}, bf16[64,4224]{1,0:T(8,128)(2,1)S(1)}, u32[]{:S(2)}, u32[]{:S(2)}) collective-permute-start(bf16[64,4224]{1,0:T(8,128)(2,1)S(1)} %get-tuple-element.48.refs_3_), channel_id=1, source_target_pairs={{0,8},{1,3},{2,10},{3,1},{4,12},{5,7},{6,14},{7,5},{8,0},{9,11},{1... | collective-permute-start | bytes 1622024 | tf_op jit(solution)/shard_map/rows/ppermute | solution.py:68
  21.8 12.4 %collective-permute-start.4 = (bf16[64,4224]{1,0:T(8,128)(2,1)S(1)}, bf16[64,4224]{1,0:T(8,128)(2,1)S(1)}, u32[]{:S(2)}, u32[]{:S(2)}) collective-permute-start(bf16[64,4224]{1,0:T(8,128)(2,1)S(1)} %get-tuple-element.47.refs_0_), channel_id=1, source_target_pairs={{0,8},{1,3},{2,10},{3,1},{4,12},{5,7},{6,14},{7,5},{8,0},{9,11},{1... | collective-permute-start | bytes 1622024 | tf_op jit(solution)/shard_map/rows/ppermute | solution.py:68
  23.3 10.9 %collective-permute-start.7 = (bf16[64,4224]{1,0:T(8,128)(2,1)S(1)}, bf16[64,4224]{1,0:T(8,128)(2,1)S(1)}, u32[]{:S(2)}, u32[]{:S(2)}) collective-permute-start(bf16[64,4224]{1,0:T(8,128)(2,1)S(1)} %get-tuple-element.48.refs_3_), channel_id=1, source_target_pairs={{0,24},{1,7},{2,26},{3,5},{4,28},{5,3},{6,30},{7,1},{8,16},{9,15},... | collective-permute-start | bytes 1622024 | tf_op jit(solution)/shard_map/rows/ppermute | solution.py:68
  28.4 13.4 %collective-permute-start.9 = (bf16[64,4224]{1,0:T(8,128)(2,1)S(1)}, bf16[64,4224]{1,0:T(8,128)(2,1)S(1)}, u32[]{:S(2)}, u32[]{:S(2)}) collective-permute-start(bf16[64,4224]{1,0:T(8,128)(2,1)S(1)} %collective-permute-done.6.refs_4_), channel_id=1, source_target_pairs={{0,24},{1,7},{2,26},{3,5},{4,28},{5,3},{6,30},{7,1},{8,16},{9,15},... | collective-permute-start | bytes 1622024 | tf_op jit(solution)/shard_map/rows/ppermute | solution.py:68
  28.6 12.3 %collective-permute-start.10 = (bf16[64,4224]{1,0:T(8,128)(2,1)S(1)}, bf16[64,4224]{1,0:T(8,128)(2,1)S(1)}, u32[]{:S(2)}, u32[]{:S(2)}) collective-permute-start(bf16[64,4224]{1,0:T(8,128)(2,1)S(1)} %collective-permute-done.5.refs_2_), channel_id=1, source_target_pairs={{0,8},{1,3},{2,10},{3,1},{4,12},{5,7},{6,14},{7,5},{8,0},{9,11},{1... | collective-permute-start | bytes 1622024 | tf_op jit(solution)/shard_map/rows/ppermute | solution.py:68
  38.1 6.5 %collective-permute-start.11 = (bf16[192,384]{1,0:T(8,128)(2,1)S(1)}, bf16[192,384]{1,0:T(8,128)(2,1)S(1)}, u32[]{:S(2)}, u32[]{:S(2)}) collective-permute-start(bf16[192,384]{1,0:T(8,128)(2,1)S(1)} %get-tuple-element.54), channel_id=1, source_target_pairs={{0,1},{1,0},{2,3},{3,2},{4,5},{5,4},{6,7},{7,6},{8,9},{9,8},{10,11... | collective-permute-start | bytes 442376 | tf_op jit(solution)/shard_map/project/ppermute | solution.py:68
  42.6 2.9 %collective-permute-start.12 = (bf16[64,384]{1,0:T(8,128)(2,1)S(1)}, bf16[64,384]{1,0:T(8,128)(2,1)S(1)}, u32[]{:S(2)}, u32[]{:S(2)}) collective-permute-start(bf16[64,384]{1,0:T(8,128)(2,1)S(1)} %get-tuple-element.55), channel_id=1, source_target_pairs={{0,1},{1,0},{2,3},{3,2},{4,5},{5,4},{6,7},{7,6},{8,9},{9,8},{10,11... | collective-permute-start | bytes 147464 | tf_op jit(solution)/shard_map/project/ppermute | solution.py:68
  47.0 13.6 %collective-permute-start.13 = (bf16[96,256]{1,0:T(8,128)(2,1)S(1)}, bf16[96,256]{1,0:T(8,128)(2,1)S(1)}, u32[]{:S(2)}, u32[]{:S(2)}) collective-permute-start(bf16[96,256]{1,0:T(8,128)(2,1)S(1)} %get-tuple-element.57), channel_id=1, source_target_pairs={{0,32},{32,64},{64,96},{96,128},{128,160},{160,192},{192,224},{224... | collective-permute-start | bytes 147464 | tf_op jit(solution)/shard_map/project/ppermute | solution.py:559
  48.7 14.2 %collective-permute-start.14 = (bf16[96,256]{1,0:T(8,128)(2,1)S(1)}, bf16[96,256]{1,0:T(8,128)(2,1)S(1)}, u32[]{:S(2)}, u32[]{:S(2)}) collective-permute-start(bf16[96,256]{1,0:T(8,128)(2,1)S(1)} %get-tuple-element.58), channel_id=1, source_target_pairs={{0,64},{32,96},{64,128},{96,160},{128,192},{160,224},{192,0},{224,... | collective-permute-start | bytes 147464 | tf_op jit(solution)/shard_map/project/ppermute | solution.py:559
  51.8 13.9 %collective-permute-start.15 = (bf16[96,256]{1,0:T(8,128)(2,1)S(1)}, bf16[96,256]{1,0:T(8,128)(2,1)S(1)}, u32[]{:S(2)}, u32[]{:S(2)}) collective-permute-start(bf16[96,256]{1,0:T(8,128)(2,1)S(1)} %get-tuple-element.59), channel_id=1, source_target_pairs={{0,96},{32,128},{64,160},{96,192},{128,224},{160,0},{192,32},{224,... | collective-permute-start | bytes 147464 | tf_op jit(solution)/shard_map/project/ppermute | solution.py:559
  55.6 10.1 %collective-permute-start.16 = (bf16[96,256]{1,0:T(8,128)(2,1)S(1)}, bf16[96,256]{1,0:T(8,128)(2,1)S(1)}, u32[]{:S(2)}, u32[]{:S(2)}) collective-permute-start(bf16[96,256]{1,0:T(8,128)(2,1)S(1)} %get-tuple-element.60), channel_id=1, source_target_pairs={{0,128},{32,160},{64,192},{96,224},{128,0},{160,32},{192,64},{224,... | collective-permute-start | bytes 147464 | tf_op jit(solution)/shard_map/project/ppermute | solution.py:559
  56.1 9.5 %collective-permute-start.17 = (bf16[96,256]{1,0:T(8,128)(2,1)S(1)}, bf16[96,256]{1,0:T(8,128)(2,1)S(1)}, u32[]{:S(2)}, u32[]{:S(2)}) collective-permute-start(bf16[96,256]{1,0:T(8,128)(2,1)S(1)} %get-tuple-element.61), channel_id=1, source_target_pairs={{0,160},{32,192},{64,224},{96,0},{128,32},{160,64},{192,96},{224,1... | collective-permute-start | bytes 147464 | tf_op jit(solution)/shard_map/project/ppermute | solution.py:559
  60.5 7.8 %collective-permute-start.18 = (bf16[96,256]{1,0:T(8,128)(2,1)S(1)}, bf16[96,256]{1,0:T(8,128)(2,1)S(1)}, u32[]{:S(2)}, u32[]{:S(2)}) collective-permute-start(bf16[96,256]{1,0:T(8,128)(2,1)S(1)} %get-tuple-element.62), channel_id=1, source_target_pairs={{0,192},{32,224},{64,0},{96,32},{128,64},{160,96},{192,128},{224,1... | collective-permute-start | bytes 147464 | tf_op jit(solution)/shard_map/project/ppermute | solution.py:559
  62.9 5.9 %collective-permute-start.19 = (bf16[96,256]{1,0:T(8,128)(2,1)S(1)}, bf16[96,256]{1,0:T(8,128)(2,1)S(1)}, u32[]{:S(2)}, u32[]{:S(2)}) collective-permute-start(bf16[96,256]{1,0:T(8,128)(2,1)S(1)} %get-tuple-element.63), channel_id=1, source_target_pairs={{0,224},{32,0},{64,32},{96,64},{128,96},{160,128},{192,160},{224,1... | collective-permute-start | bytes 147464 | tf_op jit(solution)/shard_map/project/ppermute | solution.py:559
  63.8 1.6 copy-start.4
  65.4 5.0 %copy-start.6 = (f32[1,8192]{1,0:T(1,128)S(1)}, f32[1,8192]{1,0:T(1,128)}, u32[]{:S(2)}) copy-start(f32[1,8192]{1,0:T(1,128)} %get-tuple-element.72.refs_10_.refs_8_.refs_12_) | copy-start | bytes 98308
  65.4 5.0 %copy-start.7 = (f32[16,256]{1,0:T(8,128)S(1)}, f32[16,256]{1,0:T(8,128)}, u32[]{:S(2)}) copy-start(f32[16,256]{1,0:T(8,128)} %get-tuple-element.70.refs_8_.refs_1_) | copy-start | bytes 49156
  65.4 5.0 %copy-start.8 = (f32[1,256]{1,0:T(1,128)S(1)}, f32[1,256]{1,0:T(1,128)}, u32[]{:S(2)}) copy-start(f32[1,256]{1,0:T(1,128)} %get-tuple-element.71.refs_9_.refs_2_) | copy-start | bytes 3076
  65.4 5.0 %copy-start.9 = (f32[16,128]{1,0:T(8,128)S(1)}, f32[16,128]{1,0:T(8,128)}, u32[]{:S(2)}) copy-start(f32[16,128]{1,0:T(8,128)} %get-tuple-element.67.refs_5_) | copy-start | bytes 24580
  65.4 5.0 %copy-start.10 = (f32[16,128]{1,0:T(8,128)S(1)}, f32[16,128]{1,0:T(8,128)}, u32[]{:S(2)}) copy-start(f32[16,128]{1,0:T(8,128)} %get-tuple-element.68.refs_6_) | copy-start | bytes 24580
  65.4 5.0 %copy-start.11 = (f32[16,128]{1,0:T(8,128)S(1)}, f32[16,128]{1,0:T(8,128)}, u32[]{:S(2)}) copy-start(f32[16,128]{1,0:T(8,128)} %get-tuple-element.69.refs_7_) | copy-start | bytes 24580
  65.5 18.8 %copy-start.3 = (bf16[8192,128]{1,0:T(8,128)(2,1)S(1)}, bf16[8192,128]{1,0:T(8,128)(2,1)}, u32[]{:S(2)}) copy-start(bf16[8192,128]{1,0:T(8,128)(2,1)} %refs_13_.3) | copy-start | bytes 6291460
  65.6 18.6 %copy-start.2 = (bf16[8192,128]{1,0:T(8,128)(2,1)S(1)}, bf16[8192,128]{1,0:T(8,128)(2,1)}, u32[]{:S(2)}) copy-start(bf16[8192,128]{1,0:T(8,128)(2,1)} %refs_15_.1) | copy-start | bytes 6291460

commit v8 on v7

--- a/solution.py
+++ b/solution.py
@@ -43,6 +43,7 @@
 NX = 4
 NY = 4
 EMPTY = 1e30
+HOPS = (0, 4, 3, 5, 2, 6, 1, 7)
 
 
 def head_pairs(move):
@@ -295,7 +296,7 @@
 
 
 def settle_kernel(groups, edge_row, edge_col, high_ref, low_ref, *refs):
-    parts = refs[:groups]
+    parts = [refs[HOPS.index(g)] for g in range(groups)]
     key_ref, value_ref, bias_ref, hot = refs[groups:]
     cap = parts[0].shape[0]
     slots = groups * cap
@@ -554,7 +555,7 @@
             groups, cap, own_a, own_b, ids_a, ids_b, send(other_a, CORE), send(other_b, CORE)
         )
         arrived = [leaving[0]]
-        for hop in range(1, groups):
+        for hop in HOPS[1:]:
             pairs = [(g, (g + hop) % groups) for g in range(groups)]
             arrived.append(lax.ppermute(leaving[hop], "grp", pairs))
         (w_out,) = hold([w_out], leaving[0])

time: 166 us -> 165 us (level)
  waiting for transfers between devices: 16.8 us -> 13.7 us
    ppermute x7, waiting for transfers between devices: 3.11 us -> 0.02 us  [per_device(): arrived.append(lax.ppermute(leaving[hop], 'grp', pairs))]
  transfers between devices with their start and end apart: 20 -> 20, of which waited for: 6 -> 4; matrix products, arithmetic and copies ran while one was open for 2% -> 2% of each run, Pallas kernels for 8% -> 8%
where the time goes in v8:
time: 165 us; the launch traced here: 164 us
  blocking collectives  89 us (54%)
  starting transfers between devices  34.2 us (21%)
  Pallas kernels  22.4 us (14%)
  waiting for transfers between devices  13.7 us (8%)
  local copies, waits for them, and re-layouts  3.08 us (2%)
    all_to_all x4, blocking collectives, per_device(): lax.all_to_all(term, 'head', split_axis=0, concat_axis=0, tiled=True)  51.6 us
    all_to_all x3, blocking collectives, per_device(): lax.all_to_all(spreading[0], 'head', split_axis=0, concat_axis=0, tiled=T...  37.4 us
    ppermute x7, starting transfers between devices, per_device(): arrived.append(lax.ppermute(leaving[hop], 'grp', pairs))  17.8 us
    ppermute x13, starting transfers between devices, send(): return lax.ppermute(values, 'head', pairs)  16.4 us
    ppermute x13, waiting for transfers between devices, send(): return lax.ppermute(values, 'head', pairs)  13.7 us
    pallas_call x4, Pallas kernels, attend(): pl.pallas_call(lambda *refs: attend_kernel(step, *refs), out_shape=(jax.S...  5.99 us
    pallas_call x1, Pallas kernels, first(): pl.pallas_call(first_kernel, out_shape=(small,) * 3 + tuple((jax.ShapeDty...  4.86 us
    pallas_call x1, Pallas kernels, project(): pl.pallas_call(lambda *refs: project_kernel(count, *refs), out_shape=proj...  3.92 us
  transfers between devices with their start and end apart: 20, of which 4 were waited for; matrix products, arithmetic and copies ran while one was open for 2% of the time, Pallas kernels for 8%

profile of v8, /device:TPU:1, one launch (start us, length us, event | category | flops | bytes accessed | tf_op | source)
XLA Modules:
  0.0 164.4 jit_solution(1956113529078299864)
XLA Ops:
  0.0 3.2 %collective-permute-start.3 = (bf16[8192,128]{1,0:T(8,128)(2,1)}, bf16[8192,128]{1,0:T(8,128)(2,1)}, u32[]{:S(2)}, u32[]{:S(2)}) collective-permute-start(bf16[8192,128]{1,0:T(8,128)(2,1)} %refs_14_.1), channel_id=1, source_target_pairs={{0,1},{1,0},{2,3},{3,2},{4,5},{5,4},{6,7},{7,6},{8,9},{9,8},{10,11... | collective-permute-start | bytes 6291464 | tf_op jit(solution)/shard_map/rows/ppermute | solution.py:69
  3.2 0.0 collective-permute-start.8
  3.2 1.9 %norm_rows.1.start = bf16[32,4224]{1,0:T(8,128)(2,1)} custom-call(s32[16]{0:T(128)} %group_ref.1, bf16[16,8192]{1,0:T(8,128)(2,1)} %rows_ref.1, f32[1,8192]{1,0:T(1,128)} %bitcast.16), custom_call_target="tpu_custom_call" | custom-call | tf_op jit(solution)/shard_map/rows/norm_rows/pallas_call | solution.py:98
  5.2 2.2 %collective-permute-start.1 = (bf16[32,4224]{1,0:T(8,128)(2,1)}, bf16[32,4224]{1,0:T(8,128)(2,1)S(1)}, u32[]{:S(2)}, u32[]{:S(2)}) collective-permute-start(bf16[32,4224]{1,0:T(8,128)(2,1)} %norm_rows.1.start), channel_id=1, source_target_pairs={{0,4},{1,17},{2,6},{3,19},{4,0},{5,21},{6,2},{7,23},{8,12},{9,25},... | collective-permute-start | bytes 811016 | tf_op jit(solution)/shard_map/rows/ppermute | solution.py:69
  7.3 1.7 %collective-permute-start.2 = (bf16[32,4224]{1,0:T(8,128)(2,1)}, bf16[32,4224]{1,0:T(8,128)(2,1)S(1)}, u32[]{:S(2)}, u32[]{:S(2)}) collective-permute-start(bf16[32,4224]{1,0:T(8,128)(2,1)} %norm_rows.1.start), channel_id=1, source_target_pairs={{0,6},{1,25},{2,4},{3,27},{4,2},{5,29},{6,0},{7,31},{8,14},{9,17},... | collective-permute-start | bytes 811016 | tf_op jit(solution)/shard_map/rows/ppermute | solution.py:69
  9.0 0.0 copy-start.12
  9.0 0.0 copy-start
  9.0 0.0 copy-start.1
  9.1 4.9 %first.1 = (f32[16,128]{1,0:T(8,128)}, f32[16,128]{1,0:T(8,128)}, f32[16,128]{1,0:T(8,128)}, f32[16,256]{1,0:T(8,128)}, f32[1,256]{1,0:T(1,128)}, /*index=5*/f32[1,8192]{1,0:T(1,128)}) custom-call(f32[16,8192]{1,0:T(8,128)} %state_ref.1, f32[1,8192]{1,0:T(1,128)} %bitcast.17, bf16[8192,128]{1,0:T(8,128)(2,1)} %refs_13_.3, bf16[8192,128]{1,0:T(8,128)(2,1)} %refs_14_.1, ...), custom_call_target="tpu_custom_call" | custom-call | tf_op jit(solution)/shard_map/first/first/pallas_call | solution.py:403
  13.9 0.0 collective-permute-done.3.refs_8_
  13.9 0.7 slice.9.refs_0_
  14.6 2.6 %collective-permute-done.2.f3 = bf16[32,4224]{1,0:T(8,128)(2,1)S(1)} collective-permute-done((bf16[32,4224]{1,0:T(8,128)(2,1)}, bf16[32,4224]{1,0:T(8,128)(2,1)S(1)}, u32[]{:S(2)}, u32[]{:S(2)}) %collective-permute-start.2) | collective-permute-done | bytes 270368 | tf_op jit(solution)/shard_map/rows/ppermute | solution.py:69
  17.3 0.1 lines.1
  17.3 2.6 %collective-permute-start.5 = (bf16[64,4224]{1,0:T(8,128)(2,1)S(1)}, bf16[64,4224]{1,0:T(8,128)(2,1)S(1)}, u32[]{:S(2)}, u32[]{:S(2)}) collective-permute-start(bf16[64,4224]{1,0:T(8,128)(2,1)S(1)} %get-tuple-element.47.refs_0_), channel_id=1, source_target_pairs={{0,24},{1,7},{2,26},{3,5},{4,28},{5,3},{6,30},{7,1},{8,16},{9,15},... | collective-permute-start | bytes 1622024 | tf_op jit(solution)/shard_map/rows/ppermute | solution.py:69
  19.9 0.3 multiply_cosine_fusion
  20.2 0.1 fusion.refs_2_
  20.3 0.1 subtract_convert_fusion.refs_3_
  20.4 0.6 slice.8
  21.7 0.1 select_reduce_fusion.1
  21.8 1.5 collective-permute-start.4
  23.3 0.2 collective-permute-start.7
  23.5 4.9 %collective-permute-done.6.refs_4_ = bf16[64,4224]{1,0:T(8,128)(2,1)S(1)} collective-permute-done((bf16[64,4224]{1,0:T(8,128)(2,1)S(1)}, bf16[64,4224]{1,0:T(8,128)(2,1)S(1)}, u32[]{:S(2)}, u32[]{:S(2)}) %collective-permute-start.6) | collective-permute-done | bytes 540704 | tf_op jit(solution)/shard_map/rows/ppermute | solution.py:69
  28.4 0.2 collective-permute-start.9
  28.6 0.1 select_reduce_fusion
  28.7 0.2 multiply_cosine_fusion.1
  28.9 5.2 %collective-permute-done.4.refs_1_ = bf16[64,4224]{1,0:T(8,128)(2,1)S(1)} collective-permute-done((bf16[64,4224]{1,0:T(8,128)(2,1)S(1)}, bf16[64,4224]{1,0:T(8,128)(2,1)S(1)}, u32[]{:S(2)}, u32[]{:S(2)}) %collective-permute-start.4) | collective-permute-done | bytes 540704 | tf_op jit(solution)/shard_map/rows/ppermute | solution.py:69
  34.2 3.9 %project.1 = (bf16[192,256]{1,0:T(8,128)(2,1)S(1)}, bf16[192,384]{1,0:T(8,128)(2,1)S(1)}, bf16[192,128]{1,0:T(8,128)(2,1)S(1)}, bf16[8192,512]{1,0:T(8,128)(2,1)S(1)}) custom-call(bf16[64,4224]{1,0:T(8,128)(2,1)S(1)} %get-tuple-element.47.refs_0_, bf16[64,4224]{1,0:T(8,128)(2,1)S(1)} %collective-permute-done.4.refs_1_, ...), custom_call_target="tpu_custom_call" | custom-call | tf_op jit(solution)/shard_map/project/project/pallas_call | solution.py:191
  38.1 2.8 %collective-permute-start.11 = (bf16[192,384]{1,0:T(8,128)(2,1)S(1)}, bf16[192,384]{1,0:T(8,128)(2,1)S(1)}, u32[]{:S(2)}, u32[]{:S(2)}) collective-permute-start(bf16[192,384]{1,0:T(8,128)(2,1)S(1)} %get-tuple-element.54), channel_id=1, source_target_pairs={{0,1},{1,0},{2,3},{3,2},{4,5},{5,4},{6,7},{7,6},{8,9},{9,8},{10,11... | collective-permute-start | bytes 442376 | tf_op jit(solution)/shard_map/project/ppermute | solution.py:69
  40.9 0.8 project_low.1.low_ref
  41.8 0.8 project_high.1
  42.6 2.0 %collective-permute-start.12 = (bf16[64,384]{1,0:T(8,128)(2,1)S(1)}, bf16[64,384]{1,0:T(8,128)(2,1)S(1)}, u32[]{:S(2)}, u32[]{:S(2)}) collective-permute-start(bf16[64,384]{1,0:T(8,128)(2,1)S(1)} %get-tuple-element.55), channel_id=1, source_target_pairs={{0,1},{1,0},{2,3},{3,2},{4,5},{5,4},{6,7},{7,6},{8,9},{9,8},{10,11... | collective-permute-start | bytes 147464 | tf_op jit(solution)/shard_map/project/ppermute | solution.py:69
  44.7 0.9 collective-permute-done.12.refs_5_
  45.5 1.4 finish.1
  47.0 7.0 %collective-permute-start.13 = (bf16[96,256]{1,0:T(8,128)(2,1)S(1)}, bf16[96,256]{1,0:T(8,128)(2,1)S(1)}, u32[]{:S(2)}, u32[]{:S(2)}) collective-permute-start(bf16[96,256]{1,0:T(8,128)(2,1)S(1)} %get-tuple-element.57), channel_id=1, source_target_pairs={{0,128},{32,160},{64,192},{96,224},{128,0},{160,32},{192,64},{224,... | collective-permute-start | bytes 147464 | tf_op jit(solution)/shard_map/project/ppermute | solution.py:560
  54.0 1.6 collective-permute-start.14
  55.6 0.1 pad_maximum_fusion.1.refs_0_
  55.7 2.9 %collective-permute-start.15 = (bf16[96,256]{1,0:T(8,128)(2,1)S(1)}, bf16[96,256]{1,0:T(8,128)(2,1)S(1)}, u32[]{:S(2)}, u32[]{:S(2)}) collective-permute-start(bf16[96,256]{1,0:T(8,128)(2,1)S(1)} %get-tuple-element.59), channel_id=1, source_target_pairs={{0,160},{32,192},{64,224},{96,0},{128,32},{160,64},{192,96},{224,1... | collective-permute-start | bytes 147464 | tf_op jit(solution)/shard_map/project/ppermute | solution.py:560
  58.6 1.2 collective-permute-start.16
  59.8 2.4 %collective-permute-start.17 = (bf16[96,256]{1,0:T(8,128)(2,1)S(1)}, bf16[96,256]{1,0:T(8,128)(2,1)S(1)}, u32[]{:S(2)}, u32[]{:S(2)}) collective-permute-start(bf16[96,256]{1,0:T(8,128)(2,1)S(1)} %get-tuple-element.61), channel_id=1, source_target_pairs={{0,192},{32,224},{64,0},{96,32},{128,64},{160,96},{192,128},{224,1... | collective-permute-start | bytes 147464 | tf_op jit(solution)/shard_map/project/ppermute | solution.py:560
  62.2 0.7 collective-permute-start.18
  62.9 1.9 %collective-permute-start.19 = (bf16[96,256]{1,0:T(8,128)(2,1)S(1)}, bf16[96,256]{1,0:T(8,128)(2,1)S(1)}, u32[]{:S(2)}, u32[]{:S(2)}) collective-permute-start(bf16[96,256]{1,0:T(8,128)(2,1)S(1)} %get-tuple-element.63), channel_id=1, source_target_pairs={{0,224},{32,0},{64,32},{96,64},{128,96},{160,128},{192,160},{224,1... | collective-permute-start | bytes 147464 | tf_op jit(solution)/shard_map/project/ppermute | solution.py:560
  64.9 0.1 copy.12
  65.0 0.1 broadcast_in_dim.41
  65.0 0.0 copy-start.4
  65.1 1.6 copy-done.4
  66.7 0.0 copy-start.3
  66.7 0.2 hold.1.refs_4_.refs_6_
  66.9 0.0 copy-start.2
  66.9 1.6 settle.1
  68.6 0.9 attend.4
  69.5 14.0 %all_to_all.35.refs_0_ = bf16[32,16,256]{2,1,0:T(8,128)(2,1)S(1)} all-to-all(bf16[32,16,256]{2,1,0:T(8,128)(2,1)S(1)} %get-tuple-element.75), channel_id=1, replica_groups=mesh['grp'=8,'head'=32] {'head'}, dimensions={0} | all-to-all | bytes 524288 | tf_op jit(solution)/shard_map/all_to_all | solution.py:576
  83.5 0.1 spread.4
  83.5 12.5 %all_to_all.36.refs_7_ = bf16[32,16,256]{2,1,0:T(8,128)(2,1)S(1)} all-to-all(bf16[32,16,256]{2,1,0:T(8,128)(2,1)S(1)} %get-tuple-element.76), channel_id=1, replica_groups=mesh['grp'=8,'head'=32] {'head'}, dimensions={0} | all-to-all | bytes 524288 | tf_op jit(solution)/shard_map/all_to_all | solution.py:580
  96.0 1.7 %attend.5 = (bf16[32,16,256]{2,1,0:T(8,128)(2,1)S(1)}, bf16[16,128]{1,0:T(8,128)(2,1)S(1)}, bf16[16,128]{1,0:T(8,128)(2,1)S(1)}) custom-call(f32[4,16,256]{2,1,0:T(8,128)S(1)} %pad_maximum_fusion.1.refs_0_, bf16[768,128]{1,0:T(8,128)(2,1)S(1)} %get-tuple-element.64.refs_1_, bf16[768,128]{1,0:T(8,128)(2,1)S(1)} %get-tuple-element.65.refs_2_, ...), custom_call_target="tpu_custom_call" | custom-call | tf_op jit(solution)/shard_map/attend/pallas_call | solution.py:476
  97.7 12.5 %all_to_all.37.refs_0_ = bf16[32,16,256]{2,1,0:T(8,128)(2,1)S(1)} all-to-all(bf16[32,16,256]{2,1,0:T(8,128)(2,1)S(1)} %get-tuple-element.79), channel_id=1, replica_groups=mesh['grp'=8,'head'=32] {'head'}, dimensions={0} | all-to-all | bytes 524288 | tf_op jit(solution)/shard_map/all_to_all | solution.py:576
  110.2 0.1 spread.5
  110.2 12.5 %all_to_all.38.refs_9_ = bf16[32,16,256]{2,1,0:T(8,128)(2,1)S(1)} all-to-all(bf16[32,16,256]{2,1,0:T(8,128)(2,1)S(1)} %get-tuple-element.81), channel_id=1, replica_groups=mesh['grp'=8,'head'=32] {'head'}, dimensions={0} | all-to-all | bytes 524288 | tf_op jit(solution)/shard_map/all_to_all | solution.py:580
  122.7 1.7 %attend.6 = (bf16[32,16,256]{2,1,0:T(8,128)(2,1)S(1)}, bf16[16,128]{1,0:T(8,128)(2,1)S(1)}, bf16[16,128]{1,0:T(8,128)(2,1)S(1)}) custom-call(f32[4,16,256]{2,1,0:T(8,128)S(1)} %pad_maximum_fusion.1.refs_0_, bf16[768,128]{1,0:T(8,128)(2,1)S(1)} %get-tuple-element.64.refs_1_, bf16[768,128]{1,0:T(8,128)(2,1)S(1)} %get-tuple-element.65.refs_2_, ...), custom_call_target="tpu_custom_call" | custom-call | tf_op jit(solution)/shard_map/attend/pallas_call | solution.py:476
  124.4 12.7 %all_to_all.39.refs_0_ = bf16[32,16,256]{2,1,0:T(8,128)(2,1)S(1)} all-to-all(bf16[32,16,256]{2,1,0:T(8,128)(2,1)S(1)} %get-tuple-element.84), channel_id=1, replica_groups=mesh['grp'=8,'head'=32] {'head'}, dimensions={0} | all-to-all | bytes 524288 | tf_op jit(solution)/shard_map/all_to_all | solution.py:576
  137.1 0.1 spread.6
  137.1 12.5 %all_to_all.40.refs_11_ = bf16[32,16,256]{2,1,0:T(8,128)(2,1)S(1)} all-to-all(bf16[32,16,256]{2,1,0:T(8,128)(2,1)S(1)} %get-tuple-element.86), channel_id=1, replica_groups=mesh['grp'=8,'head'=32] {'head'}, dimensions={0} | all-to-all | bytes 524288 | tf_op jit(solution)/shard_map/all_to_all | solution.py:580
  149.6 1.7 %attend.7 = (bf16[32,16,256]{2,1,0:T(8,128)(2,1)S(1)}, bf16[16,128]{1,0:T(8,128)(2,1)}, bf16[16,128]{1,0:T(8,128)(2,1)}) custom-call(f32[4,16,256]{2,1,0:T(8,128)S(1)} %pad_maximum_fusion.1.refs_0_, bf16[768,128]{1,0:T(8,128)(2,1)S(1)} %get-tuple-element.64.refs_1_, bf16[768,128]{1,0:T(8,128)(2,1)S(1)} %get-tuple-element.65.refs_2_, ...), custom_call_target="tpu_custom_call" | custom-call | tf_op jit(solution)/shard_map/attend/pallas_call | solution.py:476
  151.3 12.5 %all_to_all.41.refs_0_ = bf16[32,16,256]{2,1,0:T(8,128)(2,1)S(1)} all-to-all(bf16[32,16,256]{2,1,0:T(8,128)(2,1)S(1)} %get-tuple-element.87), channel_id=1, replica_groups=mesh['grp'=8,'head'=32] {'head'}, dimensions={0} | all-to-all | bytes 524288 | tf_op jit(solution)/shard_map/all_to_all | solution.py:576
  163.8 0.7 spread.7
  (45 shorter events, 0.1 us)
Async XLA Ops:
  0.0 13.9 %collective-permute-start.3 = (bf16[8192,128]{1,0:T(8,128)(2,1)}, bf16[8192,128]{1,0:T(8,128)(2,1)}, u32[]{:S(2)}, u32[]{:S(2)}) collective-permute-start(bf16[8192,128]{1,0:T(8,128)(2,1)} %refs_14_.1), channel_id=1, source_target_pairs={{0,1},{1,0},{2,3},{3,2},{4,5},{5,4},{6,7},{7,6},{8,9},{9,8},{10,11... | collective-permute-start | bytes 6291464 | tf_op jit(solution)/shard_map/rows/ppermute | solution.py:69
  3.2 25.7 %collective-permute-start.8 = (bf16[8192,128]{1,0:T(8,128)(2,1)}, bf16[8192,128]{1,0:T(8,128)(2,1)}, u32[]{:S(2)}, u32[]{:S(2)}) collective-permute-start(bf16[8192,128]{1,0:T(8,128)(2,1)} %refs_15_.1), channel_id=1, source_target_pairs={{0,1},{1,0},{2,3},{3,2},{4,5},{5,4},{6,7},{7,6},{8,9},{9,8},{10,11... | collective-permute-start | bytes 6291464 | tf_op jit(solution)/shard_map/rows/ppermute | solution.py:69
  5.1 9.5 %collective-permute-start = (bf16[32,4224]{1,0:T(8,128)(2,1)}, bf16[32,4224]{1,0:T(8,128)(2,1)S(1)}, u32[]{:S(2)}, u32[]{:S(2)}) collective-permute-start(bf16[32,4224]{1,0:T(8,128)(2,1)} %norm_rows.1.start), channel_id=1, source_target_pairs={{0,2},{1,9},{2,0},{3,11},{4,6},{5,13},{6,4},{7,15},{8,10},{9,1},{1... | collective-permute-start | bytes 811016 | tf_op jit(solution)/shard_map/rows/ppermute | solution.py:69
  5.2 9.5 %collective-permute-start.1 = (bf16[32,4224]{1,0:T(8,128)(2,1)}, bf16[32,4224]{1,0:T(8,128)(2,1)S(1)}, u32[]{:S(2)}, u32[]{:S(2)}) collective-permute-start(bf16[32,4224]{1,0:T(8,128)(2,1)} %norm_rows.1.start), channel_id=1, source_target_pairs={{0,4},{1,17},{2,6},{3,19},{4,0},{5,21},{6,2},{7,23},{8,12},{9,25},... | collective-permute-start | bytes 811016 | tf_op jit(solution)/shard_map/rows/ppermute | solution.py:69
  7.3 9.9 %collective-permute-start.2 = (bf16[32,4224]{1,0:T(8,128)(2,1)}, bf16[32,4224]{1,0:T(8,128)(2,1)S(1)}, u32[]{:S(2)}, u32[]{:S(2)}) collective-permute-start(bf16[32,4224]{1,0:T(8,128)(2,1)} %norm_rows.1.start), channel_id=1, source_target_pairs={{0,6},{1,25},{2,4},{3,27},{4,2},{5,29},{6,0},{7,31},{8,14},{9,17},... | collective-permute-start | bytes 811016 | tf_op jit(solution)/shard_map/rows/ppermute | solution.py:69
  9.0 8.2 %copy-start.5 = (bf16[32,4224]{1,0:T(8,128)(2,1)S(1)}, bf16[32,4224]{1,0:T(8,128)(2,1)}, u32[]{:S(2)}) copy-start(bf16[32,4224]{1,0:T(8,128)(2,1)} %norm_rows.1.start) | copy-start | bytes 811012
  9.0 12.7 %copy-start.12 = (s32[8,16]{1,0:T(8,128)S(1)}, s32[8,16]{1,0:T(8,128)}, u32[]{:S(2)}) copy-start(s32[8,16]{1,0:T(8,128)} %param.11) | copy-start | bytes 1540
  9.0 25.2 %copy-start = (bf16[8192,128]{1,0:T(8,128)(2,1)S(1)}, bf16[8192,128]{1,0:T(8,128)(2,1)}, u32[]{:S(2)}) copy-start(bf16[8192,128]{1,0:T(8,128)(2,1)} %refs_14_.1) | copy-start | bytes 6291460
  9.0 25.2 %copy-start.1 = (bf16[8192,128]{1,0:T(8,128)(2,1)S(1)}, bf16[8192,128]{1,0:T(8,128)(2,1)}, u32[]{:S(2)}) copy-start(bf16[8192,128]{1,0:T(8,128)(2,1)} %refs_15_.1) | copy-start | bytes 6291460
  17.3 11.3 %collective-permute-start.5 = (bf16[64,4224]{1,0:T(8,128)(2,1)S(1)}, bf16[64,4224]{1,0:T(8,128)(2,1)S(1)}, u32[]{:S(2)}, u32[]{:S(2)}) collective-permute-start(bf16[64,4224]{1,0:T(8,128)(2,1)S(1)} %get-tuple-element.47.refs_0_), channel_id=1, source_target_pairs={{0,24},{1,7},{2,26},{3,5},{4,28},{5,3},{6,30},{7,1},{8,16},{9,15},... | collective-permute-start | bytes 1622024 | tf_op jit(solution)/shard_map/rows/ppermute | solution.py:69
  19.9 8.5 %collective-permute-start.6 = (bf16[64,4224]{1,0:T(8,128)(2,1)S(1)}, bf16[64,4224]{1,0:T(8,128)(2,1)S(1)}, u32[]{:S(2)}, u32[]{:S(2)}) collective-permute-start(bf16[64,4224]{1,0:T(8,128)(2,1)S(1)} %get-tuple-element.48.refs_3_), channel_id=1, source_target_pairs={{0,8},{1,3},{2,10},{3,1},{4,12},{5,7},{6,14},{7,5},{8,0},{9,11},{1... | collective-permute-start | bytes 1622024 | tf_op jit(solution)/shard_map/rows/ppermute | solution.py:69
  21.8 12.4 %collective-permute-start.4 = (bf16[64,4224]{1,0:T(8,128)(2,1)S(1)}, bf16[64,4224]{1,0:T(8,128)(2,1)S(1)}, u32[]{:S(2)}, u32[]{:S(2)}) collective-permute-start(bf16[64,4224]{1,0:T(8,128)(2,1)S(1)} %get-tuple-element.47.refs_0_), channel_id=1, source_target_pairs={{0,8},{1,3},{2,10},{3,1},{4,12},{5,7},{6,14},{7,5},{8,0},{9,11},{1... | collective-permute-start | bytes 1622024 | tf_op jit(solution)/shard_map/rows/ppermute | solution.py:69
  23.3 10.9 %collective-permute-start.7 = (bf16[64,4224]{1,0:T(8,128)(2,1)S(1)}, bf16[64,4224]{1,0:T(8,128)(2,1)S(1)}, u32[]{:S(2)}, u32[]{:S(2)}) collective-permute-start(bf16[64,4224]{1,0:T(8,128)(2,1)S(1)} %get-tuple-element.48.refs_3_), channel_id=1, source_target_pairs={{0,24},{1,7},{2,26},{3,5},{4,28},{5,3},{6,30},{7,1},{8,16},{9,15},... | collective-permute-start | bytes 1622024 | tf_op jit(solution)/shard_map/rows/ppermute | solution.py:69
  28.4 13.4 %collective-permute-start.9 = (bf16[64,4224]{1,0:T(8,128)(2,1)S(1)}, bf16[64,4224]{1,0:T(8,128)(2,1)S(1)}, u32[]{:S(2)}, u32[]{:S(2)}) collective-permute-start(bf16[64,4224]{1,0:T(8,128)(2,1)S(1)} %collective-permute-done.6.refs_4_), channel_id=1, source_target_pairs={{0,24},{1,7},{2,26},{3,5},{4,28},{5,3},{6,30},{7,1},{8,16},{9,15},... | collective-permute-start | bytes 1622024 | tf_op jit(solution)/shard_map/rows/ppermute | solution.py:69
  28.6 12.3 %collective-permute-start.10 = (bf16[64,4224]{1,0:T(8,128)(2,1)S(1)}, bf16[64,4224]{1,0:T(8,128)(2,1)S(1)}, u32[]{:S(2)}, u32[]{:S(2)}) collective-permute-start(bf16[64,4224]{1,0:T(8,128)(2,1)S(1)} %collective-permute-done.5.refs_2_), channel_id=1, source_target_pairs={{0,8},{1,3},{2,10},{3,1},{4,12},{5,7},{6,14},{7,5},{8,0},{9,11},{1... | collective-permute-start | bytes 1622024 | tf_op jit(solution)/shard_map/rows/ppermute | solution.py:69
  38.1 6.5 %collective-permute-start.11 = (bf16[192,384]{1,0:T(8,128)(2,1)S(1)}, bf16[192,384]{1,0:T(8,128)(2,1)S(1)}, u32[]{:S(2)}, u32[]{:S(2)}) collective-permute-start(bf16[192,384]{1,0:T(8,128)(2,1)S(1)} %get-tuple-element.54), channel_id=1, source_target_pairs={{0,1},{1,0},{2,3},{3,2},{4,5},{5,4},{6,7},{7,6},{8,9},{9,8},{10,11... | collective-permute-start | bytes 442376 | tf_op jit(solution)/shard_map/project/ppermute | solution.py:69
  42.6 2.9 %collective-permute-start.12 = (bf16[64,384]{1,0:T(8,128)(2,1)S(1)}, bf16[64,384]{1,0:T(8,128)(2,1)S(1)}, u32[]{:S(2)}, u32[]{:S(2)}) collective-permute-start(bf16[64,384]{1,0:T(8,128)(2,1)S(1)} %get-tuple-element.55), channel_id=1, source_target_pairs={{0,1},{1,0},{2,3},{3,2},{4,5},{5,4},{6,7},{7,6},{8,9},{9,8},{10,11... | collective-permute-start | bytes 147464 | tf_op jit(solution)/shard_map/project/ppermute | solution.py:69
  47.0 15.2 %collective-permute-start.13 = (bf16[96,256]{1,0:T(8,128)(2,1)S(1)}, bf16[96,256]{1,0:T(8,128)(2,1)S(1)}, u32[]{:S(2)}, u32[]{:S(2)}) collective-permute-start(bf16[96,256]{1,0:T(8,128)(2,1)S(1)} %get-tuple-element.57), channel_id=1, source_target_pairs={{0,128},{32,160},{64,192},{96,224},{128,0},{160,32},{192,64},{224,... | collective-permute-start | bytes 147464 | tf_op jit(solution)/shard_map/project/ppermute | solution.py:560
  54.0 9.0 %collective-permute-start.14 = (bf16[96,256]{1,0:T(8,128)(2,1)S(1)}, bf16[96,256]{1,0:T(8,128)(2,1)S(1)}, u32[]{:S(2)}, u32[]{:S(2)}) collective-permute-start(bf16[96,256]{1,0:T(8,128)(2,1)S(1)} %get-tuple-element.58), channel_id=1, source_target_pairs={{0,96},{32,128},{64,160},{96,192},{128,224},{160,0},{192,32},{224,... | collective-permute-start | bytes 147464 | tf_op jit(solution)/shard_map/project/ppermute | solution.py:560
  55.7 11.2 %collective-permute-start.15 = (bf16[96,256]{1,0:T(8,128)(2,1)S(1)}, bf16[96,256]{1,0:T(8,128)(2,1)S(1)}, u32[]{:S(2)}, u32[]{:S(2)}) collective-permute-start(bf16[96,256]{1,0:T(8,128)(2,1)S(1)} %get-tuple-element.59), channel_id=1, source_target_pairs={{0,160},{32,192},{64,224},{96,0},{128,32},{160,64},{192,96},{224,1... | collective-permute-start | bytes 147464 | tf_op jit(solution)/shard_map/project/ppermute | solution.py:560
  58.6 8.3 %collective-permute-start.16 = (bf16[96,256]{1,0:T(8,128)(2,1)S(1)}, bf16[96,256]{1,0:T(8,128)(2,1)S(1)}, u32[]{:S(2)}, u32[]{:S(2)}) collective-permute-start(bf16[96,256]{1,0:T(8,128)(2,1)S(1)} %get-tuple-element.60), channel_id=1, source_target_pairs={{0,64},{32,96},{64,128},{96,160},{128,192},{160,224},{192,0},{224,... | collective-permute-start | bytes 147464 | tf_op jit(solution)/shard_map/project/ppermute | solution.py:560
  59.8 7.1 %collective-permute-start.17 = (bf16[96,256]{1,0:T(8,128)(2,1)S(1)}, bf16[96,256]{1,0:T(8,128)(2,1)S(1)}, u32[]{:S(2)}, u32[]{:S(2)}) collective-permute-start(bf16[96,256]{1,0:T(8,128)(2,1)S(1)} %get-tuple-element.61), channel_id=1, source_target_pairs={{0,192},{32,224},{64,0},{96,32},{128,64},{160,96},{192,128},{224,1... | collective-permute-start | bytes 147464 | tf_op jit(solution)/shard_map/project/ppermute | solution.py:560
  62.2 4.7 %collective-permute-start.18 = (bf16[96,256]{1,0:T(8,128)(2,1)S(1)}, bf16[96,256]{1,0:T(8,128)(2,1)S(1)}, u32[]{:S(2)}, u32[]{:S(2)}) collective-permute-start(bf16[96,256]{1,0:T(8,128)(2,1)S(1)} %get-tuple-element.62), channel_id=1, source_target_pairs={{0,32},{32,64},{64,96},{96,128},{128,160},{160,192},{192,224},{224... | collective-permute-start | bytes 147464 | tf_op jit(solution)/shard_map/project/ppermute | solution.py:560
  62.9 4.0 %collective-permute-start.19 = (bf16[96,256]{1,0:T(8,128)(2,1)S(1)}, bf16[96,256]{1,0:T(8,128)(2,1)S(1)}, u32[]{:S(2)}, u32[]{:S(2)}) collective-permute-start(bf16[96,256]{1,0:T(8,128)(2,1)S(1)} %get-tuple-element.63), channel_id=1, source_target_pairs={{0,224},{32,0},{64,32},{96,64},{128,96},{160,128},{192,160},{224,1... | collective-permute-start | bytes 147464 | tf_op jit(solution)/shard_map/project/ppermute | solution.py:560
  65.0 1.6 copy-start.4
  66.6 1.9 %copy-start.6 = (f32[1,8192]{1,0:T(1,128)S(1)}, f32[1,8192]{1,0:T(1,128)}, u32[]{:S(2)}) copy-start(f32[1,8192]{1,0:T(1,128)} %get-tuple-element.72.refs_10_.refs_8_.refs_12_) | copy-start | bytes 98308
  66.6 1.9 %copy-start.7 = (f32[16,256]{1,0:T(8,128)S(1)}, f32[16,256]{1,0:T(8,128)}, u32[]{:S(2)}) copy-start(f32[16,256]{1,0:T(8,128)} %get-tuple-element.70.refs_8_.refs_1_) | copy-start | bytes 49156
  66.7 1.9 %copy-start.8 = (f32[1,256]{1,0:T(1,128)S(1)}, f32[1,256]{1,0:T(1,128)}, u32[]{:S(2)}) copy-start(f32[1,256]{1,0:T(1,128)} %get-tuple-element.71.refs_9_.refs_2_) | copy-start | bytes 3076
  66.7 1.9 %copy-start.9 = (f32[16,128]{1,0:T(8,128)S(1)}, f32[16,128]{1,0:T(8,128)}, u32[]{:S(2)}) copy-start(f32[16,128]{1,0:T(8,128)} %get-tuple-element.67.refs_5_) | copy-start | bytes 24580
  66.7 1.9 %copy-start.10 = (f32[16,128]{1,0:T(8,128)S(1)}, f32[16,128]{1,0:T(8,128)}, u32[]{:S(2)}) copy-start(f32[16,128]{1,0:T(8,128)} %get-tuple-element.68.refs_6_) | copy-start | bytes 24580
  66.7 1.9 %copy-start.11 = (f32[16,128]{1,0:T(8,128)S(1)}, f32[16,128]{1,0:T(8,128)}, u32[]{:S(2)}) copy-start(f32[16,128]{1,0:T(8,128)} %get-tuple-element.69.refs_7_) | copy-start | bytes 24580
  66.7 16.8 %copy-start.3 = (bf16[8192,128]{1,0:T(8,128)(2,1)S(1)}, bf16[8192,128]{1,0:T(8,128)(2,1)}, u32[]{:S(2)}) copy-start(bf16[8192,128]{1,0:T(8,128)(2,1)} %refs_13_.3) | copy-start | bytes 6291460
  66.9 16.6 %copy-start.2 = (bf16[8192,128]{1,0:T(8,128)(2,1)S(1)}, bf16[8192,128]{1,0:T(8,128)(2,1)}, u32[]{:S(2)}) copy-start(bf16[8192,128]{1,0:T(8,128)(2,1)} %refs_15_.1) | copy-start | bytes 6291460

commit v9 on v8

--- a/solution.py
+++ b/solution.py
@@ -405,7 +405,7 @@
         out_shape=(small,) * 3
         + tuple(jax.ShapeDtypeStruct(d, jnp.float32) for d in ((n, share), (1, share), (1, width))),
         in_specs=[whole] * 5 + [pl.BlockSpec(memory_space=pl.ANY)] * len(deps),
-        compiler_params=params(54),
+        compiler_params=params(60),
         name="first",
     )(state, gain.reshape(1, -1), *weights, *deps)
 

time: 165 us -> 165 us (level)
  no operation moved by 1% of the time
where the time goes in v9:
time: 165 us; the launch traced here: 164 us
  blocking collectives  88.8 us (54%)
  starting transfers between devices  32.6 us (20%)
  Pallas kernels  22.4 us (14%)
  waiting for transfers between devices  13.9 us (8%)
  local copies, waits for them, and re-layouts  4.66 us (3%)
    all_to_all x4, blocking collectives, per_device(): lax.all_to_all(term, 'head', split_axis=0, concat_axis=0, tiled=True)  51.4 us
    all_to_all x3, blocking collectives, per_device(): lax.all_to_all(spreading[0], 'head', split_axis=0, concat_axis=0, tiled=T...  37.4 us
    ppermute x7, starting transfers between devices, per_device(): arrived.append(lax.ppermute(leaving[hop], 'grp', pairs))  17.8 us
    ppermute x13, starting transfers between devices, send(): return lax.ppermute(values, 'head', pairs)  14.8 us
    ppermute x13, waiting for transfers between devices, send(): return lax.ppermute(values, 'head', pairs)  13.9 us
    pallas_call x4, Pallas kernels, attend(): pl.pallas_call(lambda *refs: attend_kernel(step, *refs), out_shape=(jax.S...  5.99 us
    pallas_call x1, Pallas kernels, first(): pl.pallas_call(first_kernel, out_shape=(small,) * 3 + tuple((jax.ShapeDty...  4.86 us
    pallas_call x1, Pallas kernels, project(): pl.pallas_call(lambda *refs: project_kernel(count, *refs), out_shape=proj...  3.9 us
  transfers between devices with their start and end apart: 20, of which 4 were waited for; matrix products, arithmetic and copies ran while one was open for 2% of the time, Pallas kernels for 8%

profile of v9, /device:TPU:1, one launch (start us, length us, event | category | flops | bytes accessed | tf_op | source)
XLA Modules:
  0.0 164.4 jit_solution(1275857538931573352)
XLA Ops:
  0.0 3.2 %collective-permute-start.3 = (bf16[8192,128]{1,0:T(8,128)(2,1)}, bf16[8192,128]{1,0:T(8,128)(2,1)}, u32[]{:S(2)}, u32[]{:S(2)}) collective-permute-start(bf16[8192,128]{1,0:T(8,128)(2,1)} %refs_14_.1), channel_id=1, source_target_pairs={{0,1},{1,0},{2,3},{3,2},{4,5},{5,4},{6,7},{7,6},{8,9},{9,8},{10,11... | collective-permute-start | bytes 6291464 | tf_op jit(solution)/shard_map/rows/ppermute | solution.py:69
  3.2 0.0 collective-permute-start.8
  3.2 1.9 %norm_rows.1.start = bf16[32,4224]{1,0:T(8,128)(2,1)} custom-call(s32[16]{0:T(128)} %group_ref.1, bf16[16,8192]{1,0:T(8,128)(2,1)} %rows_ref.1, f32[1,8192]{1,0:T(1,128)} %bitcast.16), custom_call_target="tpu_custom_call" | custom-call | tf_op jit(solution)/shard_map/rows/norm_rows/pallas_call | solution.py:98
  5.2 2.2 %collective-permute-start.1 = (bf16[32,4224]{1,0:T(8,128)(2,1)}, bf16[32,4224]{1,0:T(8,128)(2,1)S(1)}, u32[]{:S(2)}, u32[]{:S(2)}) collective-permute-start(bf16[32,4224]{1,0:T(8,128)(2,1)} %norm_rows.1.start), channel_id=1, source_target_pairs={{0,4},{1,17},{2,6},{3,19},{4,0},{5,21},{6,2},{7,23},{8,12},{9,25},... | collective-permute-start | bytes 811016 | tf_op jit(solution)/shard_map/rows/ppermute | solution.py:69
  7.3 1.7 %collective-permute-start.2 = (bf16[32,4224]{1,0:T(8,128)(2,1)}, bf16[32,4224]{1,0:T(8,128)(2,1)S(1)}, u32[]{:S(2)}, u32[]{:S(2)}) collective-permute-start(bf16[32,4224]{1,0:T(8,128)(2,1)} %norm_rows.1.start), channel_id=1, source_target_pairs={{0,6},{1,25},{2,4},{3,27},{4,2},{5,29},{6,0},{7,31},{8,14},{9,17},... | collective-permute-start | bytes 811016 | tf_op jit(solution)/shard_map/rows/ppermute | solution.py:69
  9.0 0.0 copy-start.12
  9.0 0.0 copy-start
  9.0 4.9 %first.1 = (f32[16,128]{1,0:T(8,128)}, f32[16,128]{1,0:T(8,128)}, f32[16,128]{1,0:T(8,128)}, f32[16,256]{1,0:T(8,128)}, f32[1,256]{1,0:T(1,128)}, /*index=5*/f32[1,8192]{1,0:T(1,128)}) custom-call(f32[16,8192]{1,0:T(8,128)} %state_ref.1, f32[1,8192]{1,0:T(1,128)} %bitcast.17, bf16[8192,128]{1,0:T(8,128)(2,1)} %refs_13_.3, bf16[8192,128]{1,0:T(8,128)(2,1)} %refs_14_.1, ...), custom_call_target="tpu_custom_call" | custom-call | tf_op jit(solution)/shard_map/first/first/pallas_call | solution.py:403
  13.9 0.7 slice.9.refs_0_
  14.6 0.0 collective-permute-done.1.f2
  14.6 2.6 %collective-permute-done.2.f3 = bf16[32,4224]{1,0:T(8,128)(2,1)S(1)} collective-permute-done((bf16[32,4224]{1,0:T(8,128)(2,1)}, bf16[32,4224]{1,0:T(8,128)(2,1)S(1)}, u32[]{:S(2)}, u32[]{:S(2)}) %collective-permute-start.2) | collective-permute-done | bytes 270368 | tf_op jit(solution)/shard_map/rows/ppermute | solution.py:69
  17.3 0.1 lines.1
  17.3 2.6 %collective-permute-start.5 = (bf16[64,4224]{1,0:T(8,128)(2,1)S(1)}, bf16[64,4224]{1,0:T(8,128)(2,1)S(1)}, u32[]{:S(2)}, u32[]{:S(2)}) collective-permute-start(bf16[64,4224]{1,0:T(8,128)(2,1)S(1)} %get-tuple-element.47.refs_0_), channel_id=1, source_target_pairs={{0,24},{1,7},{2,26},{3,5},{4,28},{5,3},{6,30},{7,1},{8,16},{9,15},... | collective-permute-start | bytes 1622024 | tf_op jit(solution)/shard_map/rows/ppermute | solution.py:69
  19.9 0.3 multiply_cosine_fusion
  20.2 0.1 fusion.refs_2_
  20.3 0.1 subtract_convert_fusion.refs_3_
  20.4 0.6 slice.8
  21.7 0.1 select_reduce_fusion.1
  21.8 1.5 collective-permute-start.4
  23.3 0.2 collective-permute-start.7
  23.5 4.9 %collective-permute-done.6.refs_4_ = bf16[64,4224]{1,0:T(8,128)(2,1)S(1)} collective-permute-done((bf16[64,4224]{1,0:T(8,128)(2,1)S(1)}, bf16[64,4224]{1,0:T(8,128)(2,1)S(1)}, u32[]{:S(2)}, u32[]{:S(2)}) %collective-permute-start.6) | collective-permute-done | bytes 540704 | tf_op jit(solution)/shard_map/rows/ppermute | solution.py:69
  28.4 0.2 collective-permute-start.9
  28.6 0.1 select_reduce_fusion
  28.7 0.2 multiply_cosine_fusion.1
  28.9 5.2 %collective-permute-done.4.refs_1_ = bf16[64,4224]{1,0:T(8,128)(2,1)S(1)} collective-permute-done((bf16[64,4224]{1,0:T(8,128)(2,1)S(1)}, bf16[64,4224]{1,0:T(8,128)(2,1)S(1)}, u32[]{:S(2)}, u32[]{:S(2)}) %collective-permute-start.4) | collective-permute-done | bytes 540704 | tf_op jit(solution)/shard_map/rows/ppermute | solution.py:69
  34.2 1.6 copy-done.1
  35.8 3.9 %project.1 = (bf16[192,256]{1,0:T(8,128)(2,1)S(1)}, bf16[192,384]{1,0:T(8,128)(2,1)S(1)}, bf16[192,128]{1,0:T(8,128)(2,1)S(1)}, bf16[8192,512]{1,0:T(8,128)(2,1)S(1)}) custom-call(bf16[64,4224]{1,0:T(8,128)(2,1)S(1)} %get-tuple-element.47.refs_0_, bf16[64,4224]{1,0:T(8,128)(2,1)S(1)} %collective-permute-done.4.refs_1_, ...), custom_call_target="tpu_custom_call" | custom-call | tf_op jit(solution)/shard_map/project/project/pallas_call | solution.py:191
  39.7 2.8 %collective-permute-start.11 = (bf16[192,384]{1,0:T(8,128)(2,1)S(1)}, bf16[192,384]{1,0:T(8,128)(2,1)S(1)}, u32[]{:S(2)}, u32[]{:S(2)}) collective-permute-start(bf16[192,384]{1,0:T(8,128)(2,1)S(1)} %get-tuple-element.54), channel_id=1, source_target_pairs={{0,1},{1,0},{2,3},{3,2},{4,5},{5,4},{6,7},{7,6},{8,9},{9,8},{10,11... | collective-permute-start | bytes 442376 | tf_op jit(solution)/shard_map/project/ppermute | solution.py:69
  42.5 0.8 project_low.1.low_ref
  43.4 0.8 project_high.1
  44.2 0.5 collective-permute-start.12
  44.7 1.0 collective-permute-done.12.refs_5_
  45.7 1.4 finish.1
  47.1 7.0 %collective-permute-start.13 = (bf16[96,256]{1,0:T(8,128)(2,1)S(1)}, bf16[96,256]{1,0:T(8,128)(2,1)S(1)}, u32[]{:S(2)}, u32[]{:S(2)}) collective-permute-start(bf16[96,256]{1,0:T(8,128)(2,1)S(1)} %get-tuple-element.57), channel_id=1, source_target_pairs={{0,128},{32,160},{64,192},{96,224},{128,0},{160,32},{192,64},{224,... | collective-permute-start | bytes 147464 | tf_op jit(solution)/shard_map/project/ppermute | solution.py:560
  54.1 1.6 %collective-permute-start.14 = (bf16[96,256]{1,0:T(8,128)(2,1)S(1)}, bf16[96,256]{1,0:T(8,128)(2,1)S(1)}, u32[]{:S(2)}, u32[]{:S(2)}) collective-permute-start(bf16[96,256]{1,0:T(8,128)(2,1)S(1)} %get-tuple-element.58), channel_id=1, source_target_pairs={{0,96},{32,128},{64,160},{96,192},{128,224},{160,0},{192,32},{224,... | collective-permute-start | bytes 147464 | tf_op jit(solution)/shard_map/project/ppermute | solution.py:560
  55.8 0.1 pad_maximum_fusion.1.refs_0_
  55.9 2.9 %collective-permute-start.15 = (bf16[96,256]{1,0:T(8,128)(2,1)S(1)}, bf16[96,256]{1,0:T(8,128)(2,1)S(1)}, u32[]{:S(2)}, u32[]{:S(2)}) collective-permute-start(bf16[96,256]{1,0:T(8,128)(2,1)S(1)} %get-tuple-element.59), channel_id=1, source_target_pairs={{0,160},{32,192},{64,224},{96,0},{128,32},{160,64},{192,96},{224,1... | collective-permute-start | bytes 147464 | tf_op jit(solution)/shard_map/project/ppermute | solution.py:560
  58.8 1.2 collective-permute-start.16
  60.0 2.4 %collective-permute-start.17 = (bf16[96,256]{1,0:T(8,128)(2,1)S(1)}, bf16[96,256]{1,0:T(8,128)(2,1)S(1)}, u32[]{:S(2)}, u32[]{:S(2)}) collective-permute-start(bf16[96,256]{1,0:T(8,128)(2,1)S(1)} %get-tuple-element.61), channel_id=1, source_target_pairs={{0,192},{32,224},{64,0},{96,32},{128,64},{160,96},{192,128},{224,1... | collective-permute-start | bytes 147464 | tf_op jit(solution)/shard_map/project/ppermute | solution.py:560
  62.3 0.7 collective-permute-start.18
  63.1 1.9 %collective-permute-start.19 = (bf16[96,256]{1,0:T(8,128)(2,1)S(1)}, bf16[96,256]{1,0:T(8,128)(2,1)S(1)}, u32[]{:S(2)}, u32[]{:S(2)}) collective-permute-start(bf16[96,256]{1,0:T(8,128)(2,1)S(1)} %get-tuple-element.63), channel_id=1, source_target_pairs={{0,224},{32,0},{64,32},{96,64},{128,96},{160,128},{192,160},{224,1... | collective-permute-start | bytes 147464 | tf_op jit(solution)/shard_map/project/ppermute | solution.py:560
  65.0 0.1 copy.12
  65.1 0.1 broadcast_in_dim.41
  65.2 0.0 copy-start.4
  65.2 1.6 copy-done.4
  66.8 0.0 copy-start.3
  66.8 0.2 hold.1.refs_4_.refs_6_
  67.0 0.0 copy-start.2
  67.1 1.6 settle.1
  68.8 0.9 attend.4
  69.7 13.8 %all_to_all.35.refs_0_ = bf16[32,16,256]{2,1,0:T(8,128)(2,1)S(1)} all-to-all(bf16[32,16,256]{2,1,0:T(8,128)(2,1)S(1)} %get-tuple-element.75), channel_id=1, replica_groups=mesh['grp'=8,'head'=32] {'head'}, dimensions={0} | all-to-all | bytes 524288 | tf_op jit(solution)/shard_map/all_to_all | solution.py:576
  83.5 0.1 spread.4
  83.5 12.5 %all_to_all.36.refs_7_ = bf16[32,16,256]{2,1,0:T(8,128)(2,1)S(1)} all-to-all(bf16[32,16,256]{2,1,0:T(8,128)(2,1)S(1)} %get-tuple-element.76), channel_id=1, replica_groups=mesh['grp'=8,'head'=32] {'head'}, dimensions={0} | all-to-all | bytes 524288 | tf_op jit(solution)/shard_map/all_to_all | solution.py:580
  96.0 1.7 %attend.5 = (bf16[32,16,256]{2,1,0:T(8,128)(2,1)S(1)}, bf16[16,128]{1,0:T(8,128)(2,1)S(1)}, bf16[16,128]{1,0:T(8,128)(2,1)S(1)}) custom-call(f32[4,16,256]{2,1,0:T(8,128)S(1)} %pad_maximum_fusion.1.refs_0_, bf16[768,128]{1,0:T(8,128)(2,1)S(1)} %get-tuple-element.64.refs_1_, bf16[768,128]{1,0:T(8,128)(2,1)S(1)} %get-tuple-element.65.refs_2_, ...), custom_call_target="tpu_custom_call" | custom-call | tf_op jit(solution)/shard_map/attend/pallas_call | solution.py:476
  97.7 12.5 %all_to_all.37.refs_0_ = bf16[32,16,256]{2,1,0:T(8,128)(2,1)S(1)} all-to-all(bf16[32,16,256]{2,1,0:T(8,128)(2,1)S(1)} %get-tuple-element.79), channel_id=1, replica_groups=mesh['grp'=8,'head'=32] {'head'}, dimensions={0} | all-to-all | bytes 524288 | tf_op jit(solution)/shard_map/all_to_all | solution.py:576
  110.2 0.1 spread.5
  110.2 12.5 %all_to_all.38.refs_9_ = bf16[32,16,256]{2,1,0:T(8,128)(2,1)S(1)} all-to-all(bf16[32,16,256]{2,1,0:T(8,128)(2,1)S(1)} %get-tuple-element.81), channel_id=1, replica_groups=mesh['grp'=8,'head'=32] {'head'}, dimensions={0} | all-to-all | bytes 524288 | tf_op jit(solution)/shard_map/all_to_all | solution.py:580
  122.7 1.7 %attend.6 = (bf16[32,16,256]{2,1,0:T(8,128)(2,1)S(1)}, bf16[16,128]{1,0:T(8,128)(2,1)S(1)}, bf16[16,128]{1,0:T(8,128)(2,1)S(1)}) custom-call(f32[4,16,256]{2,1,0:T(8,128)S(1)} %pad_maximum_fusion.1.refs_0_, bf16[768,128]{1,0:T(8,128)(2,1)S(1)} %get-tuple-element.64.refs_1_, bf16[768,128]{1,0:T(8,128)(2,1)S(1)} %get-tuple-element.65.refs_2_, ...), custom_call_target="tpu_custom_call" | custom-call | tf_op jit(solution)/shard_map/attend/pallas_call | solution.py:476
  124.4 12.7 %all_to_all.39.refs_0_ = bf16[32,16,256]{2,1,0:T(8,128)(2,1)S(1)} all-to-all(bf16[32,16,256]{2,1,0:T(8,128)(2,1)S(1)} %get-tuple-element.84), channel_id=1, replica_groups=mesh['grp'=8,'head'=32] {'head'}, dimensions={0} | all-to-all | bytes 524288 | tf_op jit(solution)/shard_map/all_to_all | solution.py:576
  137.1 0.1 spread.6
  137.1 12.5 %all_to_all.40.refs_11_ = bf16[32,16,256]{2,1,0:T(8,128)(2,1)S(1)} all-to-all(bf16[32,16,256]{2,1,0:T(8,128)(2,1)S(1)} %get-tuple-element.86), channel_id=1, replica_groups=mesh['grp'=8,'head'=32] {'head'}, dimensions={0} | all-to-all | bytes 524288 | tf_op jit(solution)/shard_map/all_to_all | solution.py:580
  149.6 1.7 %attend.7 = (bf16[32,16,256]{2,1,0:T(8,128)(2,1)S(1)}, bf16[16,128]{1,0:T(8,128)(2,1)}, bf16[16,128]{1,0:T(8,128)(2,1)}) custom-call(f32[4,16,256]{2,1,0:T(8,128)S(1)} %pad_maximum_fusion.1.refs_0_, bf16[768,128]{1,0:T(8,128)(2,1)S(1)} %get-tuple-element.64.refs_1_, bf16[768,128]{1,0:T(8,128)(2,1)S(1)} %get-tuple-element.65.refs_2_, ...), custom_call_target="tpu_custom_call" | custom-call | tf_op jit(solution)/shard_map/attend/pallas_call | solution.py:476
  151.3 12.5 %all_to_all.41.refs_0_ = bf16[32,16,256]{2,1,0:T(8,128)(2,1)S(1)} all-to-all(bf16[32,16,256]{2,1,0:T(8,128)(2,1)S(1)} %get-tuple-element.87), channel_id=1, replica_groups=mesh['grp'=8,'head'=32] {'head'}, dimensions={0} | all-to-all | bytes 524288 | tf_op jit(solution)/shard_map/all_to_all | solution.py:576
  163.8 0.7 spread.7
  (45 shorter events, 0.1 us)
Async XLA Ops:
  0.0 13.9 %collective-permute-start.3 = (bf16[8192,128]{1,0:T(8,128)(2,1)}, bf16[8192,128]{1,0:T(8,128)(2,1)}, u32[]{:S(2)}, u32[]{:S(2)}) collective-permute-start(bf16[8192,128]{1,0:T(8,128)(2,1)} %refs_14_.1), channel_id=1, source_target_pairs={{0,1},{1,0},{2,3},{3,2},{4,5},{5,4},{6,7},{7,6},{8,9},{9,8},{10,11... | collective-permute-start | bytes 6291464 | tf_op jit(solution)/shard_map/rows/ppermute | solution.py:69
  3.2 25.7 %collective-permute-start.8 = (bf16[8192,128]{1,0:T(8,128)(2,1)}, bf16[8192,128]{1,0:T(8,128)(2,1)}, u32[]{:S(2)}, u32[]{:S(2)}) collective-permute-start(bf16[8192,128]{1,0:T(8,128)(2,1)} %refs_15_.1), channel_id=1, source_target_pairs={{0,1},{1,0},{2,3},{3,2},{4,5},{5,4},{6,7},{7,6},{8,9},{9,8},{10,11... | collective-permute-start | bytes 6291464 | tf_op jit(solution)/shard_map/rows/ppermute | solution.py:69
  5.1 9.5 %collective-permute-start = (bf16[32,4224]{1,0:T(8,128)(2,1)}, bf16[32,4224]{1,0:T(8,128)(2,1)S(1)}, u32[]{:S(2)}, u32[]{:S(2)}) collective-permute-start(bf16[32,4224]{1,0:T(8,128)(2,1)} %norm_rows.1.start), channel_id=1, source_target_pairs={{0,2},{1,9},{2,0},{3,11},{4,6},{5,13},{6,4},{7,15},{8,10},{9,1},{1... | collective-permute-start | bytes 811016 | tf_op jit(solution)/shard_map/rows/ppermute | solution.py:69
  5.2 9.5 %collective-permute-start.1 = (bf16[32,4224]{1,0:T(8,128)(2,1)}, bf16[32,4224]{1,0:T(8,128)(2,1)S(1)}, u32[]{:S(2)}, u32[]{:S(2)}) collective-permute-start(bf16[32,4224]{1,0:T(8,128)(2,1)} %norm_rows.1.start), channel_id=1, source_target_pairs={{0,4},{1,17},{2,6},{3,19},{4,0},{5,21},{6,2},{7,23},{8,12},{9,25},... | collective-permute-start | bytes 811016 | tf_op jit(solution)/shard_map/rows/ppermute | solution.py:69
  7.3 9.9 %collective-permute-start.2 = (bf16[32,4224]{1,0:T(8,128)(2,1)}, bf16[32,4224]{1,0:T(8,128)(2,1)S(1)}, u32[]{:S(2)}, u32[]{:S(2)}) collective-permute-start(bf16[32,4224]{1,0:T(8,128)(2,1)} %norm_rows.1.start), channel_id=1, source_target_pairs={{0,6},{1,25},{2,4},{3,27},{4,2},{5,29},{6,0},{7,31},{8,14},{9,17},... | collective-permute-start | bytes 811016 | tf_op jit(solution)/shard_map/rows/ppermute | solution.py:69
  9.0 8.2 %copy-start.5 = (bf16[32,4224]{1,0:T(8,128)(2,1)S(1)}, bf16[32,4224]{1,0:T(8,128)(2,1)}, u32[]{:S(2)}) copy-start(bf16[32,4224]{1,0:T(8,128)(2,1)} %norm_rows.1.start) | copy-start | bytes 811012
  9.0 12.7 %copy-start.12 = (s32[8,16]{1,0:T(8,128)S(1)}, s32[8,16]{1,0:T(8,128)}, u32[]{:S(2)}) copy-start(s32[8,16]{1,0:T(8,128)} %param.11) | copy-start | bytes 1540
  9.0 25.2 %copy-start = (bf16[8192,128]{1,0:T(8,128)(2,1)S(1)}, bf16[8192,128]{1,0:T(8,128)(2,1)}, u32[]{:S(2)}) copy-start(bf16[8192,128]{1,0:T(8,128)(2,1)} %refs_14_.1) | copy-start | bytes 6291460
  17.3 11.3 %collective-permute-start.5 = (bf16[64,4224]{1,0:T(8,128)(2,1)S(1)}, bf16[64,4224]{1,0:T(8,128)(2,1)S(1)}, u32[]{:S(2)}, u32[]{:S(2)}) collective-permute-start(bf16[64,4224]{1,0:T(8,128)(2,1)S(1)} %get-tuple-element.47.refs_0_), channel_id=1, source_target_pairs={{0,24},{1,7},{2,26},{3,5},{4,28},{5,3},{6,30},{7,1},{8,16},{9,15},... | collective-permute-start | bytes 1622024 | tf_op jit(solution)/shard_map/rows/ppermute | solution.py:69
  19.9 8.5 %collective-permute-start.6 = (bf16[64,4224]{1,0:T(8,128)(2,1)S(1)}, bf16[64,4224]{1,0:T(8,128)(2,1)S(1)}, u32[]{:S(2)}, u32[]{:S(2)}) collective-permute-start(bf16[64,4224]{1,0:T(8,128)(2,1)S(1)} %get-tuple-element.48.refs_3_), channel_id=1, source_target_pairs={{0,8},{1,3},{2,10},{3,1},{4,12},{5,7},{6,14},{7,5},{8,0},{9,11},{1... | collective-permute-start | bytes 1622024 | tf_op jit(solution)/shard_map/rows/ppermute | solution.py:69
  21.8 12.4 %collective-permute-start.4 = (bf16[64,4224]{1,0:T(8,128)(2,1)S(1)}, bf16[64,4224]{1,0:T(8,128)(2,1)S(1)}, u32[]{:S(2)}, u32[]{:S(2)}) collective-permute-start(bf16[64,4224]{1,0:T(8,128)(2,1)S(1)} %get-tuple-element.47.refs_0_), channel_id=1, source_target_pairs={{0,8},{1,3},{2,10},{3,1},{4,12},{5,7},{6,14},{7,5},{8,0},{9,11},{1... | collective-permute-start | bytes 1622024 | tf_op jit(solution)/shard_map/rows/ppermute | solution.py:69
  23.3 10.9 %collective-permute-start.7 = (bf16[64,4224]{1,0:T(8,128)(2,1)S(1)}, bf16[64,4224]{1,0:T(8,128)(2,1)S(1)}, u32[]{:S(2)}, u32[]{:S(2)}) collective-permute-start(bf16[64,4224]{1,0:T(8,128)(2,1)S(1)} %get-tuple-element.48.refs_3_), channel_id=1, source_target_pairs={{0,24},{1,7},{2,26},{3,5},{4,28},{5,3},{6,30},{7,1},{8,16},{9,15},... | collective-permute-start | bytes 1622024 | tf_op jit(solution)/shard_map/rows/ppermute | solution.py:69
  28.4 15.0 %collective-permute-start.9 = (bf16[64,4224]{1,0:T(8,128)(2,1)S(1)}, bf16[64,4224]{1,0:T(8,128)(2,1)S(1)}, u32[]{:S(2)}, u32[]{:S(2)}) collective-permute-start(bf16[64,4224]{1,0:T(8,128)(2,1)S(1)} %collective-permute-done.6.refs_4_), channel_id=1, source_target_pairs={{0,24},{1,7},{2,26},{3,5},{4,28},{5,3},{6,30},{7,1},{8,16},{9,15},... | collective-permute-start | bytes 1622024 | tf_op jit(solution)/shard_map/rows/ppermute | solution.py:69
  28.6 13.9 %collective-permute-start.10 = (bf16[64,4224]{1,0:T(8,128)(2,1)S(1)}, bf16[64,4224]{1,0:T(8,128)(2,1)S(1)}, u32[]{:S(2)}, u32[]{:S(2)}) collective-permute-start(bf16[64,4224]{1,0:T(8,128)(2,1)S(1)} %collective-permute-done.5.refs_2_), channel_id=1, source_target_pairs={{0,8},{1,3},{2,10},{3,1},{4,12},{5,7},{6,14},{7,5},{8,0},{9,11},{1... | collective-permute-start | bytes 1622024 | tf_op jit(solution)/shard_map/rows/ppermute | solution.py:69
  34.2 1.6 copy-start.1
  39.7 5.0 %collective-permute-start.11 = (bf16[192,384]{1,0:T(8,128)(2,1)S(1)}, bf16[192,384]{1,0:T(8,128)(2,1)S(1)}, u32[]{:S(2)}, u32[]{:S(2)}) collective-permute-start(bf16[192,384]{1,0:T(8,128)(2,1)S(1)} %get-tuple-element.54), channel_id=1, source_target_pairs={{0,1},{1,0},{2,3},{3,2},{4,5},{5,4},{6,7},{7,6},{8,9},{9,8},{10,11... | collective-permute-start | bytes 442376 | tf_op jit(solution)/shard_map/project/ppermute | solution.py:69
  44.2 1.5 collective-permute-start.12
  47.1 15.2 %collective-permute-start.13 = (bf16[96,256]{1,0:T(8,128)(2,1)S(1)}, bf16[96,256]{1,0:T(8,128)(2,1)S(1)}, u32[]{:S(2)}, u32[]{:S(2)}) collective-permute-start(bf16[96,256]{1,0:T(8,128)(2,1)S(1)} %get-tuple-element.57), channel_id=1, source_target_pairs={{0,128},{32,160},{64,192},{96,224},{128,0},{160,32},{192,64},{224,... | collective-permute-start | bytes 147464 | tf_op jit(solution)/shard_map/project/ppermute | solution.py:560
  54.1 9.0 %collective-permute-start.14 = (bf16[96,256]{1,0:T(8,128)(2,1)S(1)}, bf16[96,256]{1,0:T(8,128)(2,1)S(1)}, u32[]{:S(2)}, u32[]{:S(2)}) collective-permute-start(bf16[96,256]{1,0:T(8,128)(2,1)S(1)} %get-tuple-element.58), channel_id=1, source_target_pairs={{0,96},{32,128},{64,160},{96,192},{128,224},{160,0},{192,32},{224,... | collective-permute-start | bytes 147464 | tf_op jit(solution)/shard_map/project/ppermute | solution.py:560
  55.9 11.2 %collective-permute-start.15 = (bf16[96,256]{1,0:T(8,128)(2,1)S(1)}, bf16[96,256]{1,0:T(8,128)(2,1)S(1)}, u32[]{:S(2)}, u32[]{:S(2)}) collective-permute-start(bf16[96,256]{1,0:T(8,128)(2,1)S(1)} %get-tuple-element.59), channel_id=1, source_target_pairs={{0,160},{32,192},{64,224},{96,0},{128,32},{160,64},{192,96},{224,1... | collective-permute-start | bytes 147464 | tf_op jit(solution)/shard_map/project/ppermute | solution.py:560
  58.8 8.3 %collective-permute-start.16 = (bf16[96,256]{1,0:T(8,128)(2,1)S(1)}, bf16[96,256]{1,0:T(8,128)(2,1)S(1)}, u32[]{:S(2)}, u32[]{:S(2)}) collective-permute-start(bf16[96,256]{1,0:T(8,128)(2,1)S(1)} %get-tuple-element.60), channel_id=1, source_target_pairs={{0,64},{32,96},{64,128},{96,160},{128,192},{160,224},{192,0},{224,... | collective-permute-start | bytes 147464 | tf_op jit(solution)/shard_map/project/ppermute | solution.py:560
  60.0 7.1 %collective-permute-start.17 = (bf16[96,256]{1,0:T(8,128)(2,1)S(1)}, bf16[96,256]{1,0:T(8,128)(2,1)S(1)}, u32[]{:S(2)}, u32[]{:S(2)}) collective-permute-start(bf16[96,256]{1,0:T(8,128)(2,1)S(1)} %get-tuple-element.61), channel_id=1, source_target_pairs={{0,192},{32,224},{64,0},{96,32},{128,64},{160,96},{192,128},{224,1... | collective-permute-start | bytes 147464 | tf_op jit(solution)/shard_map/project/ppermute | solution.py:560
  62.3 4.7 %collective-permute-start.18 = (bf16[96,256]{1,0:T(8,128)(2,1)S(1)}, bf16[96,256]{1,0:T(8,128)(2,1)S(1)}, u32[]{:S(2)}, u32[]{:S(2)}) collective-permute-start(bf16[96,256]{1,0:T(8,128)(2,1)S(1)} %get-tuple-element.62), channel_id=1, source_target_pairs={{0,32},{32,64},{64,96},{96,128},{128,160},{160,192},{192,224},{224... | collective-permute-start | bytes 147464 | tf_op jit(solution)/shard_map/project/ppermute | solution.py:560
  63.1 4.0 %collective-permute-start.19 = (bf16[96,256]{1,0:T(8,128)(2,1)S(1)}, bf16[96,256]{1,0:T(8,128)(2,1)S(1)}, u32[]{:S(2)}, u32[]{:S(2)}) collective-permute-start(bf16[96,256]{1,0:T(8,128)(2,1)S(1)} %get-tuple-element.63), channel_id=1, source_target_pairs={{0,224},{32,0},{64,32},{96,64},{128,96},{160,128},{192,160},{224,1... | collective-permute-start | bytes 147464 | tf_op jit(solution)/shard_map/project/ppermute | solution.py:560
  65.2 1.6 copy-start.4
  66.8 1.9 %copy-start.6 = (f32[1,8192]{1,0:T(1,128)S(1)}, f32[1,8192]{1,0:T(1,128)}, u32[]{:S(2)}) copy-start(f32[1,8192]{1,0:T(1,128)} %get-tuple-element.72.refs_10_.refs_8_.refs_12_) | copy-start | bytes 98308
  66.8 1.9 %copy-start.7 = (f32[16,256]{1,0:T(8,128)S(1)}, f32[16,256]{1,0:T(8,128)}, u32[]{:S(2)}) copy-start(f32[16,256]{1,0:T(8,128)} %get-tuple-element.70.refs_8_.refs_1_) | copy-start | bytes 49156
  66.8 1.9 %copy-start.8 = (f32[1,256]{1,0:T(1,128)S(1)}, f32[1,256]{1,0:T(1,128)}, u32[]{:S(2)}) copy-start(f32[1,256]{1,0:T(1,128)} %get-tuple-element.71.refs_9_.refs_2_) | copy-start | bytes 3076
  66.8 1.9 %copy-start.9 = (f32[16,128]{1,0:T(8,128)S(1)}, f32[16,128]{1,0:T(8,128)}, u32[]{:S(2)}) copy-start(f32[16,128]{1,0:T(8,128)} %get-tuple-element.67.refs_5_) | copy-start | bytes 24580
  66.8 1.9 %copy-start.10 = (f32[16,128]{1,0:T(8,128)S(1)}, f32[16,128]{1,0:T(8,128)}, u32[]{:S(2)}) copy-start(f32[16,128]{1,0:T(8,128)} %get-tuple-element.68.refs_6_) | copy-start | bytes 24580
  66.8 1.9 %copy-start.11 = (f32[16,128]{1,0:T(8,128)S(1)}, f32[16,128]{1,0:T(8,128)}, u32[]{:S(2)}) copy-start(f32[16,128]{1,0:T(8,128)} %get-tuple-element.69.refs_7_) | copy-start | bytes 24580
  66.8 16.6 %copy-start.3 = (bf16[8192,128]{1,0:T(8,128)(2,1)S(1)}, bf16[8192,128]{1,0:T(8,128)(2,1)}, u32[]{:S(2)}) copy-start(bf16[8192,128]{1,0:T(8,128)(2,1)} %refs_13_.3) | copy-start | bytes 6291460
  67.0 16.5 %copy-start.2 = (bf16[8192,128]{1,0:T(8,128)(2,1)S(1)}, bf16[8192,128]{1,0:T(8,128)(2,1)}, u32[]{:S(2)}) copy-start(bf16[8192,128]{1,0:T(8,128)(2,1)} %refs_15_.1) | copy-start | bytes 6291460
